TPU v7x, 32 devices: a whole 2x2x4 slice. The times are simulated.
32 devices in a mesh: group: 4 (over z), row: 8 (over y, x, core).
Axes of the slice: x: 2, y: 2, z: 4, core: 2. Of those that a mesh axis runs over, the one named last changes fastest.
Arguments:
- start_basis: float32 [256, 16, 128], P(('group', 'row')), may hold values from -6 to 6
- tiles: bfloat16 [256, 16, 128, 128], P(('group', 'row')), may hold values from -60000 to 60000
- tile_cols: int32 [256, 16], P(('group', 'row')), may hold values from 0 to 27, as said below
- tile_count: int32 [256], P(('group', 'row')), may hold values from 10 to 16, as said below
- recv_list: int32 [4, 8, 8, 2], P('group', 'row'), may hold values from -1 to 255, as said below
Outputs:
- krylov: float32 [3, 256, 16, 128], P(None, ('group', 'row'))
Inputs may be any that keep to these rules, and one draw needn't show every extreme that they name: For each reader device and each other device of its range, recv_list names distinct blocks of that peer in its first slots and -1 in the rest; a reader's own entry is all -1; every reader gets exactly 2 blocks from some peer. tile_cols never names an empty receive slot, nor a rim slot of a range that does not exist (before the first or after the last group); every filled receive slot and every existing rim slot is named by some tile slot below 10. `tile_count`: every device has a row block with all 16 tiles live.
All inputs are finite; a program needn't handle non-finite values.
Results may differ from a plain program's by a relative error of at most 0.0003.
Values sent between devices are 32-bit elements; how exact they have to be, the bound alone decides.
No kernel may reach another device: no remote copies, remote signals or barrier semaphores. Data moves between devices by JAX's collectives and lax.ppermute only.
A program may use at most 64 MiB of HBM per device.

v0:
```python
import jax
import jax.numpy as jnp
from jax import lax
from jax.sharding import PartitionSpec as P

SLOTS = 2
RIM = 2
ITERS = 3


def padded(x, sides, width):
    for axis, dim in sides:
        count, length = (lax.axis_size(axis), x.shape[dim])
        up = [(i, (i + 1) % count) for i in range(count - 1)]
        down = [(j, i) for i, j in up]
        last = lax.slice_in_dim(x, length - width, length, axis=dim)
        leading = lax.slice_in_dim(x, 0, width, axis=dim)
        before = lax.ppermute(last, axis, up)
        after = lax.ppermute(leading, axis, down)
        x = jnp.concatenate([before, x, after], axis=dim)
    return x


def orthonormal(applied, gram_sum, row_total):
    vectors = applied.shape[1]
    factor = jnp.linalg.cholesky(gram_sum / row_total)
    inverse = lax.linalg.triangular_solve(
        factor, jnp.eye(vectors, dtype=jnp.float32), left_side=True, lower=True
    )
    return jnp.einsum("kl,bli->bki", inverse, applied, precision=lax.Precision.HIGHEST)


def local(start_basis, tiles, tile_cols, tile_count, recv_list):
    groups = lax.axis_size("group")
    peers = lax.axis_size("row")
    group_at = lax.axis_index("group")
    blocks = tiles.shape[0]
    per_row = tiles.shape[1]
    tile_side = tiles.shape[2]
    row_total = groups * peers * blocks * tile_side
    live_mask = (jnp.arange(per_row, dtype=jnp.int32)[None, :] < tile_count[:, None]).astype(
        jnp.float32
    )
    wide_tiles = tiles.astype(jnp.float32)
    sum_sq = jnp.einsum(
        "btij,bt->bi", wide_tiles * wide_tiles, live_mask, precision=lax.Precision.HIGHEST
    )
    inv_root = (1e-06 + sum_sq) ** (-0.25)
    wanted = recv_list.reshape(peers, SLOTS)
    gather_pick = jnp.clip(wanted - group_at * peers * blocks, 0, peers * blocks - 1).reshape(-1)
    results = []
    basis = start_basis
    for step_at in range(ITERS):
        scaled = basis * inv_root[:, None, :]
        rimmed = padded(scaled, (("group", 0),), RIM)
        group_all = lax.all_gather(scaled, "row", axis=0, tiled=True)
        received = jnp.take(group_all, gather_pick, axis=0)
        extended = jnp.concatenate([scaled, received, rimmed[:RIM], rimmed[blocks + RIM :]], axis=0)
        picked = jnp.take(extended, tile_cols, axis=0) * live_mask[:, :, None, None]
        product = jnp.einsum(
            "btij,btkj->bki",
            tiles,
            picked,
            precision=lax.Precision.HIGHEST,
            preferred_element_type=jnp.float32,
        )
        applied = product * inv_root[:, None, :]
        partial_value = jnp.einsum("bki,bli->kl", applied, applied, precision=lax.Precision.HIGHEST)
        gram_sum = lax.psum(partial_value, ("group", "row"))
        basis = orthonormal(applied, gram_sum, row_total)
        results.append(basis)
    return jnp.stack(results)


def solution(mesh):
    placed = (
        P(("group", "row"), None, None),
        P(("group", "row"), None, None, None),
        P(("group", "row"), None),
        P(("group", "row")),
        P("group", "row", None, None),
    )
    return jax.shard_map(
        local,
        mesh=mesh,
        in_specs=placed,
        out_specs=P(None, ("group", "row"), None, None),
        check_vma=False,
    )
```

profile of v0, /device:TPU:0, one launch (start us, length us, event | category | flops | bytes accessed | tf_op | source)
XLA Modules:
  0.0 211.5 jit_solution(16292445278265960483)
XLA Ops:
  0.0 4.5 %multiply_reduce_fusion = f32[8,16,128]{2,1,0:T(8,128)S(1)} fusion(bf16[8,16,128,128]{3,2,1,0:T(8,128)(2,1)} %param.13), kind=kLoop, calls=%fused_computation.6 | loop fusion | flops 6275072 | bytes 4259840 | tf_op jit(solution)/shard_map/btij,bt->bi/reduce_sum | solution.py:45
  4.5 0.0 copy-done.1
  4.5 0.0 copy-done.3
  4.5 0.1 fusion.26
  4.6 0.2 fusion.12
  4.8 0.0 copy-done
  4.8 5.0 %collective-permute-start = (f32[2,16,128]{2,1,0:T(8,128)S(1)}, f32[2,16,128]{2,1,0:T(8,128)S(1)}, u32[]{:S(2)}, u32[]{:S(2)}) collective-permute-start(f32[2,16,128]{2,1,0:T(8,128)S(1)} %get-tuple-element.13), channel_id=1, source_target_pairs={{0,8},{8,16},{16,24},{1,9},{9,17},{17,25},{2,10},{10,18},{18,26},{... | collective-permute-start | bytes 49160 | tf_op jit(solution)/shard_map/ppermute | solution.py:18
  9.8 1.3 collective-permute-start.1
  11.1 0.1 copy.20
  11.2 0.1 min.12
  11.3 9.9 %all_gather.9 = f32[64,16,128]{2,1,0:T(8,128)S(1)} all-gather(f32[8,16,128]{2,1,0:T(8,128)S(1)} %broadcast_multiply_fusion), channel_id=1, replica_groups=mesh['group'=4,'row'=8] {'row'}, dimensions={0}, use_global_device_ids=true | all-gather | bytes 589824 | tf_op jit(solution)/shard_map/all_gather | solution.py:56
  21.2 0.1 reshape.114
  21.2 0.6 gather_fusion
  21.8 0.1 broadcast_select_fusion.2
  21.9 0.0 collective-permute-done
  21.9 0.0 collective-permute-done.1
  22.0 0.8 gather_fusion.1
  22.7 5.2 %fusion.2 = f32[8,16,128]{2,1,0:T(8,128)S(1)} fusion(bf16[8,16,128,128]{3,2,1,0:T(8,128)(2,1)} %param.13, f32[8,16,16,128]{3,2,1,0:T(8,128)S(1)} %bitcast.92, f32[8,16]{1,0:T(8,128)S(1)} %get-tuple-element.15, pred[8,16]{1,0:T(8,128)(4,1)S(1)} %get-tuple-element.21, f32[8,128]{1,0:T(8,128)S(1)} %add_power_fusion), kind=kOutput, calls=%fused_computation.13 | convolution fusion | flops 403193856 | bytes 5313152 | tf_op jit(solution)/shard_map/btij,btkj->bki/dot_general | solution.py:60
  27.9 0.2 convolution_bitcast_fusion.9
  28.1 40.7 %psum.21 = f32[16,16]{0,1:T(8,128)S(1)} all-reduce(f32[16,16]{0,1:T(8,128)S(1)} %convolution_bitcast_fusion.9), channel_id=1, replica_groups=mesh['group'=4,'row'=8] {'group','row'}, use_global_device_ids=true, to_apply=%region_1.0 | all-reduce | flops 256 | bytes 2048 | tf_op jit(solution)/shard_map/psum | solution.py:69
  68.8 0.1 copy.22
  68.9 1.5 cholesky.59
  70.4 0.6 compare_reduce_fusion.2
  71.0 0.6 fusion.17
  71.7 1.2 custom-call.7
  72.9 0.2 convolution_bitcast_fusion.8
  73.1 0.2 bitcast_multiply_fusion.1
  73.3 10.6 %all_gather.10 = f32[64,16,128]{2,1,0:T(8,128)S(1)} all-gather(f32[8,16,128]{2,1,0:T(8,128)S(1)} %get-tuple-element.17), channel_id=1, replica_groups=mesh['group'=4,'row'=8] {'row'}, dimensions={0}, use_global_device_ids=true | all-gather | bytes 589824 | tf_op jit(solution)/shard_map/all_gather | solution.py:56
  84.0 3.4 %collective-permute-start.2 = (f32[2,16,128]{2,1,0:T(8,128)S(1)}, f32[2,16,128]{2,1,0:T(8,128)S(1)}, u32[]{:S(2)}, u32[]{:S(2)}) collective-permute-start(f32[2,16,128]{2,1,0:T(8,128)S(1)} %get-tuple-element.10), channel_id=1, source_target_pairs={{0,8},{8,16},{16,24},{1,9},{9,17},{17,25},{2,10},{10,18},{18,26},{... | collective-permute-start | bytes 49160 | tf_op jit(solution)/shard_map/ppermute | solution.py:18
  87.4 1.3 collective-permute-start.3
  88.7 0.6 gather_fusion.2
  89.2 0.1 broadcast_select_fusion.1
  89.3 0.0 collective-permute-done.2
  89.3 3.7 %collective-permute-done.3 = f32[2,16,128]{2,1,0:T(8,128)S(1)} collective-permute-done((f32[2,16,128]{2,1,0:T(8,128)S(1)}, f32[2,16,128]{2,1,0:T(8,128)S(1)}, u32[]{:S(2)}, u32[]{:S(2)}) %collective-permute-start.3) | collective-permute-done | bytes 16416 | tf_op jit(solution)/shard_map/ppermute | solution.py:19
  93.0 0.8 gather_fusion.3
  93.8 5.2 %fusion.1 = f32[8,16,128]{2,1,0:T(8,128)S(1)} fusion(bf16[8,16,128,128]{3,2,1,0:T(8,128)(2,1)} %param.13, f32[8,16,16,128]{3,2,1,0:T(8,128)S(1)} %bitcast.93, f32[8,16]{1,0:T(8,128)S(1)} %get-tuple-element.15, pred[8,16]{1,0:T(8,128)(4,1)S(1)} %get-tuple-element.21, f32[8,128]{1,0:T(8,128)S(1)} %add_power_fusion), kind=kOutput, calls=%fused_computation.11 | convolution fusion | flops 403193856 | bytes 5313152 | tf_op jit(solution)/shard_map/btij,btkj->bki/dot_general | solution.py:60
  99.0 0.2 convolution_bitcast_fusion.7
  99.1 39.2 %psum.22 = f32[16,16]{0,1:T(8,128)S(1)} all-reduce(f32[16,16]{0,1:T(8,128)S(1)} %convolution_bitcast_fusion.7), channel_id=1, replica_groups=mesh['group'=4,'row'=8] {'group','row'}, use_global_device_ids=true, to_apply=%region_4.9 | all-reduce | flops 256 | bytes 2048 | tf_op jit(solution)/shard_map/psum | solution.py:69
  138.4 0.1 copy.24
  138.5 1.5 cholesky.70
  140.0 0.6 compare_reduce_fusion.1
  140.6 0.6 fusion.18
  141.3 1.2 custom-call.8
  142.5 0.2 convolution_bitcast_fusion.6
  142.7 0.2 bitcast_multiply_fusion
  142.9 10.6 %all_gather.11 = f32[64,16,128]{2,1,0:T(8,128)S(1)} all-gather(f32[8,16,128]{2,1,0:T(8,128)S(1)} %get-tuple-element.19), channel_id=1, replica_groups=mesh['group'=4,'row'=8] {'row'}, dimensions={0}, use_global_device_ids=true | all-gather | bytes 589824 | tf_op jit(solution)/shard_map/all_gather | solution.py:56
  153.6 2.4 %collective-permute-start.4 = (f32[2,16,128]{2,1,0:T(8,128)S(1)}, f32[2,16,128]{2,1,0:T(8,128)S(1)}, u32[]{:S(2)}, u32[]{:S(2)}) collective-permute-start(f32[2,16,128]{2,1,0:T(8,128)S(1)} %get-tuple-element.6), channel_id=1, source_target_pairs={{0,8},{8,16},{16,24},{1,9},{9,17},{17,25},{2,10},{10,18},{18,26},{... | collective-permute-start | bytes 49160 | tf_op jit(solution)/shard_map/ppermute | solution.py:18
  156.0 1.5 collective-permute-start.5
  157.5 0.6 gather_fusion.4
  158.1 0.1 broadcast_select_fusion
  158.2 0.0 collective-permute-done.4
  158.2 3.5 %collective-permute-done.5 = f32[2,16,128]{2,1,0:T(8,128)S(1)} collective-permute-done((f32[2,16,128]{2,1,0:T(8,128)S(1)}, f32[2,16,128]{2,1,0:T(8,128)S(1)}, u32[]{:S(2)}, u32[]{:S(2)}) %collective-permute-start.5) | collective-permute-done | bytes 16416 | tf_op jit(solution)/shard_map/ppermute | solution.py:19
  161.7 0.8 gather_fusion.5
  162.4 5.2 %fusion = f32[8,16,128]{2,1,0:T(8,128)S(1)} fusion(bf16[8,16,128,128]{3,2,1,0:T(8,128)(2,1)} %param.13, f32[8,16,16,128]{3,2,1,0:T(8,128)S(1)} %bitcast.91, f32[8,16]{1,0:T(8,128)S(1)} %get-tuple-element.15, pred[8,16]{1,0:T(8,128)(4,1)S(1)} %get-tuple-element.21, f32[8,128]{1,0:T(8,128)S(1)} %add_power_fusion), kind=kOutput, calls=%fused_computation.9 | convolution fusion | flops 403193856 | bytes 5313152 | tf_op jit(solution)/shard_map/btij,btkj->bki/dot_general | solution.py:60
  167.6 0.2 convolution_bitcast_fusion.5
  167.8 38.5 %psum.23 = f32[16,16]{0,1:T(8,128)S(1)} all-reduce(f32[16,16]{0,1:T(8,128)S(1)} %convolution_bitcast_fusion.5), channel_id=1, replica_groups=mesh['group'=4,'row'=8] {'group','row'}, use_global_device_ids=true, to_apply=%region_5.10 | all-reduce | flops 256 | bytes 2048 | tf_op jit(solution)/shard_map/psum | solution.py:69
  206.3 0.1 copy.26
  206.4 1.5 cholesky.81
  207.8 0.6 compare_reduce_fusion
  208.5 0.6 fusion.19
  209.1 1.2 custom-call.9
  210.4 0.2 convolution_bitcast_fusion.4
  210.6 0.2 convolution_bitcast_fusion
  210.8 0.7 pad_maximum_fusion.3
  (28 shorter events, 0.2 us)
Async XLA Ops:
  0.0 4.5 %copy-start.1 = (s32[8,16]{1,0:T(8,128)S(1)}, s32[8,16]{1,0:T(8,128)}, u32[]{:S(2)}) copy-start(s32[8,16]{1,0:T(8,128)} %param.14) | copy-start | bytes 1540
  0.0 4.5 %copy-start.3 = (s32[8]{0:T(128)S(1)}, s32[8]{0:T(128)}, u32[]{:S(2)}) copy-start(s32[8]{0:T(128)} %param.15) | copy-start | bytes 100
  0.0 4.8 %copy-start = (f32[8,16,128]{2,1,0:T(8,128)S(1)}, f32[8,16,128]{2,1,0:T(8,128)}, u32[]{:S(2)}) copy-start(f32[8,16,128]{2,1,0:T(8,128)} %param.12) | copy-start | bytes 196612
  0.0 11.1 %copy-start.2 = (s32[1,1,8,2]{2,3,1,0:T(2,128)S(1)}, s32[1,1,8,2]{2,3,1,0:T(2,128)}, u32[]{:S(2)}) copy-start(s32[1,1,8,2]{2,3,1,0:T(2,128)} %param.16) | copy-start | bytes 196
  4.8 17.1 %collective-permute-start = (f32[2,16,128]{2,1,0:T(8,128)S(1)}, f32[2,16,128]{2,1,0:T(8,128)S(1)}, u32[]{:S(2)}, u32[]{:S(2)}) collective-permute-start(f32[2,16,128]{2,1,0:T(8,128)S(1)} %get-tuple-element.13), channel_id=1, source_target_pairs={{0,8},{8,16},{16,24},{1,9},{9,17},{17,25},{2,10},{10,18},{18,26},{... | collective-permute-start | bytes 49160 | tf_op jit(solution)/shard_map/ppermute | solution.py:18
  9.8 12.2 %collective-permute-start.1 = (f32[2,16,128]{2,1,0:T(8,128)S(1)}, f32[2,16,128]{2,1,0:T(8,128)S(1)}, u32[]{:S(2)}, u32[]{:S(2)}) collective-permute-start(f32[2,16,128]{2,1,0:T(8,128)S(1)} %get-tuple-element.14), channel_id=1, source_target_pairs={{8,0},{16,8},{24,16},{9,1},{17,9},{25,17},{10,2},{18,10},{26,18},{... | collective-permute-start | bytes 49160 | tf_op jit(solution)/shard_map/ppermute | solution.py:19
  84.0 5.4 %collective-permute-start.2 = (f32[2,16,128]{2,1,0:T(8,128)S(1)}, f32[2,16,128]{2,1,0:T(8,128)S(1)}, u32[]{:S(2)}, u32[]{:S(2)}) collective-permute-start(f32[2,16,128]{2,1,0:T(8,128)S(1)} %get-tuple-element.10), channel_id=1, source_target_pairs={{0,8},{8,16},{16,24},{1,9},{9,17},{17,25},{2,10},{10,18},{18,26},{... | collective-permute-start | bytes 49160 | tf_op jit(solution)/shard_map/ppermute | solution.py:18
  87.4 5.6 %collective-permute-start.3 = (f32[2,16,128]{2,1,0:T(8,128)S(1)}, f32[2,16,128]{2,1,0:T(8,128)S(1)}, u32[]{:S(2)}, u32[]{:S(2)}) collective-permute-start(f32[2,16,128]{2,1,0:T(8,128)S(1)} %get-tuple-element.12), channel_id=1, source_target_pairs={{8,0},{16,8},{24,16},{9,1},{17,9},{25,17},{10,2},{18,10},{26,18},{... | collective-permute-start | bytes 49160 | tf_op jit(solution)/shard_map/ppermute | solution.py:19
  153.6 4.6 %collective-permute-start.4 = (f32[2,16,128]{2,1,0:T(8,128)S(1)}, f32[2,16,128]{2,1,0:T(8,128)S(1)}, u32[]{:S(2)}, u32[]{:S(2)}) collective-permute-start(f32[2,16,128]{2,1,0:T(8,128)S(1)} %get-tuple-element.6), channel_id=1, source_target_pairs={{0,8},{8,16},{16,24},{1,9},{9,17},{17,25},{2,10},{10,18},{18,26},{... | collective-permute-start | bytes 49160 | tf_op jit(solution)/shard_map/ppermute | solution.py:18
  156.0 5.6 %collective-permute-start.5 = (f32[2,16,128]{2,1,0:T(8,128)S(1)}, f32[2,16,128]{2,1,0:T(8,128)S(1)}, u32[]{:S(2)}, u32[]{:S(2)}) collective-permute-start(f32[2,16,128]{2,1,0:T(8,128)S(1)} %get-tuple-element.8), channel_id=1, source_target_pairs={{8,0},{16,8},{24,16},{9,1},{17,9},{25,17},{10,2},{18,10},{26,18},{... | collective-permute-start | bytes 49160 | tf_op jit(solution)/shard_map/ppermute | solution.py:19
where the time goes:
time: 212 us; the launch traced here: 211 us
  blocking collectives  150 us (71%)
  other arithmetic  17.6 us (8%)
  matrix products  17.5 us (8%)
  starting transfers between devices  14.9 us (7%)
  waiting for transfers between devices  7.14 us (3%)
  local copies, waits for them, and re-layouts  4.46 us (2%)
    psum x3, blocking collectives, local(): gram_sum = lax.psum(partial_value, ('group', 'row'))  118 us
    all_gather x3, blocking collectives, local(): group_all = lax.all_gather(scaled, 'row', axis=0, tiled=True)  31.2 us
    dot_general x3, matrix products, local(): jnp.einsum('btij,btkj->bki', tiles, picked, precision=lax.Precision.HIGHE...  15.5 us
    ppermute x3, starting transfers between devices, padded(): before = lax.ppermute(last, axis, up)  10.8 us
    ppermute x3, waiting for transfers between devices, padded(): after = lax.ppermute(leading, axis, down)  7.14 us
    another operation x9, other arithmetic, orthonormal(): factor = jnp.linalg.cholesky(gram_sum / row_total)  6.39 us
    another operation x6, other arithmetic, orthonormal(): lax.linalg.triangular_solve(factor, jnp.eye(vectors, dtype=jnp.float32),...  5.63 us
    reduce_sum x1, other arithmetic, local(): jnp.einsum('btij,bt->bi', wide_tiles * wide_tiles, live_mask, precision=l...  4.46 us
  transfers between devices with their start and end apart: 6, of which 2 were waited for; matrix products, arithmetic and copies ran while one was open for 1% of the time, Pallas kernels for 0%

commit v1 on v0

v1 whole, which is shorter than its diff:
```python
import functools

import jax
import jax.numpy as jnp
from jax import lax
from jax.experimental import pallas as pl
from jax.experimental.pallas import tpu as pltpu
from jax.sharding import PartitionSpec as P

SLOTS = 2
RIM = 2
ITERS = 3
LANES = 128
PIECES = 3
VMEM_BYTES = 48 * 1024 * 1024
TRUST = 256.0
TINY = 1e-25

HIGH = lax.Precision.HIGHEST
NT = (((1,), (1,)), ((), ()))


def vmem():
    return pl.BlockSpec(memory_space=pltpu.VMEM)


def smem():
    return pl.BlockSpec(memory_space=pltpu.SMEM)


def f32(*shape):
    return jax.ShapeDtypeStruct(shape, jnp.float32)


def params():
    return pltpu.CompilerParams(vmem_limit_bytes=VMEM_BYTES)


def cost(flops, moved):
    return pl.CostEstimate(flops=flops, bytes_accessed=moved, transcendentals=0)


def roots_kernel(count_ref, tiles_ref, basis_ref, root_ref, scaled_ref):
    blocks, per_row, side, _ = tiles_ref.shape
    vectors = basis_ref.shape[1]
    for b in range(blocks):
        total = jnp.zeros((side, side), jnp.float32)
        for s in range(per_row):
            live = (s < count_ref[b]).astype(jnp.float32)
            wide = tiles_ref[b, s].astype(jnp.float32)
            total = total + wide * wide * live
        sums = jnp.sum(total.T, axis=0, keepdims=True)
        root = lax.rsqrt(jnp.sqrt(1e-06 + sums))
        root_ref[b] = root
        scaled_ref[b] = basis_ref[b] * root


def pick_kernel(me_ref, asked_ref, scaled_ref, out_ref):
    pick_into(me_ref, asked_ref, scaled_ref, out_ref)


def pick_into(me_ref, asked_ref, scaled_ref, out_ref):
    blocks = scaled_ref.shape[0]
    peers = asked_ref.shape[0]
    me, first = me_ref[0], me_ref[1]
    for p in range(peers):
        for c in range(SLOTS):
            at = jnp.clip(asked_ref[p, c, me] - first, 0, blocks - 1)
            out_ref[p * SLOTS + c] = scaled_ref[at]


def split_into(x, out_ref, slot):
    vectors = x.shape[0]
    rest = x
    for piece in range(PIECES):
        part = rest.astype(jnp.bfloat16)
        out_ref[slot, pl.ds(piece * vectors, vectors)] = part
        if piece < PIECES - 1:
            rest = rest - part.astype(jnp.float32)


def pack_grams(grams):
    half = grams[0].shape[0] // 2
    parts = [g[:half] for g in grams] + [g[half:] for g in grams]
    spare = LANES - len(parts) * grams[0].shape[1]
    return jnp.concatenate(parts + [jnp.zeros((half, spare), jnp.float32)], axis=1)


def unpack_grams(packed, vectors):
    upper = [packed[:, t * vectors : (t + 1) * vectors] for t in range(ITERS)]
    lower = [packed[:, (ITERS + t) * vectors : (ITERS + t + 1) * vectors] for t in range(ITERS)]
    return [jnp.concatenate(pair, axis=0) for pair in zip(upper, lower)]


def apply_kernel(last, *refs):
    if last:
        (count_ref, cols_ref, tiles_ref, root_ref, own_ref, recv_ref, low_ref, high_ref,
         *before, applied_ref, gram_ref, table) = refs
    else:
        (count_ref, cols_ref, me_ref, asked_ref, tiles_ref, root_ref, own_ref, recv_ref, low_ref,
         high_ref, applied_ref, gram_ref, scaled_ref, out_ref, table) = refs
    blocks, per_row, side, _ = tiles_ref.shape
    vectors = own_ref.shape[1]
    slot = 0
    for ref in (own_ref, recv_ref, low_ref, high_ref):
        for b in range(ref.shape[0]):
            split_into(ref[b], table, slot)
            slot += 1
    table[slot] = jnp.zeros(table.shape[1:], table.dtype)
    rows = []
    for b in range(blocks):
        picked = []
        for s in range(per_row):
            at = jnp.where(s < count_ref[b], cols_ref[b, s], slot)
            picked.append(table[at])
        x = jnp.concatenate(picked, axis=1)
        t = jnp.concatenate([tiles_ref[b, s] for s in range(per_row)], axis=1)
        product = lax.dot_general(x, t, NT, preferred_element_type=jnp.float32)
        total = product[(PIECES - 1) * vectors :]
        for piece in range(PIECES - 2, -1, -1):
            total = total + product[piece * vectors : (piece + 1) * vectors]
        root = root_ref[b]
        row = total * root
        applied_ref[b] = row
        rows.append(row)
        if not last:
            scaled_ref[b] = row * root
    flat = jnp.concatenate(rows, axis=1)
    gram = lax.dot_general(flat, flat, NT, precision=HIGH, preferred_element_type=jnp.float32)
    if last:
        packed = pack_grams([ref[...] for ref in before] + [gram])
        for n in range(gram_ref.shape[0]):
            gram_ref[n] = packed
    else:
        gram_ref[...] = gram
        pick_into(me_ref, asked_ref, scaled_ref, out_ref)


def finish_kernel(row_total, grams_ref, *refs):
    applied_refs, (out_ref, trust_ref) = refs[:ITERS], refs[ITERS:]
    devices = grams_ref.shape[0]
    blocks, vectors = out_ref.shape[1:3]
    total = grams_ref[0]
    for n in range(1, devices):
        total = total + grams_ref[n]
    rows = lax.broadcasted_iota(jnp.int32, (vectors, vectors), 0)
    lanes = lax.broadcasted_iota(jnp.int32, (vectors, vectors), 1)
    unit = (rows == lanes).astype(jnp.float32)
    row_at = lax.broadcasted_iota(jnp.int32, (vectors, 1), 0)
    grams = unpack_grams(total, vectors)
    work = [jnp.concatenate([gram, unit], axis=1) for gram in grams]
    for j in range(vectors):
        for t in range(ITERS):
            m = work[t]
            ratio = jnp.where(row_at > j, m[:, j : j + 1] / m[j : j + 1, j : j + 1], 0.0)
            work[t] = m - ratio * m[j : j + 1, :]
    good = jnp.bool_(True)
    for t in range(ITERS):
        m = work[t]
        pivots = jnp.sum(m[:, :vectors] * unit, axis=1, keepdims=True)
        inverse = m[:, vectors:] * lax.rsqrt(pivots / row_total)
        squares = jnp.sum(grams[t] * unit, axis=0, keepdims=True)
        norm = jnp.sum(inverse * inverse * squares) / row_total
        good = good & (norm < TRUST) & (jnp.min(squares) > TINY)
        for b in range(blocks):
            out_ref[t, b] = lax.dot_general(
                inverse, applied_refs[t][b], (((1,), (0,)), ((), ())), precision=HIGH,
                preferred_element_type=jnp.float32,
            )
    trust_ref[0] = good.astype(jnp.int32)


def neighbours(scaled):
    count, blocks = lax.axis_size("group"), scaled.shape[0]
    up = [(i, i + 1) for i in range(count - 1)]
    down = [(i + 1, i) for i in range(count - 1)]
    low = lax.ppermute(scaled[blocks - RIM :], "group", up)
    high = lax.ppermute(scaled[:RIM], "group", down)
    return low, high


def exchange(outgoing):
    return lax.all_to_all(outgoing, "row", 0, 0, tiled=True)


def stepwise(start_basis, tiles, tile_cols, tile_count, recv_list):
    groups, peers = lax.axis_size("group"), lax.axis_size("row")
    blocks, per_row, side, _ = tiles.shape
    vectors = start_basis.shape[1]
    row_total = groups * peers * blocks * side
    live = jnp.arange(per_row, dtype=jnp.int32)[None, :] < tile_count[:, None]
    live = live.astype(jnp.float32)
    wide = tiles.astype(jnp.float32)
    sums = jnp.einsum("btij,bt->bi", wide * wide, live, precision=HIGH)
    root = (1e-06 + sums) ** (-0.25)
    wanted = recv_list.reshape(peers * SLOTS)
    take = jnp.clip(wanted - lax.axis_index("group") * peers * blocks, 0, peers * blocks - 1)
    basis, results = start_basis, []
    for _ in range(ITERS):
        scaled = basis * root[:, None, :]
        low, high = neighbours(scaled)
        received = jnp.take(lax.all_gather(scaled, "row", axis=0, tiled=True), take, axis=0)
        extended = jnp.concatenate([scaled, received, low, high], axis=0)
        picked = jnp.take(extended, tile_cols, axis=0) * live[:, :, None, None]
        product = jnp.einsum(
            "btij,btkj->bki", tiles, picked, precision=HIGH, preferred_element_type=jnp.float32
        )
        applied = product * root[:, None, :]
        gram = jnp.einsum("bki,bli->kl", applied, applied, precision=HIGH)
        factor = jnp.linalg.cholesky(lax.psum(gram, ("group", "row")) / row_total)
        inverse = lax.linalg.triangular_solve(
            factor, jnp.eye(vectors, dtype=jnp.float32), left_side=True, lower=True
        )
        basis = jnp.einsum("kl,bli->bki", inverse, applied, precision=HIGH)
        results.append(basis)
    return jnp.stack(results)


def local(start_basis, tiles, tile_cols, tile_count, recv_list):
    groups, peers = lax.axis_size("group"), lax.axis_size("row")
    blocks, per_row, side, _ = tiles.shape
    vectors = start_basis.shape[1]
    row_at = lax.axis_index("row")
    first = (lax.axis_index("group") * peers + row_at) * blocks
    me = jnp.stack([row_at, first]).astype(jnp.int32)
    listed = jnp.transpose(recv_list.reshape(peers, SLOTS))
    asked = lax.all_to_all(
        jnp.broadcast_to(listed[None], (peers, SLOTS, peers)), "row", 0, 0, tiled=True
    )
    tile_bytes = tiles.size * 2
    root, scaled = pl.pallas_call(
        roots_kernel,
        out_shape=(f32(blocks, 1, side), f32(blocks, vectors, side)),
        in_specs=[smem(), vmem(), vmem()],
        out_specs=(vmem(), vmem()),
        compiler_params=params(),
        cost_estimate=cost(tiles.size * 2, tile_bytes),
        name="roots",
    )(tile_count, tiles, start_basis)
    outgoing = pl.pallas_call(
        pick_kernel,
        out_shape=f32(peers * SLOTS, vectors, side),
        in_specs=[smem(), smem(), vmem()],
        out_specs=vmem(),
        compiler_params=params(),
        name="pick",
    )(me, asked, scaled)
    slots = blocks + peers * SLOTS + 2 * RIM
    powers, grams = [], []
    for t in range(ITERS):
        last = t == ITERS - 1
        received = exchange(outgoing)
        low, high = neighbours(scaled)
        shapes = [f32(blocks, vectors, side)]
        scalars = [tile_count, tile_cols]
        arrays = [tiles, root, scaled, received, low, high]
        if last:
            shapes += [f32(groups * peers, vectors // 2, LANES)]
            arrays += grams
        else:
            shapes += [f32(vectors, vectors)]
            shapes += [f32(blocks, vectors, side), f32(peers * SLOTS, vectors, side)]
            scalars += [me, asked]
        result = pl.pallas_call(
            functools.partial(apply_kernel, last),
            out_shape=tuple(shapes),
            in_specs=[smem()] * len(scalars) + [vmem()] * len(arrays),
            out_specs=tuple(vmem() for _ in shapes),
            scratch_shapes=[pltpu.VMEM((slots + 1, PIECES * vectors, side), jnp.bfloat16)],
            compiler_params=params(),
            cost_estimate=cost(tiles.size * 2 * vectors * PIECES, tile_bytes),
            name="apply_last" if last else "apply",
        )(*scalars, *arrays)
        powers.append(result[0])
        grams.append(result[1])
        if not last:
            scaled, outgoing = result[2], result[3]
    gathered = lax.all_to_all(grams[-1], ("group", "row"), 0, 0, tiled=True)
    krylov, trust = pl.pallas_call(
        functools.partial(finish_kernel, float(groups * peers * blocks * side)),
        out_shape=(f32(ITERS, blocks, vectors, side), jax.ShapeDtypeStruct((1,), jnp.int32)),
        in_specs=[vmem()] * (1 + ITERS),
        out_specs=(vmem(), smem()),
        compiler_params=params(),
        name="finish",
    )(gathered, *powers)
    return lax.cond(
        trust[0] > 0,
        lambda *_: krylov,
        stepwise,
        start_basis, tiles, tile_cols, tile_count, recv_list,
    )


def solution(mesh):
    placed = (
        P(("group", "row"), None, None),
        P(("group", "row"), None, None, None),
        P(("group", "row"), None),
        P(("group", "row")),
        P("group", "row", None, None),
    )
    return jax.shard_map(
        local,
        mesh=mesh,
        in_specs=placed,
        out_specs=P(None, ("group", "row"), None, None),
        check_vma=False,
    )
```

time: 212 us -> 81.2 us (0.38)
  blocking collectives: 150 us -> 0 us
  starting transfers between devices: 14.9 us -> 43 us
  Pallas kernels: 0 us -> 20.7 us
  other arithmetic: 17.6 us -> 0.07 us
  matrix products: 17.5 us -> 0 us
  waiting for transfers between devices: 7.14 us -> 13.7 us
  local copies, waits for them, and re-layouts: 4.46 us -> 2.01 us
    psum x3 -> x0, blocking collectives: 118 us -> none  [local(): gram_sum = lax.psum(partial_value, ('group', 'row'))]
    all_gather x3 -> x0, blocking collectives: 31.2 us -> none  [local(): group_all = lax.all_gather(scaled, 'row', axis=0, tiled=True)]
    all_to_all x0 -> x5, starting transfers between devices: none -> 24.7 us  [the longest x3 11.6 us: exchange(): return lax.all_to_all(outgoing, 'row', 0, 0, tiled=True)]
    pallas_call x0 -> x6, Pallas kernels: none -> 20.7 us  [the longest x3 13.3 us: local(): pl.pallas_call(functools.partial(apply_kernel, last), out_shape=tuple(sha...]
    dot_general x10 -> x0, matrix products: 16.9 us -> none  [the longest x3 15.5 us: local(): jnp.einsum('btij,btkj->bki', tiles, picked, precision=lax.Precision.HIGHE...]
    another operation x16 -> x1, other arithmetic: 12.7 us -> 0.07 us  [local(): me = jnp.stack([row_at, first]).astype(jnp.int32)]
    all_to_all x0 -> x5, waiting for transfers between devices: none -> 9.47 us  [the longest x1 8.23 us: local(): gathered = lax.all_to_all(grams[-1], ('group', 'row'), 0, 0, tiled=True)]
    reduce_sum x1 -> x0, other arithmetic: 4.46 us -> none  [local(): jnp.einsum('btij,bt->bi', wide_tiles * wide_tiles, live_mask, precision=l...]
  transfers between devices with their start and end apart: 6 -> 11, of which waited for: 2 -> 5; matrix products, arithmetic and copies ran while one was open for 1% -> 0% of each run, Pallas kernels for 0% -> 4%
where the time goes in v1:
time: 81.2 us; the launch traced here: 80.5 us
  starting transfers between devices  43 us (53%)
  Pallas kernels  20.7 us (25%)
  waiting for transfers between devices  13.7 us (17%)
  local copies, waits for them, and re-layouts  2.01 us (2%)
  between operations  0.83 us (1%)
    ppermute x3, starting transfers between devices, neighbours(): low = lax.ppermute(scaled[blocks - RIM:], 'group', up)  14.3 us
    pallas_call x3, Pallas kernels, local(): pl.pallas_call(functools.partial(apply_kernel, last), out_shape=tuple(sha...  13.3 us
    all_to_all x3, starting transfers between devices, exchange(): return lax.all_to_all(outgoing, 'row', 0, 0, tiled=True)  11.6 us
    all_to_all x1, waiting for transfers between devices, local(): gathered = lax.all_to_all(grams[-1], ('group', 'row'), 0, 0, tiled=True)  8.23 us
    all_to_all x1, starting transfers between devices, local(): gathered = lax.all_to_all(grams[-1], ('group', 'row'), 0, 0, tiled=True)  7.93 us
    all_to_all x1, starting transfers between devices, local(): lax.all_to_all(jnp.broadcast_to(listed[None], (peers, SLOTS, peers)), 'ro...  5.17 us
    ppermute x3, waiting for transfers between devices, neighbours(): low = lax.ppermute(scaled[blocks - RIM:], 'group', up)  4.24 us
    ppermute x3, starting transfers between devices, neighbours(): high = lax.ppermute(scaled[:RIM], 'group', down)  3.88 us
  transfers between devices with their start and end apart: 11, of which 5 were waited for; matrix products, arithmetic and copies ran while one was open for 0% of the time, Pallas kernels for 4%

profile of v1, /device:TPU:0, one launch (start us, length us, event | category | flops | bytes accessed | tf_op | source)
XLA Modules:
  0.0 80.5 jit_solution(16478982890487160191)
XLA Ops:
  0.0 0.0 copy-start.2
  0.0 0.0 copy-start.1
  0.0 1.3 %broadcast_in_dim.20 = s32[8,2,8]{2,1,0:T(2,128)} broadcast(s32[2,8]{1,0:T(2,128)} %bitcast.103), dimensions={1,2} | broadcast | bytes 576 | tf_op jit(solution)/shard_map/broadcast_in_dim | solution.py:228
  1.3 5.2 %all-to-all-start = ((s32[8,2,8]{2,1,0:T(2,128)}), s32[8,2,8]{2,1,0:T(2,128)S(1)}, u32[]{:S(2)}, u32[]{:S(2)}) async-start(s32[8,2,8]{2,1,0:T(2,128)} %broadcast_in_dim.20), calls=%async_computation | async-start | bytes 16384 | tf_op jit(solution)/shard_map/all_to_all | solution.py:227
  6.5 0.1 pad_add_fusion.me_ref.refs_2_
  6.6 3.4 %roots.1 = (f32[8,1,128]{2,1,0:T(1,128)S(1)}, f32[8,16,128]{2,1,0:T(8,128)S(1)}) custom-call(s32[8]{0:T(128)} %refs_0_.5, bf16[8,16,128,128]{3,2,1,0:T(8,128)(2,1)} %refs_2_.1, f32[8,16,128]{2,1,0:T(8,128)} %basis_ref.1), custom_call_target="tpu_custom_call" | custom-call | flops 4194304 | bytes 4194304 | tf_op jit(solution)/shard_map/roots/pallas_call | solution.py:231
  10.0 1.2 %all-to-all-done.asked_ref.refs_3_ = s32[8,2,8]{2,1,0:T(2,128)S(1)} async-done(((s32[8,2,8]{2,1,0:T(2,128)}), s32[8,2,8]{2,1,0:T(2,128)S(1)}, u32[]{:S(2)}, u32[]{:S(2)}) %all-to-all-start) | async-done | bytes 544 | tf_op jit(solution)/shard_map/all_to_all | solution.py:227
  11.2 1.4 %pick.1 = f32[16,16,128]{2,1,0:T(8,128)} custom-call(s32[2]{0:T(128)S(1)} %pad_add_fusion.me_ref.refs_2_, s32[8,2,8]{2,1,0:T(2,128)S(1)} %all-to-all-done.asked_ref.refs_3_, f32[8,16,128]{2,1,0:T(8,128)S(1)} %get-tuple-element.43.scaled_ref.refs_6_), custom_call_target="tpu_custom_call" | custom-call | tf_op jit(solution)/shard_map/pick/pallas_call | solution.py:240
  12.6 3.4 %all-to-all-start.1 = ((f32[16,16,128]{2,1,0:T(8,128)}), f32[16,16,128]{2,1,0:T(8,128)S(1)}, u32[]{:S(2)}, u32[]{:S(2)}) async-start(f32[16,16,128]{2,1,0:T(8,128)} %pick.1), calls=%async_computation.1 | async-start | bytes 262144 | tf_op jit(solution)/shard_map/all_to_all | solution.py:183
  16.0 1.3 %collective-permute-start.7 = (f32[2,16,128]{2,1,0:T(8,128)S(1)}, f32[2,16,128]{2,1,0:T(8,128)S(1)}, u32[]{:S(2)}, u32[]{:S(2)}) collective-permute-start(f32[2,16,128]{2,1,0:T(8,128)S(1)} %get-tuple-element.88), channel_id=1, source_target_pairs={{8,0},{16,8},{24,16},{9,1},{17,9},{25,17},{10,2},{18,10},{26,18},{... | collective-permute-start | bytes 49160 | tf_op jit(solution)/shard_map/ppermute | solution.py:178
  17.3 4.6 %collective-permute-start.6 = (f32[2,16,128]{2,1,0:T(8,128)S(1)}, f32[2,16,128]{2,1,0:T(8,128)S(1)}, u32[]{:S(2)}, u32[]{:S(2)}) collective-permute-start(f32[2,16,128]{2,1,0:T(8,128)S(1)} %get-tuple-element.89), channel_id=1, source_target_pairs={{0,8},{8,16},{16,24},{1,9},{9,17},{17,25},{2,10},{10,18},{18,26},{... | collective-permute-start | bytes 49160 | tf_op jit(solution)/shard_map/ppermute | solution.py:177
  21.8 0.0 collective-permute-done.7.refs_9_
  21.8 1.4 %collective-permute-done.6.refs_8_ = f32[2,16,128]{2,1,0:T(8,128)S(1)} collective-permute-done((f32[2,16,128]{2,1,0:T(8,128)S(1)}, f32[2,16,128]{2,1,0:T(8,128)S(1)}, u32[]{:S(2)}, u32[]{:S(2)}) %collective-permute-start.6) | collective-permute-done | bytes 16416 | tf_op jit(solution)/shard_map/ppermute | solution.py:177
  23.3 0.0 all-to-all-done.1.refs_7_
  23.3 0.0 copy-done.2
  23.3 0.0 copy-done.1
  23.3 4.4 %apply.2 = (f32[8,16,128]{2,1,0:T(8,128)S(1)}, f32[16,16]{1,0:T(8,128)S(1)}, f32[8,16,128]{2,1,0:T(8,128)S(1)}, f32[16,16,128]{2,1,0:T(8,128)}) custom-call(s32[8]{0:T(128)S(1)} %copy-done.2, s32[8,16]{1,0:T(8,128)S(1)} %copy-done.1, s32[2]{0:T(128)S(1)} %pad_add_fusion.me_ref.refs_2_, s32[8,2,8]{2,1,0:T(2,128)S(1)} %all-to-all-done.asked_ref.refs_3_, ...), custom_call_target="tpu_custom_call" | custom-call | flops 201326592 | bytes 4194304 | tf_op jit(solution)/shard_map/apply/pallas_call | solution.py:264
  27.6 4.1 %all-to-all-start.2 = ((f32[16,16,128]{2,1,0:T(8,128)}), f32[16,16,128]{2,1,0:T(8,128)S(1)}, u32[]{:S(2)}, u32[]{:S(2)}) async-start(f32[16,16,128]{2,1,0:T(8,128)} %get-tuple-element.45), calls=%async_computation.2 | async-start | bytes 262144 | tf_op jit(solution)/shard_map/all_to_all | solution.py:183
  31.7 1.3 %collective-permute-start.9 = (f32[2,16,128]{2,1,0:T(8,128)S(1)}, f32[2,16,128]{2,1,0:T(8,128)S(1)}, u32[]{:S(2)}, u32[]{:S(2)}) collective-permute-start(f32[2,16,128]{2,1,0:T(8,128)S(1)} %get-tuple-element.86), channel_id=1, source_target_pairs={{8,0},{16,8},{24,16},{9,1},{17,9},{25,17},{10,2},{18,10},{26,18},{... | collective-permute-start | bytes 49160 | tf_op jit(solution)/shard_map/ppermute | solution.py:178
  33.0 0.0 copy-start
  33.0 0.0 copy-start.3
  33.0 5.0 %collective-permute-start.8 = (f32[2,16,128]{2,1,0:T(8,128)S(1)}, f32[2,16,128]{2,1,0:T(8,128)S(1)}, u32[]{:S(2)}, u32[]{:S(2)}) collective-permute-start(f32[2,16,128]{2,1,0:T(8,128)S(1)} %get-tuple-element.87), channel_id=1, source_target_pairs={{0,8},{8,16},{16,24},{1,9},{9,17},{17,25},{2,10},{10,18},{18,26},{... | collective-permute-start | bytes 49160 | tf_op jit(solution)/shard_map/ppermute | solution.py:177
  38.0 0.0 collective-permute-done.9.refs_9_
  38.0 1.4 %collective-permute-done.8.refs_8_ = f32[2,16,128]{2,1,0:T(8,128)S(1)} collective-permute-done((f32[2,16,128]{2,1,0:T(8,128)S(1)}, f32[2,16,128]{2,1,0:T(8,128)S(1)}, u32[]{:S(2)}, u32[]{:S(2)}) %collective-permute-start.8) | collective-permute-done | bytes 16416 | tf_op jit(solution)/shard_map/ppermute | solution.py:177
  39.4 0.0 all-to-all-done.2.refs_7_
  39.4 4.4 %apply.3 = (f32[8,16,128]{2,1,0:T(8,128)S(1)}, f32[16,16]{1,0:T(8,128)S(1)}, f32[8,16,128]{2,1,0:T(8,128)S(1)}, f32[16,16,128]{2,1,0:T(8,128)}) custom-call(s32[8]{0:T(128)S(1)} %copy-done.2, s32[8,16]{1,0:T(8,128)S(1)} %copy-done.1, s32[2]{0:T(128)S(1)} %pad_add_fusion.me_ref.refs_2_, s32[8,2,8]{2,1,0:T(2,128)S(1)} %all-to-all-done.asked_ref.refs_3_, ...), custom_call_target="tpu_custom_call" | custom-call | flops 201326592 | bytes 4194304 | tf_op jit(solution)/shard_map/apply/pallas_call | solution.py:264
  43.8 4.2 %all-to-all-start.3 = ((f32[16,16,128]{2,1,0:T(8,128)}), f32[16,16,128]{2,1,0:T(8,128)S(1)}, u32[]{:S(2)}, u32[]{:S(2)}) async-start(f32[16,16,128]{2,1,0:T(8,128)} %get-tuple-element.47), calls=%async_computation.3 | async-start | bytes 262144 | tf_op jit(solution)/shard_map/all_to_all | solution.py:183
  48.0 1.3 %collective-permute-start.11 = (f32[2,16,128]{2,1,0:T(8,128)S(1)}, f32[2,16,128]{2,1,0:T(8,128)S(1)}, u32[]{:S(2)}, u32[]{:S(2)}) collective-permute-start(f32[2,16,128]{2,1,0:T(8,128)S(1)} %get-tuple-element.84), channel_id=1, source_target_pairs={{8,0},{16,8},{24,16},{9,1},{17,9},{25,17},{10,2},{18,10},{26,18},{... | collective-permute-start | bytes 49160 | tf_op jit(solution)/shard_map/ppermute | solution.py:178
  49.3 4.8 %collective-permute-start.10 = (f32[2,16,128]{2,1,0:T(8,128)S(1)}, f32[2,16,128]{2,1,0:T(8,128)S(1)}, u32[]{:S(2)}, u32[]{:S(2)}) collective-permute-start(f32[2,16,128]{2,1,0:T(8,128)S(1)} %get-tuple-element.85), channel_id=1, source_target_pairs={{0,8},{8,16},{16,24},{1,9},{9,17},{17,25},{2,10},{10,18},{18,26},{... | collective-permute-start | bytes 49160 | tf_op jit(solution)/shard_map/ppermute | solution.py:177
  54.1 0.0 collective-permute-done.11.refs_7_
  54.1 1.4 %collective-permute-done.10.refs_6_ = f32[2,16,128]{2,1,0:T(8,128)S(1)} collective-permute-done((f32[2,16,128]{2,1,0:T(8,128)S(1)}, f32[2,16,128]{2,1,0:T(8,128)S(1)}, u32[]{:S(2)}, u32[]{:S(2)}) %collective-permute-start.10) | collective-permute-done | bytes 16416 | tf_op jit(solution)/shard_map/ppermute | solution.py:177
  55.5 0.0 all-to-all-done.3.refs_5_
  55.5 4.6 %apply_last.1 = (f32[8,16,128]{2,1,0:T(8,128)S(1)}, f32[32,8,128]{2,1,0:T(8,128)}) custom-call(s32[8]{0:T(128)S(1)} %copy-done.2, s32[8,16]{1,0:T(8,128)S(1)} %copy-done.1, bf16[8,16,128,128]{3,2,1,0:T(8,128)(2,1)} %refs_2_.1, f32[8,1,128]{2,1,0:T(1,128)S(1)} %get-tuple-element.42.refs_5_.refs_3_, f32[8,16,128]{2,1,0:T(8,128)S(1)} %get-tuple-element.46.refs_4_, ...), custom_call_target="tpu_custom_call" | custom-call | flops 201326592 | bytes 4194304 | tf_op jit(solution)/shard_map/apply_last/pallas_call | solution.py:264
  60.1 7.9 %all-to-all-start.4 = ((f32[32,8,128]{2,1,0:T(8,128)}), f32[32,8,128]{2,1,0:T(8,128)S(1)}, u32[]{:S(2)}, u32[]{:S(2)}) async-start(f32[32,8,128]{2,1,0:T(8,128)} %get-tuple-element.50), calls=%async_computation.4 | async-start | bytes 262144 | tf_op jit(solution)/shard_map/all_to_all | solution.py:278
  68.1 8.2 %all-to-all-done.4.grams_ref = f32[32,8,128]{2,1,0:T(8,128)S(1)} async-done(((f32[32,8,128]{2,1,0:T(8,128)}), f32[32,8,128]{2,1,0:T(8,128)S(1)}, u32[]{:S(2)}, u32[]{:S(2)}) %all-to-all-start.4) | async-done | bytes 131104 | tf_op jit(solution)/shard_map/all_to_all | solution.py:278
  76.3 2.6 %finish.1 = (f32[3,8,16,128]{3,2,1,0:T(8,128)S(1)}, s32[1]{0:T(128)}) custom-call(f32[32,8,128]{2,1,0:T(8,128)S(1)} %all-to-all-done.4.grams_ref, f32[8,16,128]{2,1,0:T(8,128)S(1)} %get-tuple-element.51.refs_0_, f32[8,16,128]{2,1,0:T(8,128)S(1)} %get-tuple-element.52.refs_1_, f32[8,16,128]{2,1,0:T(8,128)S(1)} %get-tuple-element.53.refs_2_), custom_call_target="tpu_custom_call" | custom-call | tf_op jit(solution)/shard_map/finish/pallas_call | solution.py:279
  79.5 0.0 copy-done
  79.5 0.0 copy-done.3
  79.6 0.2 conditional.1
  79.8 0.0 copy-start.4
  79.8 0.7 copy-done.4
  (3 shorter events, 0.0 us)
Async XLA Ops:
  0.0 23.3 %copy-start.2 = (s32[8]{0:T(128)S(1)}, s32[8]{0:T(128)}, u32[]{:S(2)}) copy-start(s32[8]{0:T(128)} %refs_0_.5) | copy-start | bytes 100
  0.0 23.3 %copy-start.1 = (s32[8,16]{1,0:T(8,128)S(1)}, s32[8,16]{1,0:T(8,128)}, u32[]{:S(2)}) copy-start(s32[8,16]{1,0:T(8,128)} %refs_1_.5) | copy-start | bytes 1540
  1.3 9.9 %all-to-all-start = ((s32[8,2,8]{2,1,0:T(2,128)}), s32[8,2,8]{2,1,0:T(2,128)S(1)}, u32[]{:S(2)}, u32[]{:S(2)}) async-start(s32[8,2,8]{2,1,0:T(2,128)} %broadcast_in_dim.20), calls=%async_computation | async-start | bytes 16384 | tf_op jit(solution)/shard_map/all_to_all | solution.py:227
  12.6 10.7 %all-to-all-start.1 = ((f32[16,16,128]{2,1,0:T(8,128)}), f32[16,16,128]{2,1,0:T(8,128)S(1)}, u32[]{:S(2)}, u32[]{:S(2)}) async-start(f32[16,16,128]{2,1,0:T(8,128)} %pick.1), calls=%async_computation.1 | async-start | bytes 262144 | tf_op jit(solution)/shard_map/all_to_all | solution.py:183
  16.0 5.9 %collective-permute-start.7 = (f32[2,16,128]{2,1,0:T(8,128)S(1)}, f32[2,16,128]{2,1,0:T(8,128)S(1)}, u32[]{:S(2)}, u32[]{:S(2)}) collective-permute-start(f32[2,16,128]{2,1,0:T(8,128)S(1)} %get-tuple-element.88), channel_id=1, source_target_pairs={{8,0},{16,8},{24,16},{9,1},{17,9},{25,17},{10,2},{18,10},{26,18},{... | collective-permute-start | bytes 49160 | tf_op jit(solution)/shard_map/ppermute | solution.py:178
  17.3 6.0 %collective-permute-start.6 = (f32[2,16,128]{2,1,0:T(8,128)S(1)}, f32[2,16,128]{2,1,0:T(8,128)S(1)}, u32[]{:S(2)}, u32[]{:S(2)}) collective-permute-start(f32[2,16,128]{2,1,0:T(8,128)S(1)} %get-tuple-element.89), channel_id=1, source_target_pairs={{0,8},{8,16},{16,24},{1,9},{9,17},{17,25},{2,10},{10,18},{18,26},{... | collective-permute-start | bytes 49160 | tf_op jit(solution)/shard_map/ppermute | solution.py:177
  27.6 11.8 %all-to-all-start.2 = ((f32[16,16,128]{2,1,0:T(8,128)}), f32[16,16,128]{2,1,0:T(8,128)S(1)}, u32[]{:S(2)}, u32[]{:S(2)}) async-start(f32[16,16,128]{2,1,0:T(8,128)} %get-tuple-element.45), calls=%async_computation.2 | async-start | bytes 262144 | tf_op jit(solution)/shard_map/all_to_all | solution.py:183
  31.7 6.3 %collective-permute-start.9 = (f32[2,16,128]{2,1,0:T(8,128)S(1)}, f32[2,16,128]{2,1,0:T(8,128)S(1)}, u32[]{:S(2)}, u32[]{:S(2)}) collective-permute-start(f32[2,16,128]{2,1,0:T(8,128)S(1)} %get-tuple-element.86), channel_id=1, source_target_pairs={{8,0},{16,8},{24,16},{9,1},{17,9},{25,17},{10,2},{18,10},{26,18},{... | collective-permute-start | bytes 49160 | tf_op jit(solution)/shard_map/ppermute | solution.py:178
  33.0 46.5 %copy-start = (f32[8,16,128]{2,1,0:T(8,128)S(1)}, f32[8,16,128]{2,1,0:T(8,128)}, u32[]{:S(2)}) copy-start(f32[8,16,128]{2,1,0:T(8,128)} %basis_ref.1) | copy-start | bytes 196612
  33.0 46.5 %copy-start.3 = (s32[1,1,8,2]{2,3,1,0:T(2,128)S(1)}, s32[1,1,8,2]{2,3,1,0:T(2,128)}, u32[]{:S(2)}) copy-start(s32[1,1,8,2]{2,3,1,0:T(2,128)} %param.18) | copy-start | bytes 196
  33.0 6.4 %collective-permute-start.8 = (f32[2,16,128]{2,1,0:T(8,128)S(1)}, f32[2,16,128]{2,1,0:T(8,128)S(1)}, u32[]{:S(2)}, u32[]{:S(2)}) collective-permute-start(f32[2,16,128]{2,1,0:T(8,128)S(1)} %get-tuple-element.87), channel_id=1, source_target_pairs={{0,8},{8,16},{16,24},{1,9},{9,17},{17,25},{2,10},{10,18},{18,26},{... | collective-permute-start | bytes 49160 | tf_op jit(solution)/shard_map/ppermute | solution.py:177
  43.8 11.8 %all-to-all-start.3 = ((f32[16,16,128]{2,1,0:T(8,128)}), f32[16,16,128]{2,1,0:T(8,128)S(1)}, u32[]{:S(2)}, u32[]{:S(2)}) async-start(f32[16,16,128]{2,1,0:T(8,128)} %get-tuple-element.47), calls=%async_computation.3 | async-start | bytes 262144 | tf_op jit(solution)/shard_map/all_to_all | solution.py:183
  48.0 6.1 %collective-permute-start.11 = (f32[2,16,128]{2,1,0:T(8,128)S(1)}, f32[2,16,128]{2,1,0:T(8,128)S(1)}, u32[]{:S(2)}, u32[]{:S(2)}) collective-permute-start(f32[2,16,128]{2,1,0:T(8,128)S(1)} %get-tuple-element.84), channel_id=1, source_target_pairs={{8,0},{16,8},{24,16},{9,1},{17,9},{25,17},{10,2},{18,10},{26,18},{... | collective-permute-start | bytes 49160 | tf_op jit(solution)/shard_map/ppermute | solution.py:178
  49.3 6.2 %collective-permute-start.10 = (f32[2,16,128]{2,1,0:T(8,128)S(1)}, f32[2,16,128]{2,1,0:T(8,128)S(1)}, u32[]{:S(2)}, u32[]{:S(2)}) collective-permute-start(f32[2,16,128]{2,1,0:T(8,128)S(1)} %get-tuple-element.85), channel_id=1, source_target_pairs={{0,8},{8,16},{16,24},{1,9},{9,17},{17,25},{2,10},{10,18},{18,26},{... | collective-permute-start | bytes 49160 | tf_op jit(solution)/shard_map/ppermute | solution.py:177
  60.1 16.2 %all-to-all-start.4 = ((f32[32,8,128]{2,1,0:T(8,128)}), f32[32,8,128]{2,1,0:T(8,128)S(1)}, u32[]{:S(2)}, u32[]{:S(2)}) async-start(f32[32,8,128]{2,1,0:T(8,128)} %get-tuple-element.50), calls=%async_computation.4 | async-start | bytes 262144 | tf_op jit(solution)/shard_map/all_to_all | solution.py:278
  79.8 0.7 copy-start.4

commit v2 on v1

--- a/solution.py
+++ b/solution.py
@@ -12,7 +12,7 @@
 ITERS = 3
 LANES = 128
 PIECES = 3
-VMEM_BYTES = 48 * 1024 * 1024
+VMEM_BYTES = 24 * 1024 * 1024
 TRUST = 256.0
 TINY = 1e-25
 
@@ -28,6 +28,10 @@
     return pl.BlockSpec(memory_space=pltpu.SMEM)
 
 
+def anywhere():
+    return pl.BlockSpec(memory_space=pl.ANY)
+
+
 def f32(*shape):
     return jax.ShapeDtypeStruct(shape, jnp.float32)
 
@@ -40,10 +44,26 @@
     return pl.CostEstimate(flops=flops, bytes_accessed=moved, transcendentals=0)
 
 
-def roots_kernel(count_ref, tiles_ref, basis_ref, root_ref, scaled_ref):
+def roots_kernel(group_ref, count_ref, want_ref, tiles_hbm, basis_ref, root_ref, scaled_ref,
+                 tiles_ref, spread_hbm, rim_ref, lists, tile_sems, sems):
     blocks, per_row, side, _ = tiles_ref.shape
-    vectors = basis_ref.shape[1]
+    peers = spread_hbm.shape[0]
+    loads = [
+        pltpu.make_async_copy(tiles_hbm.at[b], tiles_ref.at[b], tile_sems.at[b])
+        for b in range(blocks)
+    ]
+    for load in loads:
+        load.start()
+    half = lists.shape[2] // SLOTS
+    for p in range(peers):
+        owned = (group_ref[0] * peers + p) * blocks
+        for c in range(SLOTS):
+            at = jnp.full((half, side), want_ref[c, p] - owned, jnp.int32)
+            lists[p, 0, pl.ds(c * half, half)] = at.astype(jnp.float32)
+    sends = [pltpu.make_async_copy(lists, spread_hbm.at[:, pl.ds(blocks, 1)], sems.at[peers])]
+    sends[0].start()
     for b in range(blocks):
+        loads[b].wait()
         total = jnp.zeros((side, side), jnp.float32)
         for s in range(per_row):
             live = (s < count_ref[b]).astype(jnp.float32)
@@ -53,20 +73,36 @@
         root = lax.rsqrt(jnp.sqrt(1e-06 + sums))
         root_ref[b] = root
         scaled_ref[b] = basis_ref[b] * root
-
-
-def pick_kernel(me_ref, asked_ref, scaled_ref, out_ref):
-    pick_into(me_ref, asked_ref, scaled_ref, out_ref)
-
-
-def pick_into(me_ref, asked_ref, scaled_ref, out_ref):
+    for p in range(peers):
+        send = pltpu.make_async_copy(scaled_ref, spread_hbm.at[p, pl.ds(0, blocks)], sems.at[p])
+        send.start()
+        sends.append(send)
+    rims_into(group_ref[0], scaled_ref, rim_ref)
+    for send in sends:
+        send.wait()
+
+
+def rims_into(group, scaled_ref, rim_ref):
     blocks = scaled_ref.shape[0]
-    peers = asked_ref.shape[0]
-    me, first = me_ref[0], me_ref[1]
+    for d in range(rim_ref.shape[0]):
+        start = jnp.where(d < group, 0, blocks - RIM)
+        for h in range(RIM):
+            rim_ref[d, h] = scaled_ref[start + h]
+
+
+def pick_into(asked_ref, scaled_ref, out_ref):
+    peers, blocks, vectors, _ = asked_ref.shape
+    blocks -= 1
+    half = vectors // SLOTS
     for p in range(peers):
         for c in range(SLOTS):
-            at = jnp.clip(asked_ref[p, c, me] - first, 0, blocks - 1)
-            out_ref[p * SLOTS + c] = scaled_ref[at]
+            at = asked_ref[p, blocks, c * half : (c + 1) * half]
+            for row in range(0, vectors, half):
+                rows = slice(row, row + half)
+                value = scaled_ref[0, rows]
+                for b in range(1, blocks):
+                    value = jnp.where(at == float(b), scaled_ref[b, rows], value)
+                out_ref[p * SLOTS + c, rows] = value
 
 
 def split_into(x, out_ref, slot):
@@ -92,19 +128,39 @@
     return [jnp.concatenate(pair, axis=0) for pair in zip(upper, lower)]
 
 
-def apply_kernel(last, *refs):
+def apply_kernel(step_at, *refs):
+    last, opening = step_at == ITERS - 1, step_at == 0
+    group_ref, count_ref, cols_ref, *refs = refs
+    if opening:
+        want_ref, *refs = refs
+    tiles_ref, root_ref, own_ref, recv_ref, recv_rim_ref, *refs = refs
     if last:
-        (count_ref, cols_ref, tiles_ref, root_ref, own_ref, recv_ref, low_ref, high_ref,
-         *before, applied_ref, gram_ref, table) = refs
+        *before, applied_ref, gram_ref, table = refs
     else:
-        (count_ref, cols_ref, me_ref, asked_ref, tiles_ref, root_ref, own_ref, recv_ref, low_ref,
-         high_ref, applied_ref, gram_ref, scaled_ref, out_ref, table) = refs
+        asked_ref, refs = (recv_ref, refs) if opening else (refs[0], refs[1:])
+        applied_ref, gram_ref, scaled_ref, out_hbm, rim_ref, table, picked_ref, sem = refs
     blocks, per_row, side, _ = tiles_ref.shape
     vectors = own_ref.shape[1]
+    group = group_ref[0]
     slot = 0
-    for ref in (own_ref, recv_ref, low_ref, high_ref):
-        for b in range(ref.shape[0]):
-            split_into(ref[b], table, slot)
+    for b in range(blocks):
+        split_into(own_ref[b], table, slot)
+        slot += 1
+    if opening:
+        peers = recv_ref.shape[0]
+        for p in range(peers):
+            for c in range(SLOTS):
+                at = jnp.clip(want_ref[c, p] - (group * peers + p) * blocks, 0, blocks - 1)
+                split_into(recv_ref[p, at], table, slot)
+                slot += 1
+    else:
+        for n in range(recv_ref.shape[0]):
+            split_into(recv_ref[n], table, slot)
+            slot += 1
+    groups = recv_rim_ref.shape[0]
+    for side_at in (jnp.maximum(group - 1, 0), jnp.minimum(group + 1, groups - 1)):
+        for h in range(RIM):
+            split_into(recv_rim_ref[side_at, h], table, slot)
             slot += 1
     table[slot] = jnp.zeros(table.shape[1:], table.dtype)
     rows = []
@@ -125,6 +181,11 @@
         rows.append(row)
         if not last:
             scaled_ref[b] = row * root
+    if not last:
+        pick_into(asked_ref, scaled_ref, picked_ref)
+        send = pltpu.make_async_copy(picked_ref, out_hbm, sem)
+        send.start()
+        rims_into(group, scaled_ref, rim_ref)
     flat = jnp.concatenate(rows, axis=1)
     gram = lax.dot_general(flat, flat, NT, precision=HIGH, preferred_element_type=jnp.float32)
     if last:
@@ -133,7 +194,7 @@
             gram_ref[n] = packed
     else:
         gram_ref[...] = gram
-        pick_into(me_ref, asked_ref, scaled_ref, out_ref)
+        send.wait()
 
 
 def finish_kernel(row_total, grams_ref, *refs):
@@ -220,53 +281,60 @@
     groups, peers = lax.axis_size("group"), lax.axis_size("row")
     blocks, per_row, side, _ = tiles.shape
     vectors = start_basis.shape[1]
-    row_at = lax.axis_index("row")
-    first = (lax.axis_index("group") * peers + row_at) * blocks
-    me = jnp.stack([row_at, first]).astype(jnp.int32)
-    listed = jnp.transpose(recv_list.reshape(peers, SLOTS))
-    asked = lax.all_to_all(
-        jnp.broadcast_to(listed[None], (peers, SLOTS, peers)), "row", 0, 0, tiled=True
-    )
+    group = lax.axis_index("group").astype(jnp.int32).reshape(1)
+    wanted = jnp.transpose(recv_list.reshape(peers, SLOTS))
     tile_bytes = tiles.size * 2
-    root, scaled = pl.pallas_call(
+    block_shape = (vectors, side)
+    picked_shape = (peers * SLOTS,) + block_shape
+    rim_shape = f32(groups, RIM, *block_shape)
+    root, scaled, held, spread, rims = pl.pallas_call(
         roots_kernel,
-        out_shape=(f32(blocks, 1, side), f32(blocks, vectors, side)),
-        in_specs=[smem(), vmem(), vmem()],
-        out_specs=(vmem(), vmem()),
+        out_shape=(
+            f32(blocks, 1, side),
+            f32(blocks, *block_shape),
+            pltpu.VMEM(tiles.shape, tiles.dtype),
+            f32(peers, blocks + 1, *block_shape),
+            rim_shape,
+        ),
+        in_specs=[smem(), smem(), smem(), anywhere(), vmem()],
+        out_specs=(vmem(), vmem(), vmem(), anywhere(), vmem()),
+        scratch_shapes=[
+            pltpu.VMEM((peers, 1) + block_shape, jnp.float32),
+            pltpu.SemaphoreType.DMA((blocks,)),
+            pltpu.SemaphoreType.DMA((peers + 1,)),
+        ],
         compiler_params=params(),
         cost_estimate=cost(tiles.size * 2, tile_bytes),
         name="roots",
-    )(tile_count, tiles, start_basis)
-    outgoing = pl.pallas_call(
-        pick_kernel,
-        out_shape=f32(peers * SLOTS, vectors, side),
-        in_specs=[smem(), smem(), vmem()],
-        out_specs=vmem(),
-        compiler_params=params(),
-        name="pick",
-    )(me, asked, scaled)
+    )(group, tile_count, wanted, tiles, start_basis)
     slots = blocks + peers * SLOTS + 2 * RIM
     powers, grams = [], []
+    outgoing = spread
     for t in range(ITERS):
         last = t == ITERS - 1
         received = exchange(outgoing)
-        low, high = neighbours(scaled)
-        shapes = [f32(blocks, vectors, side)]
-        scalars = [tile_count, tile_cols]
-        arrays = [tiles, root, scaled, received, low, high]
+        if t == 0:
+            asked = received
+        beside = lax.all_to_all(rims, "group", 0, 0, tiled=True)
+        scalars = [group, tile_count, tile_cols] + ([wanted] if t == 0 else [])
+        arrays = [held, root, scaled, received, beside]
+        shapes = [f32(blocks, *block_shape)]
+        specs = [vmem(), vmem()]
+        scratch = [pltpu.VMEM((slots + 1, PIECES * vectors, side), jnp.bfloat16)]
         if last:
             shapes += [f32(groups * peers, vectors // 2, LANES)]
             arrays += grams
         else:
-            shapes += [f32(vectors, vectors)]
-            shapes += [f32(blocks, vectors, side), f32(peers * SLOTS, vectors, side)]
-            scalars += [me, asked]
+            shapes += [f32(vectors, vectors), f32(blocks, *block_shape), f32(*picked_shape), rim_shape]
+            specs += [vmem(), anywhere(), vmem()]
+            scratch += [pltpu.VMEM(picked_shape, jnp.float32), pltpu.SemaphoreType.DMA]
+            arrays += [asked] if t else []
         result = pl.pallas_call(
-            functools.partial(apply_kernel, last),
+            functools.partial(apply_kernel, t),
             out_shape=tuple(shapes),
             in_specs=[smem()] * len(scalars) + [vmem()] * len(arrays),
-            out_specs=tuple(vmem() for _ in shapes),
-            scratch_shapes=[pltpu.VMEM((slots + 1, PIECES * vectors, side), jnp.bfloat16)],
+            out_specs=tuple(specs),
+            scratch_shapes=scratch,
             compiler_params=params(),
             cost_estimate=cost(tiles.size * 2 * vectors * PIECES, tile_bytes),
             name="apply_last" if last else "apply",
@@ -274,7 +342,7 @@
         powers.append(result[0])
         grams.append(result[1])
         if not last:
-            scaled, outgoing = result[2], result[3]
+            scaled, outgoing, rims = result[2:]
     gathered = lax.all_to_all(grams[-1], ("group", "row"), 0, 0, tiled=True)
     krylov, trust = pl.pallas_call(
         functools.partial(finish_kernel, float(groups * peers * blocks * side)),

time: 81.2 us -> 86 us (1.059)
  blocking collectives: 0 us -> 57.9 us
  starting transfers between devices: 43 us -> 2.58 us
  waiting for transfers between devices: 13.7 us -> 8.23 us
  Pallas kernels: 20.7 us -> 15.3 us
  local copies, waits for them, and re-layouts: 2.01 us -> 0.69 us
    all_to_all x0 -> x6, blocking collectives: none -> 57.9 us  [the longest x3 29.8 us: exchange(): return lax.all_to_all(outgoing, 'row', 0, 0, tiled=True)]
    ppermute x6 -> x0, starting transfers between devices: 18.2 us -> none  [the longest x3 14.3 us: neighbours(): low = lax.ppermute(scaled[blocks - RIM:], 'group', up)]
    all_to_all x4 -> x0, starting transfers between devices: 16.8 us -> none  [the longest x3 11.6 us: exchange(): return lax.all_to_all(outgoing, 'row', 0, 0, tiled=True)]
    pallas_call x4 -> x3, Pallas kernels: 14.7 us -> 8.04 us  [local(): pl.pallas_call(functools.partial(apply_kernel, t), out_shape=tuple(shapes...]
    all_to_all x1, starting transfers between devices: 7.93 us -> 2.58 us  [local(): gathered = lax.all_to_all(grams[-1], ('group', 'row'), 0, 0, tiled=True)]
    ppermute x6 -> x0, waiting for transfers between devices: 4.25 us -> none  [the longest x3 4.24 us: neighbours(): low = lax.ppermute(scaled[blocks - RIM:], 'group', up)]
    broadcast_in_dim x1 -> x0, local copies, waits for them, and re-layouts: 1.31 us -> none  [local(): jnp.broadcast_to(listed[None], (peers, SLOTS, peers))]
    pallas_call x1, Pallas kernels: 3.39 us -> 4.66 us  [local(): pl.pallas_call(roots_kernel, out_shape=(f32(blocks, 1, side), f32(blocks,...]
  transfers between devices with their start and end apart: 11 -> 1, of which waited for: 5 -> 1; matrix products, arithmetic and copies ran while one was open for 0% -> 0% of each run, Pallas kernels for 4% -> 0%
where the time goes in v2:
time: 86 us; the launch traced here: 85.6 us
  blocking collectives  57.9 us (67%)
  Pallas kernels  15.3 us (18%)
  waiting for transfers between devices  8.23 us (10%)
  starting transfers between devices  2.58 us (3%)
    all_to_all x3, blocking collectives, exchange(): return lax.all_to_all(outgoing, 'row', 0, 0, tiled=True)  29.8 us
    all_to_all x3, blocking collectives, local(): beside = lax.all_to_all(rims, 'group', 0, 0, tiled=True)  28.1 us
    all_to_all x1, waiting for transfers between devices, local(): gathered = lax.all_to_all(grams[-1], ('group', 'row'), 0, 0, tiled=True)  8.23 us
    pallas_call x3, Pallas kernels, local(): pl.pallas_call(functools.partial(apply_kernel, t), out_shape=tuple(shapes...  8.04 us
    pallas_call x1, Pallas kernels, local(): pl.pallas_call(roots_kernel, out_shape=(f32(blocks, 1, side), f32(blocks,...  4.66 us
    pallas_call x1, Pallas kernels, local(): pl.pallas_call(functools.partial(finish_kernel, float(groups * peers * bl...  2.6 us
    all_to_all x1, starting transfers between devices, local(): gathered = lax.all_to_all(grams[-1], ('group', 'row'), 0, 0, tiled=True)  2.58 us
  transfers between devices with their start and end apart: 1, of which 1 were waited for; matrix products, arithmetic and copies ran while one was open for 0% of the time, Pallas kernels for 0%

profile of v2, /device:TPU:0, one launch (start us, length us, event | category | flops | bytes accessed | tf_op | source)
XLA Modules:
  0.0 85.6 jit_solution(16692119423560992349)
XLA Ops:
  0.0 0.0 copy-start.2
  0.0 0.0 copy-start.3
  0.0 0.0 copy-start.1
  0.0 4.7 %roots.1 = (f32[8,1,128]{2,1,0:T(1,128)S(1)}, f32[8,16,128]{2,1,0:T(8,128)S(1)}, bf16[8,16,128,128]{3,2,1,0:T(8,128)(2,1)S(1)}, f32[8,9,16,128]{3,2,1,0:T(8,128)S(1)}, f32[4,2,16,128]{3,2,1,0:T(8,128)S(1)}) custom-call(s32[1]{0:T(128)} %bitcast.33.group_ref.refs_0_, s32[8]{0:T(128)} %refs_1_.5, s32[2,8]{1,0:T(2,128)} %bitcast.102, ...), custom_call_target="tpu_custom_call" | custom-call | flops 4194304 | bytes 4194304 | tf_op jit(solution)/shard_map/roots/pallas_call | solution.py:290
  4.7 11.9 %all_to_all.35.refs_8_ = f32[4,2,16,128]{3,2,1,0:T(8,128)S(1)} all-to-all(f32[4,2,16,128]{3,2,1,0:T(8,128)S(1)} %get-tuple-element.51), channel_id=1, replica_groups=mesh['group'=4,'row'=8] {'group'}, dimensions={0} | all-to-all | bytes 131072 | tf_op jit(solution)/shard_map/all_to_all | solution.py:318
  16.5 14.0 %all_to_all.36.refs_7_.refs_8_ = f32[8,9,16,128]{3,2,1,0:T(8,128)S(1)} all-to-all(f32[8,9,16,128]{3,2,1,0:T(8,128)S(1)} %get-tuple-element.50), channel_id=1, replica_groups=mesh['group'=4,'row'=8] {'row'}, dimensions={0} | all-to-all | bytes 1179648 | tf_op jit(solution)/shard_map/all_to_all | solution.py:244
  30.5 0.0 copy-done.2
  30.5 0.0 copy-done.3
  30.5 0.0 copy-done.1
  30.5 2.5 %apply.2 = (f32[8,16,128]{2,1,0:T(8,128)S(1)}, f32[16,16]{1,0:T(8,128)S(1)}, f32[8,16,128]{2,1,0:T(8,128)S(1)}, f32[16,16,128]{2,1,0:T(8,128)S(1)}, f32[4,2,16,128]{3,2,1,0:T(8,128)S(1)}) custom-call(s32[1]{0:T(128)} %bitcast.33.group_ref.refs_0_, s32[8]{0:T(128)S(1)} %copy-done.2, s32[8,16]{1,0:T(8,128)S(1)} %copy-done.1, s32[2,8]{1,0:T(2,128)S(1)} %bitcast.103, ...), custom_call_target="tpu_custom_call" | custom-call | flops 201326592 | bytes 4194304 | tf_op jit(solution)/shard_map/apply/pallas_call | solution.py:332
  33.1 8.1 %all_to_all.37.refs_7_ = f32[4,2,16,128]{3,2,1,0:T(8,128)S(1)} all-to-all(f32[4,2,16,128]{3,2,1,0:T(8,128)S(1)} %get-tuple-element.54), channel_id=1, replica_groups=mesh['group'=4,'row'=8] {'group'}, dimensions={0} | all-to-all | bytes 131072 | tf_op jit(solution)/shard_map/all_to_all | solution.py:318
  41.2 7.9 %all_to_all.38.refs_6_ = f32[16,16,128]{2,1,0:T(8,128)S(1)} all-to-all(f32[16,16,128]{2,1,0:T(8,128)S(1)} %get-tuple-element.53), channel_id=1, replica_groups=mesh['group'=4,'row'=8] {'row'}, dimensions={0} | all-to-all | bytes 262144 | tf_op jit(solution)/shard_map/all_to_all | solution.py:244
  49.1 0.0 copy-start
  49.1 2.5 %apply.3 = (f32[8,16,128]{2,1,0:T(8,128)S(1)}, f32[16,16]{1,0:T(8,128)S(1)}, f32[8,16,128]{2,1,0:T(8,128)S(1)}, f32[16,16,128]{2,1,0:T(8,128)S(1)}, f32[4,2,16,128]{3,2,1,0:T(8,128)S(1)}) custom-call(s32[1]{0:T(128)} %bitcast.33.group_ref.refs_0_, s32[8]{0:T(128)S(1)} %copy-done.2, s32[8,16]{1,0:T(8,128)S(1)} %copy-done.1, ...), custom_call_target="tpu_custom_call" | custom-call | flops 201326592 | bytes 4194304 | tf_op jit(solution)/shard_map/apply/pallas_call | solution.py:332
  51.6 8.1 %all_to_all.39.refs_7_ = f32[4,2,16,128]{3,2,1,0:T(8,128)S(1)} all-to-all(f32[4,2,16,128]{3,2,1,0:T(8,128)S(1)} %get-tuple-element.57), channel_id=1, replica_groups=mesh['group'=4,'row'=8] {'group'}, dimensions={0} | all-to-all | bytes 131072 | tf_op jit(solution)/shard_map/all_to_all | solution.py:318
  59.7 7.9 %all_to_all.40.refs_6_ = f32[16,16,128]{2,1,0:T(8,128)S(1)} all-to-all(f32[16,16,128]{2,1,0:T(8,128)S(1)} %get-tuple-element.56), channel_id=1, replica_groups=mesh['group'=4,'row'=8] {'row'}, dimensions={0} | all-to-all | bytes 262144 | tf_op jit(solution)/shard_map/all_to_all | solution.py:244
  67.6 3.0 %apply_last.1 = (f32[8,16,128]{2,1,0:T(8,128)S(1)}, f32[32,8,128]{2,1,0:T(8,128)}) custom-call(s32[1]{0:T(128)} %bitcast.33.group_ref.refs_0_, s32[8]{0:T(128)S(1)} %copy-done.2, s32[8,16]{1,0:T(8,128)S(1)} %copy-done.1, bf16[8,16,128,128]{3,2,1,0:T(8,128)(2,1)S(1)} %get-tuple-element.47.refs_4_.refs_3_, f32[8,1,128]{2,1,0:T(1,128)S(1)} %get-tuple-element.48.refs_5_.refs_4_, ...), custom_call_target="tpu_custom_call" | custom-call | flops 201326592 | bytes 4194304 | tf_op jit(solution)/shard_map/apply_last/pallas_call | solution.py:332
  70.6 2.6 %all-to-all-start.6 = ((f32[32,8,128]{2,1,0:T(8,128)}), f32[32,8,128]{2,1,0:T(8,128)S(1)}, u32[]{:S(2)}, u32[]{:S(2)}) async-start(f32[32,8,128]{2,1,0:T(8,128)} %get-tuple-element.60), calls=%async_computation.6 | async-start | bytes 262144 | tf_op jit(solution)/shard_map/all_to_all | solution.py:346
  73.2 8.2 %all-to-all-done.6.grams_ref = f32[32,8,128]{2,1,0:T(8,128)S(1)} async-done(((f32[32,8,128]{2,1,0:T(8,128)}), f32[32,8,128]{2,1,0:T(8,128)S(1)}, u32[]{:S(2)}, u32[]{:S(2)}) %all-to-all-start.6) | async-done | bytes 131104 | tf_op jit(solution)/shard_map/all_to_all | solution.py:346
  81.4 2.6 %finish.1 = (f32[3,8,16,128]{3,2,1,0:T(8,128)S(1)}, s32[1]{0:T(128)}) custom-call(f32[32,8,128]{2,1,0:T(8,128)S(1)} %all-to-all-done.6.grams_ref, f32[8,16,128]{2,1,0:T(8,128)S(1)} %get-tuple-element.61.refs_0_, f32[8,16,128]{2,1,0:T(8,128)S(1)} %get-tuple-element.62.refs_1_, f32[8,16,128]{2,1,0:T(8,128)S(1)} %get-tuple-element.63.refs_2_), custom_call_target="tpu_custom_call" | custom-call | tf_op jit(solution)/shard_map/finish/pallas_call | solution.py:347
  84.7 0.0 copy-done
  84.7 0.2 conditional.1
  84.9 0.0 copy-start.4
  84.9 0.7 copy-done.4
Async XLA Ops:
  0.0 30.5 %copy-start.2 = (s32[8]{0:T(128)S(1)}, s32[8]{0:T(128)}, u32[]{:S(2)}) copy-start(s32[8]{0:T(128)} %refs_1_.5) | copy-start | bytes 100
  0.0 30.5 %copy-start.3 = (s32[1,1,8,2]{2,3,1,0:T(2,128)S(1)}, s32[1,1,8,2]{2,3,1,0:T(2,128)}, u32[]{:S(2)}) copy-start(s32[1,1,8,2]{2,3,1,0:T(2,128)} %param.18) | copy-start | bytes 196
  0.0 30.5 %copy-start.1 = (s32[8,16]{1,0:T(8,128)S(1)}, s32[8,16]{1,0:T(8,128)}, u32[]{:S(2)}) copy-start(s32[8,16]{1,0:T(8,128)} %refs_2_.5) | copy-start | bytes 1540
  49.1 35.6 %copy-start = (f32[8,16,128]{2,1,0:T(8,128)S(1)}, f32[8,16,128]{2,1,0:T(8,128)}, u32[]{:S(2)}) copy-start(f32[8,16,128]{2,1,0:T(8,128)} %basis_ref.1) | copy-start | bytes 196612
  70.6 10.8 %all-to-all-start.6 = ((f32[32,8,128]{2,1,0:T(8,128)}), f32[32,8,128]{2,1,0:T(8,128)S(1)}, u32[]{:S(2)}, u32[]{:S(2)}) async-start(f32[32,8,128]{2,1,0:T(8,128)} %get-tuple-element.60), calls=%async_computation.6 | async-start | bytes 262144 | tf_op jit(solution)/shard_map/all_to_all | solution.py:346
  84.9 0.7 copy-start.4

commit v3 on v2

--- a/solution.py
+++ b/solution.py
@@ -11,9 +11,9 @@
 RIM = 2
 ITERS = 3
 LANES = 128
-PIECES = 3
+PIECES = 2
 VMEM_BYTES = 24 * 1024 * 1024
-TRUST = 256.0
+TRUST = 64.0
 TINY = 1e-25
 
 HIGH = lax.Precision.HIGHEST
@@ -28,8 +28,8 @@
     return pl.BlockSpec(memory_space=pltpu.SMEM)
 
 
-def anywhere():
-    return pl.BlockSpec(memory_space=pl.ANY)
+def hbm():
+    return pl.BlockSpec(memory_space=pltpu.HBM)
 
 
 def f32(*shape):
@@ -44,65 +44,71 @@
     return pl.CostEstimate(flops=flops, bytes_accessed=moved, transcendentals=0)
 
 
-def roots_kernel(group_ref, count_ref, want_ref, tiles_hbm, basis_ref, root_ref, scaled_ref,
-                 tiles_ref, spread_hbm, rim_ref, lists, tile_sems, sems):
-    blocks, per_row, side, _ = tiles_ref.shape
-    peers = spread_hbm.shape[0]
+def stream(tiles_hbm, tiles_ref, sems):
     loads = [
-        pltpu.make_async_copy(tiles_hbm.at[b], tiles_ref.at[b], tile_sems.at[b])
-        for b in range(blocks)
+        pltpu.make_async_copy(tiles_hbm.at[b], tiles_ref.at[b], sems.at[b])
+        for b in range(tiles_ref.shape[0])
     ]
     for load in loads:
         load.start()
-    half = lists.shape[2] // SLOTS
+    return loads
+
+
+def stream_scratch(tiles):
+    return [pltpu.VMEM(tiles.shape, tiles.dtype), pltpu.SemaphoreType.DMA((tiles.shape[0],))]
+
+
+def roots_kernel(place_ref, count_ref, want_ref, tiles_hbm, basis_ref, root_ref, sent_ref,
+                 first_ref, second_ref, tiles_ref, load_sems):
+    blocks, per_row, side, _ = tiles_ref.shape
+    peers = want_ref.shape[1]
+    vectors = basis_ref.shape[1]
+    loads = stream(tiles_hbm, tiles_ref, load_sems)
     for p in range(peers):
-        owned = (group_ref[0] * peers + p) * blocks
+        owned = (place_ref[0] * peers + p) * blocks
         for c in range(SLOTS):
-            at = jnp.full((half, side), want_ref[c, p] - owned, jnp.int32)
-            lists[p, 0, pl.ds(c * half, half)] = at.astype(jnp.float32)
-    sends = [pltpu.make_async_copy(lists, spread_hbm.at[:, pl.ds(blocks, 1)], sems.at[peers])]
-    sends[0].start()
+            at = jnp.full((1, side), want_ref[c, p] - owned, jnp.int32).astype(jnp.float32)
+            block, row = divmod(p * SLOTS + c, vectors)
+            sent_ref[blocks + block, row : row + 1] = at
+    rows = lax.broadcasted_iota(jnp.int32, (side, side), 0)
+    lanes = lax.broadcasted_iota(jnp.int32, (side, side), 1)
+    unit = rows == lanes
     for b in range(blocks):
         loads[b].wait()
-        total = jnp.zeros((side, side), jnp.float32)
-        for s in range(per_row):
-            live = (s < count_ref[b]).astype(jnp.float32)
-            wide = tiles_ref[b, s].astype(jnp.float32)
-            total = total + wide * wide * live
-        sums = jnp.sum(total.T, axis=0, keepdims=True)
+        held = [tiles_ref[b, s] for s in range(per_row)]
+        live = [
+            jnp.where(s < count_ref[b], tile, jnp.zeros_like(tile)) for s, tile in enumerate(held)
+        ]
+        products = lax.dot_general(
+            jnp.concatenate(live, axis=1), jnp.concatenate(held, axis=1), NT,
+            preferred_element_type=jnp.float32,
+        )
+        sums = jnp.sum(jnp.where(unit, products, 0.0), axis=0, keepdims=True)
         root = lax.rsqrt(jnp.sqrt(1e-06 + sums))
         root_ref[b] = root
-        scaled_ref[b] = basis_ref[b] * root
-    for p in range(peers):
-        send = pltpu.make_async_copy(scaled_ref, spread_hbm.at[p, pl.ds(0, blocks)], sems.at[p])
-        send.start()
-        sends.append(send)
-    rims_into(group_ref[0], scaled_ref, rim_ref)
-    for send in sends:
-        send.wait()
-
-
-def rims_into(group, scaled_ref, rim_ref):
-    blocks = scaled_ref.shape[0]
-    for d in range(rim_ref.shape[0]):
-        start = jnp.where(d < group, 0, blocks - RIM)
-        for h in range(RIM):
-            rim_ref[d, h] = scaled_ref[start + h]
-
-
-def pick_into(asked_ref, scaled_ref, out_ref):
-    peers, blocks, vectors, _ = asked_ref.shape
-    blocks -= 1
-    half = vectors // SLOTS
+        sent_ref[b] = basis_ref[b] * root
+    swaps_into(place_ref[0], blocks, sent_ref, first_ref, second_ref)
+
+
+def swaps_into(group, blocks, scaled_ref, first_ref, second_ref):
+    odd = group % 2
+    for h in range(RIM):
+        first_ref[h] = scaled_ref[(1 - odd) * (blocks - RIM) + h]
+        second_ref[h] = scaled_ref[odd * (blocks - RIM) + h]
+
+
+def pick_into(row_at, asked_ref, scaled_ref, out_ref):
+    peers = asked_ref.shape[0]
+    blocks, vectors, side = scaled_ref.shape
     for p in range(peers):
         for c in range(SLOTS):
-            at = asked_ref[p, blocks, c * half : (c + 1) * half]
-            for row in range(0, vectors, half):
-                rows = slice(row, row + half)
-                value = scaled_ref[0, rows]
-                for b in range(1, blocks):
-                    value = jnp.where(at == float(b), scaled_ref[b, rows], value)
-                out_ref[p * SLOTS + c, rows] = value
+            entry = row_at * SLOTS + c
+            at = asked_ref[p, blocks + entry // vectors, pl.ds(entry % vectors, 1)]
+            at = jnp.broadcast_to(at, (vectors, side))
+            value = scaled_ref[0]
+            for b in range(1, blocks):
+                value = jnp.where(at == float(b), scaled_ref[b], value)
+            out_ref[p * SLOTS + c] = value
 
 
 def split_into(x, out_ref, slot):
@@ -130,18 +136,20 @@
 
 def apply_kernel(step_at, *refs):
     last, opening = step_at == ITERS - 1, step_at == 0
-    group_ref, count_ref, cols_ref, *refs = refs
+    place_ref, count_ref, cols_ref, *refs = refs
     if opening:
         want_ref, *refs = refs
-    tiles_ref, root_ref, own_ref, recv_ref, recv_rim_ref, *refs = refs
+    tiles_hbm, root_ref, own_ref, recv_ref, swapped_ref, swapped_next_ref, *refs = refs
+    *refs, tiles_ref, load_sems = refs
+    loads = stream(tiles_hbm, tiles_ref, load_sems)
     if last:
-        *before, applied_ref, gram_ref, table = refs
+        *before, applied_ref, gram_hbm, table, packed_ref, sems = refs
     else:
         asked_ref, refs = (recv_ref, refs) if opening else (refs[0], refs[1:])
-        applied_ref, gram_ref, scaled_ref, out_hbm, rim_ref, table, picked_ref, sem = refs
+        applied_ref, gram_ref, scaled_ref, out_hbm, first_ref, second_ref, table, picked_ref, sem = refs
     blocks, per_row, side, _ = tiles_ref.shape
     vectors = own_ref.shape[1]
-    group = group_ref[0]
+    group = place_ref[0]
     slot = 0
     for b in range(blocks):
         split_into(own_ref[b], table, slot)
@@ -157,10 +165,10 @@
         for n in range(recv_ref.shape[0]):
             split_into(recv_ref[n], table, slot)
             slot += 1
-    groups = recv_rim_ref.shape[0]
-    for side_at in (jnp.maximum(group - 1, 0), jnp.minimum(group + 1, groups - 1)):
+    odd = group % 2 == 1
+    for a_ref, b_ref in ((swapped_ref, swapped_next_ref), (swapped_next_ref, swapped_ref)):
         for h in range(RIM):
-            split_into(recv_rim_ref[side_at, h], table, slot)
+            split_into(jnp.where(odd, a_ref[h], b_ref[h]), table, slot)
             slot += 1
     table[slot] = jnp.zeros(table.shape[1:], table.dtype)
     rows = []
@@ -170,6 +178,7 @@
             at = jnp.where(s < count_ref[b], cols_ref[b, s], slot)
             picked.append(table[at])
         x = jnp.concatenate(picked, axis=1)
+        loads[b].wait()
         t = jnp.concatenate([tiles_ref[b, s] for s in range(per_row)], axis=1)
         product = lax.dot_general(x, t, NT, preferred_element_type=jnp.float32)
         total = product[(PIECES - 1) * vectors :]
@@ -182,25 +191,32 @@
         if not last:
             scaled_ref[b] = row * root
     if not last:
-        pick_into(asked_ref, scaled_ref, picked_ref)
+        pick_into(place_ref[1], asked_ref, scaled_ref, picked_ref)
         send = pltpu.make_async_copy(picked_ref, out_hbm, sem)
         send.start()
-        rims_into(group, scaled_ref, rim_ref)
+        swaps_into(group, blocks, scaled_ref, first_ref, second_ref)
     flat = jnp.concatenate(rows, axis=1)
     gram = lax.dot_general(flat, flat, NT, precision=HIGH, preferred_element_type=jnp.float32)
     if last:
-        packed = pack_grams([ref[...] for ref in before] + [gram])
-        for n in range(gram_ref.shape[0]):
-            gram_ref[n] = packed
+        packed_ref[0] = pack_grams([ref[...] for ref in before] + [gram])
+        sends = [
+            pltpu.make_async_copy(packed_ref, gram_hbm.at[pl.ds(n, 1)], sems.at[n])
+            for n in range(gram_hbm.shape[0])
+        ]
+        for send in sends:
+            send.start()
+        for send in sends:
+            send.wait()
     else:
         gram_ref[...] = gram
         send.wait()
 
 
 def finish_kernel(row_total, grams_ref, *refs):
-    applied_refs, (out_ref, trust_ref) = refs[:ITERS], refs[ITERS:]
+    applied_refs, (out_hbm, trust_ref, out_ref, sems) = refs[:ITERS], refs[ITERS:]
     devices = grams_ref.shape[0]
     blocks, vectors = out_ref.shape[1:3]
+    sends = [pltpu.make_async_copy(out_ref.at[t], out_hbm.at[t], sems.at[t]) for t in range(ITERS)]
     total = grams_ref[0]
     for n in range(1, devices):
         total = total + grams_ref[n]
@@ -228,7 +244,10 @@
                 inverse, applied_refs[t][b], (((1,), (0,)), ((), ())), precision=HIGH,
                 preferred_element_type=jnp.float32,
             )
+        sends[t].start()
     trust_ref[0] = good.astype(jnp.int32)
+    for send in sends:
+        send.wait()
 
 
 def neighbours(scaled):
@@ -240,8 +259,11 @@
     return low, high
 
 
-def exchange(outgoing):
-    return lax.all_to_all(outgoing, "row", 0, 0, tiled=True)
+def swap(first, second):
+    count = lax.axis_size("group")
+    ups = [[(i, i + 1) for i in range(start, count - 1, 2)] for start in (0, 1)]
+    pairs = [up + [(j, i) for i, j in up] for up in ups]
+    return [lax.ppermute(x, "group", pair) for x, pair in zip((first, second), pairs)]
 
 
 def stepwise(start_basis, tiles, tile_cols, tile_count, recv_list):
@@ -281,60 +303,61 @@
     groups, peers = lax.axis_size("group"), lax.axis_size("row")
     blocks, per_row, side, _ = tiles.shape
     vectors = start_basis.shape[1]
-    group = lax.axis_index("group").astype(jnp.int32).reshape(1)
+    place = jnp.stack([lax.axis_index("group"), lax.axis_index("row")]).astype(jnp.int32)
     wanted = jnp.transpose(recv_list.reshape(peers, SLOTS))
+    lists = pl.cdiv(peers * SLOTS, vectors)
     tile_bytes = tiles.size * 2
+    far_tiles = pltpu.with_memory_space_constraint(tiles, pltpu.HBM)
     block_shape = (vectors, side)
     picked_shape = (peers * SLOTS,) + block_shape
-    rim_shape = f32(groups, RIM, *block_shape)
-    root, scaled, held, spread, rims = pl.pallas_call(
+    rim_shape = f32(RIM, *block_shape)
+    root, scaled, *rims = pl.pallas_call(
         roots_kernel,
         out_shape=(
             f32(blocks, 1, side),
-            f32(blocks, *block_shape),
-            pltpu.VMEM(tiles.shape, tiles.dtype),
-            f32(peers, blocks + 1, *block_shape),
+            f32(blocks + lists, *block_shape),
+            rim_shape,
             rim_shape,
         ),
-        in_specs=[smem(), smem(), smem(), anywhere(), vmem()],
-        out_specs=(vmem(), vmem(), vmem(), anywhere(), vmem()),
-        scratch_shapes=[
-            pltpu.VMEM((peers, 1) + block_shape, jnp.float32),
-            pltpu.SemaphoreType.DMA((blocks,)),
-            pltpu.SemaphoreType.DMA((peers + 1,)),
-        ],
+        in_specs=[smem(), smem(), smem(), hbm(), vmem()],
+        out_specs=(vmem(),) * 4,
+        scratch_shapes=stream_scratch(tiles),
         compiler_params=params(),
         cost_estimate=cost(tiles.size * 2, tile_bytes),
         name="roots",
-    )(group, tile_count, wanted, tiles, start_basis)
+    )(place, tile_count, wanted, far_tiles, start_basis)
     slots = blocks + peers * SLOTS + 2 * RIM
     powers, grams = [], []
-    outgoing = spread
     for t in range(ITERS):
         last = t == ITERS - 1
-        received = exchange(outgoing)
         if t == 0:
-            asked = received
-        beside = lax.all_to_all(rims, "group", 0, 0, tiled=True)
-        scalars = [group, tile_count, tile_cols] + ([wanted] if t == 0 else [])
-        arrays = [held, root, scaled, received, beside]
+            swapped = swap(*rims)
+            received = asked = lax.all_gather(scaled, "row", axis=0)
+        else:
+            received = lax.all_to_all(outgoing, "row", 0, 0, tiled=True)
+            swapped = swap(*rims)
+        scalars = [place, tile_count, tile_cols] + ([wanted] if t == 0 else [])
+        arrays = [far_tiles, root, scaled, received, *swapped]
         shapes = [f32(blocks, *block_shape)]
         specs = [vmem(), vmem()]
         scratch = [pltpu.VMEM((slots + 1, PIECES * vectors, side), jnp.bfloat16)]
         if last:
-            shapes += [f32(groups * peers, vectors // 2, LANES)]
+            shapes += [pltpu.HBM((groups * peers, vectors // 2, LANES), jnp.float32)]
+            specs = [vmem(), hbm()]
+            scratch += [pltpu.VMEM((1, vectors // 2, LANES), jnp.float32), pltpu.SemaphoreType.DMA((groups * peers,))]
             arrays += grams
         else:
-            shapes += [f32(vectors, vectors), f32(blocks, *block_shape), f32(*picked_shape), rim_shape]
-            specs += [vmem(), anywhere(), vmem()]
+            shapes += [f32(vectors, vectors), f32(blocks, *block_shape), pltpu.HBM(picked_shape, jnp.float32)]
+            shapes += [rim_shape] * 2
+            specs += [vmem(), hbm(), vmem(), vmem()]
             scratch += [pltpu.VMEM(picked_shape, jnp.float32), pltpu.SemaphoreType.DMA]
             arrays += [asked] if t else []
         result = pl.pallas_call(
             functools.partial(apply_kernel, t),
             out_shape=tuple(shapes),
-            in_specs=[smem()] * len(scalars) + [vmem()] * len(arrays),
+            in_specs=[smem()] * len(scalars) + [hbm()] + [vmem()] * (len(arrays) - 1),
             out_specs=tuple(specs),
-            scratch_shapes=scratch,
+            scratch_shapes=scratch + stream_scratch(tiles),
             compiler_params=params(),
             cost_estimate=cost(tiles.size * 2 * vectors * PIECES, tile_bytes),
             name="apply_last" if last else "apply",
@@ -342,13 +365,17 @@
         powers.append(result[0])
         grams.append(result[1])
         if not last:
-            scaled, outgoing, rims = result[2:]
+            scaled, outgoing, *rims = result[2:]
     gathered = lax.all_to_all(grams[-1], ("group", "row"), 0, 0, tiled=True)
     krylov, trust = pl.pallas_call(
         functools.partial(finish_kernel, float(groups * peers * blocks * side)),
-        out_shape=(f32(ITERS, blocks, vectors, side), jax.ShapeDtypeStruct((1,), jnp.int32)),
+        out_shape=(pltpu.HBM((ITERS, blocks, vectors, side), jnp.float32), jax.ShapeDtypeStruct((1,), jnp.int32)),
         in_specs=[vmem()] * (1 + ITERS),
-        out_specs=(vmem(), smem()),
+        out_specs=(hbm(), smem()),
+        scratch_shapes=[
+            pltpu.VMEM((ITERS, blocks, vectors, side), jnp.float32),
+            pltpu.SemaphoreType.DMA((ITERS,)),
+        ],
         compiler_params=params(),
         name="finish",
     )(gathered, *powers)

time: 86 us -> 283 us (3.29)
  blocking collectives: 57.9 us -> 159 us
  starting transfers between devices: 2.58 us -> 38.8 us
  other arithmetic: 0 us -> 18 us
  matrix products: 0 us -> 17.5 us
  Pallas kernels: 15.3 us -> 25.9 us
  waiting for transfers between devices: 8.23 us -> 17.7 us
  local copies, waits for them, and re-layouts: 0.69 us -> 4.46 us
    psum x0 -> x3, blocking collectives: none -> 118 us  [stepwise(): factor = jnp.linalg.cholesky(lax.psum(gram, ('group', 'row')) / row_total)]
    all_to_all x6 -> x0, blocking collectives: 57.9 us -> none  [the longest x3 29.8 us: exchange(): return lax.all_to_all(outgoing, 'row', 0, 0, tiled=True)]
    all_gather x0 -> x4, blocking collectives: none -> 40.5 us  [the longest x3 30.5 us: stepwise(): lax.all_gather(scaled, 'row', axis=0, tiled=True)]
    ppermute x0 -> x12, starting transfers between devices: none -> 24.7 us  [the longest x6 13.4 us: swap(): lax.ppermute(x, 'group', pair)]
    dot_general x0 -> x10, matrix products: none -> 16.9 us  [the longest x3 15.6 us: stepwise(): jnp.einsum('btij,btkj->bki', tiles, picked, precision=HIGH, preferred_ele...]
    another operation x0 -> x17, other arithmetic: none -> 13.2 us  [the longest x9 6.63 us: stepwise(): factor = jnp.linalg.cholesky(lax.psum(gram, ('group', 'row')) / row_total)]
    ppermute x0 -> x12, waiting for transfers between devices: none -> 9.45 us  [the longest x3 7.32 us: neighbours(): high = lax.ppermute(scaled[:RIM], 'group', down)]
    pallas_call x3, Pallas kernels: 8.04 us -> 17.2 us  [local(): pl.pallas_call(functools.partial(apply_kernel, t), out_shape=tuple(shapes...]
  transfers between devices with their start and end apart: 1 -> 15, of which waited for: 1 -> 5; matrix products, arithmetic and copies ran while one was open for 0% -> 1% of each run, Pallas kernels for 0% -> 0%
where the time goes in v3:
time: 283 us; the launch traced here: 282 us
  blocking collectives  159 us (56%)
  starting transfers between devices  38.8 us (14%)
  Pallas kernels  25.9 us (9%)
  other arithmetic  18 us (6%)
  waiting for transfers between devices  17.7 us (6%)
  matrix products  17.5 us (6%)
  local copies, waits for them, and re-layouts  4.46 us (2%)
    psum x3, blocking collectives, stepwise(): factor = jnp.linalg.cholesky(lax.psum(gram, ('group', 'row')) / row_total)  118 us
    all_gather x3, blocking collectives, stepwise(): lax.all_gather(scaled, 'row', axis=0, tiled=True)  30.5 us
    pallas_call x3, Pallas kernels, local(): pl.pallas_call(functools.partial(apply_kernel, t), out_shape=tuple(shapes...  17.2 us
    dot_general x3, matrix products, stepwise(): jnp.einsum('btij,btkj->bki', tiles, picked, precision=HIGH, preferred_ele...  15.6 us
    ppermute x6, starting transfers between devices, swap(): lax.ppermute(x, 'group', pair)  13.4 us
    all_gather x1, blocking collectives, local(): received = asked = lax.all_gather(scaled, 'row', axis=0)  10 us
    all_to_all x1, waiting for transfers between devices, local(): gathered = lax.all_to_all(grams[-1], ('group', 'row'), 0, 0, tiled=True)  8.23 us
    all_to_all x2, starting transfers between devices, local(): received = lax.all_to_all(outgoing, 'row', 0, 0, tiled=True)  7.47 us
  transfers between devices with their start and end apart: 15, of which 5 were waited for; matrix products, arithmetic and copies ran while one was open for 1% of the time, Pallas kernels for 0%

profile of v3, /device:TPU:0, one launch (start us, length us, event | category | flops | bytes accessed | tf_op | source)
XLA Modules:
  0.0 282.2 jit_solution(9456024442682369958)
XLA Ops:
  0.1 5.5 %roots.1 = (f32[8,1,128]{2,1,0:T(1,128)S(1)}, f32[9,16,128]{2,1,0:T(8,128)S(1)}, f32[2,16,128]{2,1,0:T(8,128)S(1)}, f32[2,16,128]{2,1,0:T(8,128)S(1)}) custom-call(s32[2]{0:T(128)S(1)} %pad_add_fusion.place_ref.refs_0_, s32[8]{0:T(128)} %refs_1_.5, s32[2,8]{1,0:T(2,128)} %bitcast.106, bf16[8,16,128,128]{3,2,1,0:T(8,128)(2,1)} %refs_3_.3, f32[8,16,128]{2,1,0:T(8,128)} %basis_ref.1), custom_call_target="tpu_custom_call" | custom-call | flops 4194304 | bytes 4194304 | tf_op jit(solution)/shard_map/roots/pallas_call | solution.py:314
  5.6 3.1 %collective-permute-start.6 = (f32[2,16,128]{2,1,0:T(8,128)S(1)}, f32[2,16,128]{2,1,0:T(8,128)S(1)}, u32[]{:S(2)}, u32[]{:S(2)}) collective-permute-start(f32[2,16,128]{2,1,0:T(8,128)S(1)} %get-tuple-element.50), channel_id=1, source_target_pairs={{0,8},{16,24},{8,0},{24,16},{1,9},{17,25},{9,1},{25,17},{2,10},{18... | collective-permute-start | bytes 49160 | tf_op jit(solution)/shard_map/ppermute | solution.py:266
  8.7 0.7 collective-permute-start.7
  9.4 10.0 %all-gather = f32[72,16,128]{2,1,0:T(8,128)S(1)} all-gather(f32[9,16,128]{2,1,0:T(8,128)S(1)} %get-tuple-element.49.refs_6_), channel_id=2, replica_groups=mesh['group'=4,'row'=8] {'row'}, dimensions={0}, use_global_device_ids=true | all-gather | bytes 663552 | tf_op jit(solution)/shard_map/all_gather | solution.py:335
  19.4 5.6 %apply.2 = (f32[8,16,128]{2,1,0:T(8,128)S(1)}, f32[16,16]{1,0:T(8,128)S(1)}, f32[8,16,128]{2,1,0:T(8,128)S(1)}, f32[16,16,128]{2,1,0:T(8,128)}, f32[2,16,128]{2,1,0:T(8,128)S(1)}, /*index=5*/f32[2,16,128]{2,1,0:T(8,128)S(1)}) custom-call(s32[2]{0:T(128)S(1)} %pad_add_fusion.place_ref.refs_0_, s32[8]{0:T(128)S(1)} %copy-done.2, s32[8,16]{1,0:T(8,128)S(1)} %copy-done.1, ...), custom_call_target="tpu_custom_call" | custom-call | flops 134217728 | bytes 4194304 | tf_op jit(solution)/shard_map/apply/pallas_call | solution.py:355
  25.0 3.4 %all-to-all-start = ((f32[16,16,128]{2,1,0:T(8,128)}), f32[16,16,128]{2,1,0:T(8,128)S(1)}, u32[]{:S(2)}, u32[]{:S(2)}) async-start(f32[16,16,128]{2,1,0:T(8,128)} %get-tuple-element.53), calls=%async_computation | async-start | bytes 262144 | tf_op jit(solution)/shard_map/all_to_all | solution.py:337
  28.4 4.5 %collective-permute-start.8 = (f32[2,16,128]{2,1,0:T(8,128)S(1)}, f32[2,16,128]{2,1,0:T(8,128)S(1)}, u32[]{:S(2)}, u32[]{:S(2)}) collective-permute-start(f32[2,16,128]{2,1,0:T(8,128)S(1)} %get-tuple-element.54), channel_id=1, source_target_pairs={{0,8},{16,24},{8,0},{24,16},{1,9},{17,25},{9,1},{25,17},{2,10},{18... | collective-permute-start | bytes 49160 | tf_op jit(solution)/shard_map/ppermute | solution.py:266
  32.8 0.7 collective-permute-start.9
  33.5 1.1 collective-permute-done.8.refs_7_
  34.6 5.6 %apply.3 = (f32[8,16,128]{2,1,0:T(8,128)S(1)}, f32[16,16]{1,0:T(8,128)S(1)}, f32[8,16,128]{2,1,0:T(8,128)S(1)}, f32[16,16,128]{2,1,0:T(8,128)}, f32[2,16,128]{2,1,0:T(8,128)S(1)}, /*index=5*/f32[2,16,128]{2,1,0:T(8,128)S(1)}) custom-call(s32[2]{0:T(128)S(1)} %pad_add_fusion.place_ref.refs_0_, s32[8]{0:T(128)S(1)} %copy-done.2, s32[8,16]{1,0:T(8,128)S(1)} %copy-done.1, ...), custom_call_target="tpu_custom_call" | custom-call | flops 134217728 | bytes 4194304 | tf_op jit(solution)/shard_map/apply/pallas_call | solution.py:355
  40.1 4.1 %all-to-all-start.1 = ((f32[16,16,128]{2,1,0:T(8,128)}), f32[16,16,128]{2,1,0:T(8,128)S(1)}, u32[]{:S(2)}, u32[]{:S(2)}) async-start(f32[16,16,128]{2,1,0:T(8,128)} %get-tuple-element.57), calls=%async_computation.1 | async-start | bytes 262144 | tf_op jit(solution)/shard_map/all_to_all | solution.py:337
  44.2 3.9 %collective-permute-start.10 = (f32[2,16,128]{2,1,0:T(8,128)S(1)}, f32[2,16,128]{2,1,0:T(8,128)S(1)}, u32[]{:S(2)}, u32[]{:S(2)}) collective-permute-start(f32[2,16,128]{2,1,0:T(8,128)S(1)} %get-tuple-element.58), channel_id=1, source_target_pairs={{0,8},{16,24},{8,0},{24,16},{1,9},{17,25},{9,1},{25,17},{2,10},{18... | collective-permute-start | bytes 49160 | tf_op jit(solution)/shard_map/ppermute | solution.py:266
  48.1 0.7 collective-permute-start.11
  48.8 1.1 collective-permute-done.10.refs_7_
  49.8 6.1 %apply_last.1 = (f32[8,16,128]{2,1,0:T(8,128)S(1)}, f32[32,8,128]{2,1,0:T(8,128)}) custom-call(s32[2]{0:T(128)S(1)} %pad_add_fusion.place_ref.refs_0_, s32[8]{0:T(128)S(1)} %copy-done.2, s32[8,16]{1,0:T(8,128)S(1)} %copy-done.1, bf16[8,16,128,128]{3,2,1,0:T(8,128)(2,1)} %refs_3_.3, f32[8,1,128]{2,1,0:T(1,128)S(1)} %get-tuple-element.48.refs_5_.refs_4_, ...), custom_call_target="tpu_custom_call" | custom-call | flops 134217728 | bytes 4194304 | tf_op jit(solution)/shard_map/apply_last/pallas_call | solution.py:355
  55.9 6.6 %all-to-all-start.2 = ((f32[32,8,128]{2,1,0:T(8,128)}), f32[32,8,128]{2,1,0:T(8,128)S(1)}, u32[]{:S(2)}, u32[]{:S(2)}) async-start(f32[32,8,128]{2,1,0:T(8,128)} %get-tuple-element.62), calls=%async_computation.2 | async-start | bytes 262144 | tf_op jit(solution)/shard_map/all_to_all | solution.py:369
  62.6 8.2 %all-to-all-done.2.grams_ref = f32[32,8,128]{2,1,0:T(8,128)S(1)} async-done(((f32[32,8,128]{2,1,0:T(8,128)}), f32[32,8,128]{2,1,0:T(8,128)S(1)}, u32[]{:S(2)}, u32[]{:S(2)}) %all-to-all-start.2) | async-done | bytes 131104 | tf_op jit(solution)/shard_map/all_to_all | solution.py:369
  70.8 3.2 %finish.1 = (f32[3,8,16,128]{3,2,1,0:T(8,128)}, s32[1]{0:T(128)}) custom-call(f32[32,8,128]{2,1,0:T(8,128)S(1)} %all-to-all-done.2.grams_ref, f32[8,16,128]{2,1,0:T(8,128)S(1)} %get-tuple-element.63.refs_0_, f32[8,16,128]{2,1,0:T(8,128)S(1)} %get-tuple-element.64.refs_1_, f32[8,16,128]{2,1,0:T(8,128)S(1)} %get-tuple-element.65.refs_2_), custom_call_target="tpu_custom_call" | custom-call | tf_op jit(solution)/shard_map/finish/pallas_call | solution.py:370
  74.6 207.6 %conditional.1 = (f32[3,8,16,128]{3,2,1,0:T(8,128)}) conditional(s32[]{:T(128)} %bitcast.39, (bf16[8,16,128,128]{3,2,1,0:T(8,128)(2,1)}, s32[8]{0:T(128)S(1)}, f32[8,16,128]{2,1,0:T(8,128)S(1)}, s32[1,1,8,2]{2,3,1,0:T(2,128)S(1)}, s32[8,16]{1,0:T(8,128)S(1)}) %tuple.33, f32[3,8,16,128]{3,2,1,0:T(8,128)} %get-tuple-element.67), branch_computations={%region_0.11_spmd, %region_7.12_spmd} | conditional | flops 1235852416 | bytes 33198924 | solution.py:382
  74.7 4.4 %multiply_reduce_fusion = f32[8,16,128]{2,1,0:T(8,128)S(1)} fusion(bf16[8,16,128,128]{3,2,1,0:T(8,128)(2,1)} %get-tuple-element.22), kind=kLoop, calls=%fused_computation.6 | loop fusion | flops 6275072 | bytes 4259840 | tf_op jit(solution)/shard_map/cond/branch_0_fun/btij,bt->bi/reduce_sum | solution.py:277
  79.3 2.6 collective-permute-start
  81.9 1.3 collective-permute-start.1
  83.4 9.2 %all_gather.10 = f32[64,16,128]{2,1,0:T(8,128)S(1)} all-gather(f32[8,16,128]{2,1,0:T(8,128)S(1)} %broadcast_multiply_fusion), channel_id=1, replica_groups=mesh['group'=4,'row'=8] {'row'}, dimensions={0}, use_global_device_ids=true | all-gather | bytes 589824 | tf_op jit(solution)/shard_map/cond/branch_0_fun/all_gather | solution.py:285
  92.7 0.6 gather_fusion
  93.4 0.8 gather_fusion.1
  94.2 5.2 %fusion.2 = f32[8,16,128]{2,1,0:T(8,128)S(1)} fusion(bf16[8,16,128,128]{3,2,1,0:T(8,128)(2,1)} %get-tuple-element.22, f32[8,16,16,128]{3,2,1,0:T(8,128)S(1)} %bitcast.101, f32[8,16]{1,0:T(8,128)S(1)} %get-tuple-element.90, pred[8,16]{1,0:T(8,128)(4,1)S(1)} %compare_and_fusion, f32[8,128]{1,0:T(8,128)S(1)} %add_power_fusion), kind=kOutput, calls=%fused_computation.13 | convolution fusion | flops 403193856 | bytes 5313152 | tf_op jit(solution)/shard_map/cond/branch_0_fun/btij,btkj->bki/dot_general | solution.py:288
  99.4 0.2 convolution_bitcast_fusion.9
  99.5 40.4 %psum.18 = f32[16,16]{0,1:T(8,128)S(1)} all-reduce(f32[16,16]{0,1:T(8,128)S(1)} %convolution_bitcast_fusion.9), channel_id=1, replica_groups=mesh['group'=4,'row'=8] {'group','row'}, use_global_device_ids=true, to_apply=%region_2.0 | all-reduce | flops 256 | bytes 2048 | tf_op jit(solution)/shard_map/cond/branch_0_fun/psum | solution.py:293
  140.0 1.5 cholesky.59
  141.5 0.7 compare_reduce_fusion.2
  142.3 0.7 fusion.17
  143.0 1.2 custom-call.7
  144.2 0.2 convolution_bitcast_fusion.8
  144.4 0.2 bitcast_multiply_fusion.1
  144.6 10.6 %all_gather.11 = f32[64,16,128]{2,1,0:T(8,128)S(1)} all-gather(f32[8,16,128]{2,1,0:T(8,128)S(1)} %get-tuple-element.92), channel_id=1, replica_groups=mesh['group'=4,'row'=8] {'row'}, dimensions={0}, use_global_device_ids=true | all-gather | bytes 589824 | tf_op jit(solution)/shard_map/cond/branch_0_fun/all_gather | solution.py:285
  155.3 2.3 collective-permute-start.2
  157.6 1.3 collective-permute-start.3
  158.9 0.6 gather_fusion.2
  159.6 3.7 %collective-permute-done.3 = f32[2,16,128]{2,1,0:T(8,128)S(1)} collective-permute-done((f32[2,16,128]{2,1,0:T(8,128)S(1)}, f32[2,16,128]{2,1,0:T(8,128)S(1)}, u32[]{:S(2)}, u32[]{:S(2)}) %collective-permute-start.3) | collective-permute-done | bytes 16416 | tf_op jit(solution)/shard_map/cond/branch_0_fun/ppermute | solution.py:258
  163.2 0.8 gather_fusion.3
  164.0 5.2 %fusion.1 = f32[8,16,128]{2,1,0:T(8,128)S(1)} fusion(bf16[8,16,128,128]{3,2,1,0:T(8,128)(2,1)} %get-tuple-element.22, f32[8,16,16,128]{3,2,1,0:T(8,128)S(1)} %bitcast.102, f32[8,16]{1,0:T(8,128)S(1)} %get-tuple-element.90, pred[8,16]{1,0:T(8,128)(4,1)S(1)} %compare_and_fusion, f32[8,128]{1,0:T(8,128)S(1)} %add_power_fusion), kind=kOutput, calls=%fused_computation.11 | convolution fusion | flops 403193856 | bytes 5313152 | tf_op jit(solution)/shard_map/cond/branch_0_fun/btij,btkj->bki/dot_general | solution.py:288
  169.4 39.2 %psum.19 = f32[16,16]{0,1:T(8,128)S(1)} all-reduce(f32[16,16]{0,1:T(8,128)S(1)} %convolution_bitcast_fusion.7), channel_id=1, replica_groups=mesh['group'=4,'row'=8] {'group','row'}, use_global_device_ids=true, to_apply=%region_5.9 | all-reduce | flops 256 | bytes 2048 | tf_op jit(solution)/shard_map/cond/branch_0_fun/psum | solution.py:293
  208.6 1.5 cholesky.70
  210.1 0.7 compare_reduce_fusion.1
  210.8 0.7 fusion.18
  211.5 1.2 custom-call.8
  212.8 0.2 convolution_bitcast_fusion.6
  213.0 0.2 bitcast_multiply_fusion
  213.2 10.6 %all_gather.12 = f32[64,16,128]{2,1,0:T(8,128)S(1)} all-gather(f32[8,16,128]{2,1,0:T(8,128)S(1)} %get-tuple-element.94), channel_id=1, replica_groups=mesh['group'=4,'row'=8] {'row'}, dimensions={0}, use_global_device_ids=true | all-gather | bytes 589824 | tf_op jit(solution)/shard_map/cond/branch_0_fun/all_gather | solution.py:285
  223.8 2.5 collective-permute-start.4
  226.4 1.3 collective-permute-start.5
  227.7 0.6 gather_fusion.4
  228.4 3.7 %collective-permute-done.5 = f32[2,16,128]{2,1,0:T(8,128)S(1)} collective-permute-done((f32[2,16,128]{2,1,0:T(8,128)S(1)}, f32[2,16,128]{2,1,0:T(8,128)S(1)}, u32[]{:S(2)}, u32[]{:S(2)}) %collective-permute-start.5) | collective-permute-done | bytes 16416 | tf_op jit(solution)/shard_map/cond/branch_0_fun/ppermute | solution.py:258
  232.1 0.8 gather_fusion.5
  232.8 5.2 %fusion = f32[8,16,128]{2,1,0:T(8,128)S(1)} fusion(bf16[8,16,128,128]{3,2,1,0:T(8,128)(2,1)} %get-tuple-element.22, f32[8,16,16,128]{3,2,1,0:T(8,128)S(1)} %bitcast.100, f32[8,16]{1,0:T(8,128)S(1)} %get-tuple-element.90, pred[8,16]{1,0:T(8,128)(4,1)S(1)} %compare_and_fusion, f32[8,128]{1,0:T(8,128)S(1)} %add_power_fusion), kind=kOutput, calls=%fused_computation.9 | convolution fusion | flops 403193856 | bytes 5313152 | tf_op jit(solution)/shard_map/cond/branch_0_fun/btij,btkj->bki/dot_general | solution.py:288
  238.0 0.2 convolution_bitcast_fusion.5
  238.2 38.7 %psum.20 = f32[16,16]{0,1:T(8,128)S(1)} all-reduce(f32[16,16]{0,1:T(8,128)S(1)} %convolution_bitcast_fusion.5), channel_id=1, replica_groups=mesh['group'=4,'row'=8] {'group','row'}, use_global_device_ids=true, to_apply=%region_6.10 | all-reduce | flops 256 | bytes 2048 | tf_op jit(solution)/shard_map/cond/branch_0_fun/psum | solution.py:293
  276.9 1.5 cholesky.81
  278.4 0.7 compare_reduce_fusion
  279.1 0.7 fusion.19
  279.8 1.2 custom-call.9
  281.1 0.2 convolution_bitcast_fusion.4
  281.3 0.2 convolution_bitcast_fusion
  281.5 0.7 pad_maximum_fusion.3
  (55 shorter events, 1.5 us)
Async XLA Ops:
  0.0 19.4 %copy-start.2 = (s32[8]{0:T(128)S(1)}, s32[8]{0:T(128)}, u32[]{:S(2)}) copy-start(s32[8]{0:T(128)} %refs_1_.5) | copy-start | bytes 100
  0.0 19.4 %copy-start.3 = (s32[1,1,8,2]{2,3,1,0:T(2,128)S(1)}, s32[1,1,8,2]{2,3,1,0:T(2,128)}, u32[]{:S(2)}) copy-start(s32[1,1,8,2]{2,3,1,0:T(2,128)} %param.18) | copy-start | bytes 196
  0.0 19.4 %copy-start.1 = (s32[8,16]{1,0:T(8,128)S(1)}, s32[8,16]{1,0:T(8,128)}, u32[]{:S(2)}) copy-start(s32[8,16]{1,0:T(8,128)} %refs_2_.5) | copy-start | bytes 1540
  5.6 13.8 %collective-permute-start.6 = (f32[2,16,128]{2,1,0:T(8,128)S(1)}, f32[2,16,128]{2,1,0:T(8,128)S(1)}, u32[]{:S(2)}, u32[]{:S(2)}) collective-permute-start(f32[2,16,128]{2,1,0:T(8,128)S(1)} %get-tuple-element.50), channel_id=1, source_target_pairs={{0,8},{16,24},{8,0},{24,16},{1,9},{17,25},{9,1},{25,17},{2,10},{18... | collective-permute-start | bytes 49160 | tf_op jit(solution)/shard_map/ppermute | solution.py:266
  8.7 10.7 %collective-permute-start.7 = (f32[2,16,128]{2,1,0:T(8,128)S(1)}, f32[2,16,128]{2,1,0:T(8,128)S(1)}, u32[]{:S(2)}, u32[]{:S(2)}) collective-permute-start(f32[2,16,128]{2,1,0:T(8,128)S(1)} %get-tuple-element.51), channel_id=1, source_target_pairs={{8,16},{16,8},{9,17},{17,9},{10,18},{18,10},{11,19},{19,11},{12,20... | collective-permute-start | bytes 49160 | tf_op jit(solution)/shard_map/ppermute | solution.py:266
  25.0 9.6 %all-to-all-start = ((f32[16,16,128]{2,1,0:T(8,128)}), f32[16,16,128]{2,1,0:T(8,128)S(1)}, u32[]{:S(2)}, u32[]{:S(2)}) async-start(f32[16,16,128]{2,1,0:T(8,128)} %get-tuple-element.53), calls=%async_computation | async-start | bytes 262144 | tf_op jit(solution)/shard_map/all_to_all | solution.py:337
  28.4 6.2 %collective-permute-start.8 = (f32[2,16,128]{2,1,0:T(8,128)S(1)}, f32[2,16,128]{2,1,0:T(8,128)S(1)}, u32[]{:S(2)}, u32[]{:S(2)}) collective-permute-start(f32[2,16,128]{2,1,0:T(8,128)S(1)} %get-tuple-element.54), channel_id=1, source_target_pairs={{0,8},{16,24},{8,0},{24,16},{1,9},{17,25},{9,1},{25,17},{2,10},{18... | collective-permute-start | bytes 49160 | tf_op jit(solution)/shard_map/ppermute | solution.py:266
  32.8 1.7 collective-permute-start.9
  34.6 40.0 %copy-start = (f32[8,16,128]{2,1,0:T(8,128)S(1)}, f32[8,16,128]{2,1,0:T(8,128)}, u32[]{:S(2)}) copy-start(f32[8,16,128]{2,1,0:T(8,128)} %basis_ref.1) | copy-start | bytes 196612
  40.1 9.7 %all-to-all-start.1 = ((f32[16,16,128]{2,1,0:T(8,128)}), f32[16,16,128]{2,1,0:T(8,128)S(1)}, u32[]{:S(2)}, u32[]{:S(2)}) async-start(f32[16,16,128]{2,1,0:T(8,128)} %get-tuple-element.57), calls=%async_computation.1 | async-start | bytes 262144 | tf_op jit(solution)/shard_map/all_to_all | solution.py:337
  44.2 5.6 %collective-permute-start.10 = (f32[2,16,128]{2,1,0:T(8,128)S(1)}, f32[2,16,128]{2,1,0:T(8,128)S(1)}, u32[]{:S(2)}, u32[]{:S(2)}) collective-permute-start(f32[2,16,128]{2,1,0:T(8,128)S(1)} %get-tuple-element.58), channel_id=1, source_target_pairs={{0,8},{16,24},{8,0},{24,16},{1,9},{17,25},{9,1},{25,17},{2,10},{18... | collective-permute-start | bytes 49160 | tf_op jit(solution)/shard_map/ppermute | solution.py:266
  48.1 1.7 collective-permute-start.11
  55.9 14.9 %all-to-all-start.2 = ((f32[32,8,128]{2,1,0:T(8,128)}), f32[32,8,128]{2,1,0:T(8,128)S(1)}, u32[]{:S(2)}, u32[]{:S(2)}) async-start(f32[32,8,128]{2,1,0:T(8,128)} %get-tuple-element.62), calls=%async_computation.2 | async-start | bytes 262144 | tf_op jit(solution)/shard_map/all_to_all | solution.py:369
  79.3 14.0 %collective-permute-start = (f32[2,16,128]{2,1,0:T(8,128)S(1)}, f32[2,16,128]{2,1,0:T(8,128)S(1)}, u32[]{:S(2)}, u32[]{:S(2)}) collective-permute-start(f32[2,16,128]{2,1,0:T(8,128)S(1)} %get-tuple-element.88), channel_id=1, source_target_pairs={{0,8},{8,16},{16,24},{1,9},{9,17},{17,25},{2,10},{10,18},{18,26},{... | collective-permute-start | bytes 49160 | tf_op jit(solution)/shard_map/cond/branch_0_fun/ppermute | solution.py:257
  81.9 11.5 %collective-permute-start.1 = (f32[2,16,128]{2,1,0:T(8,128)S(1)}, f32[2,16,128]{2,1,0:T(8,128)S(1)}, u32[]{:S(2)}, u32[]{:S(2)}) collective-permute-start(f32[2,16,128]{2,1,0:T(8,128)S(1)} %get-tuple-element.89), channel_id=1, source_target_pairs={{8,0},{16,8},{24,16},{9,1},{17,9},{25,17},{10,2},{18,10},{26,18},{... | collective-permute-start | bytes 49160 | tf_op jit(solution)/shard_map/cond/branch_0_fun/ppermute | solution.py:258
  155.3 4.3 %collective-permute-start.2 = (f32[2,16,128]{2,1,0:T(8,128)S(1)}, f32[2,16,128]{2,1,0:T(8,128)S(1)}, u32[]{:S(2)}, u32[]{:S(2)}) collective-permute-start(f32[2,16,128]{2,1,0:T(8,128)S(1)} %get-tuple-element.86), channel_id=1, source_target_pairs={{0,8},{8,16},{16,24},{1,9},{9,17},{17,25},{2,10},{10,18},{18,26},{... | collective-permute-start | bytes 49160 | tf_op jit(solution)/shard_map/cond/branch_0_fun/ppermute | solution.py:257
  157.6 5.6 %collective-permute-start.3 = (f32[2,16,128]{2,1,0:T(8,128)S(1)}, f32[2,16,128]{2,1,0:T(8,128)S(1)}, u32[]{:S(2)}, u32[]{:S(2)}) collective-permute-start(f32[2,16,128]{2,1,0:T(8,128)S(1)} %get-tuple-element.87), channel_id=1, source_target_pairs={{8,0},{16,8},{24,16},{9,1},{17,9},{25,17},{10,2},{18,10},{26,18},{... | collective-permute-start | bytes 49160 | tf_op jit(solution)/shard_map/cond/branch_0_fun/ppermute | solution.py:258
  223.8 4.5 %collective-permute-start.4 = (f32[2,16,128]{2,1,0:T(8,128)S(1)}, f32[2,16,128]{2,1,0:T(8,128)S(1)}, u32[]{:S(2)}, u32[]{:S(2)}) collective-permute-start(f32[2,16,128]{2,1,0:T(8,128)S(1)} %get-tuple-element.84), channel_id=1, source_target_pairs={{0,8},{8,16},{16,24},{1,9},{9,17},{17,25},{2,10},{10,18},{18,26},{... | collective-permute-start | bytes 49160 | tf_op jit(solution)/shard_map/cond/branch_0_fun/ppermute | solution.py:257
  226.4 5.6 %collective-permute-start.5 = (f32[2,16,128]{2,1,0:T(8,128)S(1)}, f32[2,16,128]{2,1,0:T(8,128)S(1)}, u32[]{:S(2)}, u32[]{:S(2)}) collective-permute-start(f32[2,16,128]{2,1,0:T(8,128)S(1)} %get-tuple-element.85), channel_id=1, source_target_pairs={{8,0},{16,8},{24,16},{9,1},{17,9},{25,17},{10,2},{18,10},{26,18},{... | collective-permute-start | bytes 49160 | tf_op jit(solution)/shard_map/cond/branch_0_fun/ppermute | solution.py:258

commit v4 on v3

--- a/solution.py
+++ b/solution.py
@@ -10,7 +10,9 @@
 SLOTS = 2
 RIM = 2
 ITERS = 3
+MINLIVE = 10
 LANES = 128
+HELD_BYTES = 5 * 1024 * 1024 // 2
 PIECES = 2
 VMEM_BYTES = 24 * 1024 * 1024
 TRUST = 64.0
@@ -44,46 +46,43 @@
     return pl.CostEstimate(flops=flops, bytes_accessed=moved, transcendentals=0)
 
 
-def stream(tiles_hbm, tiles_ref, sems):
-    loads = [
-        pltpu.make_async_copy(tiles_hbm.at[b], tiles_ref.at[b], sems.at[b])
-        for b in range(tiles_ref.shape[0])
-    ]
-    for load in loads:
-        load.start()
-    return loads
-
-
-def stream_scratch(tiles):
-    return [pltpu.VMEM(tiles.shape, tiles.dtype), pltpu.SemaphoreType.DMA((tiles.shape[0],))]
+def held_blocks(tiles):
+    return min(tiles.shape[0] - 1, HELD_BYTES // (tiles.size // tiles.shape[0] * 2))
+
+
+def load(tiles_hbm, start, tiles_ref, sem):
+    copy = pltpu.make_async_copy(tiles_hbm.at[pl.ds(start, tiles_ref.shape[0])], tiles_ref, sem)
+    copy.start()
+    return copy
 
 
 def roots_kernel(place_ref, count_ref, want_ref, tiles_hbm, basis_ref, root_ref, sent_ref,
-                 first_ref, second_ref, tiles_ref, load_sems):
-    blocks, per_row, side, _ = tiles_ref.shape
+                 first_ref, second_ref, held_ref, rest_ref, sems):
+    held, per_row, side, _ = held_ref.shape
+    blocks = held + rest_ref.shape[0]
     peers = want_ref.shape[1]
     vectors = basis_ref.shape[1]
-    loads = stream(tiles_hbm, tiles_ref, load_sems)
+    rest_load = load(tiles_hbm, held, rest_ref, sems.at[0])
+    held_load = load(tiles_hbm, 0, held_ref, sems.at[1])
     for p in range(peers):
         owned = (place_ref[0] * peers + p) * blocks
         for c in range(SLOTS):
             at = jnp.full((1, side), want_ref[c, p] - owned, jnp.int32).astype(jnp.float32)
             block, row = divmod(p * SLOTS + c, vectors)
             sent_ref[blocks + block, row : row + 1] = at
-    rows = lax.broadcasted_iota(jnp.int32, (side, side), 0)
-    lanes = lax.broadcasted_iota(jnp.int32, (side, side), 1)
-    unit = rows == lanes
-    for b in range(blocks):
-        loads[b].wait()
-        held = [tiles_ref[b, s] for s in range(per_row)]
-        live = [
-            jnp.where(s < count_ref[b], tile, jnp.zeros_like(tile)) for s, tile in enumerate(held)
-        ]
-        products = lax.dot_general(
-            jnp.concatenate(live, axis=1), jnp.concatenate(held, axis=1), NT,
-            preferred_element_type=jnp.float32,
-        )
-        sums = jnp.sum(jnp.where(unit, products, 0.0), axis=0, keepdims=True)
+    rest_load.wait()
+    for b in list(range(held, blocks)) + list(range(held)):
+        if b == 0:
+            held_load.wait()
+        tile_ref = held_ref.at[b] if b < held else rest_ref.at[b - held]
+        total = jnp.zeros((side, side), jnp.float32)
+        for s in range(per_row):
+            wide = tile_ref[s].astype(jnp.float32)
+            square = wide * wide
+            if s >= MINLIVE:
+                square = square * (s < count_ref[b]).astype(jnp.float32)
+            total = total + square
+        sums = jnp.sum(total.T, axis=0, keepdims=True)
         root = lax.rsqrt(jnp.sqrt(1e-06 + sums))
         root_ref[b] = root
         sent_ref[b] = basis_ref[b] * root
@@ -97,18 +96,14 @@
         second_ref[h] = scaled_ref[odd * (blocks - RIM) + h]
 
 
-def pick_into(row_at, asked_ref, scaled_ref, out_ref):
-    peers = asked_ref.shape[0]
+def pick_into(asked_ref, scaled_ref, out_ref):
     blocks, vectors, side = scaled_ref.shape
-    for p in range(peers):
-        for c in range(SLOTS):
-            entry = row_at * SLOTS + c
-            at = asked_ref[p, blocks + entry // vectors, pl.ds(entry % vectors, 1)]
-            at = jnp.broadcast_to(at, (vectors, side))
-            value = scaled_ref[0]
-            for b in range(1, blocks):
-                value = jnp.where(at == float(b), scaled_ref[b], value)
-            out_ref[p * SLOTS + c] = value
+    for n in range(asked_ref.shape[0]):
+        at = jnp.broadcast_to(asked_ref[n : n + 1], (vectors, side))
+        value = scaled_ref[0]
+        for b in range(1, blocks):
+            value = jnp.where(at == float(b), scaled_ref[b], value)
+        out_ref[n] = value
 
 
 def split_into(x, out_ref, slot):
@@ -139,15 +134,20 @@
     place_ref, count_ref, cols_ref, *refs = refs
     if opening:
         want_ref, *refs = refs
-    tiles_hbm, root_ref, own_ref, recv_ref, swapped_ref, swapped_next_ref, *refs = refs
-    *refs, tiles_ref, load_sems = refs
-    loads = stream(tiles_hbm, tiles_ref, load_sems)
+    tiles_hbm, held_ref, root_ref, own_ref, recv_ref, swapped_ref, swapped_next_ref, *refs = refs
+    *refs, table, rest_ref, load_sem = refs
+    held, per_row, side, _ = held_ref.shape
+    blocks = held + rest_ref.shape[0]
+    rest_load = load(tiles_hbm, held, rest_ref, load_sem)
     if last:
-        *before, applied_ref, gram_hbm, table, packed_ref, sems = refs
+        *before, applied_ref, gram_hbm, packed_ref, sems = refs
     else:
-        asked_ref, refs = (recv_ref, refs) if opening else (refs[0], refs[1:])
-        applied_ref, gram_ref, scaled_ref, out_hbm, first_ref, second_ref, table, picked_ref, sem = refs
-    blocks, per_row, side, _ = tiles_ref.shape
+        if not opening:
+            asked_ref, *refs = refs
+        applied_ref, gram_ref, scaled_ref, out_hbm, first_ref, second_ref, *refs = refs
+        if opening:
+            asked_ref, *refs = refs
+        picked_ref, sem = refs
     vectors = own_ref.shape[1]
     group = place_ref[0]
     slot = 0
@@ -161,6 +161,10 @@
                 at = jnp.clip(want_ref[c, p] - (group * peers + p) * blocks, 0, blocks - 1)
                 split_into(recv_ref[p, at], table, slot)
                 slot += 1
+                entry = place_ref[1] * SLOTS + c
+                asked_ref[p * SLOTS + c : p * SLOTS + c + 1] = recv_ref[
+                    p, blocks + entry // vectors, pl.ds(entry % vectors, 1)
+                ]
     else:
         for n in range(recv_ref.shape[0]):
             split_into(recv_ref[n], table, slot)
@@ -178,8 +182,10 @@
             at = jnp.where(s < count_ref[b], cols_ref[b, s], slot)
             picked.append(table[at])
         x = jnp.concatenate(picked, axis=1)
-        loads[b].wait()
-        t = jnp.concatenate([tiles_ref[b, s] for s in range(per_row)], axis=1)
+        if b == held:
+            rest_load.wait()
+        tile_ref = held_ref.at[b] if b < held else rest_ref.at[b - held]
+        t = jnp.concatenate([tile_ref[s] for s in range(per_row)], axis=1)
         product = lax.dot_general(x, t, NT, preferred_element_type=jnp.float32)
         total = product[(PIECES - 1) * vectors :]
         for piece in range(PIECES - 2, -1, -1):
@@ -191,7 +197,7 @@
         if not last:
             scaled_ref[b] = row * root
     if not last:
-        pick_into(place_ref[1], asked_ref, scaled_ref, picked_ref)
+        pick_into(asked_ref, scaled_ref, picked_ref)
         send = pltpu.make_async_copy(picked_ref, out_hbm, sem)
         send.start()
         swaps_into(group, blocks, scaled_ref, first_ref, second_ref)
@@ -311,17 +317,20 @@
     block_shape = (vectors, side)
     picked_shape = (peers * SLOTS,) + block_shape
     rim_shape = f32(RIM, *block_shape)
-    root, scaled, *rims = pl.pallas_call(
+    kept = held_blocks(tiles)
+    rest = pltpu.VMEM((blocks - kept,) + tiles.shape[1:], tiles.dtype)
+    root, scaled, *rims, held = pl.pallas_call(
         roots_kernel,
         out_shape=(
             f32(blocks, 1, side),
             f32(blocks + lists, *block_shape),
             rim_shape,
             rim_shape,
+            pltpu.VMEM((kept,) + tiles.shape[1:], tiles.dtype),
         ),
         in_specs=[smem(), smem(), smem(), hbm(), vmem()],
-        out_specs=(vmem(),) * 4,
-        scratch_shapes=stream_scratch(tiles),
+        out_specs=(vmem(),) * 5,
+        scratch_shapes=[rest, pltpu.SemaphoreType.DMA((2,))],
         compiler_params=params(),
         cost_estimate=cost(tiles.size * 2, tile_bytes),
         name="roots",
@@ -332,32 +341,40 @@
         last = t == ITERS - 1
         if t == 0:
             swapped = swap(*rims)
-            received = asked = lax.all_gather(scaled, "row", axis=0)
+            received = lax.all_gather(scaled, "row", axis=0)
         else:
             received = lax.all_to_all(outgoing, "row", 0, 0, tiled=True)
             swapped = swap(*rims)
         scalars = [place, tile_count, tile_cols] + ([wanted] if t == 0 else [])
-        arrays = [far_tiles, root, scaled, received, *swapped]
+        arrays = [far_tiles, held, root, scaled, received, *swapped]
         shapes = [f32(blocks, *block_shape)]
         specs = [vmem(), vmem()]
-        scratch = [pltpu.VMEM((slots + 1, PIECES * vectors, side), jnp.bfloat16)]
         if last:
             shapes += [pltpu.HBM((groups * peers, vectors // 2, LANES), jnp.float32)]
             specs = [vmem(), hbm()]
-            scratch += [pltpu.VMEM((1, vectors // 2, LANES), jnp.float32), pltpu.SemaphoreType.DMA((groups * peers,))]
+            scratch = [pltpu.VMEM((1, vectors // 2, LANES), jnp.float32), pltpu.SemaphoreType.DMA((groups * peers,))]
             arrays += grams
         else:
             shapes += [f32(vectors, vectors), f32(blocks, *block_shape), pltpu.HBM(picked_shape, jnp.float32)]
             shapes += [rim_shape] * 2
             specs += [vmem(), hbm(), vmem(), vmem()]
-            scratch += [pltpu.VMEM(picked_shape, jnp.float32), pltpu.SemaphoreType.DMA]
-            arrays += [asked] if t else []
+            scratch = [pltpu.VMEM(picked_shape, jnp.float32), pltpu.SemaphoreType.DMA]
+            if t:
+                arrays += [asked]
+            else:
+                shapes += [f32(peers * SLOTS, side)]
+                specs += [vmem()]
         result = pl.pallas_call(
             functools.partial(apply_kernel, t),
             out_shape=tuple(shapes),
             in_specs=[smem()] * len(scalars) + [hbm()] + [vmem()] * (len(arrays) - 1),
             out_specs=tuple(specs),
-            scratch_shapes=scratch + stream_scratch(tiles),
+            scratch_shapes=scratch
+            + [
+                pltpu.VMEM((slots + 1, PIECES * vectors, side), jnp.bfloat16),
+                rest,
+                pltpu.SemaphoreType.DMA,
+            ],
             compiler_params=params(),
             cost_estimate=cost(tiles.size * 2 * vectors * PIECES, tile_bytes),
             name="apply_last" if last else "apply",
@@ -365,7 +382,9 @@
         powers.append(result[0])
         grams.append(result[1])
         if not last:
-            scaled, outgoing, *rims = result[2:]
+            scaled, outgoing, *rims = result[2:6]
+            if t == 0:
+                asked = result[6]
     gathered = lax.all_to_all(grams[-1], ("group", "row"), 0, 0, tiled=True)
     krylov, trust = pl.pallas_call(
         functools.partial(finish_kernel, float(groups * peers * blocks * side)),

time: 283 us -> 279 us (0.986)
  Pallas kernels: 25.9 us -> 19.9 us
    pallas_call x3, Pallas kernels: 17.2 us -> 13 us  [local(): pl.pallas_call(functools.partial(apply_kernel, t), out_shape=tuple(shapes...]
  transfers between devices with their start and end apart: 15 -> 15, of which waited for: 5 -> 5; matrix products, arithmetic and copies ran while one was open for 1% -> 0% of each run, Pallas kernels for 0% -> 0%
where the time goes in v4:
time: 279 us; the launch traced here: 277 us
  blocking collectives  159 us (57%)
  starting transfers between devices  39 us (14%)
  Pallas kernels  19.9 us (7%)
  waiting for transfers between devices  18.8 us (7%)
  other arithmetic  18 us (6%)
  matrix products  17.5 us (6%)
  local copies, waits for them, and re-layouts  4.46 us (2%)
    psum x3, blocking collectives, stepwise(): factor = jnp.linalg.cholesky(lax.psum(gram, ('group', 'row')) / row_total)  118 us
    all_gather x3, blocking collectives, stepwise(): lax.all_gather(scaled, 'row', axis=0, tiled=True)  30.3 us
    dot_general x3, matrix products, stepwise(): jnp.einsum('btij,btkj->bki', tiles, picked, precision=HIGH, preferred_ele...  15.6 us
    ppermute x6, starting transfers between devices, swap(): lax.ppermute(x, 'group', pair)  13.4 us
    pallas_call x3, Pallas kernels, local(): pl.pallas_call(functools.partial(apply_kernel, t), out_shape=tuple(shapes...  13 us
    all_gather x1, blocking collectives, local(): received = lax.all_gather(scaled, 'row', axis=0)  10 us
    ppermute x3, waiting for transfers between devices, neighbours(): high = lax.ppermute(scaled[:RIM], 'group', down)  8.42 us
    all_to_all x1, waiting for transfers between devices, local(): gathered = lax.all_to_all(grams[-1], ('group', 'row'), 0, 0, tiled=True)  8.23 us
  transfers between devices with their start and end apart: 15, of which 5 were waited for; matrix products, arithmetic and copies ran while one was open for 0% of the time, Pallas kernels for 0%

profile of v4, /device:TPU:0, one launch (start us, length us, event | category | flops | bytes accessed | tf_op | source)
XLA Modules:
  0.0 277.5 jit_solution(6358110955362797258)
XLA Ops:
  0.1 3.8 %roots.1 = (f32[8,1,128]{2,1,0:T(1,128)S(1)}, f32[9,16,128]{2,1,0:T(8,128)S(1)}, f32[2,16,128]{2,1,0:T(8,128)S(1)}, f32[2,16,128]{2,1,0:T(8,128)S(1)}, bf16[5,16,128,128]{3,2,1,0:T(8,128)(2,1)S(1)}) custom-call(s32[2]{0:T(128)S(1)} %pad_add_fusion.place_ref.refs_0_, s32[8]{0:T(128)} %refs_1_.5, s32[2,8]{1,0:T(2,128)} %bitcast.105, ...), custom_call_target="tpu_custom_call" | custom-call | flops 4194304 | bytes 4194304 | tf_op jit(solution)/shard_map/roots/pallas_call | solution.py:322
  3.8 3.1 %collective-permute-start.6 = (f32[2,16,128]{2,1,0:T(8,128)S(1)}, f32[2,16,128]{2,1,0:T(8,128)S(1)}, u32[]{:S(2)}, u32[]{:S(2)}) collective-permute-start(f32[2,16,128]{2,1,0:T(8,128)S(1)} %get-tuple-element.53), channel_id=1, source_target_pairs={{0,8},{16,24},{8,0},{24,16},{1,9},{17,25},{9,1},{25,17},{2,10},{18... | collective-permute-start | bytes 49160 | tf_op jit(solution)/shard_map/ppermute | solution.py:272
  6.9 0.7 collective-permute-start.7
  7.6 10.0 %all-gather = f32[72,16,128]{2,1,0:T(8,128)S(1)} all-gather(f32[9,16,128]{2,1,0:T(8,128)S(1)} %get-tuple-element.52.refs_7_), channel_id=2, replica_groups=mesh['group'=4,'row'=8] {'row'}, dimensions={0}, use_global_device_ids=true | all-gather | bytes 663552 | tf_op jit(solution)/shard_map/all_gather | solution.py:344
  17.6 4.2 %apply.2 = (f32[8,16,128]{2,1,0:T(8,128)S(1)}, f32[16,16]{1,0:T(8,128)S(1)}, f32[8,16,128]{2,1,0:T(8,128)S(1)}, f32[16,16,128]{2,1,0:T(8,128)}, f32[2,16,128]{2,...) custom-call(s32[2]{0:T(128)S(1)} %pad_add_fusion.place_ref.refs_0_, s32[8]{0:T(128)S(1)} %copy-done.2, ...), custom_call_target="tpu_custom_call" | custom-call | flops 134217728 | bytes 4194304 | tf_op jit(solution)/shard_map/apply/pallas_call | solution.py:367
  21.8 3.4 %all-to-all-start = ((f32[16,16,128]{2,1,0:T(8,128)}), f32[16,16,128]{2,1,0:T(8,128)S(1)}, u32[]{:S(2)}, u32[]{:S(2)}) async-start(f32[16,16,128]{2,1,0:T(8,128)} %get-tuple-element.56), calls=%async_computation | async-start | bytes 262144 | tf_op jit(solution)/shard_map/all_to_all | solution.py:346
  25.2 4.5 %collective-permute-start.8 = (f32[2,16,128]{2,1,0:T(8,128)S(1)}, f32[2,16,128]{2,1,0:T(8,128)S(1)}, u32[]{:S(2)}, u32[]{:S(2)}) collective-permute-start(f32[2,16,128]{2,1,0:T(8,128)S(1)} %get-tuple-element.57), channel_id=1, source_target_pairs={{0,8},{16,24},{8,0},{24,16},{1,9},{17,25},{9,1},{25,17},{2,10},{18... | collective-permute-start | bytes 49160 | tf_op jit(solution)/shard_map/ppermute | solution.py:272
  29.7 0.7 collective-permute-start.9
  30.3 1.1 collective-permute-done.8.refs_8_
  31.4 4.1 %apply.3 = (f32[8,16,128]{2,1,0:T(8,128)S(1)}, f32[16,16]{1,0:T(8,128)S(1)}, f32[8,16,128]{2,1,0:T(8,128)S(1)}, f32[16,16,128]{2,1,0:T(8,128)}, f32[2,16,128]{2,1,0:T(8,128)S(1)}, /*index=5*/f32[2,16,128]{2,1,0:T(8,128)S(1)}) custom-call(s32[2]{0:T(128)S(1)} %pad_add_fusion.place_ref.refs_0_, s32[8]{0:T(128)S(1)} %copy-done.2, s32[8,16]{1,0:T(8,128)S(1)} %copy-done.1, ...), custom_call_target="tpu_custom_call" | custom-call | flops 134217728 | bytes 4194304 | tf_op jit(solution)/shard_map/apply/pallas_call | solution.py:367
  35.5 4.2 %all-to-all-start.1 = ((f32[16,16,128]{2,1,0:T(8,128)}), f32[16,16,128]{2,1,0:T(8,128)S(1)}, u32[]{:S(2)}, u32[]{:S(2)}) async-start(f32[16,16,128]{2,1,0:T(8,128)} %get-tuple-element.61), calls=%async_computation.1 | async-start | bytes 262144 | tf_op jit(solution)/shard_map/all_to_all | solution.py:346
  39.8 3.9 %collective-permute-start.10 = (f32[2,16,128]{2,1,0:T(8,128)S(1)}, f32[2,16,128]{2,1,0:T(8,128)S(1)}, u32[]{:S(2)}, u32[]{:S(2)}) collective-permute-start(f32[2,16,128]{2,1,0:T(8,128)S(1)} %get-tuple-element.62), channel_id=1, source_target_pairs={{0,8},{16,24},{8,0},{24,16},{1,9},{17,25},{9,1},{25,17},{2,10},{18... | collective-permute-start | bytes 49160 | tf_op jit(solution)/shard_map/ppermute | solution.py:272
  43.7 0.7 collective-permute-start.11
  44.3 1.1 collective-permute-done.10.refs_8_
  45.4 4.7 %apply_last.1 = (f32[8,16,128]{2,1,0:T(8,128)S(1)}, f32[32,8,128]{2,1,0:T(8,128)}) custom-call(s32[2]{0:T(128)S(1)} %pad_add_fusion.place_ref.refs_0_, s32[8]{0:T(128)S(1)} %copy-done.2, s32[8,16]{1,0:T(8,128)S(1)} %copy-done.1, bf16[8,16,128,128]{3,2,1,0:T(8,128)(2,1)} %refs_3_.3, bf16[5,16,128,128]{3,2,1,0:T(8,128)(2,1)S(1)} %get-tuple-element.50.refs_5_.refs_4_, ...), custom_call_target="tpu_custom_call" | custom-call | flops 134217728 | bytes 4194304 | tf_op jit(solution)/shard_map/apply_last/pallas_call | solution.py:367
  50.1 6.6 %all-to-all-start.2 = ((f32[32,8,128]{2,1,0:T(8,128)}), f32[32,8,128]{2,1,0:T(8,128)S(1)}, u32[]{:S(2)}, u32[]{:S(2)}) async-start(f32[32,8,128]{2,1,0:T(8,128)} %get-tuple-element.66), calls=%async_computation.2 | async-start | bytes 262144 | tf_op jit(solution)/shard_map/all_to_all | solution.py:388
  56.7 8.2 %all-to-all-done.2.grams_ref = f32[32,8,128]{2,1,0:T(8,128)S(1)} async-done(((f32[32,8,128]{2,1,0:T(8,128)}), f32[32,8,128]{2,1,0:T(8,128)S(1)}, u32[]{:S(2)}, u32[]{:S(2)}) %all-to-all-start.2) | async-done | bytes 131104 | tf_op jit(solution)/shard_map/all_to_all | solution.py:388
  64.9 3.2 %finish.1 = (f32[3,8,16,128]{3,2,1,0:T(8,128)}, s32[1]{0:T(128)}) custom-call(f32[32,8,128]{2,1,0:T(8,128)S(1)} %all-to-all-done.2.grams_ref, f32[8,16,128]{2,1,0:T(8,128)S(1)} %get-tuple-element.67.refs_0_, f32[8,16,128]{2,1,0:T(8,128)S(1)} %get-tuple-element.68.refs_1_, f32[8,16,128]{2,1,0:T(8,128)S(1)} %get-tuple-element.69.refs_2_), custom_call_target="tpu_custom_call" | custom-call | tf_op jit(solution)/shard_map/finish/pallas_call | solution.py:389
  68.7 208.8 %conditional.1 = (f32[3,8,16,128]{3,2,1,0:T(8,128)}) conditional(s32[]{:T(128)} %bitcast.39, (bf16[8,16,128,128]{3,2,1,0:T(8,128)(2,1)}, s32[8]{0:T(128)S(1)}, f32[8,16,128]{2,1,0:T(8,128)S(1)}, s32[1,1,8,2]{2,3,1,0:T(2,128)S(1)}, s32[8,16]{1,0:T(8,128)S(1)}) %tuple.33, f32[3,8,16,128]{3,2,1,0:T(8,128)} %get-tuple-element.71), branch_computations={%region_0.11_spmd, %region_7.12_spmd} | conditional | flops 1235852416 | bytes 33198924 | solution.py:401
  68.7 4.4 %multiply_reduce_fusion = f32[8,16,128]{2,1,0:T(8,128)S(1)} fusion(bf16[8,16,128,128]{3,2,1,0:T(8,128)(2,1)} %get-tuple-element.22), kind=kLoop, calls=%fused_computation.6 | loop fusion | flops 6275072 | bytes 4259840 | tf_op jit(solution)/shard_map/cond/branch_0_fun/btij,bt->bi/reduce_sum | solution.py:283
  73.4 2.6 collective-permute-start
  76.0 1.3 collective-permute-start.1
  77.3 9.0 %all_gather.10 = f32[64,16,128]{2,1,0:T(8,128)S(1)} all-gather(f32[8,16,128]{2,1,0:T(8,128)S(1)} %broadcast_multiply_fusion), channel_id=1, replica_groups=mesh['group'=4,'row'=8] {'row'}, dimensions={0}, use_global_device_ids=true | all-gather | bytes 589824 | tf_op jit(solution)/shard_map/cond/branch_0_fun/all_gather | solution.py:291
  86.6 0.6 gather_fusion
  87.3 0.8 gather_fusion.1
  88.1 5.2 %fusion.2 = f32[8,16,128]{2,1,0:T(8,128)S(1)} fusion(bf16[8,16,128,128]{3,2,1,0:T(8,128)(2,1)} %get-tuple-element.22, f32[8,16,16,128]{3,2,1,0:T(8,128)S(1)} %bitcast.100, f32[8,16]{1,0:T(8,128)S(1)} %get-tuple-element.94, pred[8,16]{1,0:T(8,128)(4,1)S(1)} %compare_and_fusion, f32[8,128]{1,0:T(8,128)S(1)} %add_power_fusion), kind=kOutput, calls=%fused_computation.13 | convolution fusion | flops 403193856 | bytes 5313152 | tf_op jit(solution)/shard_map/cond/branch_0_fun/btij,btkj->bki/dot_general | solution.py:294
  93.3 0.2 convolution_bitcast_fusion.9
  93.5 40.6 %psum.18 = f32[16,16]{0,1:T(8,128)S(1)} all-reduce(f32[16,16]{0,1:T(8,128)S(1)} %convolution_bitcast_fusion.9), channel_id=1, replica_groups=mesh['group'=4,'row'=8] {'group','row'}, use_global_device_ids=true, to_apply=%region_2.0 | all-reduce | flops 256 | bytes 2048 | tf_op jit(solution)/shard_map/cond/branch_0_fun/psum | solution.py:299
  134.2 1.5 cholesky.59
  135.7 0.7 compare_reduce_fusion.2
  136.4 0.7 fusion.17
  137.1 1.2 custom-call.7
  138.3 0.2 convolution_bitcast_fusion.8
  138.5 0.2 bitcast_multiply_fusion.1
  138.7 10.6 %all_gather.11 = f32[64,16,128]{2,1,0:T(8,128)S(1)} all-gather(f32[8,16,128]{2,1,0:T(8,128)S(1)} %get-tuple-element.96), channel_id=1, replica_groups=mesh['group'=4,'row'=8] {'row'}, dimensions={0}, use_global_device_ids=true | all-gather | bytes 589824 | tf_op jit(solution)/shard_map/cond/branch_0_fun/all_gather | solution.py:291
  149.4 0.6 gather_fusion.2
  149.9 2.3 collective-permute-start.2
  152.3 1.3 collective-permute-start.3
  153.7 4.2 %collective-permute-done.3 = f32[2,16,128]{2,1,0:T(8,128)S(1)} collective-permute-done((f32[2,16,128]{2,1,0:T(8,128)S(1)}, f32[2,16,128]{2,1,0:T(8,128)S(1)}, u32[]{:S(2)}, u32[]{:S(2)}) %collective-permute-start.3) | collective-permute-done | bytes 16416 | tf_op jit(solution)/shard_map/cond/branch_0_fun/ppermute | solution.py:264
  158.0 0.8 gather_fusion.3
  158.7 5.2 %fusion.1 = f32[8,16,128]{2,1,0:T(8,128)S(1)} fusion(bf16[8,16,128,128]{3,2,1,0:T(8,128)(2,1)} %get-tuple-element.22, f32[8,16,16,128]{3,2,1,0:T(8,128)S(1)} %bitcast.101, f32[8,16]{1,0:T(8,128)S(1)} %get-tuple-element.94, pred[8,16]{1,0:T(8,128)(4,1)S(1)} %compare_and_fusion, f32[8,128]{1,0:T(8,128)S(1)} %add_power_fusion), kind=kOutput, calls=%fused_computation.11 | convolution fusion | flops 403193856 | bytes 5313152 | tf_op jit(solution)/shard_map/cond/branch_0_fun/btij,btkj->bki/dot_general | solution.py:294
  164.1 39.2 %psum.19 = f32[16,16]{0,1:T(8,128)S(1)} all-reduce(f32[16,16]{0,1:T(8,128)S(1)} %convolution_bitcast_fusion.7), channel_id=1, replica_groups=mesh['group'=4,'row'=8] {'group','row'}, use_global_device_ids=true, to_apply=%region_5.9 | all-reduce | flops 256 | bytes 2048 | tf_op jit(solution)/shard_map/cond/branch_0_fun/psum | solution.py:299
  203.3 1.5 cholesky.70
  204.8 0.7 compare_reduce_fusion.1
  205.5 0.7 fusion.18
  206.2 1.2 custom-call.8
  207.5 0.2 convolution_bitcast_fusion.6
  207.7 0.2 bitcast_multiply_fusion
  207.9 10.6 %all_gather.12 = f32[64,16,128]{2,1,0:T(8,128)S(1)} all-gather(f32[8,16,128]{2,1,0:T(8,128)S(1)} %get-tuple-element.98), channel_id=1, replica_groups=mesh['group'=4,'row'=8] {'row'}, dimensions={0}, use_global_device_ids=true | all-gather | bytes 589824 | tf_op jit(solution)/shard_map/cond/branch_0_fun/all_gather | solution.py:291
  218.5 0.6 gather_fusion.4
  219.1 2.6 collective-permute-start.4
  221.7 1.3 collective-permute-start.5
  223.1 4.2 %collective-permute-done.5 = f32[2,16,128]{2,1,0:T(8,128)S(1)} collective-permute-done((f32[2,16,128]{2,1,0:T(8,128)S(1)}, f32[2,16,128]{2,1,0:T(8,128)S(1)}, u32[]{:S(2)}, u32[]{:S(2)}) %collective-permute-start.5) | collective-permute-done | bytes 16416 | tf_op jit(solution)/shard_map/cond/branch_0_fun/ppermute | solution.py:264
  227.3 0.8 gather_fusion.5
  228.1 5.2 %fusion = f32[8,16,128]{2,1,0:T(8,128)S(1)} fusion(bf16[8,16,128,128]{3,2,1,0:T(8,128)(2,1)} %get-tuple-element.22, f32[8,16,16,128]{3,2,1,0:T(8,128)S(1)} %bitcast.99, f32[8,16]{1,0:T(8,128)S(1)} %get-tuple-element.94, pred[8,16]{1,0:T(8,128)(4,1)S(1)} %compare_and_fusion, f32[8,128]{1,0:T(8,128)S(1)} %add_power_fusion), kind=kOutput, calls=%fused_computation.9 | convolution fusion | flops 403193856 | bytes 5313152 | tf_op jit(solution)/shard_map/cond/branch_0_fun/btij,btkj->bki/dot_general | solution.py:294
  233.3 0.2 convolution_bitcast_fusion.5
  233.5 38.7 %psum.20 = f32[16,16]{0,1:T(8,128)S(1)} all-reduce(f32[16,16]{0,1:T(8,128)S(1)} %convolution_bitcast_fusion.5), channel_id=1, replica_groups=mesh['group'=4,'row'=8] {'group','row'}, use_global_device_ids=true, to_apply=%region_6.10 | all-reduce | flops 256 | bytes 2048 | tf_op jit(solution)/shard_map/cond/branch_0_fun/psum | solution.py:299
  272.2 1.5 cholesky.81
  273.7 0.7 compare_reduce_fusion
  274.4 0.7 fusion.19
  275.1 1.2 custom-call.9
  276.3 0.2 convolution_bitcast_fusion.4
  276.6 0.2 convolution_bitcast_fusion
  276.8 0.7 pad_maximum_fusion.3
  (55 shorter events, 1.6 us)
Async XLA Ops:
  0.0 17.6 %copy-start.3 = (s32[1,1,8,2]{2,3,1,0:T(2,128)S(1)}, s32[1,1,8,2]{2,3,1,0:T(2,128)}, u32[]{:S(2)}) copy-start(s32[1,1,8,2]{2,3,1,0:T(2,128)} %param.18) | copy-start | bytes 196
  0.0 17.6 %copy-start.2 = (s32[8]{0:T(128)S(1)}, s32[8]{0:T(128)}, u32[]{:S(2)}) copy-start(s32[8]{0:T(128)} %refs_1_.5) | copy-start | bytes 100
  0.0 17.6 %copy-start.1 = (s32[8,16]{1,0:T(8,128)S(1)}, s32[8,16]{1,0:T(8,128)}, u32[]{:S(2)}) copy-start(s32[8,16]{1,0:T(8,128)} %refs_2_.5) | copy-start | bytes 1540
  3.8 13.8 %collective-permute-start.6 = (f32[2,16,128]{2,1,0:T(8,128)S(1)}, f32[2,16,128]{2,1,0:T(8,128)S(1)}, u32[]{:S(2)}, u32[]{:S(2)}) collective-permute-start(f32[2,16,128]{2,1,0:T(8,128)S(1)} %get-tuple-element.53), channel_id=1, source_target_pairs={{0,8},{16,24},{8,0},{24,16},{1,9},{17,25},{9,1},{25,17},{2,10},{18... | collective-permute-start | bytes 49160 | tf_op jit(solution)/shard_map/ppermute | solution.py:272
  6.9 10.7 %collective-permute-start.7 = (f32[2,16,128]{2,1,0:T(8,128)S(1)}, f32[2,16,128]{2,1,0:T(8,128)S(1)}, u32[]{:S(2)}, u32[]{:S(2)}) collective-permute-start(f32[2,16,128]{2,1,0:T(8,128)S(1)} %get-tuple-element.54), channel_id=1, source_target_pairs={{8,16},{16,8},{9,17},{17,9},{10,18},{18,10},{11,19},{19,11},{12,20... | collective-permute-start | bytes 49160 | tf_op jit(solution)/shard_map/ppermute | solution.py:272
  21.8 9.6 %all-to-all-start = ((f32[16,16,128]{2,1,0:T(8,128)}), f32[16,16,128]{2,1,0:T(8,128)S(1)}, u32[]{:S(2)}, u32[]{:S(2)}) async-start(f32[16,16,128]{2,1,0:T(8,128)} %get-tuple-element.56), calls=%async_computation | async-start | bytes 262144 | tf_op jit(solution)/shard_map/all_to_all | solution.py:346
  25.2 6.2 %collective-permute-start.8 = (f32[2,16,128]{2,1,0:T(8,128)S(1)}, f32[2,16,128]{2,1,0:T(8,128)S(1)}, u32[]{:S(2)}, u32[]{:S(2)}) collective-permute-start(f32[2,16,128]{2,1,0:T(8,128)S(1)} %get-tuple-element.57), channel_id=1, source_target_pairs={{0,8},{16,24},{8,0},{24,16},{1,9},{17,25},{9,1},{25,17},{2,10},{18... | collective-permute-start | bytes 49160 | tf_op jit(solution)/shard_map/ppermute | solution.py:272
  29.7 1.7 collective-permute-start.9
  35.5 33.2 %copy-start = (f32[8,16,128]{2,1,0:T(8,128)S(1)}, f32[8,16,128]{2,1,0:T(8,128)}, u32[]{:S(2)}) copy-start(f32[8,16,128]{2,1,0:T(8,128)} %basis_ref.1) | copy-start | bytes 196612
  35.5 9.8 %all-to-all-start.1 = ((f32[16,16,128]{2,1,0:T(8,128)}), f32[16,16,128]{2,1,0:T(8,128)S(1)}, u32[]{:S(2)}, u32[]{:S(2)}) async-start(f32[16,16,128]{2,1,0:T(8,128)} %get-tuple-element.61), calls=%async_computation.1 | async-start | bytes 262144 | tf_op jit(solution)/shard_map/all_to_all | solution.py:346
  39.8 5.6 %collective-permute-start.10 = (f32[2,16,128]{2,1,0:T(8,128)S(1)}, f32[2,16,128]{2,1,0:T(8,128)S(1)}, u32[]{:S(2)}, u32[]{:S(2)}) collective-permute-start(f32[2,16,128]{2,1,0:T(8,128)S(1)} %get-tuple-element.62), channel_id=1, source_target_pairs={{0,8},{16,24},{8,0},{24,16},{1,9},{17,25},{9,1},{25,17},{2,10},{18... | collective-permute-start | bytes 49160 | tf_op jit(solution)/shard_map/ppermute | solution.py:272
  43.7 1.7 collective-permute-start.11
  50.1 14.9 %all-to-all-start.2 = ((f32[32,8,128]{2,1,0:T(8,128)}), f32[32,8,128]{2,1,0:T(8,128)S(1)}, u32[]{:S(2)}, u32[]{:S(2)}) async-start(f32[32,8,128]{2,1,0:T(8,128)} %get-tuple-element.66), calls=%async_computation.2 | async-start | bytes 262144 | tf_op jit(solution)/shard_map/all_to_all | solution.py:388
  73.4 13.9 %collective-permute-start = (f32[2,16,128]{2,1,0:T(8,128)S(1)}, f32[2,16,128]{2,1,0:T(8,128)S(1)}, u32[]{:S(2)}, u32[]{:S(2)}) collective-permute-start(f32[2,16,128]{2,1,0:T(8,128)S(1)} %get-tuple-element.92), channel_id=1, source_target_pairs={{0,8},{8,16},{16,24},{1,9},{9,17},{17,25},{2,10},{10,18},{18,26},{... | collective-permute-start | bytes 49160 | tf_op jit(solution)/shard_map/cond/branch_0_fun/ppermute | solution.py:263
  76.0 11.3 %collective-permute-start.1 = (f32[2,16,128]{2,1,0:T(8,128)S(1)}, f32[2,16,128]{2,1,0:T(8,128)S(1)}, u32[]{:S(2)}, u32[]{:S(2)}) collective-permute-start(f32[2,16,128]{2,1,0:T(8,128)S(1)} %get-tuple-element.93), channel_id=1, source_target_pairs={{8,0},{16,8},{24,16},{9,1},{17,9},{25,17},{10,2},{18,10},{26,18},{... | collective-permute-start | bytes 49160 | tf_op jit(solution)/shard_map/cond/branch_0_fun/ppermute | solution.py:264
  149.9 3.8 %collective-permute-start.2 = (f32[2,16,128]{2,1,0:T(8,128)S(1)}, f32[2,16,128]{2,1,0:T(8,128)S(1)}, u32[]{:S(2)}, u32[]{:S(2)}) collective-permute-start(f32[2,16,128]{2,1,0:T(8,128)S(1)} %get-tuple-element.90), channel_id=1, source_target_pairs={{0,8},{8,16},{16,24},{1,9},{9,17},{17,25},{2,10},{10,18},{18,26},{... | collective-permute-start | bytes 49160 | tf_op jit(solution)/shard_map/cond/branch_0_fun/ppermute | solution.py:263
  152.3 5.6 %collective-permute-start.3 = (f32[2,16,128]{2,1,0:T(8,128)S(1)}, f32[2,16,128]{2,1,0:T(8,128)S(1)}, u32[]{:S(2)}, u32[]{:S(2)}) collective-permute-start(f32[2,16,128]{2,1,0:T(8,128)S(1)} %get-tuple-element.91), channel_id=1, source_target_pairs={{8,0},{16,8},{24,16},{9,1},{17,9},{25,17},{10,2},{18,10},{26,18},{... | collective-permute-start | bytes 49160 | tf_op jit(solution)/shard_map/cond/branch_0_fun/ppermute | solution.py:264
  219.1 4.0 %collective-permute-start.4 = (f32[2,16,128]{2,1,0:T(8,128)S(1)}, f32[2,16,128]{2,1,0:T(8,128)S(1)}, u32[]{:S(2)}, u32[]{:S(2)}) collective-permute-start(f32[2,16,128]{2,1,0:T(8,128)S(1)} %get-tuple-element.88), channel_id=1, source_target_pairs={{0,8},{8,16},{16,24},{1,9},{9,17},{17,25},{2,10},{10,18},{18,26},{... | collective-permute-start | bytes 49160 | tf_op jit(solution)/shard_map/cond/branch_0_fun/ppermute | solution.py:263
  221.7 5.6 %collective-permute-start.5 = (f32[2,16,128]{2,1,0:T(8,128)S(1)}, f32[2,16,128]{2,1,0:T(8,128)S(1)}, u32[]{:S(2)}, u32[]{:S(2)}) collective-permute-start(f32[2,16,128]{2,1,0:T(8,128)S(1)} %get-tuple-element.89), channel_id=1, source_target_pairs={{8,0},{16,8},{24,16},{9,1},{17,9},{25,17},{10,2},{18,10},{26,18},{... | collective-permute-start | bytes 49160 | tf_op jit(solution)/shard_map/cond/branch_0_fun/ppermute | solution.py:264

commit v5 on v4

--- a/solution.py
+++ b/solution.py
@@ -34,6 +34,10 @@
     return pl.BlockSpec(memory_space=pltpu.HBM)
 
 
+def far(x):
+    return pltpu.with_memory_space_constraint(x, pltpu.HBM)
+
+
 def f32(*shape):
     return jax.ShapeDtypeStruct(shape, jnp.float32)
 
@@ -56,14 +60,24 @@
     return copy
 
 
-def roots_kernel(place_ref, count_ref, want_ref, tiles_hbm, basis_ref, root_ref, sent_ref,
-                 first_ref, second_ref, held_ref, rest_ref, sems):
+def roots_kernel(place_ref, count_hbm, want_hbm, tiles_hbm, basis_hbm, root_ref, sent_ref,
+                 first_ref, second_ref, held_ref, rest_ref, count_ref, want_ref, basis_ref, sems):
     held, per_row, side, _ = held_ref.shape
     blocks = held + rest_ref.shape[0]
     peers = want_ref.shape[1]
     vectors = basis_ref.shape[1]
     rest_load = load(tiles_hbm, held, rest_ref, sems.at[0])
+    small = [
+        pltpu.make_async_copy(source, target, sems.at[2 + n])
+        for n, (source, target) in enumerate(
+            ((count_hbm, count_ref), (want_hbm, want_ref), (basis_hbm, basis_ref))
+        )
+    ]
+    for copy in small:
+        copy.start()
     held_load = load(tiles_hbm, 0, held_ref, sems.at[1])
+    for copy in small:
+        copy.wait()
     for p in range(peers):
         owned = (place_ref[0] * peers + p) * blocks
         for c in range(SLOTS):
@@ -106,14 +120,32 @@
         out_ref[n] = value
 
 
+def pieces_of(x, count):
+    parts = []
+    for n in range(count):
+        part = x.astype(jnp.bfloat16)
+        parts.append(part)
+        if n < count - 1:
+            x = x - part.astype(jnp.float32)
+    return parts
+
+
 def split_into(x, out_ref, slot):
     vectors = x.shape[0]
-    rest = x
-    for piece in range(PIECES):
-        part = rest.astype(jnp.bfloat16)
-        out_ref[slot, pl.ds(piece * vectors, vectors)] = part
-        if piece < PIECES - 1:
-            rest = rest - part.astype(jnp.float32)
+    for n, part in enumerate(pieces_of(x, PIECES)):
+        out_ref[slot, pl.ds(n * vectors, vectors)] = part
+
+
+def gram_of(flat):
+    k = flat.shape[0]
+    stack = jnp.concatenate(pieces_of(flat, 3), axis=0)
+    full = lax.dot_general(stack, stack, NT, preferred_element_type=jnp.float32)
+    term = lambda i, j: full[i * k : (i + 1) * k, j * k : (j + 1) * k]
+    small = term(1, 1) + (term(0, 2) + term(2, 0))
+    return term(0, 0) + ((term(0, 1) + term(1, 0)) + small)
+
+
+TERMS = ((0, 0), (0, 1), (1, 0), (1, 1), (0, 2), (2, 0))
 
 
 def pack_grams(grams):
@@ -140,7 +172,7 @@
     blocks = held + rest_ref.shape[0]
     rest_load = load(tiles_hbm, held, rest_ref, load_sem)
     if last:
-        *before, applied_ref, gram_hbm, packed_ref, sems = refs
+        *before, applied_ref, gram_hbm, packed_ref, sem = refs
     else:
         if not opening:
             asked_ref, *refs = refs
@@ -202,17 +234,14 @@
         send.start()
         swaps_into(group, blocks, scaled_ref, first_ref, second_ref)
     flat = jnp.concatenate(rows, axis=1)
-    gram = lax.dot_general(flat, flat, NT, precision=HIGH, preferred_element_type=jnp.float32)
+    gram = gram_of(flat)
     if last:
-        packed_ref[0] = pack_grams([ref[...] for ref in before] + [gram])
-        sends = [
-            pltpu.make_async_copy(packed_ref, gram_hbm.at[pl.ds(n, 1)], sems.at[n])
-            for n in range(gram_hbm.shape[0])
-        ]
-        for send in sends:
-            send.start()
-        for send in sends:
-            send.wait()
+        packed = pack_grams([ref[...] for ref in before] + [gram])
+        for n in range(packed_ref.shape[0]):
+            packed_ref[n] = packed
+        send = pltpu.make_async_copy(packed_ref, gram_hbm, sem)
+        send.start()
+        send.wait()
     else:
         gram_ref[...] = gram
         send.wait()
@@ -245,11 +274,12 @@
         squares = jnp.sum(grams[t] * unit, axis=0, keepdims=True)
         norm = jnp.sum(inverse * inverse * squares) / row_total
         good = good & (norm < TRUST) & (jnp.min(squares) > TINY)
+        left = [part.astype(jnp.float32) for part in pieces_of(inverse, 3)]
+        left = jnp.concatenate([left[i] for i, _ in TERMS], axis=1).astype(jnp.bfloat16)
         for b in range(blocks):
-            out_ref[t, b] = lax.dot_general(
-                inverse, applied_refs[t][b], (((1,), (0,)), ((), ())), precision=HIGH,
-                preferred_element_type=jnp.float32,
-            )
+            right = pieces_of(applied_refs[t][b], 3)
+            right = jnp.concatenate([right[j] for _, j in TERMS], axis=0)
+            out_ref[t, b] = jnp.dot(left, right, preferred_element_type=jnp.float32)
         sends[t].start()
     trust_ref[0] = good.astype(jnp.int32)
     for send in sends:
@@ -313,7 +343,7 @@
     wanted = jnp.transpose(recv_list.reshape(peers, SLOTS))
     lists = pl.cdiv(peers * SLOTS, vectors)
     tile_bytes = tiles.size * 2
-    far_tiles = pltpu.with_memory_space_constraint(tiles, pltpu.HBM)
+    far_tiles = far(tiles)
     block_shape = (vectors, side)
     picked_shape = (peers * SLOTS,) + block_shape
     rim_shape = f32(RIM, *block_shape)
@@ -328,13 +358,19 @@
             rim_shape,
             pltpu.VMEM((kept,) + tiles.shape[1:], tiles.dtype),
         ),
-        in_specs=[smem(), smem(), smem(), hbm(), vmem()],
+        in_specs=[smem()] + [hbm()] * 4,
         out_specs=(vmem(),) * 5,
-        scratch_shapes=[rest, pltpu.SemaphoreType.DMA((2,))],
+        scratch_shapes=[
+            rest,
+            pltpu.SMEM((blocks,), jnp.int32),
+            pltpu.SMEM((SLOTS, peers), jnp.int32),
+            pltpu.VMEM((blocks,) + block_shape, jnp.float32),
+            pltpu.SemaphoreType.DMA((5,)),
+        ],
         compiler_params=params(),
         cost_estimate=cost(tiles.size * 2, tile_bytes),
         name="roots",
-    )(place, tile_count, wanted, far_tiles, start_basis)
+    )(place, far(tile_count), far(wanted), far_tiles, far(start_basis))
     slots = blocks + peers * SLOTS + 2 * RIM
     powers, grams = [], []
     for t in range(ITERS):
@@ -352,7 +388,10 @@
         if last:
             shapes += [pltpu.HBM((groups * peers, vectors // 2, LANES), jnp.float32)]
             specs = [vmem(), hbm()]
-            scratch = [pltpu.VMEM((1, vectors // 2, LANES), jnp.float32), pltpu.SemaphoreType.DMA((groups * peers,))]
+            scratch = [
+                pltpu.VMEM((groups * peers, vectors // 2, LANES), jnp.float32),
+                pltpu.SemaphoreType.DMA,
+            ]
             arrays += grams
         else:
             shapes += [f32(vectors, vectors), f32(blocks, *block_shape), pltpu.HBM(picked_shape, jnp.float32)]

time: 279 us -> 278 us (level)
  no operation moved by 1% of the time
where the time goes in v5:
time: 278 us; the launch traced here: 277 us
  blocking collectives  159 us (57%)
  starting transfers between devices  39 us (14%)
  Pallas kernels  19.1 us (7%)
  waiting for transfers between devices  18.8 us (7%)
  other arithmetic  18 us (6%)
  matrix products  17.5 us (6%)
  local copies, waits for them, and re-layouts  4.46 us (2%)
    psum x3, blocking collectives, stepwise(): factor = jnp.linalg.cholesky(lax.psum(gram, ('group', 'row')) / row_total)  118 us
    all_gather x3, blocking collectives, stepwise(): lax.all_gather(scaled, 'row', axis=0, tiled=True)  30.5 us
    dot_general x3, matrix products, stepwise(): jnp.einsum('btij,btkj->bki', tiles, picked, precision=HIGH, preferred_ele...  15.6 us
    ppermute x6, starting transfers between devices, swap(): lax.ppermute(x, 'group', pair)  13.4 us
    pallas_call x3, Pallas kernels, local(): pl.pallas_call(functools.partial(apply_kernel, t), out_shape=tuple(shapes...  12.7 us
    all_gather x1, blocking collectives, local(): received = lax.all_gather(scaled, 'row', axis=0)  10 us
    ppermute x3, waiting for transfers between devices, neighbours(): high = lax.ppermute(scaled[:RIM], 'group', down)  8.42 us
    all_to_all x1, waiting for transfers between devices, local(): gathered = lax.all_to_all(grams[-1], ('group', 'row'), 0, 0, tiled=True)  8.23 us
  transfers between devices with their start and end apart: 15, of which 5 were waited for; matrix products, arithmetic and copies ran while one was open for 0% of the time, Pallas kernels for 0%

profile of v5, /device:TPU:0, one launch (start us, length us, event | category | flops | bytes accessed | tf_op | source)
XLA Modules:
  0.0 276.7 jit_solution(9018130177365900666)
XLA Ops:
  0.1 3.5 %roots.1 = (f32[8,1,128]{2,1,0:T(1,128)S(1)}, f32[9,16,128]{2,1,0:T(8,128)S(1)}, f32[2,16,128]{2,1,0:T(8,128)S(1)}, f32[2,16,128]{2,1,0:T(8,128)S(1)}, bf16[5,16,128,128]{3,2,1,0:T(8,128)(2,1)S(1)}) custom-call(s32[2]{0:T(128)S(1)} %pad_add_fusion.place_ref.refs_0_, s32[8]{0:T(128)} %refs_1_.5, s32[2,8]{1,0:T(2,128)} %bitcast.105, ...), custom_call_target="tpu_custom_call" | custom-call | flops 4194304 | bytes 4194304 | tf_op jit(solution)/shard_map/roots/pallas_call | solution.py:352
  3.6 3.1 %collective-permute-start.6 = (f32[2,16,128]{2,1,0:T(8,128)S(1)}, f32[2,16,128]{2,1,0:T(8,128)S(1)}, u32[]{:S(2)}, u32[]{:S(2)}) collective-permute-start(f32[2,16,128]{2,1,0:T(8,128)S(1)} %get-tuple-element.53), channel_id=1, source_target_pairs={{0,8},{16,24},{8,0},{24,16},{1,9},{17,25},{9,1},{25,17},{2,10},{18... | collective-permute-start | bytes 49160 | tf_op jit(solution)/shard_map/ppermute | solution.py:302
  6.7 0.7 collective-permute-start.7
  7.3 10.0 %all-gather = f32[72,16,128]{2,1,0:T(8,128)S(1)} all-gather(f32[9,16,128]{2,1,0:T(8,128)S(1)} %get-tuple-element.52.refs_7_), channel_id=2, replica_groups=mesh['group'=4,'row'=8] {'row'}, dimensions={0}, use_global_device_ids=true | all-gather | bytes 663552 | tf_op jit(solution)/shard_map/all_gather | solution.py:380
  17.4 4.1 %apply.2 = (f32[8,16,128]{2,1,0:T(8,128)S(1)}, f32[16,16]{1,0:T(8,128)S(1)}, f32[8,16,128]{2,1,0:T(8,128)S(1)}, f32[16,16,128]{2,1,0:T(8,128)}, f32[2,16,128]{2,...) custom-call(s32[2]{0:T(128)S(1)} %pad_add_fusion.place_ref.refs_0_, s32[8]{0:T(128)S(1)} %copy-done.2, ...), custom_call_target="tpu_custom_call" | custom-call | flops 134217728 | bytes 4194304 | tf_op jit(solution)/shard_map/apply/pallas_call | solution.py:406
  21.5 3.4 %all-to-all-start = ((f32[16,16,128]{2,1,0:T(8,128)}), f32[16,16,128]{2,1,0:T(8,128)S(1)}, u32[]{:S(2)}, u32[]{:S(2)}) async-start(f32[16,16,128]{2,1,0:T(8,128)} %get-tuple-element.56), calls=%async_computation | async-start | bytes 262144 | tf_op jit(solution)/shard_map/all_to_all | solution.py:382
  24.9 4.5 %collective-permute-start.8 = (f32[2,16,128]{2,1,0:T(8,128)S(1)}, f32[2,16,128]{2,1,0:T(8,128)S(1)}, u32[]{:S(2)}, u32[]{:S(2)}) collective-permute-start(f32[2,16,128]{2,1,0:T(8,128)S(1)} %get-tuple-element.57), channel_id=1, source_target_pairs={{0,8},{16,24},{8,0},{24,16},{1,9},{17,25},{9,1},{25,17},{2,10},{18... | collective-permute-start | bytes 49160 | tf_op jit(solution)/shard_map/ppermute | solution.py:302
  29.4 0.7 collective-permute-start.9
  30.0 1.1 collective-permute-done.8.refs_8_
  31.1 4.1 %apply.3 = (f32[8,16,128]{2,1,0:T(8,128)S(1)}, f32[16,16]{1,0:T(8,128)S(1)}, f32[8,16,128]{2,1,0:T(8,128)S(1)}, f32[16,16,128]{2,1,0:T(8,128)}, f32[2,16,128]{2,1,0:T(8,128)S(1)}, /*index=5*/f32[2,16,128]{2,1,0:T(8,128)S(1)}) custom-call(s32[2]{0:T(128)S(1)} %pad_add_fusion.place_ref.refs_0_, s32[8]{0:T(128)S(1)} %copy-done.2, s32[8,16]{1,0:T(8,128)S(1)} %copy-done.1, ...), custom_call_target="tpu_custom_call" | custom-call | flops 134217728 | bytes 4194304 | tf_op jit(solution)/shard_map/apply/pallas_call | solution.py:406
  35.2 4.2 %all-to-all-start.1 = ((f32[16,16,128]{2,1,0:T(8,128)}), f32[16,16,128]{2,1,0:T(8,128)S(1)}, u32[]{:S(2)}, u32[]{:S(2)}) async-start(f32[16,16,128]{2,1,0:T(8,128)} %get-tuple-element.61), calls=%async_computation.1 | async-start | bytes 262144 | tf_op jit(solution)/shard_map/all_to_all | solution.py:382
  39.4 3.9 %collective-permute-start.10 = (f32[2,16,128]{2,1,0:T(8,128)S(1)}, f32[2,16,128]{2,1,0:T(8,128)S(1)}, u32[]{:S(2)}, u32[]{:S(2)}) collective-permute-start(f32[2,16,128]{2,1,0:T(8,128)S(1)} %get-tuple-element.62), channel_id=1, source_target_pairs={{0,8},{16,24},{8,0},{24,16},{1,9},{17,25},{9,1},{25,17},{2,10},{18... | collective-permute-start | bytes 49160 | tf_op jit(solution)/shard_map/ppermute | solution.py:302
  43.3 0.7 collective-permute-start.11
  44.0 1.1 collective-permute-done.10.refs_8_
  45.0 4.5 %apply_last.1 = (f32[8,16,128]{2,1,0:T(8,128)S(1)}, f32[32,8,128]{2,1,0:T(8,128)}) custom-call(s32[2]{0:T(128)S(1)} %pad_add_fusion.place_ref.refs_0_, s32[8]{0:T(128)S(1)} %copy-done.2, s32[8,16]{1,0:T(8,128)S(1)} %copy-done.1, bf16[8,16,128,128]{3,2,1,0:T(8,128)(2,1)} %refs_3_.3, bf16[5,16,128,128]{3,2,1,0:T(8,128)(2,1)S(1)} %get-tuple-element.50.refs_5_.refs_4_, ...), custom_call_target="tpu_custom_call" | custom-call | flops 134217728 | bytes 4194304 | tf_op jit(solution)/shard_map/apply_last/pallas_call | solution.py:406
  49.5 6.6 %all-to-all-start.2 = ((f32[32,8,128]{2,1,0:T(8,128)}), f32[32,8,128]{2,1,0:T(8,128)S(1)}, u32[]{:S(2)}, u32[]{:S(2)}) async-start(f32[32,8,128]{2,1,0:T(8,128)} %get-tuple-element.66), calls=%async_computation.2 | async-start | bytes 262144 | tf_op jit(solution)/shard_map/all_to_all | solution.py:427
  56.2 8.2 %all-to-all-done.2.grams_ref = f32[32,8,128]{2,1,0:T(8,128)S(1)} async-done(((f32[32,8,128]{2,1,0:T(8,128)}), f32[32,8,128]{2,1,0:T(8,128)S(1)}, u32[]{:S(2)}, u32[]{:S(2)}) %all-to-all-start.2) | async-done | bytes 131104 | tf_op jit(solution)/shard_map/all_to_all | solution.py:427
  64.4 2.9 %finish.1 = (f32[3,8,16,128]{3,2,1,0:T(8,128)}, s32[1]{0:T(128)}) custom-call(f32[32,8,128]{2,1,0:T(8,128)S(1)} %all-to-all-done.2.grams_ref, f32[8,16,128]{2,1,0:T(8,128)S(1)} %get-tuple-element.67.refs_0_, f32[8,16,128]{2,1,0:T(8,128)S(1)} %get-tuple-element.68.refs_1_, f32[8,16,128]{2,1,0:T(8,128)S(1)} %get-tuple-element.69.refs_2_), custom_call_target="tpu_custom_call" | custom-call | tf_op jit(solution)/shard_map/finish/pallas_call | solution.py:428
  67.9 208.8 %conditional.1 = (f32[3,8,16,128]{3,2,1,0:T(8,128)}) conditional(s32[]{:T(128)} %bitcast.39, (bf16[8,16,128,128]{3,2,1,0:T(8,128)(2,1)}, s32[8]{0:T(128)S(1)}, f32[8,16,128]{2,1,0:T(8,128)S(1)}, s32[1,1,8,2]{2,3,1,0:T(2,128)S(1)}, s32[8,16]{1,0:T(8,128)S(1)}) %tuple.33, f32[3,8,16,128]{3,2,1,0:T(8,128)} %get-tuple-element.71), branch_computations={%region_0.11_spmd, %region_7.12_spmd} | conditional | flops 1235852416 | bytes 33198924 | solution.py:440
  67.9 4.4 %multiply_reduce_fusion = f32[8,16,128]{2,1,0:T(8,128)S(1)} fusion(bf16[8,16,128,128]{3,2,1,0:T(8,128)(2,1)} %get-tuple-element.22), kind=kLoop, calls=%fused_computation.6 | loop fusion | flops 6275072 | bytes 4259840 | tf_op jit(solution)/shard_map/cond/branch_0_fun/btij,bt->bi/reduce_sum | solution.py:313
  72.6 2.6 collective-permute-start
  75.2 1.3 collective-permute-start.1
  76.5 9.0 %all_gather.10 = f32[64,16,128]{2,1,0:T(8,128)S(1)} all-gather(f32[8,16,128]{2,1,0:T(8,128)S(1)} %broadcast_multiply_fusion), channel_id=1, replica_groups=mesh['group'=4,'row'=8] {'row'}, dimensions={0}, use_global_device_ids=true | all-gather | bytes 589824 | tf_op jit(solution)/shard_map/cond/branch_0_fun/all_gather | solution.py:321
  85.8 0.6 gather_fusion
  86.6 0.8 gather_fusion.1
  87.3 5.2 %fusion.2 = f32[8,16,128]{2,1,0:T(8,128)S(1)} fusion(bf16[8,16,128,128]{3,2,1,0:T(8,128)(2,1)} %get-tuple-element.22, f32[8,16,16,128]{3,2,1,0:T(8,128)S(1)} %bitcast.100, f32[8,16]{1,0:T(8,128)S(1)} %get-tuple-element.94, pred[8,16]{1,0:T(8,128)(4,1)S(1)} %compare_and_fusion, f32[8,128]{1,0:T(8,128)S(1)} %add_power_fusion), kind=kOutput, calls=%fused_computation.13 | convolution fusion | flops 403193856 | bytes 5313152 | tf_op jit(solution)/shard_map/cond/branch_0_fun/btij,btkj->bki/dot_general | solution.py:324
  92.7 40.4 %psum.18 = f32[16,16]{0,1:T(8,128)S(1)} all-reduce(f32[16,16]{0,1:T(8,128)S(1)} %convolution_bitcast_fusion.9), channel_id=1, replica_groups=mesh['group'=4,'row'=8] {'group','row'}, use_global_device_ids=true, to_apply=%region_2.0 | all-reduce | flops 256 | bytes 2048 | tf_op jit(solution)/shard_map/cond/branch_0_fun/psum | solution.py:329
  133.2 1.5 cholesky.59
  134.7 0.7 compare_reduce_fusion.2
  135.4 0.7 fusion.17
  136.1 1.2 custom-call.7
  137.3 0.2 convolution_bitcast_fusion.8
  137.5 0.2 bitcast_multiply_fusion.1
  137.8 10.8 %all_gather.11 = f32[64,16,128]{2,1,0:T(8,128)S(1)} all-gather(f32[8,16,128]{2,1,0:T(8,128)S(1)} %get-tuple-element.96), channel_id=1, replica_groups=mesh['group'=4,'row'=8] {'row'}, dimensions={0}, use_global_device_ids=true | all-gather | bytes 589824 | tf_op jit(solution)/shard_map/cond/branch_0_fun/all_gather | solution.py:321
  148.6 0.6 gather_fusion.2
  149.2 2.3 collective-permute-start.2
  151.5 1.3 collective-permute-start.3
  152.9 4.2 %collective-permute-done.3 = f32[2,16,128]{2,1,0:T(8,128)S(1)} collective-permute-done((f32[2,16,128]{2,1,0:T(8,128)S(1)}, f32[2,16,128]{2,1,0:T(8,128)S(1)}, u32[]{:S(2)}, u32[]{:S(2)}) %collective-permute-start.3) | collective-permute-done | bytes 16416 | tf_op jit(solution)/shard_map/cond/branch_0_fun/ppermute | solution.py:294
  157.2 0.8 gather_fusion.3
  157.9 5.2 %fusion.1 = f32[8,16,128]{2,1,0:T(8,128)S(1)} fusion(bf16[8,16,128,128]{3,2,1,0:T(8,128)(2,1)} %get-tuple-element.22, f32[8,16,16,128]{3,2,1,0:T(8,128)S(1)} %bitcast.101, f32[8,16]{1,0:T(8,128)S(1)} %get-tuple-element.94, pred[8,16]{1,0:T(8,128)(4,1)S(1)} %compare_and_fusion, f32[8,128]{1,0:T(8,128)S(1)} %add_power_fusion), kind=kOutput, calls=%fused_computation.11 | convolution fusion | flops 403193856 | bytes 5313152 | tf_op jit(solution)/shard_map/cond/branch_0_fun/btij,btkj->bki/dot_general | solution.py:324
  163.1 0.2 convolution_bitcast_fusion.7
  163.3 39.2 %psum.19 = f32[16,16]{0,1:T(8,128)S(1)} all-reduce(f32[16,16]{0,1:T(8,128)S(1)} %convolution_bitcast_fusion.7), channel_id=1, replica_groups=mesh['group'=4,'row'=8] {'group','row'}, use_global_device_ids=true, to_apply=%region_5.9 | all-reduce | flops 256 | bytes 2048 | tf_op jit(solution)/shard_map/cond/branch_0_fun/psum | solution.py:329
  202.5 1.5 cholesky.70
  204.0 0.7 compare_reduce_fusion.1
  204.8 0.7 fusion.18
  205.5 1.2 custom-call.8
  206.7 0.2 convolution_bitcast_fusion.6
  206.9 0.2 bitcast_multiply_fusion
  207.1 10.6 %all_gather.12 = f32[64,16,128]{2,1,0:T(8,128)S(1)} all-gather(f32[8,16,128]{2,1,0:T(8,128)S(1)} %get-tuple-element.98), channel_id=1, replica_groups=mesh['group'=4,'row'=8] {'row'}, dimensions={0}, use_global_device_ids=true | all-gather | bytes 589824 | tf_op jit(solution)/shard_map/cond/branch_0_fun/all_gather | solution.py:321
  217.8 0.6 gather_fusion.4
  218.3 2.6 collective-permute-start.4
  220.9 1.3 collective-permute-start.5
  222.3 4.2 %collective-permute-done.5 = f32[2,16,128]{2,1,0:T(8,128)S(1)} collective-permute-done((f32[2,16,128]{2,1,0:T(8,128)S(1)}, f32[2,16,128]{2,1,0:T(8,128)S(1)}, u32[]{:S(2)}, u32[]{:S(2)}) %collective-permute-start.5) | collective-permute-done | bytes 16416 | tf_op jit(solution)/shard_map/cond/branch_0_fun/ppermute | solution.py:294
  226.5 0.8 gather_fusion.5
  227.3 5.2 %fusion = f32[8,16,128]{2,1,0:T(8,128)S(1)} fusion(bf16[8,16,128,128]{3,2,1,0:T(8,128)(2,1)} %get-tuple-element.22, f32[8,16,16,128]{3,2,1,0:T(8,128)S(1)} %bitcast.99, f32[8,16]{1,0:T(8,128)S(1)} %get-tuple-element.94, pred[8,16]{1,0:T(8,128)(4,1)S(1)} %compare_and_fusion, f32[8,128]{1,0:T(8,128)S(1)} %add_power_fusion), kind=kOutput, calls=%fused_computation.9 | convolution fusion | flops 403193856 | bytes 5313152 | tf_op jit(solution)/shard_map/cond/branch_0_fun/btij,btkj->bki/dot_general | solution.py:324
  232.5 0.2 convolution_bitcast_fusion.5
  232.7 38.7 %psum.20 = f32[16,16]{0,1:T(8,128)S(1)} all-reduce(f32[16,16]{0,1:T(8,128)S(1)} %convolution_bitcast_fusion.5), channel_id=1, replica_groups=mesh['group'=4,'row'=8] {'group','row'}, use_global_device_ids=true, to_apply=%region_6.10 | all-reduce | flops 256 | bytes 2048 | tf_op jit(solution)/shard_map/cond/branch_0_fun/psum | solution.py:329
  271.4 1.5 cholesky.81
  272.9 0.7 compare_reduce_fusion
  273.6 0.7 fusion.19
  274.3 1.2 custom-call.9
  275.6 0.2 convolution_bitcast_fusion.4
  275.8 0.2 convolution_bitcast_fusion
  276.0 0.7 pad_maximum_fusion.3
  (55 shorter events, 1.6 us)
Async XLA Ops:
  0.0 17.4 %copy-start.3 = (s32[1,1,8,2]{2,3,1,0:T(2,128)S(1)}, s32[1,1,8,2]{2,3,1,0:T(2,128)}, u32[]{:S(2)}) copy-start(s32[1,1,8,2]{2,3,1,0:T(2,128)} %param.18) | copy-start | bytes 196
  0.0 17.4 %copy-start.2 = (s32[8]{0:T(128)S(1)}, s32[8]{0:T(128)}, u32[]{:S(2)}) copy-start(s32[8]{0:T(128)} %refs_1_.5) | copy-start | bytes 100
  0.0 17.4 %copy-start.1 = (s32[8,16]{1,0:T(8,128)S(1)}, s32[8,16]{1,0:T(8,128)}, u32[]{:S(2)}) copy-start(s32[8,16]{1,0:T(8,128)} %refs_2_.5) | copy-start | bytes 1540
  3.6 13.8 %collective-permute-start.6 = (f32[2,16,128]{2,1,0:T(8,128)S(1)}, f32[2,16,128]{2,1,0:T(8,128)S(1)}, u32[]{:S(2)}, u32[]{:S(2)}) collective-permute-start(f32[2,16,128]{2,1,0:T(8,128)S(1)} %get-tuple-element.53), channel_id=1, source_target_pairs={{0,8},{16,24},{8,0},{24,16},{1,9},{17,25},{9,1},{25,17},{2,10},{18... | collective-permute-start | bytes 49160 | tf_op jit(solution)/shard_map/ppermute | solution.py:302
  6.7 10.7 %collective-permute-start.7 = (f32[2,16,128]{2,1,0:T(8,128)S(1)}, f32[2,16,128]{2,1,0:T(8,128)S(1)}, u32[]{:S(2)}, u32[]{:S(2)}) collective-permute-start(f32[2,16,128]{2,1,0:T(8,128)S(1)} %get-tuple-element.54), channel_id=1, source_target_pairs={{8,16},{16,8},{9,17},{17,9},{10,18},{18,10},{11,19},{19,11},{12,20... | collective-permute-start | bytes 49160 | tf_op jit(solution)/shard_map/ppermute | solution.py:302
  21.5 9.6 %all-to-all-start = ((f32[16,16,128]{2,1,0:T(8,128)}), f32[16,16,128]{2,1,0:T(8,128)S(1)}, u32[]{:S(2)}, u32[]{:S(2)}) async-start(f32[16,16,128]{2,1,0:T(8,128)} %get-tuple-element.56), calls=%async_computation | async-start | bytes 262144 | tf_op jit(solution)/shard_map/all_to_all | solution.py:382
  24.9 6.2 %collective-permute-start.8 = (f32[2,16,128]{2,1,0:T(8,128)S(1)}, f32[2,16,128]{2,1,0:T(8,128)S(1)}, u32[]{:S(2)}, u32[]{:S(2)}) collective-permute-start(f32[2,16,128]{2,1,0:T(8,128)S(1)} %get-tuple-element.57), channel_id=1, source_target_pairs={{0,8},{16,24},{8,0},{24,16},{1,9},{17,25},{9,1},{25,17},{2,10},{18... | collective-permute-start | bytes 49160 | tf_op jit(solution)/shard_map/ppermute | solution.py:302
  29.4 1.7 collective-permute-start.9
  35.2 32.7 %copy-start = (f32[8,16,128]{2,1,0:T(8,128)S(1)}, f32[8,16,128]{2,1,0:T(8,128)}, u32[]{:S(2)}) copy-start(f32[8,16,128]{2,1,0:T(8,128)} %basis_hbm.1) | copy-start | bytes 196612
  35.2 9.8 %all-to-all-start.1 = ((f32[16,16,128]{2,1,0:T(8,128)}), f32[16,16,128]{2,1,0:T(8,128)S(1)}, u32[]{:S(2)}, u32[]{:S(2)}) async-start(f32[16,16,128]{2,1,0:T(8,128)} %get-tuple-element.61), calls=%async_computation.1 | async-start | bytes 262144 | tf_op jit(solution)/shard_map/all_to_all | solution.py:382
  39.4 5.6 %collective-permute-start.10 = (f32[2,16,128]{2,1,0:T(8,128)S(1)}, f32[2,16,128]{2,1,0:T(8,128)S(1)}, u32[]{:S(2)}, u32[]{:S(2)}) collective-permute-start(f32[2,16,128]{2,1,0:T(8,128)S(1)} %get-tuple-element.62), channel_id=1, source_target_pairs={{0,8},{16,24},{8,0},{24,16},{1,9},{17,25},{9,1},{25,17},{2,10},{18... | collective-permute-start | bytes 49160 | tf_op jit(solution)/shard_map/ppermute | solution.py:302
  43.3 1.7 collective-permute-start.11
  49.5 14.9 %all-to-all-start.2 = ((f32[32,8,128]{2,1,0:T(8,128)}), f32[32,8,128]{2,1,0:T(8,128)S(1)}, u32[]{:S(2)}, u32[]{:S(2)}) async-start(f32[32,8,128]{2,1,0:T(8,128)} %get-tuple-element.66), calls=%async_computation.2 | async-start | bytes 262144 | tf_op jit(solution)/shard_map/all_to_all | solution.py:427
  72.6 13.9 %collective-permute-start = (f32[2,16,128]{2,1,0:T(8,128)S(1)}, f32[2,16,128]{2,1,0:T(8,128)S(1)}, u32[]{:S(2)}, u32[]{:S(2)}) collective-permute-start(f32[2,16,128]{2,1,0:T(8,128)S(1)} %get-tuple-element.92), channel_id=1, source_target_pairs={{0,8},{8,16},{16,24},{1,9},{9,17},{17,25},{2,10},{10,18},{18,26},{... | collective-permute-start | bytes 49160 | tf_op jit(solution)/shard_map/cond/branch_0_fun/ppermute | solution.py:293
  75.2 11.3 %collective-permute-start.1 = (f32[2,16,128]{2,1,0:T(8,128)S(1)}, f32[2,16,128]{2,1,0:T(8,128)S(1)}, u32[]{:S(2)}, u32[]{:S(2)}) collective-permute-start(f32[2,16,128]{2,1,0:T(8,128)S(1)} %get-tuple-element.93), channel_id=1, source_target_pairs={{8,0},{16,8},{24,16},{9,1},{17,9},{25,17},{10,2},{18,10},{26,18},{... | collective-permute-start | bytes 49160 | tf_op jit(solution)/shard_map/cond/branch_0_fun/ppermute | solution.py:294
  149.2 3.8 %collective-permute-start.2 = (f32[2,16,128]{2,1,0:T(8,128)S(1)}, f32[2,16,128]{2,1,0:T(8,128)S(1)}, u32[]{:S(2)}, u32[]{:S(2)}) collective-permute-start(f32[2,16,128]{2,1,0:T(8,128)S(1)} %get-tuple-element.90), channel_id=1, source_target_pairs={{0,8},{8,16},{16,24},{1,9},{9,17},{17,25},{2,10},{10,18},{18,26},{... | collective-permute-start | bytes 49160 | tf_op jit(solution)/shard_map/cond/branch_0_fun/ppermute | solution.py:293
  151.5 5.6 %collective-permute-start.3 = (f32[2,16,128]{2,1,0:T(8,128)S(1)}, f32[2,16,128]{2,1,0:T(8,128)S(1)}, u32[]{:S(2)}, u32[]{:S(2)}) collective-permute-start(f32[2,16,128]{2,1,0:T(8,128)S(1)} %get-tuple-element.91), channel_id=1, source_target_pairs={{8,0},{16,8},{24,16},{9,1},{17,9},{25,17},{10,2},{18,10},{26,18},{... | collective-permute-start | bytes 49160 | tf_op jit(solution)/shard_map/cond/branch_0_fun/ppermute | solution.py:294
  218.3 4.0 %collective-permute-start.4 = (f32[2,16,128]{2,1,0:T(8,128)S(1)}, f32[2,16,128]{2,1,0:T(8,128)S(1)}, u32[]{:S(2)}, u32[]{:S(2)}) collective-permute-start(f32[2,16,128]{2,1,0:T(8,128)S(1)} %get-tuple-element.88), channel_id=1, source_target_pairs={{0,8},{8,16},{16,24},{1,9},{9,17},{17,25},{2,10},{10,18},{18,26},{... | collective-permute-start | bytes 49160 | tf_op jit(solution)/shard_map/cond/branch_0_fun/ppermute | solution.py:293
  220.9 5.6 %collective-permute-start.5 = (f32[2,16,128]{2,1,0:T(8,128)S(1)}, f32[2,16,128]{2,1,0:T(8,128)S(1)}, u32[]{:S(2)}, u32[]{:S(2)}) collective-permute-start(f32[2,16,128]{2,1,0:T(8,128)S(1)} %get-tuple-element.89), channel_id=1, source_target_pairs={{8,0},{16,8},{24,16},{9,1},{17,9},{25,17},{10,2},{18,10},{26,18},{... | collective-permute-start | bytes 49160 | tf_op jit(solution)/shard_map/cond/branch_0_fun/ppermute | solution.py:294

commit v6 on v5

--- a/solution.py
+++ b/solution.py
@@ -172,14 +172,13 @@
     blocks = held + rest_ref.shape[0]
     rest_load = load(tiles_hbm, held, rest_ref, load_sem)
     if last:
-        *before, applied_ref, gram_hbm, packed_ref, sem = refs
+        *before, applied_ref, gram_ref = refs
     else:
         if not opening:
             asked_ref, *refs = refs
-        applied_ref, gram_ref, scaled_ref, out_hbm, first_ref, second_ref, *refs = refs
+        applied_ref, gram_ref, scaled_ref, out_ref, first_ref, second_ref, *refs = refs
         if opening:
-            asked_ref, *refs = refs
-        picked_ref, sem = refs
+            (asked_ref,) = refs
     vectors = own_ref.shape[1]
     group = place_ref[0]
     slot = 0
@@ -207,6 +206,7 @@
             split_into(jnp.where(odd, a_ref[h], b_ref[h]), table, slot)
             slot += 1
     table[slot] = jnp.zeros(table.shape[1:], table.dtype)
+    rest_load.wait()
     rows = []
     for b in range(blocks):
         picked = []
@@ -214,8 +214,6 @@
             at = jnp.where(s < count_ref[b], cols_ref[b, s], slot)
             picked.append(table[at])
         x = jnp.concatenate(picked, axis=1)
-        if b == held:
-            rest_load.wait()
         tile_ref = held_ref.at[b] if b < held else rest_ref.at[b - held]
         t = jnp.concatenate([tile_ref[s] for s in range(per_row)], axis=1)
         product = lax.dot_general(x, t, NT, preferred_element_type=jnp.float32)
@@ -229,22 +227,16 @@
         if not last:
             scaled_ref[b] = row * root
     if not last:
-        pick_into(asked_ref, scaled_ref, picked_ref)
-        send = pltpu.make_async_copy(picked_ref, out_hbm, sem)
-        send.start()
+        pick_into(asked_ref, scaled_ref, out_ref)
         swaps_into(group, blocks, scaled_ref, first_ref, second_ref)
     flat = jnp.concatenate(rows, axis=1)
     gram = gram_of(flat)
     if last:
         packed = pack_grams([ref[...] for ref in before] + [gram])
-        for n in range(packed_ref.shape[0]):
-            packed_ref[n] = packed
-        send = pltpu.make_async_copy(packed_ref, gram_hbm, sem)
-        send.start()
-        send.wait()
+        for n in range(gram_ref.shape[0]):
+            gram_ref[n] = packed
     else:
         gram_ref[...] = gram
-        send.wait()
 
 
 def finish_kernel(row_total, grams_ref, *refs):
@@ -384,32 +376,22 @@
         scalars = [place, tile_count, tile_cols] + ([wanted] if t == 0 else [])
         arrays = [far_tiles, held, root, scaled, received, *swapped]
         shapes = [f32(blocks, *block_shape)]
-        specs = [vmem(), vmem()]
         if last:
-            shapes += [pltpu.HBM((groups * peers, vectors // 2, LANES), jnp.float32)]
-            specs = [vmem(), hbm()]
-            scratch = [
-                pltpu.VMEM((groups * peers, vectors // 2, LANES), jnp.float32),
-                pltpu.SemaphoreType.DMA,
-            ]
+            shapes += [f32(groups * peers, vectors // 2, LANES)]
             arrays += grams
         else:
-            shapes += [f32(vectors, vectors), f32(blocks, *block_shape), pltpu.HBM(picked_shape, jnp.float32)]
+            shapes += [f32(vectors, vectors), f32(blocks, *block_shape), f32(*picked_shape)]
             shapes += [rim_shape] * 2
-            specs += [vmem(), hbm(), vmem(), vmem()]
-            scratch = [pltpu.VMEM(picked_shape, jnp.float32), pltpu.SemaphoreType.DMA]
             if t:
                 arrays += [asked]
             else:
                 shapes += [f32(peers * SLOTS, side)]
-                specs += [vmem()]
         result = pl.pallas_call(
             functools.partial(apply_kernel, t),
             out_shape=tuple(shapes),
             in_specs=[smem()] * len(scalars) + [hbm()] + [vmem()] * (len(arrays) - 1),
-            out_specs=tuple(specs),
-            scratch_shapes=scratch
-            + [
+            out_specs=tuple(vmem() for _ in shapes),
+            scratch_shapes=[
                 pltpu.VMEM((slots + 1, PIECES * vectors, side), jnp.bfloat16),
                 rest,
                 pltpu.SemaphoreType.DMA,

time: 278 us -> 278 us (level)
  no operation moved by 1% of the time
where the time goes in v6:
time: 278 us; the launch traced here: 277 us
  blocking collectives  159 us (57%)
  starting transfers between devices  39 us (14%)
  Pallas kernels  19.3 us (7%)
  waiting for transfers between devices  18.8 us (7%)
  other arithmetic  18 us (6%)
  matrix products  17.5 us (6%)
  local copies, waits for them, and re-layouts  4.46 us (2%)
    psum x3, blocking collectives, stepwise(): factor = jnp.linalg.cholesky(lax.psum(gram, ('group', 'row')) / row_total)  118 us
    all_gather x3, blocking collectives, stepwise(): lax.all_gather(scaled, 'row', axis=0, tiled=True)  30.5 us
    dot_general x3, matrix products, stepwise(): jnp.einsum('btij,btkj->bki', tiles, picked, precision=HIGH, preferred_ele...  15.5 us
    ppermute x6, starting transfers between devices, swap(): lax.ppermute(x, 'group', pair)  13.4 us
    pallas_call x3, Pallas kernels, local(): pl.pallas_call(functools.partial(apply_kernel, t), out_shape=tuple(shapes...  12.9 us
    all_gather x1, blocking collectives, local(): received = lax.all_gather(scaled, 'row', axis=0)  10 us
    ppermute x3, waiting for transfers between devices, neighbours(): high = lax.ppermute(scaled[:RIM], 'group', down)  8.42 us
    all_to_all x1, waiting for transfers between devices, local(): gathered = lax.all_to_all(grams[-1], ('group', 'row'), 0, 0, tiled=True)  8.23 us
  transfers between devices with their start and end apart: 15, of which 5 were waited for; matrix products, arithmetic and copies ran while one was open for 0% of the time, Pallas kernels for 0%

profile of v6, /device:TPU:0, one launch (start us, length us, event | category | flops | bytes accessed | tf_op | source)
XLA Modules:
  0.0 276.8 jit_solution(15324356491652153799)
XLA Ops:
  0.1 3.5 %roots.1 = (f32[8,1,128]{2,1,0:T(1,128)S(1)}, f32[9,16,128]{2,1,0:T(8,128)S(1)}, f32[2,16,128]{2,1,0:T(8,128)S(1)}, f32[2,16,128]{2,1,0:T(8,128)S(1)}, bf16[5,16,128,128]{3,2,1,0:T(8,128)(2,1)S(1)}) custom-call(s32[2]{0:T(128)S(1)} %pad_add_fusion.place_ref.refs_0_, s32[8]{0:T(128)} %refs_1_.5, s32[2,8]{1,0:T(2,128)} %bitcast.105, ...), custom_call_target="tpu_custom_call" | custom-call | flops 4194304 | bytes 4194304 | tf_op jit(solution)/shard_map/roots/pallas_call | solution.py:344
  3.6 3.1 %collective-permute-start.6 = (f32[2,16,128]{2,1,0:T(8,128)S(1)}, f32[2,16,128]{2,1,0:T(8,128)S(1)}, u32[]{:S(2)}, u32[]{:S(2)}) collective-permute-start(f32[2,16,128]{2,1,0:T(8,128)S(1)} %get-tuple-element.53), channel_id=1, source_target_pairs={{0,8},{16,24},{8,0},{24,16},{1,9},{17,25},{9,1},{25,17},{2,10},{18... | collective-permute-start | bytes 49160 | tf_op jit(solution)/shard_map/ppermute | solution.py:294
  6.7 0.7 collective-permute-start.7
  7.3 10.0 %all-gather = f32[72,16,128]{2,1,0:T(8,128)S(1)} all-gather(f32[9,16,128]{2,1,0:T(8,128)S(1)} %get-tuple-element.52.refs_7_), channel_id=2, replica_groups=mesh['group'=4,'row'=8] {'row'}, dimensions={0}, use_global_device_ids=true | all-gather | bytes 663552 | tf_op jit(solution)/shard_map/all_gather | solution.py:372
  17.4 4.2 %apply.2 = (f32[8,16,128]{2,1,0:T(8,128)S(1)}, f32[16,16]{1,0:T(8,128)S(1)}, f32[8,16,128]{2,1,0:T(8,128)S(1)}, f32[16,16,128]{2,1,0:T(8,128)}, f32[2,16,128]{2,...) custom-call(s32[2]{0:T(128)S(1)} %pad_add_fusion.place_ref.refs_0_, s32[8]{0:T(128)S(1)} %copy-done.2, ...), custom_call_target="tpu_custom_call" | custom-call | flops 134217728 | bytes 4194304 | tf_op jit(solution)/shard_map/apply/pallas_call | solution.py:389
  21.6 3.4 %all-to-all-start = ((f32[16,16,128]{2,1,0:T(8,128)}), f32[16,16,128]{2,1,0:T(8,128)S(1)}, u32[]{:S(2)}, u32[]{:S(2)}) async-start(f32[16,16,128]{2,1,0:T(8,128)} %get-tuple-element.56), calls=%async_computation | async-start | bytes 262144 | tf_op jit(solution)/shard_map/all_to_all | solution.py:374
  25.0 4.5 %collective-permute-start.8 = (f32[2,16,128]{2,1,0:T(8,128)S(1)}, f32[2,16,128]{2,1,0:T(8,128)S(1)}, u32[]{:S(2)}, u32[]{:S(2)}) collective-permute-start(f32[2,16,128]{2,1,0:T(8,128)S(1)} %get-tuple-element.57), channel_id=1, source_target_pairs={{0,8},{16,24},{8,0},{24,16},{1,9},{17,25},{9,1},{25,17},{2,10},{18... | collective-permute-start | bytes 49160 | tf_op jit(solution)/shard_map/ppermute | solution.py:294
  29.4 0.7 collective-permute-start.9
  30.1 1.1 collective-permute-done.8.refs_8_
  31.1 4.2 %apply.3 = (f32[8,16,128]{2,1,0:T(8,128)S(1)}, f32[16,16]{1,0:T(8,128)S(1)}, f32[8,16,128]{2,1,0:T(8,128)S(1)}, f32[16,16,128]{2,1,0:T(8,128)}, f32[2,16,128]{2,1,0:T(8,128)S(1)}, /*index=5*/f32[2,16,128]{2,1,0:T(8,128)S(1)}) custom-call(s32[2]{0:T(128)S(1)} %pad_add_fusion.place_ref.refs_0_, s32[8]{0:T(128)S(1)} %copy-done.2, s32[8,16]{1,0:T(8,128)S(1)} %copy-done.1, ...), custom_call_target="tpu_custom_call" | custom-call | flops 134217728 | bytes 4194304 | tf_op jit(solution)/shard_map/apply/pallas_call | solution.py:389
  35.3 4.2 %all-to-all-start.1 = ((f32[16,16,128]{2,1,0:T(8,128)}), f32[16,16,128]{2,1,0:T(8,128)S(1)}, u32[]{:S(2)}, u32[]{:S(2)}) async-start(f32[16,16,128]{2,1,0:T(8,128)} %get-tuple-element.61), calls=%async_computation.1 | async-start | bytes 262144 | tf_op jit(solution)/shard_map/all_to_all | solution.py:374
  39.5 3.9 %collective-permute-start.10 = (f32[2,16,128]{2,1,0:T(8,128)S(1)}, f32[2,16,128]{2,1,0:T(8,128)S(1)}, u32[]{:S(2)}, u32[]{:S(2)}) collective-permute-start(f32[2,16,128]{2,1,0:T(8,128)S(1)} %get-tuple-element.62), channel_id=1, source_target_pairs={{0,8},{16,24},{8,0},{24,16},{1,9},{17,25},{9,1},{25,17},{2,10},{18... | collective-permute-start | bytes 49160 | tf_op jit(solution)/shard_map/ppermute | solution.py:294
  43.4 0.7 collective-permute-start.11
  44.1 1.1 collective-permute-done.10.refs_8_
  45.1 4.6 %apply_last.1 = (f32[8,16,128]{2,1,0:T(8,128)S(1)}, f32[32,8,128]{2,1,0:T(8,128)}) custom-call(s32[2]{0:T(128)S(1)} %pad_add_fusion.place_ref.refs_0_, s32[8]{0:T(128)S(1)} %copy-done.2, s32[8,16]{1,0:T(8,128)S(1)} %copy-done.1, bf16[8,16,128,128]{3,2,1,0:T(8,128)(2,1)} %refs_3_.3, bf16[5,16,128,128]{3,2,1,0:T(8,128)(2,1)S(1)} %get-tuple-element.50.refs_5_.refs_4_, ...), custom_call_target="tpu_custom_call" | custom-call | flops 134217728 | bytes 4194304 | tf_op jit(solution)/shard_map/apply_last/pallas_call | solution.py:389
  49.7 6.6 %all-to-all-start.2 = ((f32[32,8,128]{2,1,0:T(8,128)}), f32[32,8,128]{2,1,0:T(8,128)S(1)}, u32[]{:S(2)}, u32[]{:S(2)}) async-start(f32[32,8,128]{2,1,0:T(8,128)} %get-tuple-element.66), calls=%async_computation.2 | async-start | bytes 262144 | tf_op jit(solution)/shard_map/all_to_all | solution.py:409
  56.4 8.2 %all-to-all-done.2.grams_ref = f32[32,8,128]{2,1,0:T(8,128)S(1)} async-done(((f32[32,8,128]{2,1,0:T(8,128)}), f32[32,8,128]{2,1,0:T(8,128)S(1)}, u32[]{:S(2)}, u32[]{:S(2)}) %all-to-all-start.2) | async-done | bytes 131104 | tf_op jit(solution)/shard_map/all_to_all | solution.py:409
  64.6 2.9 %finish.1 = (f32[3,8,16,128]{3,2,1,0:T(8,128)}, s32[1]{0:T(128)}) custom-call(f32[32,8,128]{2,1,0:T(8,128)S(1)} %all-to-all-done.2.grams_ref, f32[8,16,128]{2,1,0:T(8,128)S(1)} %get-tuple-element.67.refs_0_, f32[8,16,128]{2,1,0:T(8,128)S(1)} %get-tuple-element.68.refs_1_, f32[8,16,128]{2,1,0:T(8,128)S(1)} %get-tuple-element.69.refs_2_), custom_call_target="tpu_custom_call" | custom-call | tf_op jit(solution)/shard_map/finish/pallas_call | solution.py:410
  68.1 208.7 %conditional.1 = (f32[3,8,16,128]{3,2,1,0:T(8,128)}) conditional(s32[]{:T(128)} %bitcast.39, (bf16[8,16,128,128]{3,2,1,0:T(8,128)(2,1)}, s32[8]{0:T(128)S(1)}, f32[8,16,128]{2,1,0:T(8,128)S(1)}, s32[1,1,8,2]{2,3,1,0:T(2,128)S(1)}, s32[8,16]{1,0:T(8,128)S(1)}) %tuple.33, f32[3,8,16,128]{3,2,1,0:T(8,128)} %get-tuple-element.71), branch_computations={%region_0.11_spmd, %region_7.12_spmd} | conditional | flops 1235852416 | bytes 33198924 | solution.py:422
  68.1 4.4 %multiply_reduce_fusion = f32[8,16,128]{2,1,0:T(8,128)S(1)} fusion(bf16[8,16,128,128]{3,2,1,0:T(8,128)(2,1)} %get-tuple-element.22), kind=kLoop, calls=%fused_computation.6 | loop fusion | flops 6275072 | bytes 4259840 | tf_op jit(solution)/shard_map/cond/branch_0_fun/btij,bt->bi/reduce_sum | solution.py:305
  72.8 2.6 collective-permute-start
  75.4 1.3 collective-permute-start.1
  76.7 9.0 %all_gather.10 = f32[64,16,128]{2,1,0:T(8,128)S(1)} all-gather(f32[8,16,128]{2,1,0:T(8,128)S(1)} %broadcast_multiply_fusion), channel_id=1, replica_groups=mesh['group'=4,'row'=8] {'row'}, dimensions={0}, use_global_device_ids=true | all-gather | bytes 589824 | tf_op jit(solution)/shard_map/cond/branch_0_fun/all_gather | solution.py:313
  86.0 0.6 gather_fusion
  86.7 0.8 gather_fusion.1
  87.5 5.2 %fusion.2 = f32[8,16,128]{2,1,0:T(8,128)S(1)} fusion(bf16[8,16,128,128]{3,2,1,0:T(8,128)(2,1)} %get-tuple-element.22, f32[8,16,16,128]{3,2,1,0:T(8,128)S(1)} %bitcast.100, f32[8,16]{1,0:T(8,128)S(1)} %get-tuple-element.94, pred[8,16]{1,0:T(8,128)(4,1)S(1)} %compare_and_fusion, f32[8,128]{1,0:T(8,128)S(1)} %add_power_fusion), kind=kOutput, calls=%fused_computation.13 | convolution fusion | flops 403193856 | bytes 5313152 | tf_op jit(solution)/shard_map/cond/branch_0_fun/btij,btkj->bki/dot_general | solution.py:316
  92.7 0.2 convolution_bitcast_fusion.9
  92.9 40.4 %psum.18 = f32[16,16]{0,1:T(8,128)S(1)} all-reduce(f32[16,16]{0,1:T(8,128)S(1)} %convolution_bitcast_fusion.9), channel_id=1, replica_groups=mesh['group'=4,'row'=8] {'group','row'}, use_global_device_ids=true, to_apply=%region_2.0 | all-reduce | flops 256 | bytes 2048 | tf_op jit(solution)/shard_map/cond/branch_0_fun/psum | solution.py:321
  133.4 1.5 cholesky.59
  134.9 0.7 compare_reduce_fusion.2
  135.6 0.7 fusion.17
  136.3 1.2 custom-call.7
  137.5 0.2 convolution_bitcast_fusion.8
  137.7 0.2 bitcast_multiply_fusion.1
  137.9 10.8 %all_gather.11 = f32[64,16,128]{2,1,0:T(8,128)S(1)} all-gather(f32[8,16,128]{2,1,0:T(8,128)S(1)} %get-tuple-element.96), channel_id=1, replica_groups=mesh['group'=4,'row'=8] {'row'}, dimensions={0}, use_global_device_ids=true | all-gather | bytes 589824 | tf_op jit(solution)/shard_map/cond/branch_0_fun/all_gather | solution.py:313
  148.8 0.6 gather_fusion.2
  149.3 2.3 collective-permute-start.2
  151.7 1.3 collective-permute-start.3
  153.1 4.2 %collective-permute-done.3 = f32[2,16,128]{2,1,0:T(8,128)S(1)} collective-permute-done((f32[2,16,128]{2,1,0:T(8,128)S(1)}, f32[2,16,128]{2,1,0:T(8,128)S(1)}, u32[]{:S(2)}, u32[]{:S(2)}) %collective-permute-start.3) | collective-permute-done | bytes 16416 | tf_op jit(solution)/shard_map/cond/branch_0_fun/ppermute | solution.py:286
  157.3 0.8 gather_fusion.3
  158.1 5.2 %fusion.1 = f32[8,16,128]{2,1,0:T(8,128)S(1)} fusion(bf16[8,16,128,128]{3,2,1,0:T(8,128)(2,1)} %get-tuple-element.22, f32[8,16,16,128]{3,2,1,0:T(8,128)S(1)} %bitcast.101, f32[8,16]{1,0:T(8,128)S(1)} %get-tuple-element.94, pred[8,16]{1,0:T(8,128)(4,1)S(1)} %compare_and_fusion, f32[8,128]{1,0:T(8,128)S(1)} %add_power_fusion), kind=kOutput, calls=%fused_computation.11 | convolution fusion | flops 403193856 | bytes 5313152 | tf_op jit(solution)/shard_map/cond/branch_0_fun/btij,btkj->bki/dot_general | solution.py:316
  163.3 0.2 convolution_bitcast_fusion.7
  163.5 39.2 %psum.19 = f32[16,16]{0,1:T(8,128)S(1)} all-reduce(f32[16,16]{0,1:T(8,128)S(1)} %convolution_bitcast_fusion.7), channel_id=1, replica_groups=mesh['group'=4,'row'=8] {'group','row'}, use_global_device_ids=true, to_apply=%region_5.9 | all-reduce | flops 256 | bytes 2048 | tf_op jit(solution)/shard_map/cond/branch_0_fun/psum | solution.py:321
  202.7 1.5 cholesky.70
  204.2 0.7 compare_reduce_fusion.1
  204.9 0.7 fusion.18
  205.6 1.2 custom-call.8
  206.8 0.2 convolution_bitcast_fusion.6
  207.0 0.2 bitcast_multiply_fusion
  207.3 10.6 %all_gather.12 = f32[64,16,128]{2,1,0:T(8,128)S(1)} all-gather(f32[8,16,128]{2,1,0:T(8,128)S(1)} %get-tuple-element.98), channel_id=1, replica_groups=mesh['group'=4,'row'=8] {'row'}, dimensions={0}, use_global_device_ids=true | all-gather | bytes 589824 | tf_op jit(solution)/shard_map/cond/branch_0_fun/all_gather | solution.py:313
  217.9 0.6 gather_fusion.4
  218.5 2.6 collective-permute-start.4
  221.0 1.3 collective-permute-start.5
  222.5 4.2 %collective-permute-done.5 = f32[2,16,128]{2,1,0:T(8,128)S(1)} collective-permute-done((f32[2,16,128]{2,1,0:T(8,128)S(1)}, f32[2,16,128]{2,1,0:T(8,128)S(1)}, u32[]{:S(2)}, u32[]{:S(2)}) %collective-permute-start.5) | collective-permute-done | bytes 16416 | tf_op jit(solution)/shard_map/cond/branch_0_fun/ppermute | solution.py:286
  226.7 0.8 gather_fusion.5
  227.5 5.2 %fusion = f32[8,16,128]{2,1,0:T(8,128)S(1)} fusion(bf16[8,16,128,128]{3,2,1,0:T(8,128)(2,1)} %get-tuple-element.22, f32[8,16,16,128]{3,2,1,0:T(8,128)S(1)} %bitcast.99, f32[8,16]{1,0:T(8,128)S(1)} %get-tuple-element.94, pred[8,16]{1,0:T(8,128)(4,1)S(1)} %compare_and_fusion, f32[8,128]{1,0:T(8,128)S(1)} %add_power_fusion), kind=kOutput, calls=%fused_computation.9 | convolution fusion | flops 403193856 | bytes 5313152 | tf_op jit(solution)/shard_map/cond/branch_0_fun/btij,btkj->bki/dot_general | solution.py:316
  232.8 38.7 %psum.20 = f32[16,16]{0,1:T(8,128)S(1)} all-reduce(f32[16,16]{0,1:T(8,128)S(1)} %convolution_bitcast_fusion.5), channel_id=1, replica_groups=mesh['group'=4,'row'=8] {'group','row'}, use_global_device_ids=true, to_apply=%region_6.10 | all-reduce | flops 256 | bytes 2048 | tf_op jit(solution)/shard_map/cond/branch_0_fun/psum | solution.py:321
  271.6 1.5 cholesky.81
  273.1 0.7 compare_reduce_fusion
  273.8 0.7 fusion.19
  274.5 1.2 custom-call.9
  275.7 0.2 convolution_bitcast_fusion.4
  275.9 0.2 convolution_bitcast_fusion
  276.1 0.7 pad_maximum_fusion.3
  (55 shorter events, 1.6 us)
Async XLA Ops:
  0.0 17.4 %copy-start.3 = (s32[1,1,8,2]{2,3,1,0:T(2,128)S(1)}, s32[1,1,8,2]{2,3,1,0:T(2,128)}, u32[]{:S(2)}) copy-start(s32[1,1,8,2]{2,3,1,0:T(2,128)} %param.18) | copy-start | bytes 196
  0.0 17.4 %copy-start.2 = (s32[8]{0:T(128)S(1)}, s32[8]{0:T(128)}, u32[]{:S(2)}) copy-start(s32[8]{0:T(128)} %refs_1_.5) | copy-start | bytes 100
  0.0 17.4 %copy-start.1 = (s32[8,16]{1,0:T(8,128)S(1)}, s32[8,16]{1,0:T(8,128)}, u32[]{:S(2)}) copy-start(s32[8,16]{1,0:T(8,128)} %refs_2_.5) | copy-start | bytes 1540
  3.6 13.8 %collective-permute-start.6 = (f32[2,16,128]{2,1,0:T(8,128)S(1)}, f32[2,16,128]{2,1,0:T(8,128)S(1)}, u32[]{:S(2)}, u32[]{:S(2)}) collective-permute-start(f32[2,16,128]{2,1,0:T(8,128)S(1)} %get-tuple-element.53), channel_id=1, source_target_pairs={{0,8},{16,24},{8,0},{24,16},{1,9},{17,25},{9,1},{25,17},{2,10},{18... | collective-permute-start | bytes 49160 | tf_op jit(solution)/shard_map/ppermute | solution.py:294
  6.7 10.7 %collective-permute-start.7 = (f32[2,16,128]{2,1,0:T(8,128)S(1)}, f32[2,16,128]{2,1,0:T(8,128)S(1)}, u32[]{:S(2)}, u32[]{:S(2)}) collective-permute-start(f32[2,16,128]{2,1,0:T(8,128)S(1)} %get-tuple-element.54), channel_id=1, source_target_pairs={{8,16},{16,8},{9,17},{17,9},{10,18},{18,10},{11,19},{19,11},{12,20... | collective-permute-start | bytes 49160 | tf_op jit(solution)/shard_map/ppermute | solution.py:294
  21.6 9.6 %all-to-all-start = ((f32[16,16,128]{2,1,0:T(8,128)}), f32[16,16,128]{2,1,0:T(8,128)S(1)}, u32[]{:S(2)}, u32[]{:S(2)}) async-start(f32[16,16,128]{2,1,0:T(8,128)} %get-tuple-element.56), calls=%async_computation | async-start | bytes 262144 | tf_op jit(solution)/shard_map/all_to_all | solution.py:374
  25.0 6.2 %collective-permute-start.8 = (f32[2,16,128]{2,1,0:T(8,128)S(1)}, f32[2,16,128]{2,1,0:T(8,128)S(1)}, u32[]{:S(2)}, u32[]{:S(2)}) collective-permute-start(f32[2,16,128]{2,1,0:T(8,128)S(1)} %get-tuple-element.57), channel_id=1, source_target_pairs={{0,8},{16,24},{8,0},{24,16},{1,9},{17,25},{9,1},{25,17},{2,10},{18... | collective-permute-start | bytes 49160 | tf_op jit(solution)/shard_map/ppermute | solution.py:294
  29.4 1.7 collective-permute-start.9
  35.3 32.8 %copy-start = (f32[8,16,128]{2,1,0:T(8,128)S(1)}, f32[8,16,128]{2,1,0:T(8,128)}, u32[]{:S(2)}) copy-start(f32[8,16,128]{2,1,0:T(8,128)} %basis_hbm.1) | copy-start | bytes 196612
  35.3 9.8 %all-to-all-start.1 = ((f32[16,16,128]{2,1,0:T(8,128)}), f32[16,16,128]{2,1,0:T(8,128)S(1)}, u32[]{:S(2)}, u32[]{:S(2)}) async-start(f32[16,16,128]{2,1,0:T(8,128)} %get-tuple-element.61), calls=%async_computation.1 | async-start | bytes 262144 | tf_op jit(solution)/shard_map/all_to_all | solution.py:374
  39.5 5.6 %collective-permute-start.10 = (f32[2,16,128]{2,1,0:T(8,128)S(1)}, f32[2,16,128]{2,1,0:T(8,128)S(1)}, u32[]{:S(2)}, u32[]{:S(2)}) collective-permute-start(f32[2,16,128]{2,1,0:T(8,128)S(1)} %get-tuple-element.62), channel_id=1, source_target_pairs={{0,8},{16,24},{8,0},{24,16},{1,9},{17,25},{9,1},{25,17},{2,10},{18... | collective-permute-start | bytes 49160 | tf_op jit(solution)/shard_map/ppermute | solution.py:294
  43.4 1.7 collective-permute-start.11
  49.7 14.9 %all-to-all-start.2 = ((f32[32,8,128]{2,1,0:T(8,128)}), f32[32,8,128]{2,1,0:T(8,128)S(1)}, u32[]{:S(2)}, u32[]{:S(2)}) async-start(f32[32,8,128]{2,1,0:T(8,128)} %get-tuple-element.66), calls=%async_computation.2 | async-start | bytes 262144 | tf_op jit(solution)/shard_map/all_to_all | solution.py:409
  72.8 13.9 %collective-permute-start = (f32[2,16,128]{2,1,0:T(8,128)S(1)}, f32[2,16,128]{2,1,0:T(8,128)S(1)}, u32[]{:S(2)}, u32[]{:S(2)}) collective-permute-start(f32[2,16,128]{2,1,0:T(8,128)S(1)} %get-tuple-element.92), channel_id=1, source_target_pairs={{0,8},{8,16},{16,24},{1,9},{9,17},{17,25},{2,10},{10,18},{18,26},{... | collective-permute-start | bytes 49160 | tf_op jit(solution)/shard_map/cond/branch_0_fun/ppermute | solution.py:285
  75.4 11.3 %collective-permute-start.1 = (f32[2,16,128]{2,1,0:T(8,128)S(1)}, f32[2,16,128]{2,1,0:T(8,128)S(1)}, u32[]{:S(2)}, u32[]{:S(2)}) collective-permute-start(f32[2,16,128]{2,1,0:T(8,128)S(1)} %get-tuple-element.93), channel_id=1, source_target_pairs={{8,0},{16,8},{24,16},{9,1},{17,9},{25,17},{10,2},{18,10},{26,18},{... | collective-permute-start | bytes 49160 | tf_op jit(solution)/shard_map/cond/branch_0_fun/ppermute | solution.py:286
  149.3 3.8 %collective-permute-start.2 = (f32[2,16,128]{2,1,0:T(8,128)S(1)}, f32[2,16,128]{2,1,0:T(8,128)S(1)}, u32[]{:S(2)}, u32[]{:S(2)}) collective-permute-start(f32[2,16,128]{2,1,0:T(8,128)S(1)} %get-tuple-element.90), channel_id=1, source_target_pairs={{0,8},{8,16},{16,24},{1,9},{9,17},{17,25},{2,10},{10,18},{18,26},{... | collective-permute-start | bytes 49160 | tf_op jit(solution)/shard_map/cond/branch_0_fun/ppermute | solution.py:285
  151.7 5.6 %collective-permute-start.3 = (f32[2,16,128]{2,1,0:T(8,128)S(1)}, f32[2,16,128]{2,1,0:T(8,128)S(1)}, u32[]{:S(2)}, u32[]{:S(2)}) collective-permute-start(f32[2,16,128]{2,1,0:T(8,128)S(1)} %get-tuple-element.91), channel_id=1, source_target_pairs={{8,0},{16,8},{24,16},{9,1},{17,9},{25,17},{10,2},{18,10},{26,18},{... | collective-permute-start | bytes 49160 | tf_op jit(solution)/shard_map/cond/branch_0_fun/ppermute | solution.py:286
  218.5 4.0 %collective-permute-start.4 = (f32[2,16,128]{2,1,0:T(8,128)S(1)}, f32[2,16,128]{2,1,0:T(8,128)S(1)}, u32[]{:S(2)}, u32[]{:S(2)}) collective-permute-start(f32[2,16,128]{2,1,0:T(8,128)S(1)} %get-tuple-element.88), channel_id=1, source_target_pairs={{0,8},{8,16},{16,24},{1,9},{9,17},{17,25},{2,10},{10,18},{18,26},{... | collective-permute-start | bytes 49160 | tf_op jit(solution)/shard_map/cond/branch_0_fun/ppermute | solution.py:285
  221.0 5.6 %collective-permute-start.5 = (f32[2,16,128]{2,1,0:T(8,128)S(1)}, f32[2,16,128]{2,1,0:T(8,128)S(1)}, u32[]{:S(2)}, u32[]{:S(2)}) collective-permute-start(f32[2,16,128]{2,1,0:T(8,128)S(1)} %get-tuple-element.89), channel_id=1, source_target_pairs={{8,0},{16,8},{24,16},{9,1},{17,9},{25,17},{10,2},{18,10},{26,18},{... | collective-permute-start | bytes 49160 | tf_op jit(solution)/shard_map/cond/branch_0_fun/ppermute | solution.py:286

commit v7 on v5

--- a/solution.py
+++ b/solution.py
@@ -54,40 +54,55 @@
     return min(tiles.shape[0] - 1, HELD_BYTES // (tiles.size // tiles.shape[0] * 2))
 
 
-def load(tiles_hbm, start, tiles_ref, sem):
-    copy = pltpu.make_async_copy(tiles_hbm.at[pl.ds(start, tiles_ref.shape[0])], tiles_ref, sem)
-    copy.start()
-    return copy
+def load(tiles_hbm, start, tiles_ref, sems):
+    count, per_row = tiles_ref.shape[:2]
+    half = per_row // 2
+    copies = []
+    for b in range(count):
+        for n, part in enumerate((pl.ds(0, half), pl.ds(half, per_row - half))):
+            copies.append(
+                pltpu.make_async_copy(
+                    tiles_hbm.at[start + b, part], tiles_ref.at[b, part], sems.at[start + b, n]
+                )
+            )
+    for copy in copies:
+        copy.start()
+    return copies
+
+
+def wait_all(copies):
+    for copy in copies:
+        copy.wait()
 
 
 def roots_kernel(place_ref, count_hbm, want_hbm, tiles_hbm, basis_hbm, root_ref, sent_ref,
-                 first_ref, second_ref, held_ref, rest_ref, count_ref, want_ref, basis_ref, sems):
+                 first_ref, second_ref, held_ref, rest_ref, count_ref, want_ref, basis_ref,
+                 load_sems, sems):
     held, per_row, side, _ = held_ref.shape
     blocks = held + rest_ref.shape[0]
     peers = want_ref.shape[1]
     vectors = basis_ref.shape[1]
-    rest_load = load(tiles_hbm, held, rest_ref, sems.at[0])
+    rest_load = load(tiles_hbm, held, rest_ref, load_sems)
     small = [
-        pltpu.make_async_copy(source, target, sems.at[2 + n])
+        pltpu.make_async_copy(source, target, sems.at[n])
         for n, (source, target) in enumerate(
             ((count_hbm, count_ref), (want_hbm, want_ref), (basis_hbm, basis_ref))
         )
     ]
     for copy in small:
         copy.start()
-    held_load = load(tiles_hbm, 0, held_ref, sems.at[1])
-    for copy in small:
-        copy.wait()
+    held_load = load(tiles_hbm, 0, held_ref, load_sems)
+    wait_all(small)
     for p in range(peers):
         owned = (place_ref[0] * peers + p) * blocks
         for c in range(SLOTS):
             at = jnp.full((1, side), want_ref[c, p] - owned, jnp.int32).astype(jnp.float32)
             block, row = divmod(p * SLOTS + c, vectors)
             sent_ref[blocks + block, row : row + 1] = at
-    rest_load.wait()
+    wait_all(rest_load)
     for b in list(range(held, blocks)) + list(range(held)):
         if b == 0:
-            held_load.wait()
+            wait_all(held_load)
         tile_ref = held_ref.at[b] if b < held else rest_ref.at[b - held]
         total = jnp.zeros((side, side), jnp.float32)
         for s in range(per_row):
@@ -166,11 +181,16 @@
     place_ref, count_ref, cols_ref, *refs = refs
     if opening:
         want_ref, *refs = refs
-    tiles_hbm, held_ref, root_ref, own_ref, recv_ref, swapped_ref, swapped_next_ref, *refs = refs
-    *refs, table, rest_ref, load_sem = refs
+    tiles_at, held_ref, root_ref, own_ref, recv_ref, swapped_ref, swapped_next_ref, *refs = refs
+    if opening:
+        *refs, table = refs
+        rest_ref = tiles_at
+    else:
+        *refs, table, rest_ref, load_sems = refs
     held, per_row, side, _ = held_ref.shape
     blocks = held + rest_ref.shape[0]
-    rest_load = load(tiles_hbm, held, rest_ref, load_sem)
+    if not opening:
+        rest_load = load(tiles_at, held, rest_ref, load_sems)
     if last:
         *before, applied_ref, gram_hbm, packed_ref, sem = refs
     else:
@@ -214,8 +234,8 @@
             at = jnp.where(s < count_ref[b], cols_ref[b, s], slot)
             picked.append(table[at])
         x = jnp.concatenate(picked, axis=1)
-        if b == held:
-            rest_load.wait()
+        if b == held and not opening:
+            wait_all(rest_load)
         tile_ref = held_ref.at[b] if b < held else rest_ref.at[b - held]
         t = jnp.concatenate([tile_ref[s] for s in range(per_row)], axis=1)
         product = lax.dot_general(x, t, NT, preferred_element_type=jnp.float32)
@@ -349,7 +369,8 @@
     rim_shape = f32(RIM, *block_shape)
     kept = held_blocks(tiles)
     rest = pltpu.VMEM((blocks - kept,) + tiles.shape[1:], tiles.dtype)
-    root, scaled, *rims, held = pl.pallas_call(
+    load_sems = pltpu.SemaphoreType.DMA((blocks, 2))
+    root, scaled, *rims, held, opening_rest = pl.pallas_call(
         roots_kernel,
         out_shape=(
             f32(blocks, 1, side),
@@ -357,15 +378,16 @@
             rim_shape,
             rim_shape,
             pltpu.VMEM((kept,) + tiles.shape[1:], tiles.dtype),
+            rest,
         ),
         in_specs=[smem()] + [hbm()] * 4,
-        out_specs=(vmem(),) * 5,
+        out_specs=(vmem(),) * 6,
         scratch_shapes=[
-            rest,
             pltpu.SMEM((blocks,), jnp.int32),
             pltpu.SMEM((SLOTS, peers), jnp.int32),
             pltpu.VMEM((blocks,) + block_shape, jnp.float32),
-            pltpu.SemaphoreType.DMA((5,)),
+            load_sems,
+            pltpu.SemaphoreType.DMA((3,)),
         ],
         compiler_params=params(),
         cost_estimate=cost(tiles.size * 2, tile_bytes),
@@ -382,7 +404,7 @@
             received = lax.all_to_all(outgoing, "row", 0, 0, tiled=True)
             swapped = swap(*rims)
         scalars = [place, tile_count, tile_cols] + ([wanted] if t == 0 else [])
-        arrays = [far_tiles, held, root, scaled, received, *swapped]
+        arrays = [far_tiles if t else opening_rest, held, root, scaled, received, *swapped]
         shapes = [f32(blocks, *block_shape)]
         specs = [vmem(), vmem()]
         if last:
@@ -406,14 +428,15 @@
         result = pl.pallas_call(
             functools.partial(apply_kernel, t),
             out_shape=tuple(shapes),
-            in_specs=[smem()] * len(scalars) + [hbm()] + [vmem()] * (len(arrays) - 1),
+            in_specs=[smem()] * len(scalars)
+            + [hbm() if t else vmem()]
+            + [vmem()] * (len(arrays) - 1),
             out_specs=tuple(specs),
             scratch_shapes=scratch
             + [
                 pltpu.VMEM((slots + 1, PIECES * vectors, side), jnp.bfloat16),
-                rest,
-                pltpu.SemaphoreType.DMA,
-            ],
+            ]
+            + ([rest, load_sems] if t else []),
             compiler_params=params(),
             cost_estimate=cost(tiles.size * 2 * vectors * PIECES, tile_bytes),
             name="apply_last" if last else "apply",

time: 278 us -> 277 us (level)
  no operation moved by 1% of the time
where the time goes in v7:
time: 277 us; the launch traced here: 276 us
  blocking collectives  159 us (57%)
  starting transfers between devices  39 us (14%)
  waiting for transfers between devices  18.8 us (7%)
  Pallas kernels  18.6 us (7%)
  other arithmetic  18 us (6%)
  matrix products  17.5 us (6%)
  local copies, waits for them, and re-layouts  4.46 us (2%)
    psum x3, blocking collectives, stepwise(): factor = jnp.linalg.cholesky(lax.psum(gram, ('group', 'row')) / row_total)  118 us
    all_gather x3, blocking collectives, stepwise(): lax.all_gather(scaled, 'row', axis=0, tiled=True)  30.3 us
    dot_general x3, matrix products, stepwise(): jnp.einsum('btij,btkj->bki', tiles, picked, precision=HIGH, preferred_ele...  15.5 us
    ppermute x6, starting transfers between devices, swap(): lax.ppermute(x, 'group', pair)  13.4 us
    pallas_call x3, Pallas kernels, local(): pl.pallas_call(functools.partial(apply_kernel, t), out_shape=tuple(shapes...  11.8 us
    all_gather x1, blocking collectives, local(): received = lax.all_gather(scaled, 'row', axis=0)  10 us
    ppermute x3, waiting for transfers between devices, neighbours(): high = lax.ppermute(scaled[:RIM], 'group', down)  8.42 us
    all_to_all x1, waiting for transfers between devices, local(): gathered = lax.all_to_all(grams[-1], ('group', 'row'), 0, 0, tiled=True)  8.23 us
  transfers between devices with their start and end apart: 15, of which 5 were waited for; matrix products, arithmetic and copies ran while one was open for 0% of the time, Pallas kernels for 0%

profile of v7, /device:TPU:0, one launch (start us, length us, event | category | flops | bytes accessed | tf_op | source)
XLA Modules:
  0.0 276.1 jit_solution(12657448757847487761)
XLA Ops:
  0.1 3.9 %roots.1 = (f32[8,1,128]{2,1,0:T(1,128)S(1)}, f32[9,16,128]{2,1,0:T(8,128)S(1)}, f32[2,16,128]{2,1,0:T(8,128)S(1)}, f32[2,16,128]{2,1,0:T(8,128)S(1)}, bf16[5,16...) custom-call(s32[2]{0:T(128)S(1)} %pad_add_fusion.place_ref.refs_0_, s32[8]{0:T(128)} %refs_1_.5, ...), custom_call_target="tpu_custom_call" | custom-call | flops 4194304 | bytes 4194304 | tf_op jit(solution)/shard_map/roots/pallas_call | solution.py:373
  4.0 3.1 %collective-permute-start.6 = (f32[2,16,128]{2,1,0:T(8,128)S(1)}, f32[2,16,128]{2,1,0:T(8,128)S(1)}, u32[]{:S(2)}, u32[]{:S(2)}) collective-permute-start(f32[2,16,128]{2,1,0:T(8,128)S(1)} %get-tuple-element.55), channel_id=1, source_target_pairs={{0,8},{16,24},{8,0},{24,16},{1,9},{17,25},{9,1},{25,17},{2,10},{18... | collective-permute-start | bytes 49160 | tf_op jit(solution)/shard_map/ppermute | solution.py:322
  7.1 0.7 collective-permute-start.7
  7.7 10.0 %all-gather = f32[72,16,128]{2,1,0:T(8,128)S(1)} all-gather(f32[9,16,128]{2,1,0:T(8,128)S(1)} %get-tuple-element.54.refs_7_), channel_id=2, replica_groups=mesh['group'=4,'row'=8] {'row'}, dimensions={0}, use_global_device_ids=true | all-gather | bytes 663552 | tf_op jit(solution)/shard_map/all_gather | solution.py:402
  17.7 2.8 %apply.2 = (f32[8,16,128]{2,1,0:T(8,128)S(1)}, f32[16,16]{1,0:T(8,128)S(1)}, f32[8,16,128]{2,1,0:T(8,128)S(1)}, f32[16,16,128]{2,1,0:T(8,128)}, f32[2,16,128]{2,...) custom-call(s32[2]{0:T(128)S(1)} %pad_add_fusion.place_ref.refs_0_, s32[8]{0:T(128)S(1)} %copy-done.2, ...), custom_call_target="tpu_custom_call" | custom-call | flops 134217728 | bytes 4194304 | tf_op jit(solution)/shard_map/apply/pallas_call | solution.py:428
  20.5 3.4 %all-to-all-start = ((f32[16,16,128]{2,1,0:T(8,128)}), f32[16,16,128]{2,1,0:T(8,128)S(1)}, u32[]{:S(2)}, u32[]{:S(2)}) async-start(f32[16,16,128]{2,1,0:T(8,128)} %get-tuple-element.58), calls=%async_computation | async-start | bytes 262144 | tf_op jit(solution)/shard_map/all_to_all | solution.py:404
  23.9 4.5 %collective-permute-start.8 = (f32[2,16,128]{2,1,0:T(8,128)S(1)}, f32[2,16,128]{2,1,0:T(8,128)S(1)}, u32[]{:S(2)}, u32[]{:S(2)}) collective-permute-start(f32[2,16,128]{2,1,0:T(8,128)S(1)} %get-tuple-element.59), channel_id=1, source_target_pairs={{0,8},{16,24},{8,0},{24,16},{1,9},{17,25},{9,1},{25,17},{2,10},{18... | collective-permute-start | bytes 49160 | tf_op jit(solution)/shard_map/ppermute | solution.py:322
  28.4 0.7 collective-permute-start.9
  29.1 1.1 collective-permute-done.8.refs_8_
  30.1 4.3 %apply.3 = (f32[8,16,128]{2,1,0:T(8,128)S(1)}, f32[16,16]{1,0:T(8,128)S(1)}, f32[8,16,128]{2,1,0:T(8,128)S(1)}, f32[16,16,128]{2,1,0:T(8,128)}, f32[2,16,128]{2,1,0:T(8,128)S(1)}, /*index=5*/f32[2,16,128]{2,1,0:T(8,128)S(1)}) custom-call(s32[2]{0:T(128)S(1)} %pad_add_fusion.place_ref.refs_0_, s32[8]{0:T(128)S(1)} %copy-done.2, s32[8,16]{1,0:T(8,128)S(1)} %copy-done.1, ...), custom_call_target="tpu_custom_call" | custom-call | flops 134217728 | bytes 4194304 | tf_op jit(solution)/shard_map/apply/pallas_call | solution.py:428
  34.5 4.2 %all-to-all-start.1 = ((f32[16,16,128]{2,1,0:T(8,128)}), f32[16,16,128]{2,1,0:T(8,128)S(1)}, u32[]{:S(2)}, u32[]{:S(2)}) async-start(f32[16,16,128]{2,1,0:T(8,128)} %get-tuple-element.63), calls=%async_computation.1 | async-start | bytes 262144 | tf_op jit(solution)/shard_map/all_to_all | solution.py:404
  38.7 3.9 %collective-permute-start.10 = (f32[2,16,128]{2,1,0:T(8,128)S(1)}, f32[2,16,128]{2,1,0:T(8,128)S(1)}, u32[]{:S(2)}, u32[]{:S(2)}) collective-permute-start(f32[2,16,128]{2,1,0:T(8,128)S(1)} %get-tuple-element.64), channel_id=1, source_target_pairs={{0,8},{16,24},{8,0},{24,16},{1,9},{17,25},{9,1},{25,17},{2,10},{18... | collective-permute-start | bytes 49160 | tf_op jit(solution)/shard_map/ppermute | solution.py:322
  42.6 0.7 collective-permute-start.11
  43.2 1.1 collective-permute-done.10.refs_8_
  44.3 4.7 %apply_last.1 = (f32[8,16,128]{2,1,0:T(8,128)S(1)}, f32[32,8,128]{2,1,0:T(8,128)}) custom-call(s32[2]{0:T(128)S(1)} %pad_add_fusion.place_ref.refs_0_, s32[8]{0:T(128)S(1)} %copy-done.2, s32[8,16]{1,0:T(8,128)S(1)} %copy-done.1, bf16[8,16,128,128]{3,2,1,0:T(8,128)(2,1)} %refs_3_.3, bf16[5,16,128,128]{3,2,1,0:T(8,128)(2,1)S(1)} %get-tuple-element.51.refs_5_.refs_4_, ...), custom_call_target="tpu_custom_call" | custom-call | flops 134217728 | bytes 4194304 | tf_op jit(solution)/shard_map/apply_last/pallas_call | solution.py:428
  49.0 6.6 %all-to-all-start.2 = ((f32[32,8,128]{2,1,0:T(8,128)}), f32[32,8,128]{2,1,0:T(8,128)S(1)}, u32[]{:S(2)}, u32[]{:S(2)}) async-start(f32[32,8,128]{2,1,0:T(8,128)} %get-tuple-element.68), calls=%async_computation.2 | async-start | bytes 262144 | tf_op jit(solution)/shard_map/all_to_all | solution.py:450
  55.6 8.2 %all-to-all-done.2.grams_ref = f32[32,8,128]{2,1,0:T(8,128)S(1)} async-done(((f32[32,8,128]{2,1,0:T(8,128)}), f32[32,8,128]{2,1,0:T(8,128)S(1)}, u32[]{:S(2)}, u32[]{:S(2)}) %all-to-all-start.2) | async-done | bytes 131104 | tf_op jit(solution)/shard_map/all_to_all | solution.py:450
  63.8 2.9 %finish.1 = (f32[3,8,16,128]{3,2,1,0:T(8,128)}, s32[1]{0:T(128)}) custom-call(f32[32,8,128]{2,1,0:T(8,128)S(1)} %all-to-all-done.2.grams_ref, f32[8,16,128]{2,1,0:T(8,128)S(1)} %get-tuple-element.69.refs_0_, f32[8,16,128]{2,1,0:T(8,128)S(1)} %get-tuple-element.70.refs_1_, f32[8,16,128]{2,1,0:T(8,128)S(1)} %get-tuple-element.71.refs_2_), custom_call_target="tpu_custom_call" | custom-call | tf_op jit(solution)/shard_map/finish/pallas_call | solution.py:451
  67.4 208.7 %conditional.1 = (f32[3,8,16,128]{3,2,1,0:T(8,128)}) conditional(s32[]{:T(128)} %bitcast.39, (bf16[8,16,128,128]{3,2,1,0:T(8,128)(2,1)}, s32[8]{0:T(128)S(1)}, f32[8,16,128]{2,1,0:T(8,128)S(1)}, s32[1,1,8,2]{2,3,1,0:T(2,128)S(1)}, s32[8,16]{1,0:T(8,128)S(1)}) %tuple.33, f32[3,8,16,128]{3,2,1,0:T(8,128)} %get-tuple-element.73), branch_computations={%region_0.11_spmd, %region_7.12_spmd} | conditional | flops 1235852416 | bytes 33198924 | solution.py:463
  67.4 4.4 %multiply_reduce_fusion = f32[8,16,128]{2,1,0:T(8,128)S(1)} fusion(bf16[8,16,128,128]{3,2,1,0:T(8,128)(2,1)} %get-tuple-element.22), kind=kLoop, calls=%fused_computation.6 | loop fusion | flops 6275072 | bytes 4259840 | tf_op jit(solution)/shard_map/cond/branch_0_fun/btij,bt->bi/reduce_sum | solution.py:333
  72.1 2.6 collective-permute-start
  74.7 1.3 collective-permute-start.1
  76.0 9.0 %all_gather.10 = f32[64,16,128]{2,1,0:T(8,128)S(1)} all-gather(f32[8,16,128]{2,1,0:T(8,128)S(1)} %broadcast_multiply_fusion), channel_id=1, replica_groups=mesh['group'=4,'row'=8] {'row'}, dimensions={0}, use_global_device_ids=true | all-gather | bytes 589824 | tf_op jit(solution)/shard_map/cond/branch_0_fun/all_gather | solution.py:341
  85.3 0.6 gather_fusion
  86.0 0.8 gather_fusion.1
  86.8 5.2 %fusion.2 = f32[8,16,128]{2,1,0:T(8,128)S(1)} fusion(bf16[8,16,128,128]{3,2,1,0:T(8,128)(2,1)} %get-tuple-element.22, f32[8,16,16,128]{3,2,1,0:T(8,128)S(1)} %bitcast.100, f32[8,16]{1,0:T(8,128)S(1)} %get-tuple-element.96, pred[8,16]{1,0:T(8,128)(4,1)S(1)} %compare_and_fusion, f32[8,128]{1,0:T(8,128)S(1)} %add_power_fusion), kind=kOutput, calls=%fused_computation.13 | convolution fusion | flops 403193856 | bytes 5313152 | tf_op jit(solution)/shard_map/cond/branch_0_fun/btij,btkj->bki/dot_general | solution.py:344
  91.9 0.2 convolution_bitcast_fusion.9
  92.1 40.6 %psum.18 = f32[16,16]{0,1:T(8,128)S(1)} all-reduce(f32[16,16]{0,1:T(8,128)S(1)} %convolution_bitcast_fusion.9), channel_id=1, replica_groups=mesh['group'=4,'row'=8] {'group','row'}, use_global_device_ids=true, to_apply=%region_2.0 | all-reduce | flops 256 | bytes 2048 | tf_op jit(solution)/shard_map/cond/branch_0_fun/psum | solution.py:349
  132.8 1.5 cholesky.59
  134.3 0.7 compare_reduce_fusion.2
  135.0 0.7 fusion.17
  135.7 1.2 custom-call.7
  137.0 0.2 convolution_bitcast_fusion.8
  137.2 0.2 bitcast_multiply_fusion.1
  137.4 10.6 %all_gather.11 = f32[64,16,128]{2,1,0:T(8,128)S(1)} all-gather(f32[8,16,128]{2,1,0:T(8,128)S(1)} %get-tuple-element.98), channel_id=1, replica_groups=mesh['group'=4,'row'=8] {'row'}, dimensions={0}, use_global_device_ids=true | all-gather | bytes 589824 | tf_op jit(solution)/shard_map/cond/branch_0_fun/all_gather | solution.py:341
  148.0 0.6 gather_fusion.2
  148.6 2.3 collective-permute-start.2
  150.9 1.3 collective-permute-start.3
  152.4 4.2 %collective-permute-done.3 = f32[2,16,128]{2,1,0:T(8,128)S(1)} collective-permute-done((f32[2,16,128]{2,1,0:T(8,128)S(1)}, f32[2,16,128]{2,1,0:T(8,128)S(1)}, u32[]{:S(2)}, u32[]{:S(2)}) %collective-permute-start.3) | collective-permute-done | bytes 16416 | tf_op jit(solution)/shard_map/cond/branch_0_fun/ppermute | solution.py:314
  156.6 0.8 gather_fusion.3
  157.4 5.2 %fusion.1 = f32[8,16,128]{2,1,0:T(8,128)S(1)} fusion(bf16[8,16,128,128]{3,2,1,0:T(8,128)(2,1)} %get-tuple-element.22, f32[8,16,16,128]{3,2,1,0:T(8,128)S(1)} %bitcast.101, f32[8,16]{1,0:T(8,128)S(1)} %get-tuple-element.96, pred[8,16]{1,0:T(8,128)(4,1)S(1)} %compare_and_fusion, f32[8,128]{1,0:T(8,128)S(1)} %add_power_fusion), kind=kOutput, calls=%fused_computation.11 | convolution fusion | flops 403193856 | bytes 5313152 | tf_op jit(solution)/shard_map/cond/branch_0_fun/btij,btkj->bki/dot_general | solution.py:344
  162.5 0.2 convolution_bitcast_fusion.7
  162.7 39.2 %psum.19 = f32[16,16]{0,1:T(8,128)S(1)} all-reduce(f32[16,16]{0,1:T(8,128)S(1)} %convolution_bitcast_fusion.7), channel_id=1, replica_groups=mesh['group'=4,'row'=8] {'group','row'}, use_global_device_ids=true, to_apply=%region_5.9 | all-reduce | flops 256 | bytes 2048 | tf_op jit(solution)/shard_map/cond/branch_0_fun/psum | solution.py:349
  202.0 1.5 cholesky.70
  203.5 0.7 compare_reduce_fusion.1
  204.2 0.7 fusion.18
  204.9 1.2 custom-call.8
  206.1 0.2 convolution_bitcast_fusion.6
  206.3 0.2 bitcast_multiply_fusion
  206.5 10.6 %all_gather.12 = f32[64,16,128]{2,1,0:T(8,128)S(1)} all-gather(f32[8,16,128]{2,1,0:T(8,128)S(1)} %get-tuple-element.100), channel_id=1, replica_groups=mesh['group'=4,'row'=8] {'row'}, dimensions={0}, use_global_device_ids=true | all-gather | bytes 589824 | tf_op jit(solution)/shard_map/cond/branch_0_fun/all_gather | solution.py:341
  217.2 0.6 gather_fusion.4
  217.8 2.6 collective-permute-start.4
  220.3 1.3 collective-permute-start.5
  221.7 4.2 %collective-permute-done.5 = f32[2,16,128]{2,1,0:T(8,128)S(1)} collective-permute-done((f32[2,16,128]{2,1,0:T(8,128)S(1)}, f32[2,16,128]{2,1,0:T(8,128)S(1)}, u32[]{:S(2)}, u32[]{:S(2)}) %collective-permute-start.5) | collective-permute-done | bytes 16416 | tf_op jit(solution)/shard_map/cond/branch_0_fun/ppermute | solution.py:314
  226.0 0.8 gather_fusion.5
  226.7 5.2 %fusion = f32[8,16,128]{2,1,0:T(8,128)S(1)} fusion(bf16[8,16,128,128]{3,2,1,0:T(8,128)(2,1)} %get-tuple-element.22, f32[8,16,16,128]{3,2,1,0:T(8,128)S(1)} %bitcast.99, f32[8,16]{1,0:T(8,128)S(1)} %get-tuple-element.96, pred[8,16]{1,0:T(8,128)(4,1)S(1)} %compare_and_fusion, f32[8,128]{1,0:T(8,128)S(1)} %add_power_fusion), kind=kOutput, calls=%fused_computation.9 | convolution fusion | flops 403193856 | bytes 5313152 | tf_op jit(solution)/shard_map/cond/branch_0_fun/btij,btkj->bki/dot_general | solution.py:344
  232.1 38.7 %psum.20 = f32[16,16]{0,1:T(8,128)S(1)} all-reduce(f32[16,16]{0,1:T(8,128)S(1)} %convolution_bitcast_fusion.5), channel_id=1, replica_groups=mesh['group'=4,'row'=8] {'group','row'}, use_global_device_ids=true, to_apply=%region_6.10 | all-reduce | flops 256 | bytes 2048 | tf_op jit(solution)/shard_map/cond/branch_0_fun/psum | solution.py:349
  270.8 1.5 cholesky.81
  272.3 0.7 compare_reduce_fusion
  273.1 0.7 fusion.19
  273.8 1.2 custom-call.9
  275.0 0.2 convolution_bitcast_fusion.4
  275.2 0.2 convolution_bitcast_fusion
  275.4 0.7 pad_maximum_fusion.3
  (55 shorter events, 1.6 us)
Async XLA Ops:
  0.0 17.7 %copy-start.3 = (s32[1,1,8,2]{2,3,1,0:T(2,128)S(1)}, s32[1,1,8,2]{2,3,1,0:T(2,128)}, u32[]{:S(2)}) copy-start(s32[1,1,8,2]{2,3,1,0:T(2,128)} %param.18) | copy-start | bytes 196
  0.0 17.7 %copy-start.2 = (s32[8]{0:T(128)S(1)}, s32[8]{0:T(128)}, u32[]{:S(2)}) copy-start(s32[8]{0:T(128)} %refs_1_.5) | copy-start | bytes 100
  0.0 17.7 %copy-start.1 = (s32[8,16]{1,0:T(8,128)S(1)}, s32[8,16]{1,0:T(8,128)}, u32[]{:S(2)}) copy-start(s32[8,16]{1,0:T(8,128)} %refs_2_.5) | copy-start | bytes 1540
  4.0 13.8 %collective-permute-start.6 = (f32[2,16,128]{2,1,0:T(8,128)S(1)}, f32[2,16,128]{2,1,0:T(8,128)S(1)}, u32[]{:S(2)}, u32[]{:S(2)}) collective-permute-start(f32[2,16,128]{2,1,0:T(8,128)S(1)} %get-tuple-element.55), channel_id=1, source_target_pairs={{0,8},{16,24},{8,0},{24,16},{1,9},{17,25},{9,1},{25,17},{2,10},{18... | collective-permute-start | bytes 49160 | tf_op jit(solution)/shard_map/ppermute | solution.py:322
  7.1 10.7 %collective-permute-start.7 = (f32[2,16,128]{2,1,0:T(8,128)S(1)}, f32[2,16,128]{2,1,0:T(8,128)S(1)}, u32[]{:S(2)}, u32[]{:S(2)}) collective-permute-start(f32[2,16,128]{2,1,0:T(8,128)S(1)} %get-tuple-element.56), channel_id=1, source_target_pairs={{8,16},{16,8},{9,17},{17,9},{10,18},{18,10},{11,19},{19,11},{12,20... | collective-permute-start | bytes 49160 | tf_op jit(solution)/shard_map/ppermute | solution.py:322
  20.5 9.6 %all-to-all-start = ((f32[16,16,128]{2,1,0:T(8,128)}), f32[16,16,128]{2,1,0:T(8,128)S(1)}, u32[]{:S(2)}, u32[]{:S(2)}) async-start(f32[16,16,128]{2,1,0:T(8,128)} %get-tuple-element.58), calls=%async_computation | async-start | bytes 262144 | tf_op jit(solution)/shard_map/all_to_all | solution.py:404
  23.9 6.2 %collective-permute-start.8 = (f32[2,16,128]{2,1,0:T(8,128)S(1)}, f32[2,16,128]{2,1,0:T(8,128)S(1)}, u32[]{:S(2)}, u32[]{:S(2)}) collective-permute-start(f32[2,16,128]{2,1,0:T(8,128)S(1)} %get-tuple-element.59), channel_id=1, source_target_pairs={{0,8},{16,24},{8,0},{24,16},{1,9},{17,25},{9,1},{25,17},{2,10},{18... | collective-permute-start | bytes 49160 | tf_op jit(solution)/shard_map/ppermute | solution.py:322
  28.4 1.7 collective-permute-start.9
  34.5 32.9 %copy-start = (f32[8,16,128]{2,1,0:T(8,128)S(1)}, f32[8,16,128]{2,1,0:T(8,128)}, u32[]{:S(2)}) copy-start(f32[8,16,128]{2,1,0:T(8,128)} %basis_hbm.1) | copy-start | bytes 196612
  34.5 9.8 %all-to-all-start.1 = ((f32[16,16,128]{2,1,0:T(8,128)}), f32[16,16,128]{2,1,0:T(8,128)S(1)}, u32[]{:S(2)}, u32[]{:S(2)}) async-start(f32[16,16,128]{2,1,0:T(8,128)} %get-tuple-element.63), calls=%async_computation.1 | async-start | bytes 262144 | tf_op jit(solution)/shard_map/all_to_all | solution.py:404
  38.7 5.6 %collective-permute-start.10 = (f32[2,16,128]{2,1,0:T(8,128)S(1)}, f32[2,16,128]{2,1,0:T(8,128)S(1)}, u32[]{:S(2)}, u32[]{:S(2)}) collective-permute-start(f32[2,16,128]{2,1,0:T(8,128)S(1)} %get-tuple-element.64), channel_id=1, source_target_pairs={{0,8},{16,24},{8,0},{24,16},{1,9},{17,25},{9,1},{25,17},{2,10},{18... | collective-permute-start | bytes 49160 | tf_op jit(solution)/shard_map/ppermute | solution.py:322
  42.6 1.7 collective-permute-start.11
  49.0 14.9 %all-to-all-start.2 = ((f32[32,8,128]{2,1,0:T(8,128)}), f32[32,8,128]{2,1,0:T(8,128)S(1)}, u32[]{:S(2)}, u32[]{:S(2)}) async-start(f32[32,8,128]{2,1,0:T(8,128)} %get-tuple-element.68), calls=%async_computation.2 | async-start | bytes 262144 | tf_op jit(solution)/shard_map/all_to_all | solution.py:450
  72.1 13.9 %collective-permute-start = (f32[2,16,128]{2,1,0:T(8,128)S(1)}, f32[2,16,128]{2,1,0:T(8,128)S(1)}, u32[]{:S(2)}, u32[]{:S(2)}) collective-permute-start(f32[2,16,128]{2,1,0:T(8,128)S(1)} %get-tuple-element.94), channel_id=1, source_target_pairs={{0,8},{8,16},{16,24},{1,9},{9,17},{17,25},{2,10},{10,18},{18,26},{... | collective-permute-start | bytes 49160 | tf_op jit(solution)/shard_map/cond/branch_0_fun/ppermute | solution.py:313
  74.7 11.3 %collective-permute-start.1 = (f32[2,16,128]{2,1,0:T(8,128)S(1)}, f32[2,16,128]{2,1,0:T(8,128)S(1)}, u32[]{:S(2)}, u32[]{:S(2)}) collective-permute-start(f32[2,16,128]{2,1,0:T(8,128)S(1)} %get-tuple-element.95), channel_id=1, source_target_pairs={{8,0},{16,8},{24,16},{9,1},{17,9},{25,17},{10,2},{18,10},{26,18},{... | collective-permute-start | bytes 49160 | tf_op jit(solution)/shard_map/cond/branch_0_fun/ppermute | solution.py:314
  148.6 3.8 %collective-permute-start.2 = (f32[2,16,128]{2,1,0:T(8,128)S(1)}, f32[2,16,128]{2,1,0:T(8,128)S(1)}, u32[]{:S(2)}, u32[]{:S(2)}) collective-permute-start(f32[2,16,128]{2,1,0:T(8,128)S(1)} %get-tuple-element.92), channel_id=1, source_target_pairs={{0,8},{8,16},{16,24},{1,9},{9,17},{17,25},{2,10},{10,18},{18,26},{... | collective-permute-start | bytes 49160 | tf_op jit(solution)/shard_map/cond/branch_0_fun/ppermute | solution.py:313
  150.9 5.6 %collective-permute-start.3 = (f32[2,16,128]{2,1,0:T(8,128)S(1)}, f32[2,16,128]{2,1,0:T(8,128)S(1)}, u32[]{:S(2)}, u32[]{:S(2)}) collective-permute-start(f32[2,16,128]{2,1,0:T(8,128)S(1)} %get-tuple-element.93), channel_id=1, source_target_pairs={{8,0},{16,8},{24,16},{9,1},{17,9},{25,17},{10,2},{18,10},{26,18},{... | collective-permute-start | bytes 49160 | tf_op jit(solution)/shard_map/cond/branch_0_fun/ppermute | solution.py:314
  217.8 4.0 %collective-permute-start.4 = (f32[2,16,128]{2,1,0:T(8,128)S(1)}, f32[2,16,128]{2,1,0:T(8,128)S(1)}, u32[]{:S(2)}, u32[]{:S(2)}) collective-permute-start(f32[2,16,128]{2,1,0:T(8,128)S(1)} %get-tuple-element.90), channel_id=1, source_target_pairs={{0,8},{8,16},{16,24},{1,9},{9,17},{17,25},{2,10},{10,18},{18,26},{... | collective-permute-start | bytes 49160 | tf_op jit(solution)/shard_map/cond/branch_0_fun/ppermute | solution.py:313
  220.3 5.6 %collective-permute-start.5 = (f32[2,16,128]{2,1,0:T(8,128)S(1)}, f32[2,16,128]{2,1,0:T(8,128)S(1)}, u32[]{:S(2)}, u32[]{:S(2)}) collective-permute-start(f32[2,16,128]{2,1,0:T(8,128)S(1)} %get-tuple-element.91), channel_id=1, source_target_pairs={{8,0},{16,8},{24,16},{9,1},{17,9},{25,17},{10,2},{18,10},{26,18},{... | collective-permute-start | bytes 49160 | tf_op jit(solution)/shard_map/cond/branch_0_fun/ppermute | solution.py:314

commit v8 on v5

--- a/solution.py
+++ b/solution.py
@@ -12,7 +12,7 @@
 ITERS = 3
 MINLIVE = 10
 LANES = 128
-HELD_BYTES = 5 * 1024 * 1024 // 2
+HELD_BYTES = 3 * 1024 * 1024
 PIECES = 2
 VMEM_BYTES = 24 * 1024 * 1024
 TRUST = 64.0
@@ -66,16 +66,16 @@
     blocks = held + rest_ref.shape[0]
     peers = want_ref.shape[1]
     vectors = basis_ref.shape[1]
-    rest_load = load(tiles_hbm, held, rest_ref, sems.at[0])
+    rest_load = load(tiles_hbm, held, rest_ref, sems.at[3])
     small = [
-        pltpu.make_async_copy(source, target, sems.at[2 + n])
+        pltpu.make_async_copy(source, target, sems.at[n])
         for n, (source, target) in enumerate(
             ((count_hbm, count_ref), (want_hbm, want_ref), (basis_hbm, basis_ref))
         )
     ]
     for copy in small:
         copy.start()
-    held_load = load(tiles_hbm, 0, held_ref, sems.at[1])
+    held_load = load(tiles_hbm, 0, held_ref, sems.at[4])
     for copy in small:
         copy.wait()
     for p in range(peers):
@@ -166,11 +166,16 @@
     place_ref, count_ref, cols_ref, *refs = refs
     if opening:
         want_ref, *refs = refs
-    tiles_hbm, held_ref, root_ref, own_ref, recv_ref, swapped_ref, swapped_next_ref, *refs = refs
-    *refs, table, rest_ref, load_sem = refs
+    tiles_at, held_ref, root_ref, own_ref, recv_ref, swapped_ref, swapped_next_ref, *refs = refs
+    if opening:
+        *refs, table = refs
+        rest_ref = tiles_at
+    else:
+        *refs, table, rest_ref, load_sem = refs
     held, per_row, side, _ = held_ref.shape
     blocks = held + rest_ref.shape[0]
-    rest_load = load(tiles_hbm, held, rest_ref, load_sem)
+    if not opening:
+        rest_load = load(tiles_at, held, rest_ref, load_sem)
     if last:
         *before, applied_ref, gram_hbm, packed_ref, sem = refs
     else:
@@ -214,7 +219,7 @@
             at = jnp.where(s < count_ref[b], cols_ref[b, s], slot)
             picked.append(table[at])
         x = jnp.concatenate(picked, axis=1)
-        if b == held:
+        if b == held and not opening:
             rest_load.wait()
         tile_ref = held_ref.at[b] if b < held else rest_ref.at[b - held]
         t = jnp.concatenate([tile_ref[s] for s in range(per_row)], axis=1)
@@ -248,7 +253,14 @@
 
 
 def finish_kernel(row_total, grams_ref, *refs):
-    applied_refs, (out_hbm, trust_ref, out_ref, sems) = refs[:ITERS], refs[ITERS:]
+    *earlier, final_ref, out_hbm, trust_ref, earlier_ref, out_ref, sems, load_sems = refs
+    loads = [
+        pltpu.make_async_copy(source, earlier_ref.at[t], load_sems.at[t])
+        for t, source in enumerate(earlier)
+    ]
+    for copy in loads:
+        copy.start()
+    applied_refs = [earlier_ref.at[t] for t in range(ITERS - 1)] + [final_ref]
     devices = grams_ref.shape[0]
     blocks, vectors = out_ref.shape[1:3]
     sends = [pltpu.make_async_copy(out_ref.at[t], out_hbm.at[t], sems.at[t]) for t in range(ITERS)]
@@ -258,19 +270,26 @@
     rows = lax.broadcasted_iota(jnp.int32, (vectors, vectors), 0)
     lanes = lax.broadcasted_iota(jnp.int32, (vectors, vectors), 1)
     unit = (rows == lanes).astype(jnp.float32)
-    row_at = lax.broadcasted_iota(jnp.int32, (vectors, 1), 0)
     grams = unpack_grams(total, vectors)
-    work = [jnp.concatenate([gram, unit], axis=1) for gram in grams]
+    columns = [
+        [jnp.broadcast_to(gram[:, k : k + 1], (vectors, vectors)) for k in range(vectors)]
+        for gram in grams
+    ]
+    inverses = [unit] * ITERS
     for j in range(vectors):
-        for t in range(ITERS):
-            m = work[t]
-            ratio = jnp.where(row_at > j, m[:, j : j + 1] / m[j : j + 1, j : j + 1], 0.0)
-            work[t] = m - ratio * m[j : j + 1, :]
+        for t, column in enumerate(columns):
+            ratio = jnp.where(rows > j, column[j] * (1.0 / column[j][j : j + 1]), 0.0)
+            for k in range(j + 1, vectors):
+                column[k] = column[k] - ratio * column[k][j : j + 1]
+            inverses[t] = inverses[t] - ratio * inverses[t][j : j + 1]
+    for copy in loads:
+        copy.wait()
     good = jnp.bool_(True)
     for t in range(ITERS):
-        m = work[t]
-        pivots = jnp.sum(m[:, :vectors] * unit, axis=1, keepdims=True)
-        inverse = m[:, vectors:] * lax.rsqrt(pivots / row_total)
+        pivots = columns[t][0]
+        for j in range(1, vectors):
+            pivots = jnp.where(rows == j, columns[t][j], pivots)
+        inverse = inverses[t] * lax.rsqrt(pivots / row_total)
         squares = jnp.sum(grams[t] * unit, axis=0, keepdims=True)
         norm = jnp.sum(inverse * inverse * squares) / row_total
         good = good & (norm < TRUST) & (jnp.min(squares) > TINY)
@@ -349,7 +368,7 @@
     rim_shape = f32(RIM, *block_shape)
     kept = held_blocks(tiles)
     rest = pltpu.VMEM((blocks - kept,) + tiles.shape[1:], tiles.dtype)
-    root, scaled, *rims, held = pl.pallas_call(
+    root, scaled, *rims, held, opening_rest = pl.pallas_call(
         roots_kernel,
         out_shape=(
             f32(blocks, 1, side),
@@ -357,11 +376,11 @@
             rim_shape,
             rim_shape,
             pltpu.VMEM((kept,) + tiles.shape[1:], tiles.dtype),
+            rest,
         ),
         in_specs=[smem()] + [hbm()] * 4,
-        out_specs=(vmem(),) * 5,
+        out_specs=(vmem(),) * 6,
         scratch_shapes=[
-            rest,
             pltpu.SMEM((blocks,), jnp.int32),
             pltpu.SMEM((SLOTS, peers), jnp.int32),
             pltpu.VMEM((blocks,) + block_shape, jnp.float32),
@@ -382,8 +401,8 @@
             received = lax.all_to_all(outgoing, "row", 0, 0, tiled=True)
             swapped = swap(*rims)
         scalars = [place, tile_count, tile_cols] + ([wanted] if t == 0 else [])
-        arrays = [far_tiles, held, root, scaled, received, *swapped]
-        shapes = [f32(blocks, *block_shape)]
+        arrays = [far_tiles if t else opening_rest, held, root, scaled, received, *swapped]
+        shapes = [f32(blocks, *block_shape) if last else pltpu.HBM((blocks,) + block_shape, jnp.float32)]
         specs = [vmem(), vmem()]
         if last:
             shapes += [pltpu.HBM((groups * peers, vectors // 2, LANES), jnp.float32)]
@@ -406,14 +425,15 @@
         result = pl.pallas_call(
             functools.partial(apply_kernel, t),
             out_shape=tuple(shapes),
-            in_specs=[smem()] * len(scalars) + [hbm()] + [vmem()] * (len(arrays) - 1),
+            in_specs=[smem()] * len(scalars)
+            + [hbm() if t else vmem()]
+            + [vmem()] * (len(arrays) - 1),
             out_specs=tuple(specs),
             scratch_shapes=scratch
             + [
                 pltpu.VMEM((slots + 1, PIECES * vectors, side), jnp.bfloat16),
-                rest,
-                pltpu.SemaphoreType.DMA,
-            ],
+            ]
+            + ([rest, pltpu.SemaphoreType.DMA] if t else []),
             compiler_params=params(),
             cost_estimate=cost(tiles.size * 2 * vectors * PIECES, tile_bytes),
             name="apply_last" if last else "apply",
@@ -428,15 +448,17 @@
     krylov, trust = pl.pallas_call(
         functools.partial(finish_kernel, float(groups * peers * blocks * side)),
         out_shape=(pltpu.HBM((ITERS, blocks, vectors, side), jnp.float32), jax.ShapeDtypeStruct((1,), jnp.int32)),
-        in_specs=[vmem()] * (1 + ITERS),
+        in_specs=[vmem()] + [hbm()] * (ITERS - 1) + [vmem()],
         out_specs=(hbm(), smem()),
         scratch_shapes=[
+            pltpu.VMEM((ITERS - 1, blocks, vectors, side), jnp.float32),
             pltpu.VMEM((ITERS, blocks, vectors, side), jnp.float32),
             pltpu.SemaphoreType.DMA((ITERS,)),
+            pltpu.SemaphoreType.DMA((ITERS - 1,)),
         ],
         compiler_params=params(),
         name="finish",
-    )(gathered, *powers)
+    )(gathered, *[far(power) for power in powers[:-1]], powers[-1])
     return lax.cond(
         trust[0] > 0,
         lambda *_: krylov,

time: 278 us -> 277 us (level)
  no operation moved by 1% of the time
where the time goes in v8:
time: 277 us; the launch traced here: 276 us
  blocking collectives  159 us (57%)
  starting transfers between devices  38.8 us (14%)
  waiting for transfers between devices  18.8 us (7%)
  Pallas kernels  18.4 us (7%)
  other arithmetic  18.1 us (7%)
  matrix products  17.5 us (6%)
  local copies, waits for them, and re-layouts  4.46 us (2%)
    psum x3, blocking collectives, stepwise(): factor = jnp.linalg.cholesky(lax.psum(gram, ('group', 'row')) / row_total)  118 us
    all_gather x3, blocking collectives, stepwise(): lax.all_gather(scaled, 'row', axis=0, tiled=True)  30.3 us
    dot_general x3, matrix products, stepwise(): jnp.einsum('btij,btkj->bki', tiles, picked, precision=HIGH, preferred_ele...  15.6 us
    ppermute x6, starting transfers between devices, swap(): lax.ppermute(x, 'group', pair)  13.4 us
    pallas_call x3, Pallas kernels, local(): pl.pallas_call(functools.partial(apply_kernel, t), out_shape=tuple(shapes...  12 us
    all_gather x1, blocking collectives, local(): received = lax.all_gather(scaled, 'row', axis=0)  10 us
    ppermute x3, waiting for transfers between devices, neighbours(): high = lax.ppermute(scaled[:RIM], 'group', down)  8.42 us
    all_to_all x1, waiting for transfers between devices, local(): gathered = lax.all_to_all(grams[-1], ('group', 'row'), 0, 0, tiled=True)  8.23 us
  transfers between devices with their start and end apart: 15, of which 5 were waited for; matrix products, arithmetic and copies ran while one was open for 0% of the time, Pallas kernels for 0%

profile of v8, /device:TPU:0, one launch (start us, length us, event | category | flops | bytes accessed | tf_op | source)
XLA Modules:
  0.0 275.8 jit_solution(12470091322176536552)
XLA Ops:
  0.1 3.6 %roots.1 = (f32[8,1,128]{2,1,0:T(1,128)S(1)}, f32[9,16,128]{2,1,0:T(8,128)S(1)}, f32[2,16,128]{2,1,0:T(8,128)S(1)}, f32[2,16,128]{2,1,0:T(8,128)S(1)}, bf16[6,16...) custom-call(s32[2]{0:T(128)S(1)} %pad_add_fusion.place_ref.refs_0_, s32[8]{0:T(128)} %refs_1_.5, ...), custom_call_target="tpu_custom_call" | custom-call | flops 4194304 | bytes 4194304 | tf_op jit(solution)/shard_map/roots/pallas_call | solution.py:371
  3.7 3.1 %collective-permute-start.6 = (f32[2,16,128]{2,1,0:T(8,128)S(1)}, f32[2,16,128]{2,1,0:T(8,128)S(1)}, u32[]{:S(2)}, u32[]{:S(2)}) collective-permute-start(f32[2,16,128]{2,1,0:T(8,128)S(1)} %get-tuple-element.55), channel_id=1, source_target_pairs={{0,8},{16,24},{8,0},{24,16},{1,9},{17,25},{9,1},{25,17},{2,10},{18... | collective-permute-start | bytes 49160 | tf_op jit(solution)/shard_map/ppermute | solution.py:321
  6.8 0.7 collective-permute-start.7
  7.5 10.0 %all-gather = f32[72,16,128]{2,1,0:T(8,128)S(1)} all-gather(f32[9,16,128]{2,1,0:T(8,128)S(1)} %get-tuple-element.54.refs_7_), channel_id=2, replica_groups=mesh['group'=4,'row'=8] {'row'}, dimensions={0}, use_global_device_ids=true | all-gather | bytes 663552 | tf_op jit(solution)/shard_map/all_gather | solution.py:399
  17.5 3.4 %apply.2 = (f32[8,16,128]{2,1,0:T(8,128)}, f32[16,16]{1,0:T(8,128)S(1)}, f32[8,16,128]{2,1,0:T(8,128)S(1)}, f32[16,16,128]{2,1,0:T(8,128)}, f32[2,16,128]{2,1,0:...) custom-call(s32[2]{0:T(128)S(1)} %pad_add_fusion.place_ref.refs_0_, s32[8]{0:T(128)S(1)} %copy-done.2, ...), custom_call_target="tpu_custom_call" | custom-call | flops 134217728 | bytes 4194304 | tf_op jit(solution)/shard_map/apply/pallas_call | solution.py:425
  20.9 3.4 %all-to-all-start = ((f32[16,16,128]{2,1,0:T(8,128)}), f32[16,16,128]{2,1,0:T(8,128)S(1)}, u32[]{:S(2)}, u32[]{:S(2)}) async-start(f32[16,16,128]{2,1,0:T(8,128)} %get-tuple-element.58), calls=%async_computation | async-start | bytes 262144 | tf_op jit(solution)/shard_map/all_to_all | solution.py:401
  24.3 4.5 %collective-permute-start.8 = (f32[2,16,128]{2,1,0:T(8,128)S(1)}, f32[2,16,128]{2,1,0:T(8,128)S(1)}, u32[]{:S(2)}, u32[]{:S(2)}) collective-permute-start(f32[2,16,128]{2,1,0:T(8,128)S(1)} %get-tuple-element.59), channel_id=1, source_target_pairs={{0,8},{16,24},{8,0},{24,16},{1,9},{17,25},{9,1},{25,17},{2,10},{18... | collective-permute-start | bytes 49160 | tf_op jit(solution)/shard_map/ppermute | solution.py:321
  28.8 0.7 collective-permute-start.9
  29.4 1.1 collective-permute-done.8.refs_8_
  30.5 4.4 %apply.3 = (f32[8,16,128]{2,1,0:T(8,128)}, f32[16,16]{1,0:T(8,128)S(1)}, f32[8,16,128]{2,1,0:T(8,128)S(1)}, f32[16,16,128]{2,1,0:T(8,128)}, f32[2,16,128]{2,1,0:T(8,128)S(1)}, /*index=5*/f32[2,16,128]{2,1,0:T(8,128)S(1)}) custom-call(s32[2]{0:T(128)S(1)} %pad_add_fusion.place_ref.refs_0_, s32[8]{0:T(128)S(1)} %copy-done.2, s32[8,16]{1,0:T(8,128)S(1)} %copy-done.1, ...), custom_call_target="tpu_custom_call" | custom-call | flops 134217728 | bytes 4194304 | tf_op jit(solution)/shard_map/apply/pallas_call | solution.py:425
  34.9 4.1 %all-to-all-start.1 = ((f32[16,16,128]{2,1,0:T(8,128)}), f32[16,16,128]{2,1,0:T(8,128)S(1)}, u32[]{:S(2)}, u32[]{:S(2)}) async-start(f32[16,16,128]{2,1,0:T(8,128)} %get-tuple-element.63), calls=%async_computation.1 | async-start | bytes 262144 | tf_op jit(solution)/shard_map/all_to_all | solution.py:401
  39.0 3.9 %collective-permute-start.10 = (f32[2,16,128]{2,1,0:T(8,128)S(1)}, f32[2,16,128]{2,1,0:T(8,128)S(1)}, u32[]{:S(2)}, u32[]{:S(2)}) collective-permute-start(f32[2,16,128]{2,1,0:T(8,128)S(1)} %get-tuple-element.64), channel_id=1, source_target_pairs={{0,8},{16,24},{8,0},{24,16},{1,9},{17,25},{9,1},{25,17},{2,10},{18... | collective-permute-start | bytes 49160 | tf_op jit(solution)/shard_map/ppermute | solution.py:321
  42.9 0.7 collective-permute-start.11
  43.5 1.1 collective-permute-done.10.refs_8_
  44.6 4.2 %apply_last.1 = (f32[8,16,128]{2,1,0:T(8,128)S(1)}, f32[32,8,128]{2,1,0:T(8,128)}) custom-call(s32[2]{0:T(128)S(1)} %pad_add_fusion.place_ref.refs_0_, s32[8]{0:T(128)S(1)} %copy-done.2, s32[8,16]{1,0:T(8,128)S(1)} %copy-done.1, bf16[8,16,128,128]{3,2,1,0:T(8,128)(2,1)} %refs_3_.3, bf16[6,16,128,128]{3,2,1,0:T(8,128)(2,1)S(1)} %get-tuple-element.51.refs_5_.refs_4_, ...), custom_call_target="tpu_custom_call" | custom-call | flops 134217728 | bytes 4194304 | tf_op jit(solution)/shard_map/apply_last/pallas_call | solution.py:425
  48.8 6.6 %all-to-all-start.2 = ((f32[32,8,128]{2,1,0:T(8,128)}), f32[32,8,128]{2,1,0:T(8,128)S(1)}, u32[]{:S(2)}, u32[]{:S(2)}) async-start(f32[32,8,128]{2,1,0:T(8,128)} %get-tuple-element.68), calls=%async_computation.2 | async-start | bytes 262144 | tf_op jit(solution)/shard_map/all_to_all | solution.py:447
  55.5 8.2 %all-to-all-done.2.grams_ref = f32[32,8,128]{2,1,0:T(8,128)S(1)} async-done(((f32[32,8,128]{2,1,0:T(8,128)}), f32[32,8,128]{2,1,0:T(8,128)S(1)}, u32[]{:S(2)}, u32[]{:S(2)}) %all-to-all-start.2) | async-done | bytes 131104 | tf_op jit(solution)/shard_map/all_to_all | solution.py:447
  63.7 2.8 %finish.1 = (f32[3,8,16,128]{3,2,1,0:T(8,128)}, s32[1]{0:T(128)}) custom-call(f32[32,8,128]{2,1,0:T(8,128)S(1)} %all-to-all-done.2.grams_ref, f32[8,16,128]{2,1,0:T(8,128)} %get-tuple-element.69.refs_0_, f32[8,16,128]{2,1,0:T(8,128)} %get-tuple-element.70.refs_1_, f32[8,16,128]{2,1,0:T(8,128)S(1)} %get-tuple-element.71.refs_2_), custom_call_target="tpu_custom_call" | custom-call | tf_op jit(solution)/shard_map/finish/pallas_call | solution.py:448
  67.0 208.8 %conditional.1 = (f32[3,8,16,128]{3,2,1,0:T(8,128)}) conditional(s32[]{:T(128)} %bitcast.39, (bf16[8,16,128,128]{3,2,1,0:T(8,128)(2,1)}, s32[8]{0:T(128)S(1)}, f32[8,16,128]{2,1,0:T(8,128)}, s32[1,1,8,2]{2,3,1,0:T(2,128)S(1)}, s32[8,16]{1,0:T(8,128)S(1)}) %tuple.32, f32[3,8,16,128]{3,2,1,0:T(8,128)} %get-tuple-element.73), branch_computations={%region_0.11_spmd, %region_7.12_spmd} | conditional | flops 1235852416 | bytes 33461096 | solution.py:462
  67.1 4.5 %multiply_reduce_fusion = f32[8,16,128]{2,1,0:T(8,128)S(1)} fusion(bf16[8,16,128,128]{3,2,1,0:T(8,128)(2,1)} %get-tuple-element.22), kind=kLoop, calls=%fused_computation.6 | loop fusion | flops 6275072 | bytes 4259840 | tf_op jit(solution)/shard_map/cond/branch_0_fun/btij,bt->bi/reduce_sum | solution.py:332
  71.8 2.6 collective-permute-start
  74.4 1.3 collective-permute-start.1
  75.7 9.0 %all_gather.10 = f32[64,16,128]{2,1,0:T(8,128)S(1)} all-gather(f32[8,16,128]{2,1,0:T(8,128)S(1)} %broadcast_multiply_fusion), channel_id=1, replica_groups=mesh['group'=4,'row'=8] {'row'}, dimensions={0}, use_global_device_ids=true | all-gather | bytes 589824 | tf_op jit(solution)/shard_map/cond/branch_0_fun/all_gather | solution.py:340
  85.0 0.6 gather_fusion
  85.7 0.8 gather_fusion.1
  86.5 5.2 %fusion.2 = f32[8,16,128]{2,1,0:T(8,128)S(1)} fusion(bf16[8,16,128,128]{3,2,1,0:T(8,128)(2,1)} %get-tuple-element.22, f32[8,16,16,128]{3,2,1,0:T(8,128)S(1)} %bitcast.100, f32[8,16]{1,0:T(8,128)S(1)} %get-tuple-element.96, pred[8,16]{1,0:T(8,128)(4,1)S(1)} %compare_and_fusion, f32[8,128]{1,0:T(8,128)S(1)} %add_power_fusion), kind=kOutput, calls=%fused_computation.13 | convolution fusion | flops 403193856 | bytes 5313152 | tf_op jit(solution)/shard_map/cond/branch_0_fun/btij,btkj->bki/dot_general | solution.py:343
  91.7 0.2 convolution_bitcast_fusion.9
  91.9 40.6 %psum.18 = f32[16,16]{0,1:T(8,128)S(1)} all-reduce(f32[16,16]{0,1:T(8,128)S(1)} %convolution_bitcast_fusion.9), channel_id=1, replica_groups=mesh['group'=4,'row'=8] {'group','row'}, use_global_device_ids=true, to_apply=%region_2.0 | all-reduce | flops 256 | bytes 2048 | tf_op jit(solution)/shard_map/cond/branch_0_fun/psum | solution.py:348
  132.5 1.5 cholesky.59
  134.0 0.7 compare_reduce_fusion.2
  134.8 0.7 fusion.17
  135.5 1.2 custom-call.7
  136.7 0.2 convolution_bitcast_fusion.8
  136.9 0.2 bitcast_multiply_fusion.1
  137.1 10.6 %all_gather.11 = f32[64,16,128]{2,1,0:T(8,128)S(1)} all-gather(f32[8,16,128]{2,1,0:T(8,128)S(1)} %get-tuple-element.98), channel_id=1, replica_groups=mesh['group'=4,'row'=8] {'row'}, dimensions={0}, use_global_device_ids=true | all-gather | bytes 589824 | tf_op jit(solution)/shard_map/cond/branch_0_fun/all_gather | solution.py:340
  147.8 0.6 gather_fusion.2
  148.3 2.3 collective-permute-start.2
  150.7 1.3 collective-permute-start.3
  152.1 4.2 %collective-permute-done.3 = f32[2,16,128]{2,1,0:T(8,128)S(1)} collective-permute-done((f32[2,16,128]{2,1,0:T(8,128)S(1)}, f32[2,16,128]{2,1,0:T(8,128)S(1)}, u32[]{:S(2)}, u32[]{:S(2)}) %collective-permute-start.3) | collective-permute-done | bytes 16416 | tf_op jit(solution)/shard_map/cond/branch_0_fun/ppermute | solution.py:313
  156.3 0.8 gather_fusion.3
  157.1 5.2 %fusion.1 = f32[8,16,128]{2,1,0:T(8,128)S(1)} fusion(bf16[8,16,128,128]{3,2,1,0:T(8,128)(2,1)} %get-tuple-element.22, f32[8,16,16,128]{3,2,1,0:T(8,128)S(1)} %bitcast.101, f32[8,16]{1,0:T(8,128)S(1)} %get-tuple-element.96, pred[8,16]{1,0:T(8,128)(4,1)S(1)} %compare_and_fusion, f32[8,128]{1,0:T(8,128)S(1)} %add_power_fusion), kind=kOutput, calls=%fused_computation.11 | convolution fusion | flops 403193856 | bytes 5313152 | tf_op jit(solution)/shard_map/cond/branch_0_fun/btij,btkj->bki/dot_general | solution.py:343
  162.5 39.1 %psum.19 = f32[16,16]{0,1:T(8,128)S(1)} all-reduce(f32[16,16]{0,1:T(8,128)S(1)} %convolution_bitcast_fusion.7), channel_id=1, replica_groups=mesh['group'=4,'row'=8] {'group','row'}, use_global_device_ids=true, to_apply=%region_5.9 | all-reduce | flops 256 | bytes 2048 | tf_op jit(solution)/shard_map/cond/branch_0_fun/psum | solution.py:348
  201.7 1.5 cholesky.70
  203.2 0.7 compare_reduce_fusion.1
  203.9 0.7 fusion.18
  204.6 1.2 custom-call.8
  205.8 0.2 convolution_bitcast_fusion.6
  206.0 0.2 bitcast_multiply_fusion
  206.2 10.6 %all_gather.12 = f32[64,16,128]{2,1,0:T(8,128)S(1)} all-gather(f32[8,16,128]{2,1,0:T(8,128)S(1)} %get-tuple-element.100), channel_id=1, replica_groups=mesh['group'=4,'row'=8] {'row'}, dimensions={0}, use_global_device_ids=true | all-gather | bytes 589824 | tf_op jit(solution)/shard_map/cond/branch_0_fun/all_gather | solution.py:340
  216.9 0.6 gather_fusion.4
  217.5 2.6 collective-permute-start.4
  220.0 1.3 collective-permute-start.5
  221.5 4.2 %collective-permute-done.5 = f32[2,16,128]{2,1,0:T(8,128)S(1)} collective-permute-done((f32[2,16,128]{2,1,0:T(8,128)S(1)}, f32[2,16,128]{2,1,0:T(8,128)S(1)}, u32[]{:S(2)}, u32[]{:S(2)}) %collective-permute-start.5) | collective-permute-done | bytes 16416 | tf_op jit(solution)/shard_map/cond/branch_0_fun/ppermute | solution.py:313
  225.7 0.8 gather_fusion.5
  226.4 5.2 %fusion = f32[8,16,128]{2,1,0:T(8,128)S(1)} fusion(bf16[8,16,128,128]{3,2,1,0:T(8,128)(2,1)} %get-tuple-element.22, f32[8,16,16,128]{3,2,1,0:T(8,128)S(1)} %bitcast.99, f32[8,16]{1,0:T(8,128)S(1)} %get-tuple-element.96, pred[8,16]{1,0:T(8,128)(4,1)S(1)} %compare_and_fusion, f32[8,128]{1,0:T(8,128)S(1)} %add_power_fusion), kind=kOutput, calls=%fused_computation.9 | convolution fusion | flops 403193856 | bytes 5313152 | tf_op jit(solution)/shard_map/cond/branch_0_fun/btij,btkj->bki/dot_general | solution.py:343
  231.6 0.2 convolution_bitcast_fusion.5
  231.8 38.6 %psum.20 = f32[16,16]{0,1:T(8,128)S(1)} all-reduce(f32[16,16]{0,1:T(8,128)S(1)} %convolution_bitcast_fusion.5), channel_id=1, replica_groups=mesh['group'=4,'row'=8] {'group','row'}, use_global_device_ids=true, to_apply=%region_6.10 | all-reduce | flops 256 | bytes 2048 | tf_op jit(solution)/shard_map/cond/branch_0_fun/psum | solution.py:348
  270.5 1.5 cholesky.81
  272.0 0.7 compare_reduce_fusion
  272.8 0.7 fusion.19
  273.5 1.2 custom-call.9
  274.7 0.2 convolution_bitcast_fusion.4
  274.9 0.2 convolution_bitcast_fusion
  275.1 0.7 pad_maximum_fusion.3
  (55 shorter events, 1.6 us)
Async XLA Ops:
  0.0 17.5 %copy-start.3 = (s32[1,1,8,2]{2,3,1,0:T(2,128)S(1)}, s32[1,1,8,2]{2,3,1,0:T(2,128)}, u32[]{:S(2)}) copy-start(s32[1,1,8,2]{2,3,1,0:T(2,128)} %param.18) | copy-start | bytes 196
  0.0 17.5 %copy-start.2 = (s32[8]{0:T(128)S(1)}, s32[8]{0:T(128)}, u32[]{:S(2)}) copy-start(s32[8]{0:T(128)} %refs_1_.5) | copy-start | bytes 100
  0.0 17.5 %copy-start.1 = (s32[8,16]{1,0:T(8,128)S(1)}, s32[8,16]{1,0:T(8,128)}, u32[]{:S(2)}) copy-start(s32[8,16]{1,0:T(8,128)} %refs_2_.5) | copy-start | bytes 1540
  3.7 13.8 %collective-permute-start.6 = (f32[2,16,128]{2,1,0:T(8,128)S(1)}, f32[2,16,128]{2,1,0:T(8,128)S(1)}, u32[]{:S(2)}, u32[]{:S(2)}) collective-permute-start(f32[2,16,128]{2,1,0:T(8,128)S(1)} %get-tuple-element.55), channel_id=1, source_target_pairs={{0,8},{16,24},{8,0},{24,16},{1,9},{17,25},{9,1},{25,17},{2,10},{18... | collective-permute-start | bytes 49160 | tf_op jit(solution)/shard_map/ppermute | solution.py:321
  6.8 10.7 %collective-permute-start.7 = (f32[2,16,128]{2,1,0:T(8,128)S(1)}, f32[2,16,128]{2,1,0:T(8,128)S(1)}, u32[]{:S(2)}, u32[]{:S(2)}) collective-permute-start(f32[2,16,128]{2,1,0:T(8,128)S(1)} %get-tuple-element.56), channel_id=1, source_target_pairs={{8,16},{16,8},{9,17},{17,9},{10,18},{18,10},{11,19},{19,11},{12,20... | collective-permute-start | bytes 49160 | tf_op jit(solution)/shard_map/ppermute | solution.py:321
  20.9 9.6 %all-to-all-start = ((f32[16,16,128]{2,1,0:T(8,128)}), f32[16,16,128]{2,1,0:T(8,128)S(1)}, u32[]{:S(2)}, u32[]{:S(2)}) async-start(f32[16,16,128]{2,1,0:T(8,128)} %get-tuple-element.58), calls=%async_computation | async-start | bytes 262144 | tf_op jit(solution)/shard_map/all_to_all | solution.py:401
  24.3 6.2 %collective-permute-start.8 = (f32[2,16,128]{2,1,0:T(8,128)S(1)}, f32[2,16,128]{2,1,0:T(8,128)S(1)}, u32[]{:S(2)}, u32[]{:S(2)}) collective-permute-start(f32[2,16,128]{2,1,0:T(8,128)S(1)} %get-tuple-element.59), channel_id=1, source_target_pairs={{0,8},{16,24},{8,0},{24,16},{1,9},{17,25},{9,1},{25,17},{2,10},{18... | collective-permute-start | bytes 49160 | tf_op jit(solution)/shard_map/ppermute | solution.py:321
  28.8 1.7 collective-permute-start.9
  34.9 9.7 %all-to-all-start.1 = ((f32[16,16,128]{2,1,0:T(8,128)}), f32[16,16,128]{2,1,0:T(8,128)S(1)}, u32[]{:S(2)}, u32[]{:S(2)}) async-start(f32[16,16,128]{2,1,0:T(8,128)} %get-tuple-element.63), calls=%async_computation.1 | async-start | bytes 262144 | tf_op jit(solution)/shard_map/all_to_all | solution.py:401
  39.0 5.6 %collective-permute-start.10 = (f32[2,16,128]{2,1,0:T(8,128)S(1)}, f32[2,16,128]{2,1,0:T(8,128)S(1)}, u32[]{:S(2)}, u32[]{:S(2)}) collective-permute-start(f32[2,16,128]{2,1,0:T(8,128)S(1)} %get-tuple-element.64), channel_id=1, source_target_pairs={{0,8},{16,24},{8,0},{24,16},{1,9},{17,25},{9,1},{25,17},{2,10},{18... | collective-permute-start | bytes 49160 | tf_op jit(solution)/shard_map/ppermute | solution.py:321
  42.9 1.7 collective-permute-start.11
  48.8 14.9 %all-to-all-start.2 = ((f32[32,8,128]{2,1,0:T(8,128)}), f32[32,8,128]{2,1,0:T(8,128)S(1)}, u32[]{:S(2)}, u32[]{:S(2)}) async-start(f32[32,8,128]{2,1,0:T(8,128)} %get-tuple-element.68), calls=%async_computation.2 | async-start | bytes 262144 | tf_op jit(solution)/shard_map/all_to_all | solution.py:447
  67.1 4.7 %copy-start = (f32[8,16,128]{2,1,0:T(8,128)S(1)}, f32[8,16,128]{2,1,0:T(8,128)}, u32[]{:S(2)}) copy-start(f32[8,16,128]{2,1,0:T(8,128)} %get-tuple-element.20) | copy-start | bytes 196612 | tf_op jit(solution)/shard_map/cond
  71.8 13.9 %collective-permute-start = (f32[2,16,128]{2,1,0:T(8,128)S(1)}, f32[2,16,128]{2,1,0:T(8,128)S(1)}, u32[]{:S(2)}, u32[]{:S(2)}) collective-permute-start(f32[2,16,128]{2,1,0:T(8,128)S(1)} %get-tuple-element.94), channel_id=1, source_target_pairs={{0,8},{8,16},{16,24},{1,9},{9,17},{17,25},{2,10},{10,18},{18,26},{... | collective-permute-start | bytes 49160 | tf_op jit(solution)/shard_map/cond/branch_0_fun/ppermute | solution.py:312
  74.4 11.3 %collective-permute-start.1 = (f32[2,16,128]{2,1,0:T(8,128)S(1)}, f32[2,16,128]{2,1,0:T(8,128)S(1)}, u32[]{:S(2)}, u32[]{:S(2)}) collective-permute-start(f32[2,16,128]{2,1,0:T(8,128)S(1)} %get-tuple-element.95), channel_id=1, source_target_pairs={{8,0},{16,8},{24,16},{9,1},{17,9},{25,17},{10,2},{18,10},{26,18},{... | collective-permute-start | bytes 49160 | tf_op jit(solution)/shard_map/cond/branch_0_fun/ppermute | solution.py:313
  148.3 3.8 %collective-permute-start.2 = (f32[2,16,128]{2,1,0:T(8,128)S(1)}, f32[2,16,128]{2,1,0:T(8,128)S(1)}, u32[]{:S(2)}, u32[]{:S(2)}) collective-permute-start(f32[2,16,128]{2,1,0:T(8,128)S(1)} %get-tuple-element.92), channel_id=1, source_target_pairs={{0,8},{8,16},{16,24},{1,9},{9,17},{17,25},{2,10},{10,18},{18,26},{... | collective-permute-start | bytes 49160 | tf_op jit(solution)/shard_map/cond/branch_0_fun/ppermute | solution.py:312
  150.7 5.6 %collective-permute-start.3 = (f32[2,16,128]{2,1,0:T(8,128)S(1)}, f32[2,16,128]{2,1,0:T(8,128)S(1)}, u32[]{:S(2)}, u32[]{:S(2)}) collective-permute-start(f32[2,16,128]{2,1,0:T(8,128)S(1)} %get-tuple-element.93), channel_id=1, source_target_pairs={{8,0},{16,8},{24,16},{9,1},{17,9},{25,17},{10,2},{18,10},{26,18},{... | collective-permute-start | bytes 49160 | tf_op jit(solution)/shard_map/cond/branch_0_fun/ppermute | solution.py:313
  217.5 4.0 %collective-permute-start.4 = (f32[2,16,128]{2,1,0:T(8,128)S(1)}, f32[2,16,128]{2,1,0:T(8,128)S(1)}, u32[]{:S(2)}, u32[]{:S(2)}) collective-permute-start(f32[2,16,128]{2,1,0:T(8,128)S(1)} %get-tuple-element.90), channel_id=1, source_target_pairs={{0,8},{8,16},{16,24},{1,9},{9,17},{17,25},{2,10},{10,18},{18,26},{... | collective-permute-start | bytes 49160 | tf_op jit(solution)/shard_map/cond/branch_0_fun/ppermute | solution.py:312
  220.0 5.6 %collective-permute-start.5 = (f32[2,16,128]{2,1,0:T(8,128)S(1)}, f32[2,16,128]{2,1,0:T(8,128)S(1)}, u32[]{:S(2)}, u32[]{:S(2)}) collective-permute-start(f32[2,16,128]{2,1,0:T(8,128)S(1)} %get-tuple-element.91), channel_id=1, source_target_pairs={{8,0},{16,8},{24,16},{9,1},{17,9},{25,17},{10,2},{18,10},{26,18},{... | collective-permute-start | bytes 49160 | tf_op jit(solution)/shard_map/cond/branch_0_fun/ppermute | solution.py:313

commit v9 on v8

--- a/solution.py
+++ b/solution.py
@@ -12,7 +12,7 @@
 ITERS = 3
 MINLIVE = 10
 LANES = 128
-HELD_BYTES = 3 * 1024 * 1024
+HELD_BYTES = 5 * 1024 * 1024 // 2
 PIECES = 2
 VMEM_BYTES = 24 * 1024 * 1024
 TRUST = 64.0
@@ -166,12 +166,13 @@
     place_ref, count_ref, cols_ref, *refs = refs
     if opening:
         want_ref, *refs = refs
-    tiles_at, held_ref, root_ref, own_ref, recv_ref, swapped_ref, swapped_next_ref, *refs = refs
+    tiles_at, held_ref, root_ref, own_ref, recv_ref, *refs = refs
     if opening:
+        swapped_ref, swapped_next_ref, *refs = refs
         *refs, table = refs
         rest_ref = tiles_at
     else:
-        *refs, table, rest_ref, load_sem = refs
+        edges_recv_ref, *refs, table, rest_ref, load_sem = refs
     held, per_row, side, _ = held_ref.shape
     blocks = held + rest_ref.shape[0]
     if not opening:
@@ -181,7 +182,7 @@
     else:
         if not opening:
             asked_ref, *refs = refs
-        applied_ref, gram_ref, scaled_ref, out_hbm, first_ref, second_ref, *refs = refs
+        applied_ref, gram_ref, scaled_ref, out_hbm, edges_ref, *refs = refs
         if opening:
             asked_ref, *refs = refs
         picked_ref, sem = refs
@@ -206,11 +207,19 @@
         for n in range(recv_ref.shape[0]):
             split_into(recv_ref[n], table, slot)
             slot += 1
-    odd = group % 2 == 1
-    for a_ref, b_ref in ((swapped_ref, swapped_next_ref), (swapped_next_ref, swapped_ref)):
-        for h in range(RIM):
-            split_into(jnp.where(odd, a_ref[h], b_ref[h]), table, slot)
-            slot += 1
+    if opening:
+        odd = group % 2 == 1
+        for a_ref, b_ref in ((swapped_ref, swapped_next_ref), (swapped_next_ref, swapped_ref)):
+            for h in range(RIM):
+                split_into(jnp.where(odd, a_ref[h], b_ref[h]), table, slot)
+                slot += 1
+    else:
+        below = jnp.maximum(group - 1, 0)
+        above = jnp.minimum(group + 1, edges_recv_ref.shape[0] - 1)
+        for at, first in ((below, RIM), (above, 0)):
+            for h in range(RIM):
+                split_into(edges_recv_ref[at, first + h], table, slot)
+                slot += 1
     table[slot] = jnp.zeros(table.shape[1:], table.dtype)
     rows = []
     for b in range(blocks):
@@ -237,7 +246,9 @@
         pick_into(asked_ref, scaled_ref, picked_ref)
         send = pltpu.make_async_copy(picked_ref, out_hbm, sem)
         send.start()
-        swaps_into(group, blocks, scaled_ref, first_ref, second_ref)
+        for h in range(RIM):
+            edges_ref[h] = scaled_ref[h]
+            edges_ref[RIM + h] = scaled_ref[blocks - RIM + h]
     flat = jnp.concatenate(rows, axis=1)
     gram = gram_of(flat)
     if last:
@@ -253,14 +264,7 @@
 
 
 def finish_kernel(row_total, grams_ref, *refs):
-    *earlier, final_ref, out_hbm, trust_ref, earlier_ref, out_ref, sems, load_sems = refs
-    loads = [
-        pltpu.make_async_copy(source, earlier_ref.at[t], load_sems.at[t])
-        for t, source in enumerate(earlier)
-    ]
-    for copy in loads:
-        copy.start()
-    applied_refs = [earlier_ref.at[t] for t in range(ITERS - 1)] + [final_ref]
+    applied_refs, (out_hbm, trust_ref, out_ref, sems) = refs[:ITERS], refs[ITERS:]
     devices = grams_ref.shape[0]
     blocks, vectors = out_ref.shape[1:3]
     sends = [pltpu.make_async_copy(out_ref.at[t], out_hbm.at[t], sems.at[t]) for t in range(ITERS)]
@@ -282,8 +286,6 @@
             for k in range(j + 1, vectors):
                 column[k] = column[k] - ratio * column[k][j : j + 1]
             inverses[t] = inverses[t] - ratio * inverses[t][j : j + 1]
-    for copy in loads:
-        copy.wait()
     good = jnp.bool_(True)
     for t in range(ITERS):
         pivots = columns[t][0]
@@ -395,14 +397,14 @@
     for t in range(ITERS):
         last = t == ITERS - 1
         if t == 0:
-            swapped = swap(*rims)
+            beside = swap(*rims)
             received = lax.all_gather(scaled, "row", axis=0)
         else:
             received = lax.all_to_all(outgoing, "row", 0, 0, tiled=True)
-            swapped = swap(*rims)
+            beside = [lax.all_gather(edges, "group", axis=0)]
         scalars = [place, tile_count, tile_cols] + ([wanted] if t == 0 else [])
-        arrays = [far_tiles if t else opening_rest, held, root, scaled, received, *swapped]
-        shapes = [f32(blocks, *block_shape) if last else pltpu.HBM((blocks,) + block_shape, jnp.float32)]
+        arrays = [far_tiles if t else opening_rest, held, root, scaled, received, *beside]
+        shapes = [f32(blocks, *block_shape)]
         specs = [vmem(), vmem()]
         if last:
             shapes += [pltpu.HBM((groups * peers, vectors // 2, LANES), jnp.float32)]
@@ -414,8 +416,8 @@
             arrays += grams
         else:
             shapes += [f32(vectors, vectors), f32(blocks, *block_shape), pltpu.HBM(picked_shape, jnp.float32)]
-            shapes += [rim_shape] * 2
-            specs += [vmem(), hbm(), vmem(), vmem()]
+            shapes += [f32(2 * RIM, *block_shape)]
+            specs += [vmem(), hbm(), vmem()]
             scratch = [pltpu.VMEM(picked_shape, jnp.float32), pltpu.SemaphoreType.DMA]
             if t:
                 arrays += [asked]
@@ -441,24 +443,22 @@
         powers.append(result[0])
         grams.append(result[1])
         if not last:
-            scaled, outgoing, *rims = result[2:6]
+            scaled, outgoing, edges = result[2:5]
             if t == 0:
-                asked = result[6]
+                asked = result[5]
     gathered = lax.all_to_all(grams[-1], ("group", "row"), 0, 0, tiled=True)
     krylov, trust = pl.pallas_call(
         functools.partial(finish_kernel, float(groups * peers * blocks * side)),
         out_shape=(pltpu.HBM((ITERS, blocks, vectors, side), jnp.float32), jax.ShapeDtypeStruct((1,), jnp.int32)),
-        in_specs=[vmem()] + [hbm()] * (ITERS - 1) + [vmem()],
+        in_specs=[vmem()] * (1 + ITERS),
         out_specs=(hbm(), smem()),
         scratch_shapes=[
-            pltpu.VMEM((ITERS - 1, blocks, vectors, side), jnp.float32),
             pltpu.VMEM((ITERS, blocks, vectors, side), jnp.float32),
             pltpu.SemaphoreType.DMA((ITERS,)),
-            pltpu.SemaphoreType.DMA((ITERS - 1,)),
         ],
         compiler_params=params(),
         name="finish",
-    )(gathered, *[far(power) for power in powers[:-1]], powers[-1])
+    )(gathered, *powers)
     return lax.cond(
         trust[0] > 0,
         lambda *_: krylov,

time: 277 us -> 291 us (1.051)
  blocking collectives: 159 us -> 187 us
  starting transfers between devices: 38.8 us -> 28.6 us
    all_gather x0 -> x2, blocking collectives: none -> 28.4 us  [local(): beside = [lax.all_gather(edges, 'group', axis=0)]]
    ppermute x6 -> x2, starting transfers between devices: 13.4 us -> 3.75 us  [swap(): lax.ppermute(x, 'group', pair)]
  transfers between devices with their start and end apart: 15 -> 11, of which waited for: 5 -> 3; matrix products, arithmetic and copies ran while one was open for 0% -> 0% of each run, Pallas kernels for 0% -> 0%
where the time goes in v9:
time: 291 us; the launch traced here: 290 us
  blocking collectives  187 us (64%)
  starting transfers between devices  28.6 us (10%)
  other arithmetic  17.8 us (6%)
  matrix products  17.5 us (6%)
  Pallas kernels  16.8 us (6%)
  waiting for transfers between devices  16.7 us (6%)
  local copies, waits for them, and re-layouts  4.46 us (2%)
    psum x3, blocking collectives, stepwise(): factor = jnp.linalg.cholesky(lax.psum(gram, ('group', 'row')) / row_total)  118 us
    all_gather x3, blocking collectives, stepwise(): lax.all_gather(scaled, 'row', axis=0, tiled=True)  30.5 us
    all_gather x2, blocking collectives, local(): beside = [lax.all_gather(edges, 'group', axis=0)]  28.4 us
    dot_general x3, matrix products, stepwise(): jnp.einsum('btij,btkj->bki', tiles, picked, precision=HIGH, preferred_ele...  15.6 us
    pallas_call x3, Pallas kernels, local(): pl.pallas_call(functools.partial(apply_kernel, t), out_shape=tuple(shapes...  11.3 us
    all_gather x1, blocking collectives, local(): received = lax.all_gather(scaled, 'row', axis=0)  10 us
    ppermute x3, waiting for transfers between devices, neighbours(): high = lax.ppermute(scaled[:RIM], 'group', down)  8.42 us
    all_to_all x1, waiting for transfers between devices, local(): gathered = lax.all_to_all(grams[-1], ('group', 'row'), 0, 0, tiled=True)  8.23 us
  transfers between devices with their start and end apart: 11, of which 3 were waited for; matrix products, arithmetic and copies ran while one was open for 0% of the time, Pallas kernels for 0%

profile of v9, /device:TPU:0, one launch (start us, length us, event | category | flops | bytes accessed | tf_op | source)
XLA Modules:
  0.0 290.1 jit_solution(14659395401261460012)
XLA Ops:
  0.1 3.5 %roots.1 = (f32[8,1,128]{2,1,0:T(1,128)S(1)}, f32[9,16,128]{2,1,0:T(8,128)S(1)}, f32[2,16,128]{2,1,0:T(8,128)S(1)}, f32[2,16,128]{2,1,0:T(8,128)S(1)}, bf16[5,16...) custom-call(s32[2]{0:T(128)S(1)} %pad_add_fusion.place_ref.refs_0_, s32[8]{0:T(128)} %refs_1_.5, ...), custom_call_target="tpu_custom_call" | custom-call | flops 4194304 | bytes 4194304 | tf_op jit(solution)/shard_map/roots/pallas_call | solution.py:373
  3.6 3.1 %collective-permute-start.6 = (f32[2,16,128]{2,1,0:T(8,128)S(1)}, f32[2,16,128]{2,1,0:T(8,128)S(1)}, u32[]{:S(2)}, u32[]{:S(2)}) collective-permute-start(f32[2,16,128]{2,1,0:T(8,128)S(1)} %get-tuple-element.53), channel_id=1, source_target_pairs={{0,8},{16,24},{8,0},{24,16},{1,9},{17,25},{9,1},{25,17},{2,10},{18... | collective-permute-start | bytes 49160 | tf_op jit(solution)/shard_map/ppermute | solution.py:323
  6.7 0.7 collective-permute-start.7
  7.3 10.0 %all-gather = f32[72,16,128]{2,1,0:T(8,128)S(1)} all-gather(f32[9,16,128]{2,1,0:T(8,128)S(1)} %get-tuple-element.52.refs_7_), channel_id=2, replica_groups=mesh['group'=4,'row'=8] {'row'}, dimensions={0}, use_global_device_ids=true | all-gather | bytes 663552 | tf_op jit(solution)/shard_map/all_gather | solution.py:401
  17.4 2.8 apply.2
  20.2 3.4 %all-to-all-start = ((f32[16,16,128]{2,1,0:T(8,128)}), f32[16,16,128]{2,1,0:T(8,128)S(1)}, u32[]{:S(2)}, u32[]{:S(2)}) async-start(f32[16,16,128]{2,1,0:T(8,128)} %get-tuple-element.56), calls=%async_computation | async-start | bytes 262144 | tf_op jit(solution)/shard_map/all_to_all | solution.py:403
  23.6 15.0 %all-gather.1 = f32[16,16,128]{2,1,0:T(8,128)S(1)} all-gather(f32[4,16,128]{2,1,0:T(8,128)S(1)} %get-tuple-element.57), channel_id=3, replica_groups=mesh['group'=4,'row'=8] {'group'}, dimensions={0}, use_global_device_ids=true | all-gather | bytes 163840 | tf_op jit(solution)/shard_map/all_gather | solution.py:404
  38.5 4.1 %apply.3 = (f32[8,16,128]{2,1,0:T(8,128)S(1)}, f32[16,16]{1,0:T(8,128)S(1)}, f32[8,16,128]{2,1,0:T(8,128)S(1)}, f32[16,16,128]{2,1,0:T(8,128)}, f32[4,16,128]{2,1,0:T(8,128)S(1)}) custom-call(s32[2]{0:T(128)S(1)} %pad_add_fusion.place_ref.refs_0_, s32[8]{0:T(128)S(1)} %copy-done.2, s32[8,16]{1,0:T(8,128)S(1)} %copy-done.1, ...), custom_call_target="tpu_custom_call" | custom-call | flops 134217728 | bytes 4194304 | tf_op jit(solution)/shard_map/apply/pallas_call | solution.py:427
  42.6 4.1 %all-to-all-start.1 = ((f32[16,16,128]{2,1,0:T(8,128)}), f32[16,16,128]{2,1,0:T(8,128)S(1)}, u32[]{:S(2)}, u32[]{:S(2)}) async-start(f32[16,16,128]{2,1,0:T(8,128)} %get-tuple-element.60), calls=%async_computation.1 | async-start | bytes 262144 | tf_op jit(solution)/shard_map/all_to_all | solution.py:403
  46.8 13.4 %all-gather.2 = f32[16,16,128]{2,1,0:T(8,128)S(1)} all-gather(f32[4,16,128]{2,1,0:T(8,128)S(1)} %get-tuple-element.61), channel_id=4, replica_groups=mesh['group'=4,'row'=8] {'group'}, dimensions={0}, use_global_device_ids=true | all-gather | bytes 163840 | tf_op jit(solution)/shard_map/all_gather | solution.py:404
  60.2 4.5 %apply_last.1 = (f32[8,16,128]{2,1,0:T(8,128)S(1)}, f32[32,8,128]{2,1,0:T(8,128)}) custom-call(s32[2]{0:T(128)S(1)} %pad_add_fusion.place_ref.refs_0_, s32[8]{0:T(128)S(1)} %copy-done.2, s32[8,16]{1,0:T(8,128)S(1)} %copy-done.1, bf16[8,16,128,128]{3,2,1,0:T(8,128)(2,1)} %refs_3_.3, bf16[5,16,128,128]{3,2,1,0:T(8,128)(2,1)S(1)} %get-tuple-element.49.refs_5_.refs_4_, ...), custom_call_target="tpu_custom_call" | custom-call | flops 134217728 | bytes 4194304 | tf_op jit(solution)/shard_map/apply_last/pallas_call | solution.py:427
  64.7 6.0 %all-to-all-start.2 = ((f32[32,8,128]{2,1,0:T(8,128)}), f32[32,8,128]{2,1,0:T(8,128)S(1)}, u32[]{:S(2)}, u32[]{:S(2)}) async-start(f32[32,8,128]{2,1,0:T(8,128)} %get-tuple-element.64), calls=%async_computation.2 | async-start | bytes 262144 | tf_op jit(solution)/shard_map/all_to_all | solution.py:449
  70.7 8.2 %all-to-all-done.2.grams_ref = f32[32,8,128]{2,1,0:T(8,128)S(1)} async-done(((f32[32,8,128]{2,1,0:T(8,128)}), f32[32,8,128]{2,1,0:T(8,128)S(1)}, u32[]{:S(2)}, u32[]{:S(2)}) %all-to-all-start.2) | async-done | bytes 131104 | tf_op jit(solution)/shard_map/all_to_all | solution.py:449
  78.9 2.0 finish.1
  81.6 208.5 %conditional.1 = (f32[3,8,16,128]{3,2,1,0:T(8,128)}) conditional(s32[]{:T(128)} %bitcast.41, (bf16[8,16,128,128]{3,2,1,0:T(8,128)(2,1)}, s32[8]{0:T(128)S(1)}, f32[8,16,128]{2,1,0:T(8,128)S(1)}, s32[1,1,8,2]{2,3,1,0:T(2,128)S(1)}, s32[8,16]{1,0:T(8,128)S(1)}) %tuple.33, f32[3,8,16,128]{3,2,1,0:T(8,128)} %get-tuple-element.69), branch_computations={%region_0.11_spmd, %region_7.12_spmd} | conditional | flops 1235852416 | bytes 33198924 | solution.py:462
  81.6 4.4 %multiply_reduce_fusion = f32[8,16,128]{2,1,0:T(8,128)S(1)} fusion(bf16[8,16,128,128]{3,2,1,0:T(8,128)(2,1)} %get-tuple-element.22), kind=kLoop, calls=%fused_computation.6 | loop fusion | flops 6275072 | bytes 4259840 | tf_op jit(solution)/shard_map/cond/branch_0_fun/btij,bt->bi/reduce_sum | solution.py:334
  86.1 0.2 fusion.12
  86.3 2.6 collective-permute-start
  88.9 1.3 collective-permute-start.1
  90.2 9.0 %all_gather.18 = f32[64,16,128]{2,1,0:T(8,128)S(1)} all-gather(f32[8,16,128]{2,1,0:T(8,128)S(1)} %broadcast_multiply_fusion), channel_id=1, replica_groups=mesh['group'=4,'row'=8] {'row'}, dimensions={0}, use_global_device_ids=true | all-gather | bytes 589824 | tf_op jit(solution)/shard_map/cond/branch_0_fun/all_gather | solution.py:342
  99.5 0.6 gather_fusion
  100.1 0.1 broadcast_select_fusion.2
  100.2 0.8 gather_fusion.1
  101.0 5.2 %fusion.2 = f32[8,16,128]{2,1,0:T(8,128)S(1)} fusion(bf16[8,16,128,128]{3,2,1,0:T(8,128)(2,1)} %get-tuple-element.22, f32[8,16,16,128]{3,2,1,0:T(8,128)S(1)} %bitcast.104, f32[8,16]{1,0:T(8,128)S(1)} %get-tuple-element.92, pred[8,16]{1,0:T(8,128)(4,1)S(1)} %compare_and_fusion, f32[8,128]{1,0:T(8,128)S(1)} %add_power_fusion), kind=kOutput, calls=%fused_computation.13 | convolution fusion | flops 403193856 | bytes 5313152 | tf_op jit(solution)/shard_map/cond/branch_0_fun/btij,btkj->bki/dot_general | solution.py:345
  106.2 0.2 convolution_bitcast_fusion.9
  106.4 40.4 %psum.18 = f32[16,16]{0,1:T(8,128)S(1)} all-reduce(f32[16,16]{0,1:T(8,128)S(1)} %convolution_bitcast_fusion.9), channel_id=1, replica_groups=mesh['group'=4,'row'=8] {'group','row'}, use_global_device_ids=true, to_apply=%region_2.0 | all-reduce | flops 256 | bytes 2048 | tf_op jit(solution)/shard_map/cond/branch_0_fun/psum | solution.py:350
  146.9 1.5 cholesky.59
  148.4 0.7 compare_reduce_fusion.2
  149.1 0.6 fusion.17
  149.7 1.2 custom-call.7
  150.9 0.2 convolution_bitcast_fusion.8
  151.1 0.2 bitcast_multiply_fusion.1
  151.4 10.8 %all_gather.19 = f32[64,16,128]{2,1,0:T(8,128)S(1)} all-gather(f32[8,16,128]{2,1,0:T(8,128)S(1)} %get-tuple-element.94), channel_id=1, replica_groups=mesh['group'=4,'row'=8] {'row'}, dimensions={0}, use_global_device_ids=true | all-gather | bytes 589824 | tf_op jit(solution)/shard_map/cond/branch_0_fun/all_gather | solution.py:342
  162.2 0.6 gather_fusion.2
  162.8 2.3 collective-permute-start.2
  165.1 1.3 collective-permute-start.3
  166.4 0.1 broadcast_select_fusion.1
  166.5 4.2 %collective-permute-done.3 = f32[2,16,128]{2,1,0:T(8,128)S(1)} collective-permute-done((f32[2,16,128]{2,1,0:T(8,128)S(1)}, f32[2,16,128]{2,1,0:T(8,128)S(1)}, u32[]{:S(2)}, u32[]{:S(2)}) %collective-permute-start.3) | collective-permute-done | bytes 16416 | tf_op jit(solution)/shard_map/cond/branch_0_fun/ppermute | solution.py:315
  170.7 0.8 gather_fusion.3
  171.5 5.2 %fusion.1 = f32[8,16,128]{2,1,0:T(8,128)S(1)} fusion(bf16[8,16,128,128]{3,2,1,0:T(8,128)(2,1)} %get-tuple-element.22, f32[8,16,16,128]{3,2,1,0:T(8,128)S(1)} %bitcast.105, f32[8,16]{1,0:T(8,128)S(1)} %get-tuple-element.92, pred[8,16]{1,0:T(8,128)(4,1)S(1)} %compare_and_fusion, f32[8,128]{1,0:T(8,128)S(1)} %add_power_fusion), kind=kOutput, calls=%fused_computation.11 | convolution fusion | flops 403193856 | bytes 5313152 | tf_op jit(solution)/shard_map/cond/branch_0_fun/btij,btkj->bki/dot_general | solution.py:345
  176.7 0.2 convolution_bitcast_fusion.7
  176.9 39.2 %psum.19 = f32[16,16]{0,1:T(8,128)S(1)} all-reduce(f32[16,16]{0,1:T(8,128)S(1)} %convolution_bitcast_fusion.7), channel_id=1, replica_groups=mesh['group'=4,'row'=8] {'group','row'}, use_global_device_ids=true, to_apply=%region_5.9 | all-reduce | flops 256 | bytes 2048 | tf_op jit(solution)/shard_map/cond/branch_0_fun/psum | solution.py:350
  216.1 1.5 cholesky.70
  217.6 0.7 compare_reduce_fusion.1
  218.3 0.6 fusion.18
  219.0 1.2 custom-call.8
  220.2 0.2 convolution_bitcast_fusion.6
  220.4 0.2 bitcast_multiply_fusion
  220.6 10.6 %all_gather.20 = f32[64,16,128]{2,1,0:T(8,128)S(1)} all-gather(f32[8,16,128]{2,1,0:T(8,128)S(1)} %get-tuple-element.96), channel_id=1, replica_groups=mesh['group'=4,'row'=8] {'row'}, dimensions={0}, use_global_device_ids=true | all-gather | bytes 589824 | tf_op jit(solution)/shard_map/cond/branch_0_fun/all_gather | solution.py:342
  231.3 0.6 gather_fusion.4
  231.8 2.6 collective-permute-start.4
  234.4 1.3 collective-permute-start.5
  235.8 4.2 %collective-permute-done.5 = f32[2,16,128]{2,1,0:T(8,128)S(1)} collective-permute-done((f32[2,16,128]{2,1,0:T(8,128)S(1)}, f32[2,16,128]{2,1,0:T(8,128)S(1)}, u32[]{:S(2)}, u32[]{:S(2)}) %collective-permute-start.5) | collective-permute-done | bytes 16416 | tf_op jit(solution)/shard_map/cond/branch_0_fun/ppermute | solution.py:315
  240.0 0.8 gather_fusion.5
  240.8 5.2 %fusion = f32[8,16,128]{2,1,0:T(8,128)S(1)} fusion(bf16[8,16,128,128]{3,2,1,0:T(8,128)(2,1)} %get-tuple-element.22, f32[8,16,16,128]{3,2,1,0:T(8,128)S(1)} %bitcast.103, f32[8,16]{1,0:T(8,128)S(1)} %get-tuple-element.92, pred[8,16]{1,0:T(8,128)(4,1)S(1)} %compare_and_fusion, f32[8,128]{1,0:T(8,128)S(1)} %add_power_fusion), kind=kOutput, calls=%fused_computation.9 | convolution fusion | flops 403193856 | bytes 5313152 | tf_op jit(solution)/shard_map/cond/branch_0_fun/btij,btkj->bki/dot_general | solution.py:345
  246.0 0.2 convolution_bitcast_fusion.5
  246.2 38.7 %psum.20 = f32[16,16]{0,1:T(8,128)S(1)} all-reduce(f32[16,16]{0,1:T(8,128)S(1)} %convolution_bitcast_fusion.5), channel_id=1, replica_groups=mesh['group'=4,'row'=8] {'group','row'}, use_global_device_ids=true, to_apply=%region_6.10 | all-reduce | flops 256 | bytes 2048 | tf_op jit(solution)/shard_map/cond/branch_0_fun/psum | solution.py:350
  284.9 1.5 cholesky.81
  286.4 0.7 compare_reduce_fusion
  287.1 0.6 fusion.19
  287.8 1.2 custom-call.9
  289.0 0.2 convolution_bitcast_fusion.4
  289.2 0.2 convolution_bitcast_fusion
  289.4 0.7 pad_maximum_fusion.3
  (49 shorter events, 1.0 us)
Async XLA Ops:
  0.0 17.3 %copy-start.3 = (s32[1,1,8,2]{2,3,1,0:T(2,128)S(1)}, s32[1,1,8,2]{2,3,1,0:T(2,128)}, u32[]{:S(2)}) copy-start(s32[1,1,8,2]{2,3,1,0:T(2,128)} %param.18) | copy-start | bytes 196
  0.0 17.4 %copy-start.2 = (s32[8]{0:T(128)S(1)}, s32[8]{0:T(128)}, u32[]{:S(2)}) copy-start(s32[8]{0:T(128)} %refs_1_.5) | copy-start | bytes 100
  0.0 17.4 %copy-start.1 = (s32[8,16]{1,0:T(8,128)S(1)}, s32[8,16]{1,0:T(8,128)}, u32[]{:S(2)}) copy-start(s32[8,16]{1,0:T(8,128)} %refs_2_.5) | copy-start | bytes 1540
  3.6 13.8 %collective-permute-start.6 = (f32[2,16,128]{2,1,0:T(8,128)S(1)}, f32[2,16,128]{2,1,0:T(8,128)S(1)}, u32[]{:S(2)}, u32[]{:S(2)}) collective-permute-start(f32[2,16,128]{2,1,0:T(8,128)S(1)} %get-tuple-element.53), channel_id=1, source_target_pairs={{0,8},{16,24},{8,0},{24,16},{1,9},{17,25},{9,1},{25,17},{2,10},{18... | collective-permute-start | bytes 49160 | tf_op jit(solution)/shard_map/ppermute | solution.py:323
  6.7 10.7 %collective-permute-start.7 = (f32[2,16,128]{2,1,0:T(8,128)S(1)}, f32[2,16,128]{2,1,0:T(8,128)S(1)}, u32[]{:S(2)}, u32[]{:S(2)}) collective-permute-start(f32[2,16,128]{2,1,0:T(8,128)S(1)} %get-tuple-element.54), channel_id=1, source_target_pairs={{8,16},{16,8},{9,17},{17,9},{10,18},{18,10},{11,19},{19,11},{12,20... | collective-permute-start | bytes 49160 | tf_op jit(solution)/shard_map/ppermute | solution.py:323
  20.2 18.4 %all-to-all-start = ((f32[16,16,128]{2,1,0:T(8,128)}), f32[16,16,128]{2,1,0:T(8,128)S(1)}, u32[]{:S(2)}, u32[]{:S(2)}) async-start(f32[16,16,128]{2,1,0:T(8,128)} %get-tuple-element.56), calls=%async_computation | async-start | bytes 262144 | tf_op jit(solution)/shard_map/all_to_all | solution.py:403
  42.6 39.0 %copy-start = (f32[8,16,128]{2,1,0:T(8,128)S(1)}, f32[8,16,128]{2,1,0:T(8,128)}, u32[]{:S(2)}) copy-start(f32[8,16,128]{2,1,0:T(8,128)} %basis_hbm.1) | copy-start | bytes 196612
  42.6 17.6 %all-to-all-start.1 = ((f32[16,16,128]{2,1,0:T(8,128)}), f32[16,16,128]{2,1,0:T(8,128)S(1)}, u32[]{:S(2)}, u32[]{:S(2)}) async-start(f32[16,16,128]{2,1,0:T(8,128)} %get-tuple-element.60), calls=%async_computation.1 | async-start | bytes 262144 | tf_op jit(solution)/shard_map/all_to_all | solution.py:403
  64.7 14.2 %all-to-all-start.2 = ((f32[32,8,128]{2,1,0:T(8,128)}), f32[32,8,128]{2,1,0:T(8,128)S(1)}, u32[]{:S(2)}, u32[]{:S(2)}) async-start(f32[32,8,128]{2,1,0:T(8,128)} %get-tuple-element.64), calls=%async_computation.2 | async-start | bytes 262144 | tf_op jit(solution)/shard_map/all_to_all | solution.py:449
  86.3 13.9 %collective-permute-start = (f32[2,16,128]{2,1,0:T(8,128)S(1)}, f32[2,16,128]{2,1,0:T(8,128)S(1)}, u32[]{:S(2)}, u32[]{:S(2)}) collective-permute-start(f32[2,16,128]{2,1,0:T(8,128)S(1)} %get-tuple-element.90), channel_id=1, source_target_pairs={{0,8},{8,16},{16,24},{1,9},{9,17},{17,25},{2,10},{10,18},{18,26},{... | collective-permute-start | bytes 49160 | tf_op jit(solution)/shard_map/cond/branch_0_fun/ppermute | solution.py:314
  88.9 11.3 %collective-permute-start.1 = (f32[2,16,128]{2,1,0:T(8,128)S(1)}, f32[2,16,128]{2,1,0:T(8,128)S(1)}, u32[]{:S(2)}, u32[]{:S(2)}) collective-permute-start(f32[2,16,128]{2,1,0:T(8,128)S(1)} %get-tuple-element.91), channel_id=1, source_target_pairs={{8,0},{16,8},{24,16},{9,1},{17,9},{25,17},{10,2},{18,10},{26,18},{... | collective-permute-start | bytes 49160 | tf_op jit(solution)/shard_map/cond/branch_0_fun/ppermute | solution.py:315
  162.8 3.8 %collective-permute-start.2 = (f32[2,16,128]{2,1,0:T(8,128)S(1)}, f32[2,16,128]{2,1,0:T(8,128)S(1)}, u32[]{:S(2)}, u32[]{:S(2)}) collective-permute-start(f32[2,16,128]{2,1,0:T(8,128)S(1)} %get-tuple-element.88), channel_id=1, source_target_pairs={{0,8},{8,16},{16,24},{1,9},{9,17},{17,25},{2,10},{10,18},{18,26},{... | collective-permute-start | bytes 49160 | tf_op jit(solution)/shard_map/cond/branch_0_fun/ppermute | solution.py:314
  165.1 5.6 %collective-permute-start.3 = (f32[2,16,128]{2,1,0:T(8,128)S(1)}, f32[2,16,128]{2,1,0:T(8,128)S(1)}, u32[]{:S(2)}, u32[]{:S(2)}) collective-permute-start(f32[2,16,128]{2,1,0:T(8,128)S(1)} %get-tuple-element.89), channel_id=1, source_target_pairs={{8,0},{16,8},{24,16},{9,1},{17,9},{25,17},{10,2},{18,10},{26,18},{... | collective-permute-start | bytes 49160 | tf_op jit(solution)/shard_map/cond/branch_0_fun/ppermute | solution.py:315
  231.8 4.0 %collective-permute-start.4 = (f32[2,16,128]{2,1,0:T(8,128)S(1)}, f32[2,16,128]{2,1,0:T(8,128)S(1)}, u32[]{:S(2)}, u32[]{:S(2)}) collective-permute-start(f32[2,16,128]{2,1,0:T(8,128)S(1)} %get-tuple-element.86), channel_id=1, source_target_pairs={{0,8},{8,16},{16,24},{1,9},{9,17},{17,25},{2,10},{10,18},{18,26},{... | collective-permute-start | bytes 49160 | tf_op jit(solution)/shard_map/cond/branch_0_fun/ppermute | solution.py:314
  234.4 5.6 %collective-permute-start.5 = (f32[2,16,128]{2,1,0:T(8,128)S(1)}, f32[2,16,128]{2,1,0:T(8,128)S(1)}, u32[]{:S(2)}, u32[]{:S(2)}) collective-permute-start(f32[2,16,128]{2,1,0:T(8,128)S(1)} %get-tuple-element.87), channel_id=1, source_target_pairs={{8,0},{16,8},{24,16},{9,1},{17,9},{25,17},{10,2},{18,10},{26,18},{... | collective-permute-start | bytes 49160 | tf_op jit(solution)/shard_map/cond/branch_0_fun/ppermute | solution.py:315

commit v10 on v8

--- a/solution.py
+++ b/solution.py
@@ -12,7 +12,7 @@
 ITERS = 3
 MINLIVE = 10
 LANES = 128
-HELD_BYTES = 3 * 1024 * 1024
+HELD_BYTES = 5 * 1024 * 1024 // 2
 PIECES = 2
 VMEM_BYTES = 24 * 1024 * 1024
 TRUST = 64.0
@@ -60,13 +60,17 @@
     return copy
 
 
-def roots_kernel(place_ref, count_hbm, want_hbm, tiles_hbm, basis_hbm, root_ref, sent_ref,
+def tile(ref, at):
+    side = ref.shape[1]
+    return ref[at * side : (at + 1) * side]
+
+
+def roots_kernel(per_row, place_ref, count_hbm, want_hbm, tiles_hbm, basis_hbm, root_ref, sent_ref,
                  first_ref, second_ref, held_ref, rest_ref, count_ref, want_ref, basis_ref, sems):
-    held, per_row, side, _ = held_ref.shape
-    blocks = held + rest_ref.shape[0]
+    blocks, vectors, side = basis_ref.shape
+    held = held_ref.shape[0] // (per_row * side)
     peers = want_ref.shape[1]
-    vectors = basis_ref.shape[1]
-    rest_load = load(tiles_hbm, held, rest_ref, sems.at[3])
+    rest_load = load(tiles_hbm, held_ref.shape[0], rest_ref, sems.at[3])
     small = [
         pltpu.make_async_copy(source, target, sems.at[n])
         for n, (source, target) in enumerate(
@@ -88,10 +92,10 @@
     for b in list(range(held, blocks)) + list(range(held)):
         if b == 0:
             held_load.wait()
-        tile_ref = held_ref.at[b] if b < held else rest_ref.at[b - held]
+        tile_ref, first = (held_ref, b * per_row) if b < held else (rest_ref, (b - held) * per_row)
         total = jnp.zeros((side, side), jnp.float32)
         for s in range(per_row):
-            wide = tile_ref[s].astype(jnp.float32)
+            wide = tile(tile_ref, first + s).astype(jnp.float32)
             square = wide * wide
             if s >= MINLIVE:
                 square = square * (s < count_ref[b]).astype(jnp.float32)
@@ -172,10 +176,11 @@
         rest_ref = tiles_at
     else:
         *refs, table, rest_ref, load_sem = refs
-    held, per_row, side, _ = held_ref.shape
-    blocks = held + rest_ref.shape[0]
+    blocks, _, side = root_ref.shape
+    per_row = cols_ref.shape[1]
+    held = held_ref.shape[0] // (per_row * side)
     if not opening:
-        rest_load = load(tiles_at, held, rest_ref, load_sem)
+        rest_load = load(tiles_at, held_ref.shape[0], rest_ref, load_sem)
     if last:
         *before, applied_ref, gram_hbm, packed_ref, sem = refs
     else:
@@ -221,8 +226,8 @@
         x = jnp.concatenate(picked, axis=1)
         if b == held and not opening:
             rest_load.wait()
-        tile_ref = held_ref.at[b] if b < held else rest_ref.at[b - held]
-        t = jnp.concatenate([tile_ref[s] for s in range(per_row)], axis=1)
+        tile_ref, first = (held_ref, b * per_row) if b < held else (rest_ref, (b - held) * per_row)
+        t = jnp.concatenate([tile(tile_ref, first + s) for s in range(per_row)], axis=1)
         product = lax.dot_general(x, t, NT, preferred_element_type=jnp.float32)
         total = product[(PIECES - 1) * vectors :]
         for piece in range(PIECES - 2, -1, -1):
@@ -253,14 +258,7 @@
 
 
 def finish_kernel(row_total, grams_ref, *refs):
-    *earlier, final_ref, out_hbm, trust_ref, earlier_ref, out_ref, sems, load_sems = refs
-    loads = [
-        pltpu.make_async_copy(source, earlier_ref.at[t], load_sems.at[t])
-        for t, source in enumerate(earlier)
-    ]
-    for copy in loads:
-        copy.start()
-    applied_refs = [earlier_ref.at[t] for t in range(ITERS - 1)] + [final_ref]
+    applied_refs, (out_hbm, trust_ref, out_ref, sems) = refs[:ITERS], refs[ITERS:]
     devices = grams_ref.shape[0]
     blocks, vectors = out_ref.shape[1:3]
     sends = [pltpu.make_async_copy(out_ref.at[t], out_hbm.at[t], sems.at[t]) for t in range(ITERS)]
@@ -282,8 +280,6 @@
             for k in range(j + 1, vectors):
                 column[k] = column[k] - ratio * column[k][j : j + 1]
             inverses[t] = inverses[t] - ratio * inverses[t][j : j + 1]
-    for copy in loads:
-        copy.wait()
     good = jnp.bool_(True)
     for t in range(ITERS):
         pivots = columns[t][0]
@@ -362,20 +358,20 @@
     wanted = jnp.transpose(recv_list.reshape(peers, SLOTS))
     lists = pl.cdiv(peers * SLOTS, vectors)
     tile_bytes = tiles.size * 2
-    far_tiles = far(tiles)
+    far_tiles = far(tiles.reshape(-1, side))
     block_shape = (vectors, side)
     picked_shape = (peers * SLOTS,) + block_shape
     rim_shape = f32(RIM, *block_shape)
     kept = held_blocks(tiles)
-    rest = pltpu.VMEM((blocks - kept,) + tiles.shape[1:], tiles.dtype)
+    rest = pltpu.VMEM(((blocks - kept) * per_row * side, side), tiles.dtype)
     root, scaled, *rims, held, opening_rest = pl.pallas_call(
-        roots_kernel,
+        functools.partial(roots_kernel, per_row),
         out_shape=(
             f32(blocks, 1, side),
             f32(blocks + lists, *block_shape),
             rim_shape,
             rim_shape,
-            pltpu.VMEM((kept,) + tiles.shape[1:], tiles.dtype),
+            pltpu.VMEM((kept * per_row * side, side), tiles.dtype),
             rest,
         ),
         in_specs=[smem()] + [hbm()] * 4,
@@ -395,14 +391,14 @@
     for t in range(ITERS):
         last = t == ITERS - 1
         if t == 0:
-            swapped = swap(*rims)
+            beside = swap(*rims)
             received = lax.all_gather(scaled, "row", axis=0)
         else:
             received = lax.all_to_all(outgoing, "row", 0, 0, tiled=True)
-            swapped = swap(*rims)
+            beside = swap(*rims)
         scalars = [place, tile_count, tile_cols] + ([wanted] if t == 0 else [])
-        arrays = [far_tiles if t else opening_rest, held, root, scaled, received, *swapped]
-        shapes = [f32(blocks, *block_shape) if last else pltpu.HBM((blocks,) + block_shape, jnp.float32)]
+        arrays = [far_tiles if t else opening_rest, held, root, scaled, received, *beside]
+        shapes = [f32(blocks, *block_shape)]
         specs = [vmem(), vmem()]
         if last:
             shapes += [pltpu.HBM((groups * peers, vectors // 2, LANES), jnp.float32)]
@@ -448,17 +444,15 @@
     krylov, trust = pl.pallas_call(
         functools.partial(finish_kernel, float(groups * peers * blocks * side)),
         out_shape=(pltpu.HBM((ITERS, blocks, vectors, side), jnp.float32), jax.ShapeDtypeStruct((1,), jnp.int32)),
-        in_specs=[vmem()] + [hbm()] * (ITERS - 1) + [vmem()],
+        in_specs=[vmem()] * (1 + ITERS),
         out_specs=(hbm(), smem()),
         scratch_shapes=[
-            pltpu.VMEM((ITERS - 1, blocks, vectors, side), jnp.float32),
             pltpu.VMEM((ITERS, blocks, vectors, side), jnp.float32),
             pltpu.SemaphoreType.DMA((ITERS,)),
-            pltpu.SemaphoreType.DMA((ITERS - 1,)),
         ],
         compiler_params=params(),
         name="finish",
-    )(gathered, *[far(power) for power in powers[:-1]], powers[-1])
+    )(gathered, *powers)
     return lax.cond(
         trust[0] > 0,
         lambda *_: krylov,

time: 277 us -> 276 us (level)
  no operation moved by 1% of the time
where the time goes in v10:
time: 276 us; the launch traced here: 274 us
  blocking collectives  159 us (58%)
  starting transfers between devices  39 us (14%)
  waiting for transfers between devices  18.8 us (7%)
  other arithmetic  18 us (7%)
  matrix products  17.5 us (6%)
  Pallas kernels  16.8 us (6%)
  local copies, waits for them, and re-layouts  4.46 us (2%)
    psum x3, blocking collectives, stepwise(): factor = jnp.linalg.cholesky(lax.psum(gram, ('group', 'row')) / row_total)  118 us
    all_gather x3, blocking collectives, stepwise(): lax.all_gather(scaled, 'row', axis=0, tiled=True)  30.3 us
    dot_general x3, matrix products, stepwise(): jnp.einsum('btij,btkj->bki', tiles, picked, precision=HIGH, preferred_ele...  15.5 us
    ppermute x6, starting transfers between devices, swap(): lax.ppermute(x, 'group', pair)  13.4 us
    pallas_call x3, Pallas kernels, local(): pl.pallas_call(functools.partial(apply_kernel, t), out_shape=tuple(shapes...  11.4 us
    all_gather x1, blocking collectives, local(): received = lax.all_gather(scaled, 'row', axis=0)  10 us
    ppermute x3, waiting for transfers between devices, neighbours(): high = lax.ppermute(scaled[:RIM], 'group', down)  8.42 us
    all_to_all x1, waiting for transfers between devices, local(): gathered = lax.all_to_all(grams[-1], ('group', 'row'), 0, 0, tiled=True)  8.23 us
  transfers between devices with their start and end apart: 15, of which 5 were waited for; matrix products, arithmetic and copies ran while one was open for 0% of the time, Pallas kernels for 0%

profile of v10, /device:TPU:0, one launch (start us, length us, event | category | flops | bytes accessed | tf_op | source)
XLA Modules:
  0.0 274.4 jit_solution(2187846589744678676)
XLA Ops:
  0.1 3.5 %roots.1 = (f32[8,1,128]{2,1,0:T(1,128)S(1)}, f32[9,16,128]{2,1,0:T(8,128)S(1)}, f32[2,16,128]{2,1,0:T(8,128)S(1)}, f32[2,16,128]{2,1,0:T(8,128)S(1)}, bf16[1024...) custom-call(s32[2]{0:T(128)S(1)} %pad_add_fusion.place_ref.refs_0_, s32[8]{0:T(128)} %refs_1_.5, s32[2,8]{1,0:T(2,128)} %bitcast.109, ...), custom_call_target="tpu_custom_call" | custom-call | flops 4194304 | bytes 4194304 | tf_op jit(solution)/shard_map/roots/pallas_call | solution.py:367
  3.6 3.1 %collective-permute-start.6 = (f32[2,16,128]{2,1,0:T(8,128)S(1)}, f32[2,16,128]{2,1,0:T(8,128)S(1)}, u32[]{:S(2)}, u32[]{:S(2)}) collective-permute-start(f32[2,16,128]{2,1,0:T(8,128)S(1)} %get-tuple-element.55), channel_id=1, source_target_pairs={{0,8},{16,24},{8,0},{24,16},{1,9},{17,25},{9,1},{25,17},{2,10},{18... | collective-permute-start | bytes 49160 | tf_op jit(solution)/shard_map/ppermute | solution.py:317
  6.7 0.7 collective-permute-start.7
  7.3 10.0 %all-gather = f32[72,16,128]{2,1,0:T(8,128)S(1)} all-gather(f32[9,16,128]{2,1,0:T(8,128)S(1)} %get-tuple-element.54.refs_7_), channel_id=2, replica_groups=mesh['group'=4,'row'=8] {'row'}, dimensions={0}, use_global_device_ids=true | all-gather | bytes 663552 | tf_op jit(solution)/shard_map/all_gather | solution.py:395
  17.4 2.8 %apply.2 = (f32[8,16,128]{2,1,0:T(8,128)S(1)}, f32[16,16]{1,0:T(8,128)S(1)}, f32[8,16,128]{2,1,0:T(8,128)S(1)}, f32[16,16,128]{2,1,0:T(8,128)}, f32[2,16,128]{2,...) custom-call(s32[2]{0:T(128)S(1)} %pad_add_fusion.place_ref.refs_0_, s32[8]{0:T(128)S(1)} %copy-done.2, ...), custom_call_target="tpu_custom_call" | custom-call | flops 134217728 | bytes 4194304 | tf_op jit(solution)/shard_map/apply/pallas_call | solution.py:421
  20.2 3.4 %all-to-all-start = ((f32[16,16,128]{2,1,0:T(8,128)}), f32[16,16,128]{2,1,0:T(8,128)S(1)}, u32[]{:S(2)}, u32[]{:S(2)}) async-start(f32[16,16,128]{2,1,0:T(8,128)} %get-tuple-element.58), calls=%async_computation | async-start | bytes 262144 | tf_op jit(solution)/shard_map/all_to_all | solution.py:397
  23.6 4.5 %collective-permute-start.8 = (f32[2,16,128]{2,1,0:T(8,128)S(1)}, f32[2,16,128]{2,1,0:T(8,128)S(1)}, u32[]{:S(2)}, u32[]{:S(2)}) collective-permute-start(f32[2,16,128]{2,1,0:T(8,128)S(1)} %get-tuple-element.59), channel_id=1, source_target_pairs={{0,8},{16,24},{8,0},{24,16},{1,9},{17,25},{9,1},{25,17},{2,10},{18... | collective-permute-start | bytes 49160 | tf_op jit(solution)/shard_map/ppermute | solution.py:317
  28.0 0.7 collective-permute-start.9
  28.7 1.1 collective-permute-done.8.refs_8_
  29.7 4.1 %apply.3 = (f32[8,16,128]{2,1,0:T(8,128)S(1)}, f32[16,16]{1,0:T(8,128)S(1)}, f32[8,16,128]{2,1,0:T(8,128)S(1)}, f32[16,16,128]{2,1,0:T(8,128)}, f32[2,16,128]{2,1,0:T(8,128)S(1)}, /*index=5*/f32[2,16,128]{2,1,0:T(8,128)S(1)}) custom-call(s32[2]{0:T(128)S(1)} %pad_add_fusion.place_ref.refs_0_, s32[8]{0:T(128)S(1)} %copy-done.2, s32[8,16]{1,0:T(8,128)S(1)} %copy-done.1, ...), custom_call_target="tpu_custom_call" | custom-call | flops 134217728 | bytes 4194304 | tf_op jit(solution)/shard_map/apply/pallas_call | solution.py:421
  33.8 4.2 %all-to-all-start.1 = ((f32[16,16,128]{2,1,0:T(8,128)}), f32[16,16,128]{2,1,0:T(8,128)S(1)}, u32[]{:S(2)}, u32[]{:S(2)}) async-start(f32[16,16,128]{2,1,0:T(8,128)} %get-tuple-element.63), calls=%async_computation.1 | async-start | bytes 262144 | tf_op jit(solution)/shard_map/all_to_all | solution.py:397
  38.0 3.9 %collective-permute-start.10 = (f32[2,16,128]{2,1,0:T(8,128)S(1)}, f32[2,16,128]{2,1,0:T(8,128)S(1)}, u32[]{:S(2)}, u32[]{:S(2)}) collective-permute-start(f32[2,16,128]{2,1,0:T(8,128)S(1)} %get-tuple-element.64), channel_id=1, source_target_pairs={{0,8},{16,24},{8,0},{24,16},{1,9},{17,25},{9,1},{25,17},{2,10},{18... | collective-permute-start | bytes 49160 | tf_op jit(solution)/shard_map/ppermute | solution.py:317
  42.0 0.7 collective-permute-start.11
  42.6 1.1 collective-permute-done.10.refs_8_
  43.7 4.5 %apply_last.1 = (f32[8,16,128]{2,1,0:T(8,128)S(1)}, f32[32,8,128]{2,1,0:T(8,128)}) custom-call(s32[2]{0:T(128)S(1)} %pad_add_fusion.place_ref.refs_0_, s32[8]{0:T(128)S(1)} %copy-done.2, s32[8,16]{1,0:T(8,128)S(1)} %copy-done.1, bf16[16384,128]{1,0:T(8,128)(2,1)} %bitcast.102, bf16[10240,128]{1,0:T(8,128)(2,1)S(1)} %get-tuple-element.51.refs_5_.refs_4_, ...), custom_call_target="tpu_custom_call" | custom-call | flops 134217728 | bytes 4194304 | tf_op jit(solution)/shard_map/apply_last/pallas_call | solution.py:421
  48.2 6.6 %all-to-all-start.2 = ((f32[32,8,128]{2,1,0:T(8,128)}), f32[32,8,128]{2,1,0:T(8,128)S(1)}, u32[]{:S(2)}, u32[]{:S(2)}) async-start(f32[32,8,128]{2,1,0:T(8,128)} %get-tuple-element.68), calls=%async_computation.2 | async-start | bytes 262144 | tf_op jit(solution)/shard_map/all_to_all | solution.py:443
  54.8 8.2 %all-to-all-done.2.grams_ref = f32[32,8,128]{2,1,0:T(8,128)S(1)} async-done(((f32[32,8,128]{2,1,0:T(8,128)}), f32[32,8,128]{2,1,0:T(8,128)S(1)}, u32[]{:S(2)}, u32[]{:S(2)}) %all-to-all-start.2) | async-done | bytes 131104 | tf_op jit(solution)/shard_map/all_to_all | solution.py:443
  63.0 2.0 finish.1
  65.6 208.8 %conditional.1 = (f32[3,8,16,128]{3,2,1,0:T(8,128)}) conditional(s32[]{:T(128)} %bitcast.40, (bf16[8,16,128,128]{3,2,1,0:T(8,128)(2,1)}, s32[8]{0:T(128)S(1)}, f32[8,16,128]{2,1,0:T(8,128)S(1)}, s32[1,1,8,2]{2,3,1,0:T(2,128)S(1)}, s32[8,16]{1,0:T(8,128)S(1)}) %tuple.33, f32[3,8,16,128]{3,2,1,0:T(8,128)} %get-tuple-element.73), branch_computations={%region_0.11_spmd, %region_7.12_spmd} | conditional | flops 1235852416 | bytes 33198924 | solution.py:456
  65.6 4.4 %multiply_reduce_fusion = f32[8,16,128]{2,1,0:T(8,128)S(1)} fusion(bf16[8,16,128,128]{3,2,1,0:T(8,128)(2,1)} %get-tuple-element.22), kind=kLoop, calls=%fused_computation.6 | loop fusion | flops 6275072 | bytes 4259840 | tf_op jit(solution)/shard_map/cond/branch_0_fun/btij,bt->bi/reduce_sum | solution.py:328
  70.4 2.6 collective-permute-start
  72.9 1.3 collective-permute-start.1
  74.2 9.0 %all_gather.10 = f32[64,16,128]{2,1,0:T(8,128)S(1)} all-gather(f32[8,16,128]{2,1,0:T(8,128)S(1)} %broadcast_multiply_fusion), channel_id=1, replica_groups=mesh['group'=4,'row'=8] {'row'}, dimensions={0}, use_global_device_ids=true | all-gather | bytes 589824 | tf_op jit(solution)/shard_map/cond/branch_0_fun/all_gather | solution.py:336
  83.5 0.6 gather_fusion
  84.3 0.8 gather_fusion.1
  85.0 5.2 %fusion.2 = f32[8,16,128]{2,1,0:T(8,128)S(1)} fusion(bf16[8,16,128,128]{3,2,1,0:T(8,128)(2,1)} %get-tuple-element.22, f32[8,16,16,128]{3,2,1,0:T(8,128)S(1)} %bitcast.104, f32[8,16]{1,0:T(8,128)S(1)} %get-tuple-element.96, pred[8,16]{1,0:T(8,128)(4,1)S(1)} %compare_and_fusion, f32[8,128]{1,0:T(8,128)S(1)} %add_power_fusion), kind=kOutput, calls=%fused_computation.13 | convolution fusion | flops 403193856 | bytes 5313152 | tf_op jit(solution)/shard_map/cond/branch_0_fun/btij,btkj->bki/dot_general | solution.py:339
  90.2 0.2 convolution_bitcast_fusion.9
  90.4 40.6 %psum.18 = f32[16,16]{0,1:T(8,128)S(1)} all-reduce(f32[16,16]{0,1:T(8,128)S(1)} %convolution_bitcast_fusion.9), channel_id=1, replica_groups=mesh['group'=4,'row'=8] {'group','row'}, use_global_device_ids=true, to_apply=%region_2.0 | all-reduce | flops 256 | bytes 2048 | tf_op jit(solution)/shard_map/cond/branch_0_fun/psum | solution.py:344
  131.1 1.5 cholesky.59
  132.6 0.7 compare_reduce_fusion.2
  133.3 0.7 fusion.17
  134.0 1.2 custom-call.7
  135.2 0.2 convolution_bitcast_fusion.8
  135.4 0.2 bitcast_multiply_fusion.1
  135.6 10.6 %all_gather.11 = f32[64,16,128]{2,1,0:T(8,128)S(1)} all-gather(f32[8,16,128]{2,1,0:T(8,128)S(1)} %get-tuple-element.98), channel_id=1, replica_groups=mesh['group'=4,'row'=8] {'row'}, dimensions={0}, use_global_device_ids=true | all-gather | bytes 589824 | tf_op jit(solution)/shard_map/cond/branch_0_fun/all_gather | solution.py:336
  146.3 0.6 gather_fusion.2
  146.9 2.3 collective-permute-start.2
  149.2 1.3 collective-permute-start.3
  150.6 4.2 %collective-permute-done.3 = f32[2,16,128]{2,1,0:T(8,128)S(1)} collective-permute-done((f32[2,16,128]{2,1,0:T(8,128)S(1)}, f32[2,16,128]{2,1,0:T(8,128)S(1)}, u32[]{:S(2)}, u32[]{:S(2)}) %collective-permute-start.3) | collective-permute-done | bytes 16416 | tf_op jit(solution)/shard_map/cond/branch_0_fun/ppermute | solution.py:309
  154.9 0.8 gather_fusion.3
  155.6 5.2 %fusion.1 = f32[8,16,128]{2,1,0:T(8,128)S(1)} fusion(bf16[8,16,128,128]{3,2,1,0:T(8,128)(2,1)} %get-tuple-element.22, f32[8,16,16,128]{3,2,1,0:T(8,128)S(1)} %bitcast.105, f32[8,16]{1,0:T(8,128)S(1)} %get-tuple-element.96, pred[8,16]{1,0:T(8,128)(4,1)S(1)} %compare_and_fusion, f32[8,128]{1,0:T(8,128)S(1)} %add_power_fusion), kind=kOutput, calls=%fused_computation.11 | convolution fusion | flops 403193856 | bytes 5313152 | tf_op jit(solution)/shard_map/cond/branch_0_fun/btij,btkj->bki/dot_general | solution.py:339
  160.8 0.2 convolution_bitcast_fusion.7
  161.0 39.2 %psum.19 = f32[16,16]{0,1:T(8,128)S(1)} all-reduce(f32[16,16]{0,1:T(8,128)S(1)} %convolution_bitcast_fusion.7), channel_id=1, replica_groups=mesh['group'=4,'row'=8] {'group','row'}, use_global_device_ids=true, to_apply=%region_5.9 | all-reduce | flops 256 | bytes 2048 | tf_op jit(solution)/shard_map/cond/branch_0_fun/psum | solution.py:344
  200.2 1.5 cholesky.70
  201.7 0.7 compare_reduce_fusion.1
  202.5 0.7 fusion.18
  203.2 1.2 custom-call.8
  204.4 0.2 convolution_bitcast_fusion.6
  204.6 0.2 bitcast_multiply_fusion
  204.8 10.6 %all_gather.12 = f32[64,16,128]{2,1,0:T(8,128)S(1)} all-gather(f32[8,16,128]{2,1,0:T(8,128)S(1)} %get-tuple-element.100), channel_id=1, replica_groups=mesh['group'=4,'row'=8] {'row'}, dimensions={0}, use_global_device_ids=true | all-gather | bytes 589824 | tf_op jit(solution)/shard_map/cond/branch_0_fun/all_gather | solution.py:336
  215.5 0.6 gather_fusion.4
  216.0 2.6 collective-permute-start.4
  218.6 1.3 collective-permute-start.5
  220.0 4.2 %collective-permute-done.5 = f32[2,16,128]{2,1,0:T(8,128)S(1)} collective-permute-done((f32[2,16,128]{2,1,0:T(8,128)S(1)}, f32[2,16,128]{2,1,0:T(8,128)S(1)}, u32[]{:S(2)}, u32[]{:S(2)}) %collective-permute-start.5) | collective-permute-done | bytes 16416 | tf_op jit(solution)/shard_map/cond/branch_0_fun/ppermute | solution.py:309
  224.2 0.8 gather_fusion.5
  225.0 5.2 %fusion = f32[8,16,128]{2,1,0:T(8,128)S(1)} fusion(bf16[8,16,128,128]{3,2,1,0:T(8,128)(2,1)} %get-tuple-element.22, f32[8,16,16,128]{3,2,1,0:T(8,128)S(1)} %bitcast.103, f32[8,16]{1,0:T(8,128)S(1)} %get-tuple-element.96, pred[8,16]{1,0:T(8,128)(4,1)S(1)} %compare_and_fusion, f32[8,128]{1,0:T(8,128)S(1)} %add_power_fusion), kind=kOutput, calls=%fused_computation.9 | convolution fusion | flops 403193856 | bytes 5313152 | tf_op jit(solution)/shard_map/cond/branch_0_fun/btij,btkj->bki/dot_general | solution.py:339
  230.4 38.7 %psum.20 = f32[16,16]{0,1:T(8,128)S(1)} all-reduce(f32[16,16]{0,1:T(8,128)S(1)} %convolution_bitcast_fusion.5), channel_id=1, replica_groups=mesh['group'=4,'row'=8] {'group','row'}, use_global_device_ids=true, to_apply=%region_6.10 | all-reduce | flops 256 | bytes 2048 | tf_op jit(solution)/shard_map/cond/branch_0_fun/psum | solution.py:344
  269.1 1.5 cholesky.81
  270.6 0.7 compare_reduce_fusion
  271.3 0.7 fusion.19
  272.0 1.2 custom-call.9
  273.3 0.2 convolution_bitcast_fusion.4
  273.5 0.2 convolution_bitcast_fusion
  273.7 0.7 pad_maximum_fusion.3
  (55 shorter events, 1.6 us)
Async XLA Ops:
  0.0 17.3 %copy-start.3 = (s32[1,1,8,2]{2,3,1,0:T(2,128)S(1)}, s32[1,1,8,2]{2,3,1,0:T(2,128)}, u32[]{:S(2)}) copy-start(s32[1,1,8,2]{2,3,1,0:T(2,128)} %param.18) | copy-start | bytes 196
  0.0 17.4 %copy-start.2 = (s32[8]{0:T(128)S(1)}, s32[8]{0:T(128)}, u32[]{:S(2)}) copy-start(s32[8]{0:T(128)} %refs_1_.5) | copy-start | bytes 100
  0.0 17.4 %copy-start.1 = (s32[8,16]{1,0:T(8,128)S(1)}, s32[8,16]{1,0:T(8,128)}, u32[]{:S(2)}) copy-start(s32[8,16]{1,0:T(8,128)} %refs_2_.5) | copy-start | bytes 1540
  3.6 13.8 %collective-permute-start.6 = (f32[2,16,128]{2,1,0:T(8,128)S(1)}, f32[2,16,128]{2,1,0:T(8,128)S(1)}, u32[]{:S(2)}, u32[]{:S(2)}) collective-permute-start(f32[2,16,128]{2,1,0:T(8,128)S(1)} %get-tuple-element.55), channel_id=1, source_target_pairs={{0,8},{16,24},{8,0},{24,16},{1,9},{17,25},{9,1},{25,17},{2,10},{18... | collective-permute-start | bytes 49160 | tf_op jit(solution)/shard_map/ppermute | solution.py:317
  6.7 10.7 %collective-permute-start.7 = (f32[2,16,128]{2,1,0:T(8,128)S(1)}, f32[2,16,128]{2,1,0:T(8,128)S(1)}, u32[]{:S(2)}, u32[]{:S(2)}) collective-permute-start(f32[2,16,128]{2,1,0:T(8,128)S(1)} %get-tuple-element.56), channel_id=1, source_target_pairs={{8,16},{16,8},{9,17},{17,9},{10,18},{18,10},{11,19},{19,11},{12,20... | collective-permute-start | bytes 49160 | tf_op jit(solution)/shard_map/ppermute | solution.py:317
  20.2 9.6 %all-to-all-start = ((f32[16,16,128]{2,1,0:T(8,128)}), f32[16,16,128]{2,1,0:T(8,128)S(1)}, u32[]{:S(2)}, u32[]{:S(2)}) async-start(f32[16,16,128]{2,1,0:T(8,128)} %get-tuple-element.58), calls=%async_computation | async-start | bytes 262144 | tf_op jit(solution)/shard_map/all_to_all | solution.py:397
  23.6 6.2 %collective-permute-start.8 = (f32[2,16,128]{2,1,0:T(8,128)S(1)}, f32[2,16,128]{2,1,0:T(8,128)S(1)}, u32[]{:S(2)}, u32[]{:S(2)}) collective-permute-start(f32[2,16,128]{2,1,0:T(8,128)S(1)} %get-tuple-element.59), channel_id=1, source_target_pairs={{0,8},{16,24},{8,0},{24,16},{1,9},{17,25},{9,1},{25,17},{2,10},{18... | collective-permute-start | bytes 49160 | tf_op jit(solution)/shard_map/ppermute | solution.py:317
  28.0 1.7 collective-permute-start.9
  33.8 31.8 %copy-start = (f32[8,16,128]{2,1,0:T(8,128)S(1)}, f32[8,16,128]{2,1,0:T(8,128)}, u32[]{:S(2)}) copy-start(f32[8,16,128]{2,1,0:T(8,128)} %basis_hbm.1) | copy-start | bytes 196612
  33.8 9.8 %all-to-all-start.1 = ((f32[16,16,128]{2,1,0:T(8,128)}), f32[16,16,128]{2,1,0:T(8,128)S(1)}, u32[]{:S(2)}, u32[]{:S(2)}) async-start(f32[16,16,128]{2,1,0:T(8,128)} %get-tuple-element.63), calls=%async_computation.1 | async-start | bytes 262144 | tf_op jit(solution)/shard_map/all_to_all | solution.py:397
  38.0 5.6 %collective-permute-start.10 = (f32[2,16,128]{2,1,0:T(8,128)S(1)}, f32[2,16,128]{2,1,0:T(8,128)S(1)}, u32[]{:S(2)}, u32[]{:S(2)}) collective-permute-start(f32[2,16,128]{2,1,0:T(8,128)S(1)} %get-tuple-element.64), channel_id=1, source_target_pairs={{0,8},{16,24},{8,0},{24,16},{1,9},{17,25},{9,1},{25,17},{2,10},{18... | collective-permute-start | bytes 49160 | tf_op jit(solution)/shard_map/ppermute | solution.py:317
  42.0 1.7 collective-permute-start.11
  48.2 14.9 %all-to-all-start.2 = ((f32[32,8,128]{2,1,0:T(8,128)}), f32[32,8,128]{2,1,0:T(8,128)S(1)}, u32[]{:S(2)}, u32[]{:S(2)}) async-start(f32[32,8,128]{2,1,0:T(8,128)} %get-tuple-element.68), calls=%async_computation.2 | async-start | bytes 262144 | tf_op jit(solution)/shard_map/all_to_all | solution.py:443
  70.4 13.9 %collective-permute-start = (f32[2,16,128]{2,1,0:T(8,128)S(1)}, f32[2,16,128]{2,1,0:T(8,128)S(1)}, u32[]{:S(2)}, u32[]{:S(2)}) collective-permute-start(f32[2,16,128]{2,1,0:T(8,128)S(1)} %get-tuple-element.94), channel_id=1, source_target_pairs={{0,8},{8,16},{16,24},{1,9},{9,17},{17,25},{2,10},{10,18},{18,26},{... | collective-permute-start | bytes 49160 | tf_op jit(solution)/shard_map/cond/branch_0_fun/ppermute | solution.py:308
  72.9 11.3 %collective-permute-start.1 = (f32[2,16,128]{2,1,0:T(8,128)S(1)}, f32[2,16,128]{2,1,0:T(8,128)S(1)}, u32[]{:S(2)}, u32[]{:S(2)}) collective-permute-start(f32[2,16,128]{2,1,0:T(8,128)S(1)} %get-tuple-element.95), channel_id=1, source_target_pairs={{8,0},{16,8},{24,16},{9,1},{17,9},{25,17},{10,2},{18,10},{26,18},{... | collective-permute-start | bytes 49160 | tf_op jit(solution)/shard_map/cond/branch_0_fun/ppermute | solution.py:309
  146.9 3.8 %collective-permute-start.2 = (f32[2,16,128]{2,1,0:T(8,128)S(1)}, f32[2,16,128]{2,1,0:T(8,128)S(1)}, u32[]{:S(2)}, u32[]{:S(2)}) collective-permute-start(f32[2,16,128]{2,1,0:T(8,128)S(1)} %get-tuple-element.92), channel_id=1, source_target_pairs={{0,8},{8,16},{16,24},{1,9},{9,17},{17,25},{2,10},{10,18},{18,26},{... | collective-permute-start | bytes 49160 | tf_op jit(solution)/shard_map/cond/branch_0_fun/ppermute | solution.py:308
  149.2 5.6 %collective-permute-start.3 = (f32[2,16,128]{2,1,0:T(8,128)S(1)}, f32[2,16,128]{2,1,0:T(8,128)S(1)}, u32[]{:S(2)}, u32[]{:S(2)}) collective-permute-start(f32[2,16,128]{2,1,0:T(8,128)S(1)} %get-tuple-element.93), channel_id=1, source_target_pairs={{8,0},{16,8},{24,16},{9,1},{17,9},{25,17},{10,2},{18,10},{26,18},{... | collective-permute-start | bytes 49160 | tf_op jit(solution)/shard_map/cond/branch_0_fun/ppermute | solution.py:309
  216.0 4.0 %collective-permute-start.4 = (f32[2,16,128]{2,1,0:T(8,128)S(1)}, f32[2,16,128]{2,1,0:T(8,128)S(1)}, u32[]{:S(2)}, u32[]{:S(2)}) collective-permute-start(f32[2,16,128]{2,1,0:T(8,128)S(1)} %get-tuple-element.90), channel_id=1, source_target_pairs={{0,8},{8,16},{16,24},{1,9},{9,17},{17,25},{2,10},{10,18},{18,26},{... | collective-permute-start | bytes 49160 | tf_op jit(solution)/shard_map/cond/branch_0_fun/ppermute | solution.py:308
  218.6 5.6 %collective-permute-start.5 = (f32[2,16,128]{2,1,0:T(8,128)S(1)}, f32[2,16,128]{2,1,0:T(8,128)S(1)}, u32[]{:S(2)}, u32[]{:S(2)}) collective-permute-start(f32[2,16,128]{2,1,0:T(8,128)S(1)} %get-tuple-element.91), channel_id=1, source_target_pairs={{8,0},{16,8},{24,16},{9,1},{17,9},{25,17},{10,2},{18,10},{26,18},{... | collective-permute-start | bytes 49160 | tf_op jit(solution)/shard_map/cond/branch_0_fun/ppermute | solution.py:309

commit v11 on v10

--- a/solution.py
+++ b/solution.py
@@ -60,30 +60,34 @@
     return copy
 
 
+def start_all(pairs, sems):
+    copies = [
+        pltpu.make_async_copy(source, target, sems.at[n])
+        for n, (source, target) in enumerate(pairs)
+    ]
+    for copy in copies:
+        copy.start()
+    return copies
+
+
 def tile(ref, at):
     side = ref.shape[1]
     return ref[at * side : (at + 1) * side]
 
 
-def roots_kernel(per_row, place_ref, count_hbm, want_hbm, tiles_hbm, basis_hbm, root_ref, sent_ref,
+def roots_kernel(per_row, count_hbm, want_hbm, tiles_hbm, basis_hbm, root_ref, sent_ref,
                  first_ref, second_ref, held_ref, rest_ref, count_ref, want_ref, basis_ref, sems):
     blocks, vectors, side = basis_ref.shape
     held = held_ref.shape[0] // (per_row * side)
     peers = want_ref.shape[1]
+    group = lax.axis_index("group")
     rest_load = load(tiles_hbm, held_ref.shape[0], rest_ref, sems.at[3])
-    small = [
-        pltpu.make_async_copy(source, target, sems.at[n])
-        for n, (source, target) in enumerate(
-            ((count_hbm, count_ref), (want_hbm, want_ref), (basis_hbm, basis_ref))
-        )
-    ]
-    for copy in small:
-        copy.start()
+    small = start_all(((count_hbm, count_ref), (want_hbm, want_ref), (basis_hbm, basis_ref)), sems)
     held_load = load(tiles_hbm, 0, held_ref, sems.at[4])
     for copy in small:
         copy.wait()
     for p in range(peers):
-        owned = (place_ref[0] * peers + p) * blocks
+        owned = (group * peers + p) * blocks
         for c in range(SLOTS):
             at = jnp.full((1, side), want_ref[c, p] - owned, jnp.int32).astype(jnp.float32)
             block, row = divmod(p * SLOTS + c, vectors)
@@ -104,7 +108,7 @@
         root = lax.rsqrt(jnp.sqrt(1e-06 + sums))
         root_ref[b] = root
         sent_ref[b] = basis_ref[b] * root
-    swaps_into(place_ref[0], blocks, sent_ref, first_ref, second_ref)
+    swaps_into(group, blocks, sent_ref, first_ref, second_ref)
 
 
 def swaps_into(group, blocks, scaled_ref, first_ref, second_ref):
@@ -167,20 +171,23 @@
 
 def apply_kernel(step_at, *refs):
     last, opening = step_at == ITERS - 1, step_at == 0
-    place_ref, count_ref, cols_ref, *refs = refs
+    scalars = 3 if opening else 2
+    scalars_hbm, refs = refs[:scalars], refs[scalars:]
+    tiles_at, held_ref, root_ref, own_ref, recv_ref, swapped_ref, swapped_next_ref, *refs = refs
+    *refs, scalar_sems = refs
+    scalar_refs, refs = refs[-scalars:], refs[:-scalars]
+    count_ref, cols_ref = scalar_refs[:2]
     if opening:
-        want_ref, *refs = refs
-    tiles_at, held_ref, root_ref, own_ref, recv_ref, swapped_ref, swapped_next_ref, *refs = refs
-    if opening:
+        want_ref = scalar_refs[2]
         *refs, table = refs
         rest_ref = tiles_at
     else:
         *refs, table, rest_ref, load_sem = refs
+        rest_load = load(tiles_at, held_ref.shape[0], rest_ref, load_sem)
+    small = start_all(zip(scalars_hbm, scalar_refs), scalar_sems)
     blocks, _, side = root_ref.shape
     per_row = cols_ref.shape[1]
     held = held_ref.shape[0] // (per_row * side)
-    if not opening:
-        rest_load = load(tiles_at, held_ref.shape[0], rest_ref, load_sem)
     if last:
         *before, applied_ref, gram_hbm, packed_ref, sem = refs
     else:
@@ -191,11 +198,13 @@
             asked_ref, *refs = refs
         picked_ref, sem = refs
     vectors = own_ref.shape[1]
-    group = place_ref[0]
+    group = lax.axis_index("group")
     slot = 0
     for b in range(blocks):
         split_into(own_ref[b], table, slot)
         slot += 1
+    for copy in small:
+        copy.wait()
     if opening:
         peers = recv_ref.shape[0]
         for p in range(peers):
@@ -203,7 +212,7 @@
                 at = jnp.clip(want_ref[c, p] - (group * peers + p) * blocks, 0, blocks - 1)
                 split_into(recv_ref[p, at], table, slot)
                 slot += 1
-                entry = place_ref[1] * SLOTS + c
+                entry = lax.axis_index("row") * SLOTS + c
                 asked_ref[p * SLOTS + c : p * SLOTS + c + 1] = recv_ref[
                     p, blocks + entry // vectors, pl.ds(entry % vectors, 1)
                 ]
@@ -354,7 +363,6 @@
     groups, peers = lax.axis_size("group"), lax.axis_size("row")
     blocks, per_row, side, _ = tiles.shape
     vectors = start_basis.shape[1]
-    place = jnp.stack([lax.axis_index("group"), lax.axis_index("row")]).astype(jnp.int32)
     wanted = jnp.transpose(recv_list.reshape(peers, SLOTS))
     lists = pl.cdiv(peers * SLOTS, vectors)
     tile_bytes = tiles.size * 2
@@ -374,7 +382,7 @@
             pltpu.VMEM((kept * per_row * side, side), tiles.dtype),
             rest,
         ),
-        in_specs=[smem()] + [hbm()] * 4,
+        in_specs=[hbm()] * 4,
         out_specs=(vmem(),) * 6,
         scratch_shapes=[
             pltpu.SMEM((blocks,), jnp.int32),
@@ -385,7 +393,7 @@
         compiler_params=params(),
         cost_estimate=cost(tiles.size * 2, tile_bytes),
         name="roots",
-    )(place, far(tile_count), far(wanted), far_tiles, far(start_basis))
+    )(far(tile_count), far(wanted), far_tiles, far(start_basis))
     slots = blocks + peers * SLOTS + 2 * RIM
     powers, grams = [], []
     for t in range(ITERS):
@@ -396,7 +404,7 @@
         else:
             received = lax.all_to_all(outgoing, "row", 0, 0, tiled=True)
             beside = swap(*rims)
-        scalars = [place, tile_count, tile_cols] + ([wanted] if t == 0 else [])
+        scalars = [tile_count, tile_cols] + ([wanted] if t == 0 else [])
         arrays = [far_tiles if t else opening_rest, held, root, scaled, received, *beside]
         shapes = [f32(blocks, *block_shape)]
         specs = [vmem(), vmem()]
@@ -421,7 +429,7 @@
         result = pl.pallas_call(
             functools.partial(apply_kernel, t),
             out_shape=tuple(shapes),
-            in_specs=[smem()] * len(scalars)
+            in_specs=[hbm()] * len(scalars)
             + [hbm() if t else vmem()]
             + [vmem()] * (len(arrays) - 1),
             out_specs=tuple(specs),
@@ -429,11 +437,13 @@
             + [
                 pltpu.VMEM((slots + 1, PIECES * vectors, side), jnp.bfloat16),
             ]
-            + ([rest, pltpu.SemaphoreType.DMA] if t else []),
+            + ([rest, pltpu.SemaphoreType.DMA] if t else [])
+            + [pltpu.SMEM(x.shape, jnp.int32) for x in scalars]
+            + [pltpu.SemaphoreType.DMA((len(scalars),))],
             compiler_params=params(),
             cost_estimate=cost(tiles.size * 2 * vectors * PIECES, tile_bytes),
             name="apply_last" if last else "apply",
-        )(*scalars, *arrays)
+        )(*[far(x) for x in scalars], *arrays)
         powers.append(result[0])
         grams.append(result[1])
         if not last:

time: 276 us -> 274 us (level)
  no operation moved by 1% of the time
where the time goes in v11:
time: 274 us; the launch traced here: 272 us
  blocking collectives  159 us (58%)
  starting transfers between devices  38.9 us (14%)
  waiting for transfers between devices  18.8 us (7%)
  other arithmetic  18 us (7%)
  matrix products  17.5 us (6%)
  Pallas kernels  14.9 us (5%)
  local copies, waits for them, and re-layouts  4.47 us (2%)
    psum x3, blocking collectives, stepwise(): factor = jnp.linalg.cholesky(lax.psum(gram, ('group', 'row')) / row_total)  118 us
    all_gather x3, blocking collectives, stepwise(): lax.all_gather(scaled, 'row', axis=0, tiled=True)  30.3 us
    dot_general x3, matrix products, stepwise(): jnp.einsum('btij,btkj->bki', tiles, picked, precision=HIGH, preferred_ele...  15.5 us
    ppermute x6, starting transfers between devices, swap(): lax.ppermute(x, 'group', pair)  13.4 us
    all_gather x1, blocking collectives, local(): received = lax.all_gather(scaled, 'row', axis=0)  10 us
    pallas_call x3, Pallas kernels, local(): pl.pallas_call(functools.partial(apply_kernel, t), out_shape=tuple(shapes...  9.98 us
    ppermute x3, waiting for transfers between devices, neighbours(): high = lax.ppermute(scaled[:RIM], 'group', down)  8.42 us
    all_to_all x1, waiting for transfers between devices, local(): gathered = lax.all_to_all(grams[-1], ('group', 'row'), 0, 0, tiled=True)  8.23 us
  transfers between devices with their start and end apart: 15, of which 5 were waited for; matrix products, arithmetic and copies ran while one was open for 0% of the time, Pallas kernels for 0%

profile of v11, /device:TPU:0, one launch (start us, length us, event | category | flops | bytes accessed | tf_op | source)
XLA Modules:
  0.0 272.4 jit_solution(3287563344038991727)
XLA Ops:
  0.0 2.9 %roots.1 = (f32[8,1,128]{2,1,0:T(1,128)S(1)}, f32[9,16,128]{2,1,0:T(8,128)S(1)}, f32[2,16,128]{2,1,0:T(8,128)S(1)}, f32[2,16,128]{2,1,0:T(8,128)S(1)}, bf16[1024...) custom-call(s32[8]{0:T(128)} %refs_0_.5, s32[2,8]{1,0:T(2,128)} %bitcast.107, bf16[16384,128]{1,0:T(8,128)(2,1)} %bitcast.98, ...), custom_call_target="tpu_custom_call" | custom-call | flops 4194304 | bytes 4194304 | tf_op jit(solution)/shard_map/roots/pallas_call | solution.py:375
  3.0 3.1 %collective-permute-start.6 = (f32[2,16,128]{2,1,0:T(8,128)S(1)}, f32[2,16,128]{2,1,0:T(8,128)S(1)}, u32[]{:S(2)}, u32[]{:S(2)}) collective-permute-start(f32[2,16,128]{2,1,0:T(8,128)S(1)} %get-tuple-element.55), channel_id=1, source_target_pairs={{0,8},{16,24},{8,0},{24,16},{1,9},{17,25},{9,1},{25,17},{2,10},{18... | collective-permute-start | bytes 49160 | tf_op jit(solution)/shard_map/ppermute | solution.py:326
  6.0 0.7 collective-permute-start.7
  6.7 10.0 %all-gather = f32[72,16,128]{2,1,0:T(8,128)S(1)} all-gather(f32[9,16,128]{2,1,0:T(8,128)S(1)} %get-tuple-element.54.refs_6_), channel_id=2, replica_groups=mesh['group'=4,'row'=8] {'row'}, dimensions={0}, use_global_device_ids=true | all-gather | bytes 663552 | tf_op jit(solution)/shard_map/all_gather | solution.py:403
  16.7 2.9 %apply.2 = (f32[8,16,128]{2,1,0:T(8,128)S(1)}, f32[16,16]{1,0:T(8,128)S(1)}, f32[8,16,128]{2,1,0:T(8,128)S(1)}, f32[16,16,128]{2,1,0:T(8,128)}, f32[2,16,128]{2,...) custom-call(s32[8]{0:T(128)} %refs_0_.5, s32[8,16]{1,0:T(8,128)} %refs_1_.5, s32[2,8]{1,0:T(2,128)} %bitcast.108, ...), custom_call_target="tpu_custom_call" | custom-call | flops 134217728 | bytes 4194304 | tf_op jit(solution)/shard_map/apply/pallas_call | solution.py:429
  19.7 3.4 %all-to-all-start = ((f32[16,16,128]{2,1,0:T(8,128)}), f32[16,16,128]{2,1,0:T(8,128)S(1)}, u32[]{:S(2)}, u32[]{:S(2)}) async-start(f32[16,16,128]{2,1,0:T(8,128)} %get-tuple-element.58), calls=%async_computation | async-start | bytes 262144 | tf_op jit(solution)/shard_map/all_to_all | solution.py:405
  23.0 4.5 %collective-permute-start.8 = (f32[2,16,128]{2,1,0:T(8,128)S(1)}, f32[2,16,128]{2,1,0:T(8,128)S(1)}, u32[]{:S(2)}, u32[]{:S(2)}) collective-permute-start(f32[2,16,128]{2,1,0:T(8,128)S(1)} %get-tuple-element.59), channel_id=1, source_target_pairs={{0,8},{16,24},{8,0},{24,16},{1,9},{17,25},{9,1},{25,17},{2,10},{18... | collective-permute-start | bytes 49160 | tf_op jit(solution)/shard_map/ppermute | solution.py:326
  27.5 0.7 collective-permute-start.9
  28.2 1.1 collective-permute-done.8.refs_7_
  29.2 3.3 %apply.3 = (f32[8,16,128]{2,1,0:T(8,128)S(1)}, f32[16,16]{1,0:T(8,128)S(1)}, f32[8,16,128]{2,1,0:T(8,128)S(1)}, f32[16,16,128]{2,1,0:T(8,128)}, f32[2,16,128]{2,1,0:T(8,128)S(1)}, /*index=5*/f32[2,16,128]{2,1,0:T(8,128)S(1)}) custom-call(s32[8]{0:T(128)} %refs_0_.5, s32[8,16]{1,0:T(8,128)} %refs_1_.5, bf16[16384,128]{1,0:T(8,128)(2,1)} %bitcast.99, ...), custom_call_target="tpu_custom_call" | custom-call | flops 134217728 | bytes 4194304 | tf_op jit(solution)/shard_map/apply/pallas_call | solution.py:429
  32.6 4.2 %all-to-all-start.1 = ((f32[16,16,128]{2,1,0:T(8,128)}), f32[16,16,128]{2,1,0:T(8,128)S(1)}, u32[]{:S(2)}, u32[]{:S(2)}) async-start(f32[16,16,128]{2,1,0:T(8,128)} %get-tuple-element.63), calls=%async_computation.1 | async-start | bytes 262144 | tf_op jit(solution)/shard_map/all_to_all | solution.py:405
  36.8 3.9 %collective-permute-start.10 = (f32[2,16,128]{2,1,0:T(8,128)S(1)}, f32[2,16,128]{2,1,0:T(8,128)S(1)}, u32[]{:S(2)}, u32[]{:S(2)}) collective-permute-start(f32[2,16,128]{2,1,0:T(8,128)S(1)} %get-tuple-element.64), channel_id=1, source_target_pairs={{0,8},{16,24},{8,0},{24,16},{1,9},{17,25},{9,1},{25,17},{2,10},{18... | collective-permute-start | bytes 49160 | tf_op jit(solution)/shard_map/ppermute | solution.py:326
  40.7 0.7 collective-permute-start.11
  41.4 1.1 collective-permute-done.10.refs_7_
  42.4 3.7 %apply_last.1 = (f32[8,16,128]{2,1,0:T(8,128)S(1)}, f32[32,8,128]{2,1,0:T(8,128)}) custom-call(s32[8]{0:T(128)} %refs_0_.5, s32[8,16]{1,0:T(8,128)} %refs_1_.5, bf16[16384,128]{1,0:T(8,128)(2,1)} %bitcast.100, bf16[10240,128]{1,0:T(8,128)(2,1)S(1)} %get-tuple-element.51.refs_4_.refs_3_, f32[8,1,128]{2,1,0:T(1,128)S(1)} %get-tuple-element.52.refs_5_.refs_4_, ...), custom_call_target="tpu_custom_call" | custom-call | flops 134217728 | bytes 4194304 | tf_op jit(solution)/shard_map/apply_last/pallas_call | solution.py:429
  46.2 6.6 %all-to-all-start.2 = ((f32[32,8,128]{2,1,0:T(8,128)}), f32[32,8,128]{2,1,0:T(8,128)S(1)}, u32[]{:S(2)}, u32[]{:S(2)}) async-start(f32[32,8,128]{2,1,0:T(8,128)} %get-tuple-element.68), calls=%async_computation.2 | async-start | bytes 262144 | tf_op jit(solution)/shard_map/all_to_all | solution.py:453
  52.8 8.2 %all-to-all-done.2.grams_ref = f32[32,8,128]{2,1,0:T(8,128)S(1)} async-done(((f32[32,8,128]{2,1,0:T(8,128)}), f32[32,8,128]{2,1,0:T(8,128)S(1)}, u32[]{:S(2)}, u32[]{:S(2)}) %all-to-all-start.2) | async-done | bytes 131104 | tf_op jit(solution)/shard_map/all_to_all | solution.py:453
  61.0 2.0 finish.1
  63.7 208.7 %conditional.1 = (f32[3,8,16,128]{3,2,1,0:T(8,128)}) conditional(s32[]{:T(128)} %bitcast.38, (bf16[8,16,128,128]{3,2,1,0:T(8,128)(2,1)}, s32[8]{0:T(128)S(1)}, f32[8,16,128]{2,1,0:T(8,128)S(1)}, s32[1,1,8,2]{2,3,1,0:T(2,128)S(1)}, s32[8,16]{1,0:T(8,128)S(1)}) %tuple.33, f32[3,8,16,128]{3,2,1,0:T(8,128)} %get-tuple-element.73), branch_computations={%region_0.11_spmd, %region_7.12_spmd} | conditional | flops 1235852416 | bytes 33198924 | solution.py:466
  63.7 4.4 %multiply_reduce_fusion = f32[8,16,128]{2,1,0:T(8,128)S(1)} fusion(bf16[8,16,128,128]{3,2,1,0:T(8,128)(2,1)} %get-tuple-element.22), kind=kLoop, calls=%fused_computation.6 | loop fusion | flops 6275072 | bytes 4259840 | tf_op jit(solution)/shard_map/cond/branch_0_fun/btij,bt->bi/reduce_sum | solution.py:337
  68.4 2.6 collective-permute-start
  70.9 1.3 collective-permute-start.1
  72.2 9.0 %all_gather.10 = f32[64,16,128]{2,1,0:T(8,128)S(1)} all-gather(f32[8,16,128]{2,1,0:T(8,128)S(1)} %broadcast_multiply_fusion), channel_id=1, replica_groups=mesh['group'=4,'row'=8] {'row'}, dimensions={0}, use_global_device_ids=true | all-gather | bytes 589824 | tf_op jit(solution)/shard_map/cond/branch_0_fun/all_gather | solution.py:345
  81.6 0.6 gather_fusion
  82.3 0.8 gather_fusion.1
  83.1 5.2 %fusion.2 = f32[8,16,128]{2,1,0:T(8,128)S(1)} fusion(bf16[8,16,128,128]{3,2,1,0:T(8,128)(2,1)} %get-tuple-element.22, f32[8,16,16,128]{3,2,1,0:T(8,128)S(1)} %bitcast.102, f32[8,16]{1,0:T(8,128)S(1)} %get-tuple-element.96, pred[8,16]{1,0:T(8,128)(4,1)S(1)} %compare_and_fusion, f32[8,128]{1,0:T(8,128)S(1)} %add_power_fusion), kind=kOutput, calls=%fused_computation.13 | convolution fusion | flops 403193856 | bytes 5313152 | tf_op jit(solution)/shard_map/cond/branch_0_fun/btij,btkj->bki/dot_general | solution.py:348
  88.2 0.2 convolution_bitcast_fusion.9
  88.4 40.6 %psum.18 = f32[16,16]{0,1:T(8,128)S(1)} all-reduce(f32[16,16]{0,1:T(8,128)S(1)} %convolution_bitcast_fusion.9), channel_id=1, replica_groups=mesh['group'=4,'row'=8] {'group','row'}, use_global_device_ids=true, to_apply=%region_2.0 | all-reduce | flops 256 | bytes 2048 | tf_op jit(solution)/shard_map/cond/branch_0_fun/psum | solution.py:353
  129.1 1.5 cholesky.59
  130.6 0.7 compare_reduce_fusion.2
  131.3 0.7 fusion.17
  132.0 1.2 custom-call.7
  133.3 0.2 convolution_bitcast_fusion.8
  133.5 0.2 bitcast_multiply_fusion.1
  133.7 10.6 %all_gather.11 = f32[64,16,128]{2,1,0:T(8,128)S(1)} all-gather(f32[8,16,128]{2,1,0:T(8,128)S(1)} %get-tuple-element.98), channel_id=1, replica_groups=mesh['group'=4,'row'=8] {'row'}, dimensions={0}, use_global_device_ids=true | all-gather | bytes 589824 | tf_op jit(solution)/shard_map/cond/branch_0_fun/all_gather | solution.py:345
  144.3 0.6 gather_fusion.2
  144.9 2.3 collective-permute-start.2
  147.2 1.3 collective-permute-start.3
  148.7 4.2 %collective-permute-done.3 = f32[2,16,128]{2,1,0:T(8,128)S(1)} collective-permute-done((f32[2,16,128]{2,1,0:T(8,128)S(1)}, f32[2,16,128]{2,1,0:T(8,128)S(1)}, u32[]{:S(2)}, u32[]{:S(2)}) %collective-permute-start.3) | collective-permute-done | bytes 16416 | tf_op jit(solution)/shard_map/cond/branch_0_fun/ppermute | solution.py:318
  152.9 0.8 gather_fusion.3
  153.7 5.2 %fusion.1 = f32[8,16,128]{2,1,0:T(8,128)S(1)} fusion(bf16[8,16,128,128]{3,2,1,0:T(8,128)(2,1)} %get-tuple-element.22, f32[8,16,16,128]{3,2,1,0:T(8,128)S(1)} %bitcast.103, f32[8,16]{1,0:T(8,128)S(1)} %get-tuple-element.96, pred[8,16]{1,0:T(8,128)(4,1)S(1)} %compare_and_fusion, f32[8,128]{1,0:T(8,128)S(1)} %add_power_fusion), kind=kOutput, calls=%fused_computation.11 | convolution fusion | flops 403193856 | bytes 5313152 | tf_op jit(solution)/shard_map/cond/branch_0_fun/btij,btkj->bki/dot_general | solution.py:348
  158.8 0.2 convolution_bitcast_fusion.7
  159.0 39.2 %psum.19 = f32[16,16]{0,1:T(8,128)S(1)} all-reduce(f32[16,16]{0,1:T(8,128)S(1)} %convolution_bitcast_fusion.7), channel_id=1, replica_groups=mesh['group'=4,'row'=8] {'group','row'}, use_global_device_ids=true, to_apply=%region_5.9 | all-reduce | flops 256 | bytes 2048 | tf_op jit(solution)/shard_map/cond/branch_0_fun/psum | solution.py:353
  198.3 1.5 cholesky.70
  199.8 0.7 compare_reduce_fusion.1
  200.5 0.7 fusion.18
  201.2 1.2 custom-call.8
  202.4 0.2 convolution_bitcast_fusion.6
  202.6 0.2 bitcast_multiply_fusion
  202.8 10.6 %all_gather.12 = f32[64,16,128]{2,1,0:T(8,128)S(1)} all-gather(f32[8,16,128]{2,1,0:T(8,128)S(1)} %get-tuple-element.100), channel_id=1, replica_groups=mesh['group'=4,'row'=8] {'row'}, dimensions={0}, use_global_device_ids=true | all-gather | bytes 589824 | tf_op jit(solution)/shard_map/cond/branch_0_fun/all_gather | solution.py:345
  213.5 0.6 gather_fusion.4
  214.1 2.6 collective-permute-start.4
  216.6 1.3 collective-permute-start.5
  218.0 4.2 %collective-permute-done.5 = f32[2,16,128]{2,1,0:T(8,128)S(1)} collective-permute-done((f32[2,16,128]{2,1,0:T(8,128)S(1)}, f32[2,16,128]{2,1,0:T(8,128)S(1)}, u32[]{:S(2)}, u32[]{:S(2)}) %collective-permute-start.5) | collective-permute-done | bytes 16416 | tf_op jit(solution)/shard_map/cond/branch_0_fun/ppermute | solution.py:318
  222.3 0.8 gather_fusion.5
  223.0 5.2 %fusion = f32[8,16,128]{2,1,0:T(8,128)S(1)} fusion(bf16[8,16,128,128]{3,2,1,0:T(8,128)(2,1)} %get-tuple-element.22, f32[8,16,16,128]{3,2,1,0:T(8,128)S(1)} %bitcast.101, f32[8,16]{1,0:T(8,128)S(1)} %get-tuple-element.96, pred[8,16]{1,0:T(8,128)(4,1)S(1)} %compare_and_fusion, f32[8,128]{1,0:T(8,128)S(1)} %add_power_fusion), kind=kOutput, calls=%fused_computation.9 | convolution fusion | flops 403193856 | bytes 5313152 | tf_op jit(solution)/shard_map/cond/branch_0_fun/btij,btkj->bki/dot_general | solution.py:348
  228.4 38.7 %psum.20 = f32[16,16]{0,1:T(8,128)S(1)} all-reduce(f32[16,16]{0,1:T(8,128)S(1)} %convolution_bitcast_fusion.5), channel_id=1, replica_groups=mesh['group'=4,'row'=8] {'group','row'}, use_global_device_ids=true, to_apply=%region_6.10 | all-reduce | flops 256 | bytes 2048 | tf_op jit(solution)/shard_map/cond/branch_0_fun/psum | solution.py:353
  267.1 1.5 cholesky.81
  268.6 0.7 compare_reduce_fusion
  269.4 0.7 fusion.19
  270.1 1.2 custom-call.9
  271.3 0.2 convolution_bitcast_fusion.4
  271.5 0.2 convolution_bitcast_fusion
  271.7 0.7 pad_maximum_fusion.3
  (54 shorter events, 1.5 us)
Async XLA Ops:
  3.0 13.8 %collective-permute-start.6 = (f32[2,16,128]{2,1,0:T(8,128)S(1)}, f32[2,16,128]{2,1,0:T(8,128)S(1)}, u32[]{:S(2)}, u32[]{:S(2)}) collective-permute-start(f32[2,16,128]{2,1,0:T(8,128)S(1)} %get-tuple-element.55), channel_id=1, source_target_pairs={{0,8},{16,24},{8,0},{24,16},{1,9},{17,25},{9,1},{25,17},{2,10},{18... | collective-permute-start | bytes 49160 | tf_op jit(solution)/shard_map/ppermute | solution.py:326
  6.0 10.7 %collective-permute-start.7 = (f32[2,16,128]{2,1,0:T(8,128)S(1)}, f32[2,16,128]{2,1,0:T(8,128)S(1)}, u32[]{:S(2)}, u32[]{:S(2)}) collective-permute-start(f32[2,16,128]{2,1,0:T(8,128)S(1)} %get-tuple-element.56), channel_id=1, source_target_pairs={{8,16},{16,8},{9,17},{17,9},{10,18},{18,10},{11,19},{19,11},{12,20... | collective-permute-start | bytes 49160 | tf_op jit(solution)/shard_map/ppermute | solution.py:326
  19.7 9.6 %all-to-all-start = ((f32[16,16,128]{2,1,0:T(8,128)}), f32[16,16,128]{2,1,0:T(8,128)S(1)}, u32[]{:S(2)}, u32[]{:S(2)}) async-start(f32[16,16,128]{2,1,0:T(8,128)} %get-tuple-element.58), calls=%async_computation | async-start | bytes 262144 | tf_op jit(solution)/shard_map/all_to_all | solution.py:405
  23.0 6.2 %collective-permute-start.8 = (f32[2,16,128]{2,1,0:T(8,128)S(1)}, f32[2,16,128]{2,1,0:T(8,128)S(1)}, u32[]{:S(2)}, u32[]{:S(2)}) collective-permute-start(f32[2,16,128]{2,1,0:T(8,128)S(1)} %get-tuple-element.59), channel_id=1, source_target_pairs={{0,8},{16,24},{8,0},{24,16},{1,9},{17,25},{9,1},{25,17},{2,10},{18... | collective-permute-start | bytes 49160 | tf_op jit(solution)/shard_map/ppermute | solution.py:326
  27.5 1.7 collective-permute-start.9
  32.6 31.0 %copy-start = (f32[8,16,128]{2,1,0:T(8,128)S(1)}, f32[8,16,128]{2,1,0:T(8,128)}, u32[]{:S(2)}) copy-start(f32[8,16,128]{2,1,0:T(8,128)} %basis_hbm.1) | copy-start | bytes 196612
  32.6 31.0 %copy-start.1 = (s32[8,16]{1,0:T(8,128)S(1)}, s32[8,16]{1,0:T(8,128)}, u32[]{:S(2)}) copy-start(s32[8,16]{1,0:T(8,128)} %refs_1_.5) | copy-start | bytes 1540
  32.6 31.0 %copy-start.2 = (s32[8]{0:T(128)S(1)}, s32[8]{0:T(128)}, u32[]{:S(2)}) copy-start(s32[8]{0:T(128)} %refs_0_.5) | copy-start | bytes 100
  32.6 31.0 %copy-start.3 = (s32[1,1,8,2]{2,3,1,0:T(2,128)S(1)}, s32[1,1,8,2]{2,3,1,0:T(2,128)}, u32[]{:S(2)}) copy-start(s32[1,1,8,2]{2,3,1,0:T(2,128)} %param.18) | copy-start | bytes 196
  32.6 9.8 %all-to-all-start.1 = ((f32[16,16,128]{2,1,0:T(8,128)}), f32[16,16,128]{2,1,0:T(8,128)S(1)}, u32[]{:S(2)}, u32[]{:S(2)}) async-start(f32[16,16,128]{2,1,0:T(8,128)} %get-tuple-element.63), calls=%async_computation.1 | async-start | bytes 262144 | tf_op jit(solution)/shard_map/all_to_all | solution.py:405
  36.8 5.6 %collective-permute-start.10 = (f32[2,16,128]{2,1,0:T(8,128)S(1)}, f32[2,16,128]{2,1,0:T(8,128)S(1)}, u32[]{:S(2)}, u32[]{:S(2)}) collective-permute-start(f32[2,16,128]{2,1,0:T(8,128)S(1)} %get-tuple-element.64), channel_id=1, source_target_pairs={{0,8},{16,24},{8,0},{24,16},{1,9},{17,25},{9,1},{25,17},{2,10},{18... | collective-permute-start | bytes 49160 | tf_op jit(solution)/shard_map/ppermute | solution.py:326
  40.7 1.7 collective-permute-start.11
  46.2 14.9 %all-to-all-start.2 = ((f32[32,8,128]{2,1,0:T(8,128)}), f32[32,8,128]{2,1,0:T(8,128)S(1)}, u32[]{:S(2)}, u32[]{:S(2)}) async-start(f32[32,8,128]{2,1,0:T(8,128)} %get-tuple-element.68), calls=%async_computation.2 | async-start | bytes 262144 | tf_op jit(solution)/shard_map/all_to_all | solution.py:453
  68.4 13.9 %collective-permute-start = (f32[2,16,128]{2,1,0:T(8,128)S(1)}, f32[2,16,128]{2,1,0:T(8,128)S(1)}, u32[]{:S(2)}, u32[]{:S(2)}) collective-permute-start(f32[2,16,128]{2,1,0:T(8,128)S(1)} %get-tuple-element.94), channel_id=1, source_target_pairs={{0,8},{8,16},{16,24},{1,9},{9,17},{17,25},{2,10},{10,18},{18,26},{... | collective-permute-start | bytes 49160 | tf_op jit(solution)/shard_map/cond/branch_0_fun/ppermute | solution.py:317
  70.9 11.3 %collective-permute-start.1 = (f32[2,16,128]{2,1,0:T(8,128)S(1)}, f32[2,16,128]{2,1,0:T(8,128)S(1)}, u32[]{:S(2)}, u32[]{:S(2)}) collective-permute-start(f32[2,16,128]{2,1,0:T(8,128)S(1)} %get-tuple-element.95), channel_id=1, source_target_pairs={{8,0},{16,8},{24,16},{9,1},{17,9},{25,17},{10,2},{18,10},{26,18},{... | collective-permute-start | bytes 49160 | tf_op jit(solution)/shard_map/cond/branch_0_fun/ppermute | solution.py:318
  144.9 3.8 %collective-permute-start.2 = (f32[2,16,128]{2,1,0:T(8,128)S(1)}, f32[2,16,128]{2,1,0:T(8,128)S(1)}, u32[]{:S(2)}, u32[]{:S(2)}) collective-permute-start(f32[2,16,128]{2,1,0:T(8,128)S(1)} %get-tuple-element.92), channel_id=1, source_target_pairs={{0,8},{8,16},{16,24},{1,9},{9,17},{17,25},{2,10},{10,18},{18,26},{... | collective-permute-start | bytes 49160 | tf_op jit(solution)/shard_map/cond/branch_0_fun/ppermute | solution.py:317
  147.2 5.6 %collective-permute-start.3 = (f32[2,16,128]{2,1,0:T(8,128)S(1)}, f32[2,16,128]{2,1,0:T(8,128)S(1)}, u32[]{:S(2)}, u32[]{:S(2)}) collective-permute-start(f32[2,16,128]{2,1,0:T(8,128)S(1)} %get-tuple-element.93), channel_id=1, source_target_pairs={{8,0},{16,8},{24,16},{9,1},{17,9},{25,17},{10,2},{18,10},{26,18},{... | collective-permute-start | bytes 49160 | tf_op jit(solution)/shard_map/cond/branch_0_fun/ppermute | solution.py:318
  214.1 4.0 %collective-permute-start.4 = (f32[2,16,128]{2,1,0:T(8,128)S(1)}, f32[2,16,128]{2,1,0:T(8,128)S(1)}, u32[]{:S(2)}, u32[]{:S(2)}) collective-permute-start(f32[2,16,128]{2,1,0:T(8,128)S(1)} %get-tuple-element.90), channel_id=1, source_target_pairs={{0,8},{8,16},{16,24},{1,9},{9,17},{17,25},{2,10},{10,18},{18,26},{... | collective-permute-start | bytes 49160 | tf_op jit(solution)/shard_map/cond/branch_0_fun/ppermute | solution.py:317
  216.6 5.6 %collective-permute-start.5 = (f32[2,16,128]{2,1,0:T(8,128)S(1)}, f32[2,16,128]{2,1,0:T(8,128)S(1)}, u32[]{:S(2)}, u32[]{:S(2)}) collective-permute-start(f32[2,16,128]{2,1,0:T(8,128)S(1)} %get-tuple-element.91), channel_id=1, source_target_pairs={{8,0},{16,8},{24,16},{9,1},{17,9},{25,17},{10,2},{18,10},{26,18},{... | collective-permute-start | bytes 49160 | tf_op jit(solution)/shard_map/cond/branch_0_fun/ppermute | solution.py:318

commit v12 on v11

--- a/solution.py
+++ b/solution.py
@@ -12,7 +12,7 @@
 ITERS = 3
 MINLIVE = 10
 LANES = 128
-HELD_BYTES = 5 * 1024 * 1024 // 2
+HELD_BYTES = 11 * 1024 * 1024 // 4
 PIECES = 2
 VMEM_BYTES = 24 * 1024 * 1024
 TRUST = 64.0
@@ -50,8 +50,9 @@
     return pl.CostEstimate(flops=flops, bytes_accessed=moved, transcendentals=0)
 
 
-def held_blocks(tiles):
-    return min(tiles.shape[0] - 1, HELD_BYTES // (tiles.size // tiles.shape[0] * 2))
+def held_tiles(tiles):
+    count = tiles.shape[0] * tiles.shape[1]
+    return min(count - 1, HELD_BYTES // (tiles.size // count * 2))
 
 
 def load(tiles_hbm, start, tiles_ref, sem):
@@ -70,15 +71,17 @@
     return copies
 
 
-def tile(ref, at):
-    side = ref.shape[1]
+def tile(held_ref, rest_ref, at):
+    side = held_ref.shape[1]
+    held = held_ref.shape[0] // side
+    ref, at = (held_ref, at) if at < held else (rest_ref, at - held)
     return ref[at * side : (at + 1) * side]
 
 
 def roots_kernel(per_row, count_hbm, want_hbm, tiles_hbm, basis_hbm, root_ref, sent_ref,
                  first_ref, second_ref, held_ref, rest_ref, count_ref, want_ref, basis_ref, sems):
     blocks, vectors, side = basis_ref.shape
-    held = held_ref.shape[0] // (per_row * side)
+    touched = pl.cdiv(held_ref.shape[0], per_row * side)
     peers = want_ref.shape[1]
     group = lax.axis_index("group")
     rest_load = load(tiles_hbm, held_ref.shape[0], rest_ref, sems.at[3])
@@ -93,13 +96,12 @@
             block, row = divmod(p * SLOTS + c, vectors)
             sent_ref[blocks + block, row : row + 1] = at
     rest_load.wait()
-    for b in list(range(held, blocks)) + list(range(held)):
+    for b in list(range(touched, blocks)) + list(range(touched)):
         if b == 0:
             held_load.wait()
-        tile_ref, first = (held_ref, b * per_row) if b < held else (rest_ref, (b - held) * per_row)
         total = jnp.zeros((side, side), jnp.float32)
         for s in range(per_row):
-            wide = tile(tile_ref, first + s).astype(jnp.float32)
+            wide = tile(held_ref, rest_ref, b * per_row + s).astype(jnp.float32)
             square = wide * wide
             if s >= MINLIVE:
                 square = square * (s < count_ref[b]).astype(jnp.float32)
@@ -235,8 +237,8 @@
         x = jnp.concatenate(picked, axis=1)
         if b == held and not opening:
             rest_load.wait()
-        tile_ref, first = (held_ref, b * per_row) if b < held else (rest_ref, (b - held) * per_row)
-        t = jnp.concatenate([tile(tile_ref, first + s) for s in range(per_row)], axis=1)
+        t = [tile(held_ref, rest_ref, b * per_row + s) for s in range(per_row)]
+        t = jnp.concatenate(t, axis=1)
         product = lax.dot_general(x, t, NT, preferred_element_type=jnp.float32)
         total = product[(PIECES - 1) * vectors :]
         for piece in range(PIECES - 2, -1, -1):
@@ -370,8 +372,8 @@
     block_shape = (vectors, side)
     picked_shape = (peers * SLOTS,) + block_shape
     rim_shape = f32(RIM, *block_shape)
-    kept = held_blocks(tiles)
-    rest = pltpu.VMEM(((blocks - kept) * per_row * side, side), tiles.dtype)
+    kept = held_tiles(tiles)
+    rest = pltpu.VMEM(((blocks * per_row - kept) * side, side), tiles.dtype)
     root, scaled, *rims, held, opening_rest = pl.pallas_call(
         functools.partial(roots_kernel, per_row),
         out_shape=(
@@ -379,7 +381,7 @@
             f32(blocks + lists, *block_shape),
             rim_shape,
             rim_shape,
-            pltpu.VMEM((kept * per_row * side, side), tiles.dtype),
+            pltpu.VMEM((kept * side, side), tiles.dtype),
             rest,
         ),
         in_specs=[hbm()] * 4,

time: 274 us -> 274 us (level)
  no operation moved by 1% of the time
where the time goes in v12:
time: 274 us; the launch traced here: 273 us
  blocking collectives  159 us (58%)
  starting transfers between devices  39 us (14%)
  waiting for transfers between devices  18.8 us (7%)
  other arithmetic  18 us (7%)
  matrix products  17.5 us (6%)
  Pallas kernels  15 us (5%)
  local copies, waits for them, and re-layouts  4.47 us (2%)
    psum x3, blocking collectives, stepwise(): factor = jnp.linalg.cholesky(lax.psum(gram, ('group', 'row')) / row_total)  118 us
    all_gather x3, blocking collectives, stepwise(): lax.all_gather(scaled, 'row', axis=0, tiled=True)  30.3 us
    dot_general x3, matrix products, stepwise(): jnp.einsum('btij,btkj->bki', tiles, picked, precision=HIGH, preferred_ele...  15.5 us
    ppermute x6, starting transfers between devices, swap(): lax.ppermute(x, 'group', pair)  13.4 us
    all_gather x1, blocking collectives, local(): received = lax.all_gather(scaled, 'row', axis=0)  10 us
    pallas_call x3, Pallas kernels, local(): pl.pallas_call(functools.partial(apply_kernel, t), out_shape=tuple(shapes...  9.98 us
    ppermute x3, waiting for transfers between devices, neighbours(): high = lax.ppermute(scaled[:RIM], 'group', down)  8.42 us
    all_to_all x1, waiting for transfers between devices, local(): gathered = lax.all_to_all(grams[-1], ('group', 'row'), 0, 0, tiled=True)  8.23 us
  transfers between devices with their start and end apart: 15, of which 5 were waited for; matrix products, arithmetic and copies ran while one was open for 0% of the time, Pallas kernels for 0%

profile of v12, /device:TPU:0, one launch (start us, length us, event | category | flops | bytes accessed | tf_op | source)
XLA Modules:
  0.0 272.5 jit_solution(8288437071457001398)
XLA Ops:
  0.0 3.1 %roots.1 = (f32[8,1,128]{2,1,0:T(1,128)S(1)}, f32[9,16,128]{2,1,0:T(8,128)S(1)}, f32[2,16,128]{2,1,0:T(8,128)S(1)}, f32[2,16,128]{2,1,0:T(8,128)S(1)}, bf16[1126...) custom-call(s32[8]{0:T(128)} %refs_0_.5, s32[2,8]{1,0:T(2,128)} %bitcast.107, bf16[16384,128]{1,0:T(8,128)(2,1)} %bitcast.98, ...), custom_call_target="tpu_custom_call" | custom-call | flops 4194304 | bytes 4194304 | tf_op jit(solution)/shard_map/roots/pallas_call | solution.py:377
  3.1 3.1 %collective-permute-start.6 = (f32[2,16,128]{2,1,0:T(8,128)S(1)}, f32[2,16,128]{2,1,0:T(8,128)S(1)}, u32[]{:S(2)}, u32[]{:S(2)}) collective-permute-start(f32[2,16,128]{2,1,0:T(8,128)S(1)} %get-tuple-element.55), channel_id=1, source_target_pairs={{0,8},{16,24},{8,0},{24,16},{1,9},{17,25},{9,1},{25,17},{2,10},{18... | collective-permute-start | bytes 49160 | tf_op jit(solution)/shard_map/ppermute | solution.py:328
  6.2 0.7 collective-permute-start.7
  6.8 10.0 %all-gather = f32[72,16,128]{2,1,0:T(8,128)S(1)} all-gather(f32[9,16,128]{2,1,0:T(8,128)S(1)} %get-tuple-element.54.refs_6_), channel_id=2, replica_groups=mesh['group'=4,'row'=8] {'row'}, dimensions={0}, use_global_device_ids=true | all-gather | bytes 663552 | tf_op jit(solution)/shard_map/all_gather | solution.py:405
  16.8 2.9 %apply.2 = (f32[8,16,128]{2,1,0:T(8,128)S(1)}, f32[16,16]{1,0:T(8,128)S(1)}, f32[8,16,128]{2,1,0:T(8,128)S(1)}, f32[16,16,128]{2,1,0:T(8,128)}, f32[2,16,128]{2,...) custom-call(s32[8]{0:T(128)} %refs_0_.5, s32[8,16]{1,0:T(8,128)} %refs_1_.5, s32[2,8]{1,0:T(2,128)} %bitcast.108, ...), custom_call_target="tpu_custom_call" | custom-call | flops 134217728 | bytes 4194304 | tf_op jit(solution)/shard_map/apply/pallas_call | solution.py:431
  19.8 3.4 %all-to-all-start = ((f32[16,16,128]{2,1,0:T(8,128)}), f32[16,16,128]{2,1,0:T(8,128)S(1)}, u32[]{:S(2)}, u32[]{:S(2)}) async-start(f32[16,16,128]{2,1,0:T(8,128)} %get-tuple-element.58), calls=%async_computation | async-start | bytes 262144 | tf_op jit(solution)/shard_map/all_to_all | solution.py:407
  23.2 4.5 %collective-permute-start.8 = (f32[2,16,128]{2,1,0:T(8,128)S(1)}, f32[2,16,128]{2,1,0:T(8,128)S(1)}, u32[]{:S(2)}, u32[]{:S(2)}) collective-permute-start(f32[2,16,128]{2,1,0:T(8,128)S(1)} %get-tuple-element.59), channel_id=1, source_target_pairs={{0,8},{16,24},{8,0},{24,16},{1,9},{17,25},{9,1},{25,17},{2,10},{18... | collective-permute-start | bytes 49160 | tf_op jit(solution)/shard_map/ppermute | solution.py:328
  27.6 0.7 collective-permute-start.9
  28.3 1.1 collective-permute-done.8.refs_7_
  29.4 3.3 %apply.3 = (f32[8,16,128]{2,1,0:T(8,128)S(1)}, f32[16,16]{1,0:T(8,128)S(1)}, f32[8,16,128]{2,1,0:T(8,128)S(1)}, f32[16,16,128]{2,1,0:T(8,128)}, f32[2,16,128]{2,1,0:T(8,128)S(1)}, /*index=5*/f32[2,16,128]{2,1,0:T(8,128)S(1)}) custom-call(s32[8]{0:T(128)} %refs_0_.5, s32[8,16]{1,0:T(8,128)} %refs_1_.5, bf16[16384,128]{1,0:T(8,128)(2,1)} %bitcast.99, ...), custom_call_target="tpu_custom_call" | custom-call | flops 134217728 | bytes 4194304 | tf_op jit(solution)/shard_map/apply/pallas_call | solution.py:431
  32.7 4.2 %all-to-all-start.1 = ((f32[16,16,128]{2,1,0:T(8,128)}), f32[16,16,128]{2,1,0:T(8,128)S(1)}, u32[]{:S(2)}, u32[]{:S(2)}) async-start(f32[16,16,128]{2,1,0:T(8,128)} %get-tuple-element.63), calls=%async_computation.1 | async-start | bytes 262144 | tf_op jit(solution)/shard_map/all_to_all | solution.py:407
  36.9 3.9 %collective-permute-start.10 = (f32[2,16,128]{2,1,0:T(8,128)S(1)}, f32[2,16,128]{2,1,0:T(8,128)S(1)}, u32[]{:S(2)}, u32[]{:S(2)}) collective-permute-start(f32[2,16,128]{2,1,0:T(8,128)S(1)} %get-tuple-element.64), channel_id=1, source_target_pairs={{0,8},{16,24},{8,0},{24,16},{1,9},{17,25},{9,1},{25,17},{2,10},{18... | collective-permute-start | bytes 49160 | tf_op jit(solution)/shard_map/ppermute | solution.py:328
  40.8 0.7 collective-permute-start.11
  41.5 1.1 collective-permute-done.10.refs_7_
  42.6 3.7 %apply_last.1 = (f32[8,16,128]{2,1,0:T(8,128)S(1)}, f32[32,8,128]{2,1,0:T(8,128)}) custom-call(s32[8]{0:T(128)} %refs_0_.5, s32[8,16]{1,0:T(8,128)} %refs_1_.5, bf16[16384,128]{1,0:T(8,128)(2,1)} %bitcast.100, bf16[11264,128]{1,0:T(8,128)(2,1)S(1)} %get-tuple-element.51.refs_4_.refs_3_, f32[8,1,128]{2,1,0:T(1,128)S(1)} %get-tuple-element.52.refs_5_.refs_4_, ...), custom_call_target="tpu_custom_call" | custom-call | flops 134217728 | bytes 4194304 | tf_op jit(solution)/shard_map/apply_last/pallas_call | solution.py:431
  46.3 6.6 %all-to-all-start.2 = ((f32[32,8,128]{2,1,0:T(8,128)}), f32[32,8,128]{2,1,0:T(8,128)S(1)}, u32[]{:S(2)}, u32[]{:S(2)}) async-start(f32[32,8,128]{2,1,0:T(8,128)} %get-tuple-element.68), calls=%async_computation.2 | async-start | bytes 262144 | tf_op jit(solution)/shard_map/all_to_all | solution.py:455
  52.9 8.2 %all-to-all-done.2.grams_ref = f32[32,8,128]{2,1,0:T(8,128)S(1)} async-done(((f32[32,8,128]{2,1,0:T(8,128)}), f32[32,8,128]{2,1,0:T(8,128)S(1)}, u32[]{:S(2)}, u32[]{:S(2)}) %all-to-all-start.2) | async-done | bytes 131104 | tf_op jit(solution)/shard_map/all_to_all | solution.py:455
  61.2 2.0 finish.1
  63.8 208.7 %conditional.1 = (f32[3,8,16,128]{3,2,1,0:T(8,128)}) conditional(s32[]{:T(128)} %bitcast.38, (bf16[8,16,128,128]{3,2,1,0:T(8,128)(2,1)}, s32[8]{0:T(128)S(1)}, f32[8,16,128]{2,1,0:T(8,128)S(1)}, s32[1,1,8,2]{2,3,1,0:T(2,128)S(1)}, s32[8,16]{1,0:T(8,128)S(1)}) %tuple.33, f32[3,8,16,128]{3,2,1,0:T(8,128)} %get-tuple-element.73), branch_computations={%region_0.11_spmd, %region_7.12_spmd} | conditional | flops 1235852416 | bytes 33198924 | solution.py:468
  63.8 4.4 %multiply_reduce_fusion = f32[8,16,128]{2,1,0:T(8,128)S(1)} fusion(bf16[8,16,128,128]{3,2,1,0:T(8,128)(2,1)} %get-tuple-element.22), kind=kLoop, calls=%fused_computation.6 | loop fusion | flops 6275072 | bytes 4259840 | tf_op jit(solution)/shard_map/cond/branch_0_fun/btij,bt->bi/reduce_sum | solution.py:339
  68.5 2.6 collective-permute-start
  71.1 1.3 collective-permute-start.1
  72.4 9.0 %all_gather.10 = f32[64,16,128]{2,1,0:T(8,128)S(1)} all-gather(f32[8,16,128]{2,1,0:T(8,128)S(1)} %broadcast_multiply_fusion), channel_id=1, replica_groups=mesh['group'=4,'row'=8] {'row'}, dimensions={0}, use_global_device_ids=true | all-gather | bytes 589824 | tf_op jit(solution)/shard_map/cond/branch_0_fun/all_gather | solution.py:347
  81.7 0.6 gather_fusion
  82.4 0.8 gather_fusion.1
  83.2 5.2 %fusion.2 = f32[8,16,128]{2,1,0:T(8,128)S(1)} fusion(bf16[8,16,128,128]{3,2,1,0:T(8,128)(2,1)} %get-tuple-element.22, f32[8,16,16,128]{3,2,1,0:T(8,128)S(1)} %bitcast.102, f32[8,16]{1,0:T(8,128)S(1)} %get-tuple-element.96, pred[8,16]{1,0:T(8,128)(4,1)S(1)} %compare_and_fusion, f32[8,128]{1,0:T(8,128)S(1)} %add_power_fusion), kind=kOutput, calls=%fused_computation.13 | convolution fusion | flops 403193856 | bytes 5313152 | tf_op jit(solution)/shard_map/cond/branch_0_fun/btij,btkj->bki/dot_general | solution.py:350
  88.4 0.2 convolution_bitcast_fusion.9
  88.5 40.6 %psum.18 = f32[16,16]{0,1:T(8,128)S(1)} all-reduce(f32[16,16]{0,1:T(8,128)S(1)} %convolution_bitcast_fusion.9), channel_id=1, replica_groups=mesh['group'=4,'row'=8] {'group','row'}, use_global_device_ids=true, to_apply=%region_2.0 | all-reduce | flops 256 | bytes 2048 | tf_op jit(solution)/shard_map/cond/branch_0_fun/psum | solution.py:355
  129.2 1.5 cholesky.59
  130.7 0.7 compare_reduce_fusion.2
  131.5 0.7 fusion.17
  132.2 1.2 custom-call.7
  133.4 0.2 convolution_bitcast_fusion.8
  133.6 0.2 bitcast_multiply_fusion.1
  133.8 10.6 %all_gather.11 = f32[64,16,128]{2,1,0:T(8,128)S(1)} all-gather(f32[8,16,128]{2,1,0:T(8,128)S(1)} %get-tuple-element.98), channel_id=1, replica_groups=mesh['group'=4,'row'=8] {'row'}, dimensions={0}, use_global_device_ids=true | all-gather | bytes 589824 | tf_op jit(solution)/shard_map/cond/branch_0_fun/all_gather | solution.py:347
  144.4 0.6 gather_fusion.2
  145.0 2.3 collective-permute-start.2
  147.4 1.3 collective-permute-start.3
  148.8 4.2 %collective-permute-done.3 = f32[2,16,128]{2,1,0:T(8,128)S(1)} collective-permute-done((f32[2,16,128]{2,1,0:T(8,128)S(1)}, f32[2,16,128]{2,1,0:T(8,128)S(1)}, u32[]{:S(2)}, u32[]{:S(2)}) %collective-permute-start.3) | collective-permute-done | bytes 16416 | tf_op jit(solution)/shard_map/cond/branch_0_fun/ppermute | solution.py:320
  153.0 0.8 gather_fusion.3
  153.8 5.2 %fusion.1 = f32[8,16,128]{2,1,0:T(8,128)S(1)} fusion(bf16[8,16,128,128]{3,2,1,0:T(8,128)(2,1)} %get-tuple-element.22, f32[8,16,16,128]{3,2,1,0:T(8,128)S(1)} %bitcast.103, f32[8,16]{1,0:T(8,128)S(1)} %get-tuple-element.96, pred[8,16]{1,0:T(8,128)(4,1)S(1)} %compare_and_fusion, f32[8,128]{1,0:T(8,128)S(1)} %add_power_fusion), kind=kOutput, calls=%fused_computation.11 | convolution fusion | flops 403193856 | bytes 5313152 | tf_op jit(solution)/shard_map/cond/branch_0_fun/btij,btkj->bki/dot_general | solution.py:350
  159.0 0.2 convolution_bitcast_fusion.7
  159.1 39.2 %psum.19 = f32[16,16]{0,1:T(8,128)S(1)} all-reduce(f32[16,16]{0,1:T(8,128)S(1)} %convolution_bitcast_fusion.7), channel_id=1, replica_groups=mesh['group'=4,'row'=8] {'group','row'}, use_global_device_ids=true, to_apply=%region_5.9 | all-reduce | flops 256 | bytes 2048 | tf_op jit(solution)/shard_map/cond/branch_0_fun/psum | solution.py:355
  198.4 1.5 cholesky.70
  199.9 0.7 compare_reduce_fusion.1
  200.6 0.7 fusion.18
  201.3 1.2 custom-call.8
  202.5 0.2 convolution_bitcast_fusion.6
  202.7 0.2 bitcast_multiply_fusion
  203.0 10.6 %all_gather.12 = f32[64,16,128]{2,1,0:T(8,128)S(1)} all-gather(f32[8,16,128]{2,1,0:T(8,128)S(1)} %get-tuple-element.100), channel_id=1, replica_groups=mesh['group'=4,'row'=8] {'row'}, dimensions={0}, use_global_device_ids=true | all-gather | bytes 589824 | tf_op jit(solution)/shard_map/cond/branch_0_fun/all_gather | solution.py:347
  213.6 0.6 gather_fusion.4
  214.2 2.6 collective-permute-start.4
  216.7 1.3 collective-permute-start.5
  218.2 4.2 %collective-permute-done.5 = f32[2,16,128]{2,1,0:T(8,128)S(1)} collective-permute-done((f32[2,16,128]{2,1,0:T(8,128)S(1)}, f32[2,16,128]{2,1,0:T(8,128)S(1)}, u32[]{:S(2)}, u32[]{:S(2)}) %collective-permute-start.5) | collective-permute-done | bytes 16416 | tf_op jit(solution)/shard_map/cond/branch_0_fun/ppermute | solution.py:320
  222.4 0.8 gather_fusion.5
  223.2 5.2 %fusion = f32[8,16,128]{2,1,0:T(8,128)S(1)} fusion(bf16[8,16,128,128]{3,2,1,0:T(8,128)(2,1)} %get-tuple-element.22, f32[8,16,16,128]{3,2,1,0:T(8,128)S(1)} %bitcast.101, f32[8,16]{1,0:T(8,128)S(1)} %get-tuple-element.96, pred[8,16]{1,0:T(8,128)(4,1)S(1)} %compare_and_fusion, f32[8,128]{1,0:T(8,128)S(1)} %add_power_fusion), kind=kOutput, calls=%fused_computation.9 | convolution fusion | flops 403193856 | bytes 5313152 | tf_op jit(solution)/shard_map/cond/branch_0_fun/btij,btkj->bki/dot_general | solution.py:350
  228.5 38.7 %psum.20 = f32[16,16]{0,1:T(8,128)S(1)} all-reduce(f32[16,16]{0,1:T(8,128)S(1)} %convolution_bitcast_fusion.5), channel_id=1, replica_groups=mesh['group'=4,'row'=8] {'group','row'}, use_global_device_ids=true, to_apply=%region_6.10 | all-reduce | flops 256 | bytes 2048 | tf_op jit(solution)/shard_map/cond/branch_0_fun/psum | solution.py:355
  267.3 1.5 cholesky.81
  268.8 0.7 compare_reduce_fusion
  269.5 0.7 fusion.19
  270.2 1.2 custom-call.9
  271.4 0.2 convolution_bitcast_fusion.4
  271.6 0.2 convolution_bitcast_fusion
  271.8 0.7 pad_maximum_fusion.3
  (54 shorter events, 1.5 us)
Async XLA Ops:
  3.1 13.8 %collective-permute-start.6 = (f32[2,16,128]{2,1,0:T(8,128)S(1)}, f32[2,16,128]{2,1,0:T(8,128)S(1)}, u32[]{:S(2)}, u32[]{:S(2)}) collective-permute-start(f32[2,16,128]{2,1,0:T(8,128)S(1)} %get-tuple-element.55), channel_id=1, source_target_pairs={{0,8},{16,24},{8,0},{24,16},{1,9},{17,25},{9,1},{25,17},{2,10},{18... | collective-permute-start | bytes 49160 | tf_op jit(solution)/shard_map/ppermute | solution.py:328
  6.2 10.7 %collective-permute-start.7 = (f32[2,16,128]{2,1,0:T(8,128)S(1)}, f32[2,16,128]{2,1,0:T(8,128)S(1)}, u32[]{:S(2)}, u32[]{:S(2)}) collective-permute-start(f32[2,16,128]{2,1,0:T(8,128)S(1)} %get-tuple-element.56), channel_id=1, source_target_pairs={{8,16},{16,8},{9,17},{17,9},{10,18},{18,10},{11,19},{19,11},{12,20... | collective-permute-start | bytes 49160 | tf_op jit(solution)/shard_map/ppermute | solution.py:328
  19.8 9.6 %all-to-all-start = ((f32[16,16,128]{2,1,0:T(8,128)}), f32[16,16,128]{2,1,0:T(8,128)S(1)}, u32[]{:S(2)}, u32[]{:S(2)}) async-start(f32[16,16,128]{2,1,0:T(8,128)} %get-tuple-element.58), calls=%async_computation | async-start | bytes 262144 | tf_op jit(solution)/shard_map/all_to_all | solution.py:407
  23.2 6.2 %collective-permute-start.8 = (f32[2,16,128]{2,1,0:T(8,128)S(1)}, f32[2,16,128]{2,1,0:T(8,128)S(1)}, u32[]{:S(2)}, u32[]{:S(2)}) collective-permute-start(f32[2,16,128]{2,1,0:T(8,128)S(1)} %get-tuple-element.59), channel_id=1, source_target_pairs={{0,8},{16,24},{8,0},{24,16},{1,9},{17,25},{9,1},{25,17},{2,10},{18... | collective-permute-start | bytes 49160 | tf_op jit(solution)/shard_map/ppermute | solution.py:328
  27.6 1.7 collective-permute-start.9
  32.7 31.1 %copy-start = (f32[8,16,128]{2,1,0:T(8,128)S(1)}, f32[8,16,128]{2,1,0:T(8,128)}, u32[]{:S(2)}) copy-start(f32[8,16,128]{2,1,0:T(8,128)} %basis_hbm.1) | copy-start | bytes 196612
  32.7 31.1 %copy-start.1 = (s32[8,16]{1,0:T(8,128)S(1)}, s32[8,16]{1,0:T(8,128)}, u32[]{:S(2)}) copy-start(s32[8,16]{1,0:T(8,128)} %refs_1_.5) | copy-start | bytes 1540
  32.7 31.1 %copy-start.2 = (s32[8]{0:T(128)S(1)}, s32[8]{0:T(128)}, u32[]{:S(2)}) copy-start(s32[8]{0:T(128)} %refs_0_.5) | copy-start | bytes 100
  32.7 31.0 %copy-start.3 = (s32[1,1,8,2]{2,3,1,0:T(2,128)S(1)}, s32[1,1,8,2]{2,3,1,0:T(2,128)}, u32[]{:S(2)}) copy-start(s32[1,1,8,2]{2,3,1,0:T(2,128)} %param.18) | copy-start | bytes 196
  32.7 9.8 %all-to-all-start.1 = ((f32[16,16,128]{2,1,0:T(8,128)}), f32[16,16,128]{2,1,0:T(8,128)S(1)}, u32[]{:S(2)}, u32[]{:S(2)}) async-start(f32[16,16,128]{2,1,0:T(8,128)} %get-tuple-element.63), calls=%async_computation.1 | async-start | bytes 262144 | tf_op jit(solution)/shard_map/all_to_all | solution.py:407
  36.9 5.6 %collective-permute-start.10 = (f32[2,16,128]{2,1,0:T(8,128)S(1)}, f32[2,16,128]{2,1,0:T(8,128)S(1)}, u32[]{:S(2)}, u32[]{:S(2)}) collective-permute-start(f32[2,16,128]{2,1,0:T(8,128)S(1)} %get-tuple-element.64), channel_id=1, source_target_pairs={{0,8},{16,24},{8,0},{24,16},{1,9},{17,25},{9,1},{25,17},{2,10},{18... | collective-permute-start | bytes 49160 | tf_op jit(solution)/shard_map/ppermute | solution.py:328
  40.8 1.7 collective-permute-start.11
  46.3 14.9 %all-to-all-start.2 = ((f32[32,8,128]{2,1,0:T(8,128)}), f32[32,8,128]{2,1,0:T(8,128)S(1)}, u32[]{:S(2)}, u32[]{:S(2)}) async-start(f32[32,8,128]{2,1,0:T(8,128)} %get-tuple-element.68), calls=%async_computation.2 | async-start | bytes 262144 | tf_op jit(solution)/shard_map/all_to_all | solution.py:455
  68.5 13.9 %collective-permute-start = (f32[2,16,128]{2,1,0:T(8,128)S(1)}, f32[2,16,128]{2,1,0:T(8,128)S(1)}, u32[]{:S(2)}, u32[]{:S(2)}) collective-permute-start(f32[2,16,128]{2,1,0:T(8,128)S(1)} %get-tuple-element.94), channel_id=1, source_target_pairs={{0,8},{8,16},{16,24},{1,9},{9,17},{17,25},{2,10},{10,18},{18,26},{... | collective-permute-start | bytes 49160 | tf_op jit(solution)/shard_map/cond/branch_0_fun/ppermute | solution.py:319
  71.1 11.3 %collective-permute-start.1 = (f32[2,16,128]{2,1,0:T(8,128)S(1)}, f32[2,16,128]{2,1,0:T(8,128)S(1)}, u32[]{:S(2)}, u32[]{:S(2)}) collective-permute-start(f32[2,16,128]{2,1,0:T(8,128)S(1)} %get-tuple-element.95), channel_id=1, source_target_pairs={{8,0},{16,8},{24,16},{9,1},{17,9},{25,17},{10,2},{18,10},{26,18},{... | collective-permute-start | bytes 49160 | tf_op jit(solution)/shard_map/cond/branch_0_fun/ppermute | solution.py:320
  145.0 3.8 %collective-permute-start.2 = (f32[2,16,128]{2,1,0:T(8,128)S(1)}, f32[2,16,128]{2,1,0:T(8,128)S(1)}, u32[]{:S(2)}, u32[]{:S(2)}) collective-permute-start(f32[2,16,128]{2,1,0:T(8,128)S(1)} %get-tuple-element.92), channel_id=1, source_target_pairs={{0,8},{8,16},{16,24},{1,9},{9,17},{17,25},{2,10},{10,18},{18,26},{... | collective-permute-start | bytes 49160 | tf_op jit(solution)/shard_map/cond/branch_0_fun/ppermute | solution.py:319
  147.4 5.6 %collective-permute-start.3 = (f32[2,16,128]{2,1,0:T(8,128)S(1)}, f32[2,16,128]{2,1,0:T(8,128)S(1)}, u32[]{:S(2)}, u32[]{:S(2)}) collective-permute-start(f32[2,16,128]{2,1,0:T(8,128)S(1)} %get-tuple-element.93), channel_id=1, source_target_pairs={{8,0},{16,8},{24,16},{9,1},{17,9},{25,17},{10,2},{18,10},{26,18},{... | collective-permute-start | bytes 49160 | tf_op jit(solution)/shard_map/cond/branch_0_fun/ppermute | solution.py:320
  214.2 4.0 %collective-permute-start.4 = (f32[2,16,128]{2,1,0:T(8,128)S(1)}, f32[2,16,128]{2,1,0:T(8,128)S(1)}, u32[]{:S(2)}, u32[]{:S(2)}) collective-permute-start(f32[2,16,128]{2,1,0:T(8,128)S(1)} %get-tuple-element.90), channel_id=1, source_target_pairs={{0,8},{8,16},{16,24},{1,9},{9,17},{17,25},{2,10},{10,18},{18,26},{... | collective-permute-start | bytes 49160 | tf_op jit(solution)/shard_map/cond/branch_0_fun/ppermute | solution.py:319
  216.7 5.6 %collective-permute-start.5 = (f32[2,16,128]{2,1,0:T(8,128)S(1)}, f32[2,16,128]{2,1,0:T(8,128)S(1)}, u32[]{:S(2)}, u32[]{:S(2)}) collective-permute-start(f32[2,16,128]{2,1,0:T(8,128)S(1)} %get-tuple-element.91), channel_id=1, source_target_pairs={{8,0},{16,8},{24,16},{9,1},{17,9},{25,17},{10,2},{18,10},{26,18},{... | collective-permute-start | bytes 49160 | tf_op jit(solution)/shard_map/cond/branch_0_fun/ppermute | solution.py:320
